TPU v7x, 32 devices: a whole 2x2x4 slice. The times are simulated.
32 devices in a mesh: section: 2 (over x), wide: 16 (over z, y, core).
Axes of the slice: x: 2, y: 2, z: 4, core: 2. Of those that a mesh axis runs over, the one named last changes fastest.
Arguments:
- tokens: bfloat16 [2, 2048, 1152], P(None, 'wide'), may hold values from -6 to 6
- cotangent: bfloat16 [2, 2048, 1152], P(None, 'wide'), may hold values from -6 to 6
- image_of_block: int32 [2, 16], replicated, may hold values from 0 to 3, never falling along the last dimension, each value on 1 to 6 neighbouring positions
- ln1_gain: bfloat16 [2, 1152], P('section', 'wide'), may hold values from 0.5 to 1.5
- ln1_bias: bfloat16 [2, 1152], P('section', 'wide'), may hold values from -1.25 to 1.25
- qkv_weight: bfloat16 [2, 1152, 3456], P('section', 'wide'), may hold values from -0.1875 to 0.1875
- qv_bias: bfloat16 [2, 2, 1152], P('section', None, 'wide'), may hold values from -1.25 to 1.25
- out_weight: bfloat16 [2, 1152, 1152], P('section', 'wide'), may hold values from -0.75 to 0.75
- out_bias: bfloat16 [2, 1152], P('section', 'wide'), may hold values from -1.25 to 1.25
- ln2_gain: bfloat16 [2, 1152], P('section', 'wide'), may hold values from 0.5 to 1.5
- ln2_bias: bfloat16 [2, 1152], P('section', 'wide'), may hold values from -1.25 to 1.25
- fc1_weight: bfloat16 [2, 1152, 4304], P('section', 'wide'), may hold values from -0.1875 to 0.1875
- fc1_bias: bfloat16 [2, 4304], P('section'), may hold values from -1.75 to 1.75
- fc2_weight: bfloat16 [2, 4304, 1152], P('section', None, 'wide'), may hold values from -0.09375 to 0.09375
- fc2_bias: bfloat16 [2, 1152], P('section', 'wide'), may hold values from -1.25 to 1.25
Outputs:
- section_outputs: bfloat16 [2, 2, 2048, 1152], P('section', None, 'wide')
- section_input_grads: float32 [2, 2, 2048, 1152], P('section', None, 'wide')
- ln1_gain_grad: float32 [2, 1152], P('section', 'wide')
- ln1_bias_grad: float32 [2, 1152], P('section', 'wide')
- qkv_weight_grad: float32 [2, 1152, 3456], P('section', 'wide')
- qv_bias_grad: float32 [2, 2, 1152], P('section', None, 'wide')
- out_weight_grad: float32 [2, 1152, 1152], P('section', 'wide')
- out_bias_grad: float32 [2, 1152], P('section', 'wide')
- ln2_gain_grad: float32 [2, 1152], P('section', 'wide')
- ln2_bias_grad: float32 [2, 1152], P('section', 'wide')
- fc1_weight_grad: float32 [2, 1152, 4304], P('section', 'wide')
- fc1_bias_grad: float32 [2, 4304], P('section')
- fc2_weight_grad: float32 [2, 4304, 1152], P('section', None, 'wide')
- fc2_bias_grad: float32 [2, 1152], P('section', 'wide')
Inputs may be any that keep to these rules, and one draw needn't show every extreme that they name: `image_of_block`: in each micro-batch the image numbers never fall along the blocks and each image covers 1 to 6 consecutive blocks; some image covers exactly 6.
All inputs are finite; a program needn't handle non-finite values.
Results may differ from a plain program's by a relative error of at most 0.014.
Values may be sent and summed in bfloat16 or wider, within the bound.
A program may use at most 320 MiB of HBM per device.

v0:
```python
import math

import jax
import jax.numpy as jnp
from jax import lax
from jax.sharding import PartitionSpec as P

D = 1152
HEADS = 16
HEAD_DIM = 72
BLOCK = 128
BLK_DEV = 1
REACH = 5


EPSILON = 1e-06
MASKED_SCORE = -1e30


def shifted(value, axis, steps):
    count = lax.axis_size(axis)
    initial, last = (max(0, -steps), min(count, count - steps))
    return lax.ppermute(value, axis, [(source, source + steps) for source in range(initial, last)])


def layer_norm(values_in, scale_gain, shift_bias):
    row_mean = jnp.mean(values_in, axis=-1, keepdims=True)
    centred = values_in - row_mean
    row_var = jnp.mean(centred * centred, axis=-1, keepdims=True)
    return centred * lax.rsqrt(row_var + EPSILON) * scale_gain + shift_bias


def gelu_tanh(pre_value):
    return jax.nn.gelu(pre_value, approximate=True)


def heads_of(values_in):
    return values_in.reshape(values_in.shape[0], HEADS, HEAD_DIM)


def image_mask(image_of_block, batch_slot, wide_rank):
    padding = REACH * BLK_DEV
    padded = jnp.pad(image_of_block, ((0, 0), (padding, padding)), constant_values=-1)
    image_row = lax.dynamic_index_in_dim(padded, batch_slot, 0, keepdims=False)
    key_blocks = lax.dynamic_slice_in_dim(image_row, wide_rank * BLK_DEV, (2 * REACH + 1) * BLK_DEV)
    query_blocks = lax.dynamic_slice_in_dim(image_row, wide_rank * BLK_DEV + padding, BLK_DEV)
    return jnp.repeat(query_blocks, BLOCK)[:, None] == jnp.repeat(key_blocks, BLOCK)[None, :]


def keep_slot(buffer_all, new_value, batch_slot, is_live):
    previous = lax.dynamic_index_in_dim(buffer_all, batch_slot, 0, keepdims=False)
    chosen = jnp.where(is_live, new_value, previous)
    return lax.dynamic_update_index_in_dim(buffer_all, chosen, batch_slot, 0)


def near_keys(key_own, value_own, backward_pass):
    key_parts = []
    value_parts = []
    for offset in range(-REACH, REACH + 1):
        if offset == 0:
            received = (key_own, value_own)
        elif backward_pass:
            received = shifted((key_own, value_own), "wide", -offset)
        else:
            received = shifted((key_own, value_own), "wide", -offset)
        key_parts.append(received[0])
        value_parts.append(received[1])
    return (jnp.concatenate(key_parts, axis=0), jnp.concatenate(value_parts, axis=0))


def return_key_grads(key_terms, value_terms):
    row_count = key_terms.shape[0] // (2 * REACH + 1)
    key_total = key_terms[REACH * row_count : (REACH + 1) * row_count]
    value_total = value_terms[REACH * row_count : (REACH + 1) * row_count]
    for position, offset in enumerate(range(-REACH, REACH + 1)):
        if offset != 0:
            piece_pair = (
                key_terms[position * row_count : (position + 1) * row_count],
                value_terms[position * row_count : (position + 1) * row_count],
            )
            received = shifted((piece_pair[0], piece_pair[1]), "wide", offset)
            key_total = key_total + received[0]
            value_total = value_total + received[1]
    return (key_total, value_total)


def project_qkv(layer_in, weights):
    layer_float = layer_in.astype(jnp.float32)
    normed_one = layer_norm(
        layer_float, weights[0].astype(jnp.float32), weights[1].astype(jnp.float32)
    ).astype(jnp.bfloat16)
    mixed = jnp.dot(normed_one, weights[2], preferred_element_type=jnp.float32)
    queries = (mixed[:, :D] + weights[3][0].astype(jnp.float32)).astype(jnp.bfloat16)
    key_own = mixed[:, D : 2 * D].astype(jnp.bfloat16)
    value_own = (mixed[:, 2 * D :] + weights[3][1].astype(jnp.float32)).astype(jnp.bfloat16)
    return (layer_float, normed_one, queries, key_own, value_own)


def attention_probs(queries, keys_near, same_image):
    score_scale = 1.0 / math.sqrt(HEAD_DIM)
    scores = (
        jnp.einsum(
            "qhd,khd->hqk",
            heads_of(queries),
            heads_of(keys_near),
            preferred_element_type=jnp.float32,
        )
        * score_scale
    )
    scores = jnp.where(same_image[None], scores, MASKED_SCORE)
    row_max = jnp.max(scores, axis=-1, keepdims=True)
    exponent = jnp.exp(scores - row_max)
    return exponent / jnp.sum(exponent, axis=-1, keepdims=True)


def finish_layer(layer_float, queries, keys_near, values_near, same_image, weights, hidden_bias):
    probs = attention_probs(queries, keys_near, same_image)
    probs_low = probs.astype(jnp.bfloat16)
    attended = jnp.einsum(
        "hqk,khd->qhd", probs_low, heads_of(values_near), preferred_element_type=jnp.float32
    )
    attended = attended.reshape(queries.shape[0], D).astype(jnp.bfloat16)
    residual = (
        layer_float
        + jnp.dot(attended, weights[4], preferred_element_type=jnp.float32)
        + weights[5].astype(jnp.float32)
    )
    normed_two = layer_norm(
        residual, weights[6].astype(jnp.float32), weights[7].astype(jnp.float32)
    ).astype(jnp.bfloat16)
    hidden_pre = jnp.dot(
        normed_two, weights[8], preferred_element_type=jnp.float32
    ) + hidden_bias.astype(jnp.float32)
    hidden = gelu_tanh(hidden_pre).astype(jnp.bfloat16)
    output = (
        residual
        + jnp.dot(hidden, weights[9], preferred_element_type=jnp.float32)
        + weights[10].astype(jnp.float32)
    )
    return (probs, probs_low, attended, residual, normed_two, hidden_pre, hidden, output)


def layer_backward(
    layer_float,
    normed_one,
    queries,
    keys_near,
    values_near,
    same_image,
    weights,
    hidden_bias,
    grad_out,
):
    score_scale = 1.0 / math.sqrt(HEAD_DIM)
    probs, probs_low, attended, residual, normed_two, hidden_pre, hidden, output = finish_layer(
        layer_float, queries, keys_near, values_near, same_image, weights, hidden_bias
    )
    feed_grad = grad_out.astype(jnp.bfloat16)
    grad_fc2_weight = jnp.einsum("tf,td->fd", hidden, feed_grad, preferred_element_type=jnp.float32)
    grad_fc2_bias = jnp.sum(feed_grad.astype(jnp.float32), axis=0)
    hidden_grad = jnp.einsum("td,fd->tf", feed_grad, weights[9], preferred_element_type=jnp.float32)
    primal_gelu, gelu_pull = jax.vjp(gelu_tanh, hidden_pre)
    pre_grad = gelu_pull(hidden_grad)[0].astype(jnp.bfloat16)
    grad_fc1_bias = jnp.sum(pre_grad.astype(jnp.float32), axis=0)
    grad_fc1_weight = jnp.einsum(
        "td,tf->df", normed_two, pre_grad, preferred_element_type=jnp.float32
    )
    normed_two_grad = jnp.einsum(
        "tf,df->td", pre_grad, weights[8], preferred_element_type=jnp.float32
    )
    primal_two, norm_two_pull = jax.vjp(
        layer_norm, residual, weights[6].astype(jnp.float32), weights[7].astype(jnp.float32)
    )
    residual_part, grad_ln2_gain, grad_ln2_bias = norm_two_pull(normed_two_grad)
    residual_grad = grad_out + residual_part
    branch_grad = residual_grad.astype(jnp.bfloat16)
    grad_out_bias = jnp.sum(branch_grad.astype(jnp.float32), axis=0)
    grad_out_weight = jnp.einsum(
        "tc,td->cd", attended, branch_grad, preferred_element_type=jnp.float32
    )
    attended_grad = jnp.einsum(
        "td,cd->tc", branch_grad, weights[4], preferred_element_type=jnp.float32
    ).astype(jnp.bfloat16)
    attended_heads = heads_of(attended_grad)
    probs_grad = jnp.einsum(
        "qhd,khd->hqk", attended_heads, heads_of(values_near), preferred_element_type=jnp.float32
    )
    value_terms = jnp.einsum(
        "hqk,qhd->khd", probs_low, attended_heads, preferred_element_type=jnp.float32
    )
    score_grad = (
        probs * (probs_grad - jnp.sum(probs * probs_grad, axis=-1, keepdims=True))
    ).astype(jnp.bfloat16)
    query_grad = (
        jnp.einsum(
            "hqk,khd->qhd", score_grad, heads_of(keys_near), preferred_element_type=jnp.float32
        )
        * score_scale
    )
    query_grad = query_grad.reshape(queries.shape[0], D).astype(jnp.bfloat16)
    key_terms = (
        jnp.einsum(
            "hqk,qhd->khd", score_grad, heads_of(queries), preferred_element_type=jnp.float32
        )
        * score_scale
    )
    key_total, value_total = return_key_grads(key_terms.reshape(-1, D), value_terms.reshape(-1, D))
    key_grad = key_total.astype(jnp.bfloat16)
    value_grad = value_total.astype(jnp.bfloat16)
    grad_qv_bias = jnp.stack(
        [
            jnp.sum(query_grad.astype(jnp.float32), axis=0),
            jnp.sum(value_grad.astype(jnp.float32), axis=0),
        ]
    )
    mixed_grad = jnp.concatenate([query_grad, key_grad, value_grad], axis=1)
    grad_qkv_weight = jnp.einsum(
        "tc,tk->ck", normed_one, mixed_grad, preferred_element_type=jnp.float32
    )
    normed_one_grad = jnp.einsum(
        "tk,ck->tc", mixed_grad, weights[2], preferred_element_type=jnp.float32
    )
    primal_one, norm_one_pull = jax.vjp(
        layer_norm, layer_float, weights[0].astype(jnp.float32), weights[1].astype(jnp.float32)
    )
    input_part, grad_ln1_gain, grad_ln1_bias = norm_one_pull(normed_one_grad)
    input_grad = residual_grad + input_part
    grad_terms = (
        grad_ln1_gain,
        grad_ln1_bias,
        grad_qkv_weight,
        grad_qv_bias,
        grad_out_weight,
        grad_out_bias,
        grad_ln2_gain,
        grad_ln2_bias,
        grad_fc1_weight,
        grad_fc2_weight,
        grad_fc2_bias,
    )
    return (input_grad, grad_terms, grad_fc1_bias)


def on_device(
    tokens,
    cotangent,
    image_of_block,
    ln1_gain,
    ln1_bias,
    qkv_weight,
    qv_bias,
    out_weight,
    out_bias,
    ln2_gain,
    ln2_bias,
    fc1_weight,
    fc1_bias,
    fc2_weight,
    fc2_bias,
):
    section_rank = lax.axis_index("section")
    wide_rank = lax.axis_index("wide")
    micro_count = tokens.shape[0]
    weights = (
        lax.all_gather(ln1_gain[0], "wide", axis=0, tiled=True),
        lax.all_gather(ln1_bias[0], "wide", axis=0, tiled=True),
        lax.all_gather(qkv_weight[0], "wide", axis=0, tiled=True),
        lax.all_gather(qv_bias[0], "wide", axis=1, tiled=True),
        lax.all_gather(out_weight[0], "wide", axis=0, tiled=True),
        lax.all_gather(out_bias[0], "wide", axis=0, tiled=True),
        lax.all_gather(ln2_gain[0], "wide", axis=0, tiled=True),
        lax.all_gather(ln2_bias[0], "wide", axis=0, tiled=True),
        lax.all_gather(fc1_weight[0], "wide", axis=0, tiled=True),
        lax.all_gather(fc2_weight[0], "wide", axis=1, tiled=True),
        lax.all_gather(fc2_bias[0], "wide", axis=0, tiled=True),
    )
    hidden_bias = fc1_bias[0]
    inputs_kept = jnp.zeros_like(tokens)
    outputs_kept = jnp.zeros_like(tokens)
    incoming = jnp.zeros_like(tokens[0])
    for tick_number in range(micro_count + 1):
        batch_index = tick_number - section_rank
        is_live = (batch_index >= 0) & (batch_index < micro_count)
        batch_slot = jnp.clip(batch_index, 0, micro_count - 1)
        own_tokens = tokens[min(tick_number, micro_count - 1)]
        layer_in = jnp.where(section_rank == 0, own_tokens, incoming)
        same_image = image_mask(image_of_block, batch_slot, wide_rank)
        layer_float, normed_one, queries, key_own, value_own = project_qkv(layer_in, weights)
        keys_near, values_near = near_keys(key_own, value_own, False)
        output = finish_layer(
            layer_float, queries, keys_near, values_near, same_image, weights, hidden_bias
        )[-1]
        output_low = output.astype(jnp.bfloat16)
        inputs_kept = keep_slot(inputs_kept, layer_in, batch_slot, is_live)
        outputs_kept = keep_slot(outputs_kept, output_low, batch_slot, is_live)
        if tick_number < micro_count:
            incoming = shifted(output_low, "section", 1)
    weights_back = (
        lax.all_gather(ln1_gain[0], "wide", axis=0, tiled=True),
        lax.all_gather(ln1_bias[0], "wide", axis=0, tiled=True),
        lax.all_gather(qkv_weight[0], "wide", axis=0, tiled=True),
        lax.all_gather(qv_bias[0], "wide", axis=1, tiled=True),
        lax.all_gather(out_weight[0], "wide", axis=0, tiled=True),
        lax.all_gather(out_bias[0], "wide", axis=0, tiled=True),
        lax.all_gather(ln2_gain[0], "wide", axis=0, tiled=True),
        lax.all_gather(ln2_bias[0], "wide", axis=0, tiled=True),
        lax.all_gather(fc1_weight[0], "wide", axis=0, tiled=True),
        lax.all_gather(fc2_weight[0], "wide", axis=1, tiled=True),
        lax.all_gather(fc2_bias[0], "wide", axis=0, tiled=True),
    )
    grad_totals = tuple((jnp.zeros(array.shape, jnp.float32) for array in weights_back))
    hidden_bias_total = jnp.zeros(hidden_bias.shape, jnp.float32)
    input_grads = jnp.zeros(tokens.shape, jnp.float32)
    incoming_grad = jnp.zeros(tokens.shape[1:], jnp.bfloat16)
    for tick_number in range(micro_count + 1):
        batch_index = tick_number - 1 + section_rank
        is_live = (batch_index >= 0) & (batch_index < micro_count)
        batch_slot = jnp.clip(batch_index, 0, micro_count - 1)
        from_cotangent = cotangent[min(tick_number, micro_count - 1)].astype(jnp.float32)
        grad_out = jnp.where(
            section_rank == 1, from_cotangent, incoming_grad.astype(jnp.float32)
        ) * is_live.astype(jnp.float32)
        layer_in = lax.dynamic_index_in_dim(inputs_kept, batch_slot, 0, keepdims=False)
        same_image = image_mask(image_of_block, batch_slot, wide_rank)
        layer_float, normed_one, queries, key_own, value_own = project_qkv(layer_in, weights_back)
        keys_near, values_near = near_keys(key_own, value_own, True)
        input_grad, grad_terms, hidden_bias_term = layer_backward(
            layer_float,
            normed_one,
            queries,
            keys_near,
            values_near,
            same_image,
            weights_back,
            hidden_bias,
            grad_out,
        )
        grad_totals = tuple(
            (old_total + new_term for old_total, new_term in zip(grad_totals, grad_terms))
        )
        hidden_bias_total = hidden_bias_total + hidden_bias_term
        input_grads = keep_slot(input_grads, input_grad, batch_slot, is_live)
        if tick_number < micro_count:
            incoming_grad = shifted(input_grad.astype(jnp.bfloat16), "section", -1)
    (
        grad_ln1_gain,
        grad_ln1_bias,
        grad_qkv_weight,
        grad_qv_bias,
        grad_out_weight,
        grad_out_bias,
        grad_ln2_gain,
        grad_ln2_bias,
        grad_fc1_weight,
        grad_fc2_weight,
        grad_fc2_bias,
    ) = grad_totals
    row_sums = (
        lax.psum_scatter(grad_ln1_gain, "wide", scatter_dimension=0, tiled=True),
        lax.psum_scatter(grad_ln1_bias, "wide", scatter_dimension=0, tiled=True),
        lax.psum_scatter(grad_qkv_weight, "wide", scatter_dimension=0, tiled=True),
        lax.psum_scatter(grad_out_weight, "wide", scatter_dimension=0, tiled=True),
        lax.psum_scatter(grad_out_bias, "wide", scatter_dimension=0, tiled=True),
        lax.psum_scatter(grad_ln2_gain, "wide", scatter_dimension=0, tiled=True),
        lax.psum_scatter(grad_ln2_bias, "wide", scatter_dimension=0, tiled=True),
        lax.psum_scatter(grad_fc1_weight, "wide", scatter_dimension=0, tiled=True),
        lax.psum_scatter(grad_fc2_bias, "wide", scatter_dimension=0, tiled=True),
    )
    column_sums = (
        lax.psum_scatter(grad_qv_bias, "wide", scatter_dimension=1, tiled=True),
        lax.psum_scatter(grad_fc2_weight, "wide", scatter_dimension=1, tiled=True),
    )
    hidden_bias_sum = lax.psum(hidden_bias_total, "wide")
    return (
        outputs_kept[None],
        input_grads[None],
        row_sums[0][None],
        row_sums[1][None],
        row_sums[2][None],
        column_sums[0][None],
        row_sums[3][None],
        row_sums[4][None],
        row_sums[5][None],
        row_sums[6][None],
        row_sums[7][None],
        hidden_bias_sum[None],
        column_sums[1][None],
        row_sums[8][None],
    )


def solution(mesh):
    in_specs = (
        P(None, "wide", None),
        P(None, "wide", None),
        P(),
        P("section", "wide"),
        P("section", "wide"),
        P("section", "wide", None),
        P("section", None, "wide"),
        P("section", "wide", None),
        P("section", "wide"),
        P("section", "wide"),
        P("section", "wide"),
        P("section", "wide", None),
        P("section", None),
        P("section", None, "wide"),
        P("section", "wide"),
    )
    out_specs = (
        P("section", None, "wide", None),
        P("section", None, "wide", None),
        P("section", "wide"),
        P("section", "wide"),
        P("section", "wide", None),
        P("section", None, "wide"),
        P("section", "wide", None),
        P("section", "wide"),
        P("section", "wide"),
        P("section", "wide"),
        P("section", "wide", None),
        P("section", None),
        P("section", None, "wide"),
        P("section", "wide"),
    )
    return jax.shard_map(
        on_device, mesh=mesh, in_specs=in_specs, out_specs=out_specs, check_vma=False
    )
```

profile of v0, /device:TPU:10, one launch (start us, length us, event | category | flops | bytes accessed | tf_op | source)
XLA Modules:
  0.0 2435.6 jit_solution(13437101935652691484)
XLA Ops:
  17.1 55.0 %all-reduce.17 = (bf16[1152]{0:T(1024)(128)(2,1)S(1)}, bf16[1152]{0:T(1024)(128)(2,1)S(1)}, bf16[1152]{0:T(1024)(128)(2,1)S(1)}, bf16[1152]{0:T(1024)(128)(2,1)S...) all-reduce(bf16[1152]{0:T(1024)(128)(2,1)S(1)} %dynamic-update-slic, ...), channel_id=3, replica_groups=mesh['section'=2,'wide'=16] {'wide'}, use_global_device_ids=true, to_apply=%add.2 | all-reduce | flops 6912 | bytes 27648
  74.5 24.8 %all-gather.3 = bf16[1,2,1152]{1,0,2:T(2,128)(2,1)S(1)} all-gather(bf16[1,2,72]{1,0,2:T(2,128)(2,1)S(1)} %copy.105), channel_id=5, replica_groups=mesh['section'=2,'wide'=16] {'wide'}, dimensions={2}, use_global_device_ids=true | all-gather | bytes 4896 | tf_op jit(solution)/shard_map/all_gather | solution.py:268
  109.1 18.6 fusion.383
  163.3 13.7 collective-permute-start.13
  178.7 19.3 collective-permute-done.12
  198.0 12.6 collective-permute-start.14
  221.5 24.5 %collective-permute-start.3 = (bf16[128,1152]{1,0:T(8,128)(2,1)S(1)}, bf16[128,1152]{1,0:T(8,128)(2,1)S(1)}, u32[]{:S(2)}, u32[]{:S(2)}) collective-permute-start(bf16[128,1152]{1,0:T(8,128)(2,1)S(1)} %get-tuple-element.162), channel_id=1, source_target_pairs={{0,2},{1,3},{2,4},{3,5},{4,6},{5,7},{6,8},{7,9},{8,10},{9,11},{10,... | collective-permute-start | bytes 884744 | tf_op jit(solution)/shard_map/ppermute | solution.py:23
  284.8 21.1 collective-permute-done.8
  332.7 51.9 %collective-permute-done.18 = bf16[128,1152]{1,0:T(8,128)(2,1)S(1)} collective-permute-done((bf16[128,1152]{1,0:T(8,128)(2,1)}, bf16[128,1152]{1,0:T(8,128)(2,1)S(1)}, u32[]{:S(2)}, u32[]{:S(2)}) %collective-permute-start.18) | collective-permute-done | bytes 294944 | tf_op jit(solution)/shard_map/ppermute | solution.py:23
  412.3 13.7 bitcast_dynamic-update-slice_fusion.6
  543.5 10.4 collective-permute-done.39
  561.0 10.6 fusion.580
  581.2 17.6 bitcast_dynamic-update-slice_fusion.5
  636.6 11.6 collective-permute-start.74
  727.4 12.1 collective-permute-done.80
  748.6 10.7 fusion.584
  772.2 11.4 convert_reduce_fusion.2
  845.0 19.5 collective-permute-done.98
  918.8 22.2 collective-permute-done.88
  951.3 12.9 collective-permute-done.85
  1009.1 14.2 collective-permute-start.115
  1103.3 10.7 collective-permute-done.121
  1122.9 10.7 fusion.586
  1148.5 10.4 convert_reduce_fusion.1
  1176.4 11.8 multiply_reduce_fusion.1
  1222.6 20.9 collective-permute-done.139
  1270.1 11.5 collective-permute-done.133
  1297.0 17.4 collective-permute-done.129
  1325.0 16.9 collective-permute-done.126
  1356.6 12.1 collective-permute-start.144
  1479.7 11.8 collective-permute-done.162
  1500.5 10.6 fusion.590
  1526.0 10.7 convert_reduce_fusion
  1605.2 18.3 collective-permute-done.179
  1633.7 17.0 collective-permute-done.177
  1730.1 21.1 collective-permute-done.165
  1774.7 19.8 convolution_add_fusion.3
  1794.5 13.1 convolution_add_fusion.2
  1808.6 11.2 fusion.285
  1819.9 13.7 convolution_add_fusion.1
  1833.6 13.8 convolution_add_fusion
  1910.3 12.6 collective-permute-done.59
  1939.8 10.5 fusion.588
  1983.1 15.9 collective-permute-done.49
  2028.3 16.8 fusion.204
  2052.1 62.0 %all-reduce.16 = (f32[1152]{0:T(1024)S(1)}, f32[1152]{0:T(1024)S(1)}, f32[2,1152]{1,0:T(2,128)S(1)}, f32[1152]{0:T(1024)S(1)}, f32[1152]{0:T(1024)S(1)}, /*index...) all-reduce(f32[1152]{0:T(1024)S(1)} %add_add_fusion.16, ...), channel_id=13, replica_groups=mesh['section'=2,'wide'=16] {'wide'}, use_global_device_ids=true, to_apply=%region_54.55.clone | all-reduce | flops 13520 | bytes 108160
  2119.3 100.6 %reduce-scatter.10.cloned.1.call-done = f32[72,4304]{1,0:T(8,128)} async-done(((f32[1152,4304]{1,0:T(8,128)}), f32[72,4304]{1,0:T(8,128)}) %reduce-scatter.10.cloned.1.call-update) | async-done | bytes 1239568 | tf_op jit(solution)/shard_map/reduce_scatter | solution.py:366
  2219.9 208.7 %reduce-scatter.12.cloned.1.call-done = f32[4304,72]{0,1:T(8,128)} async-done(((f32[4304,1152]{0,1:T(8,128)}), f32[4304,72]{0,1:T(8,128)}) %reduce-scatter.12.cloned.1.call-update) | async-done | bytes 1239568 | tf_op jit(solution)/shard_map/reduce_scatter | solution.py:371
  (1202 shorter events, 1296.0 us)
Async XLA Ops:
  7.2 120.6 %all-gather.16.cloned.1.call-start = ((), (), s32[]{:S(2)}) async-start(), calls=%async_computation.6 | async-start | bytes 8460288 | tf_op jit(solution)/shard_map/all_gather | solution.py:267
  7.9 401.5 %all-gather.18.cloned.1.call-start = ((), (), s32[]{:S(2)}) async-start(), calls=%async_computation.7 | async-start | bytes 2820096 | tf_op jit(solution)/shard_map/all_gather | solution.py:269
  8.7 403.5 %all-gather.22.cloned.1.call-start = ((), (), s32[]{:S(2)}) async-start(), calls=%async_computation.9 | async-start | bytes 10653696 | tf_op jit(solution)/shard_map/all_gather | solution.py:274
  9.4 402.8 %all-gather.20.cloned.1.call-start = ((), (), s32[]{:S(2)}) async-start(), calls=%async_computation.8 | async-start | bytes 10653696 | tf_op jit(solution)/shard_map/all_gather | solution.py:273
  10.0 2109.4 %reduce-scatter.16.cloned.1.call-start = ((), (), s32[]{:S(2)}) async-start(), calls=%async_computation.11 | async-start | bytes 5640192
  139.6 112.6 %collective-permute-start = (bf16[128,1152]{1,0:T(8,128)(2,1)S(1)}, bf16[128,1152]{1,0:T(8,128)(2,1)}, u32[]{:S(2)}, u32[]{:S(2)}) collective-permute-start(bf16[128,1152]{1,0:T(8,128)(2,1)S(1)} %get-tuple-element.162), channel_id=1, source_target_pairs={{0,5},{1,6},{2,7},{3,8},{4,9},{5,10},{6,11},{7,12},{8,13},{9,14},{... | collective-permute-start | bytes 884744 | tf_op jit(solution)/shard_map/ppermute | solution.py:23
  144.5 112.0 %collective-permute-start.1 = (bf16[128,1152]{1,0:T(8,128)(2,1)S(1)}, bf16[128,1152]{1,0:T(8,128)(2,1)}, u32[]{:S(2)}, u32[]{:S(2)}) collective-permute-start(bf16[128,1152]{1,0:T(8,128)(2,1)S(1)} %get-tuple-element.162), channel_id=1, source_target_pairs={{0,4},{1,5},{2,6},{3,7},{4,8},{5,9},{6,10},{7,11},{8,12},{9,13},{1... | collective-permute-start | bytes 884744 | tf_op jit(solution)/shard_map/ppermute | solution.py:23
  146.4 113.7 %collective-permute-start.2 = (bf16[128,1152]{1,0:T(8,128)(2,1)S(1)}, bf16[128,1152]{1,0:T(8,128)(2,1)}, u32[]{:S(2)}, u32[]{:S(2)}) collective-permute-start(bf16[128,1152]{1,0:T(8,128)(2,1)S(1)} %get-tuple-element.162), channel_id=1, source_target_pairs={{0,3},{1,4},{2,5},{3,6},{4,7},{5,8},{6,9},{7,10},{8,11},{9,12},{10... | collective-permute-start | bytes 884744 | tf_op jit(solution)/shard_map/ppermute | solution.py:23
  150.2 47.8 %collective-permute-start.12 = (bf16[128,1152]{1,0:T(8,128)(2,1)}, bf16[128,1152]{1,0:T(8,128)(2,1)S(1)}, u32[]{:S(2)}, u32[]{:S(2)}) collective-permute-start(bf16[128,1152]{1,0:T(8,128)(2,1)} %slice.808), channel_id=1, source_target_pairs={{0,3},{1,4},{2,5},{3,6},{4,7},{5,8},{6,9},{7,10},{8,11},{9,12},{10... | collective-permute-start | bytes 884744 | tf_op jit(solution)/shard_map/ppermute | solution.py:23
  163.3 58.2 %collective-permute-start.13 = (bf16[128,1152]{1,0:T(8,128)(2,1)}, bf16[128,1152]{1,0:T(8,128)(2,1)S(1)}, u32[]{:S(2)}, u32[]{:S(2)}) collective-permute-start(bf16[128,1152]{1,0:T(8,128)(2,1)} %slice.808), channel_id=1, source_target_pairs={{0,2},{1,3},{2,4},{3,5},{4,6},{5,7},{6,8},{7,9},{8,10},{9,11},{10,... | collective-permute-start | bytes 884744 | tf_op jit(solution)/shard_map/ppermute | solution.py:23
  198.0 48.8 %collective-permute-start.14 = (bf16[128,1152]{1,0:T(8,128)(2,1)}, bf16[128,1152]{1,0:T(8,128)(2,1)S(1)}, u32[]{:S(2)}, u32[]{:S(2)}) collective-permute-start(bf16[128,1152]{1,0:T(8,128)(2,1)} %slice.808), channel_id=1, source_target_pairs={{0,1},{1,2},{2,3},{3,4},{4,5},{5,6},{6,7},{7,8},{8,9},{9,10},{10,1... | collective-permute-start | bytes 884744 | tf_op jit(solution)/shard_map/ppermute | solution.py:23
  266.4 49.1 %collective-permute-start.9 = (bf16[128,1152]{1,0:T(8,128)(2,1)S(1)}, bf16[128,1152]{1,0:T(8,128)(2,1)S(1)}, u32[]{:S(2)}, u32[]{:S(2)}) collective-permute-start(bf16[128,1152]{1,0:T(8,128)(2,1)S(1)} %get-tuple-element.162), channel_id=1, source_target_pairs={{5,0},{6,1},{7,2},{8,3},{9,4},{10,5},{11,6},{12,7},{13,8},{14,9},{... | collective-permute-start | bytes 884744 | tf_op jit(solution)/shard_map/ppermute | solution.py:23
  269.2 48.3 %collective-permute-start.15 = (bf16[128,1152]{1,0:T(8,128)(2,1)}, bf16[128,1152]{1,0:T(8,128)(2,1)S(1)}, u32[]{:S(2)}, u32[]{:S(2)}) collective-permute-start(bf16[128,1152]{1,0:T(8,128)(2,1)} %slice.808), channel_id=1, source_target_pairs={{1,0},{2,1},{3,2},{4,3},{5,4},{6,5},{7,6},{8,7},{9,8},{10,9},{11,1... | collective-permute-start | bytes 884744 | tf_op jit(solution)/shard_map/ppermute | solution.py:23
  271.8 46.4 %collective-permute-start.16 = (bf16[128,1152]{1,0:T(8,128)(2,1)}, bf16[128,1152]{1,0:T(8,128)(2,1)S(1)}, u32[]{:S(2)}, u32[]{:S(2)}) collective-permute-start(bf16[128,1152]{1,0:T(8,128)(2,1)} %slice.808), channel_id=1, source_target_pairs={{2,0},{3,1},{4,2},{5,3},{6,4},{7,5},{8,6},{9,7},{10,8},{11,9},{12,... | collective-permute-start | bytes 884744 | tf_op jit(solution)/shard_map/ppermute | solution.py:23
  306.0 78.6 %collective-permute-start.18 = (bf16[128,1152]{1,0:T(8,128)(2,1)}, bf16[128,1152]{1,0:T(8,128)(2,1)S(1)}, u32[]{:S(2)}, u32[]{:S(2)}) collective-permute-start(bf16[128,1152]{1,0:T(8,128)(2,1)} %slice.808), channel_id=1, source_target_pairs={{4,0},{5,1},{6,2},{7,3},{8,4},{9,5},{10,6},{11,7},{12,8},{13,9},{1... | collective-permute-start | bytes 884744 | tf_op jit(solution)/shard_map/ppermute | solution.py:23
  315.5 69.9 %collective-permute-start.19 = (bf16[128,1152]{1,0:T(8,128)(2,1)}, bf16[128,1152]{1,0:T(8,128)(2,1)S(1)}, u32[]{:S(2)}, u32[]{:S(2)}) collective-permute-start(bf16[128,1152]{1,0:T(8,128)(2,1)} %slice.808), channel_id=1, source_target_pairs={{5,0},{6,1},{7,2},{8,3},{9,4},{10,5},{11,6},{12,7},{13,8},{14,9},{... | collective-permute-start | bytes 884744 | tf_op jit(solution)/shard_map/ppermute | solution.py:23
  450.6 46.1 %collective-permute-start.23 = (bf16[128,1152]{1,0:T(8,128)(2,1)S(1)}, bf16[128,1152]{1,0:T(8,128)(2,1)}, u32[]{:S(2)}, u32[]{:S(2)}) collective-permute-start(bf16[128,1152]{1,0:T(8,128)(2,1)S(1)} %get-tuple-element.160), channel_id=1, source_target_pairs={{0,3},{1,4},{2,5},{3,6},{4,7},{5,8},{6,9},{7,10},{8,11},{9,12},{10... | collective-permute-start | bytes 884744 | tf_op jit(solution)/shard_map/ppermute | solution.py:23
  616.3 54.4 %collective-permute-start.62 = (bf16[128,1152]{1,0:T(8,128)(2,1)}, bf16[128,1152]{1,0:T(8,128)(2,1)}, u32[]{:S(2)}, u32[]{:S(2)}) collective-permute-start(bf16[128,1152]{1,0:T(8,128)(2,1)} %get-tuple-element.156), channel_id=1, source_target_pairs={{0,5},{1,6},{2,7},{3,8},{4,9},{5,10},{6,11},{7,12},{8,13},{9,14},{... | collective-permute-start | bytes 884744 | tf_op jit(solution)/shard_map/ppermute | solution.py:23
  618.3 58.4 %collective-permute-start.63 = (bf16[128,1152]{1,0:T(8,128)(2,1)}, bf16[128,1152]{1,0:T(8,128)(2,1)}, u32[]{:S(2)}, u32[]{:S(2)}) collective-permute-start(bf16[128,1152]{1,0:T(8,128)(2,1)} %get-tuple-element.156), channel_id=1, source_target_pairs={{0,4},{1,5},{2,6},{3,7},{4,8},{5,9},{6,10},{7,11},{8,12},{9,13},{1... | collective-permute-start | bytes 884744 | tf_op jit(solution)/shard_map/ppermute | solution.py:23
  622.2 58.2 %collective-permute-start.64 = (bf16[128,1152]{1,0:T(8,128)(2,1)}, bf16[128,1152]{1,0:T(8,128)(2,1)}, u32[]{:S(2)}, u32[]{:S(2)}) collective-permute-start(bf16[128,1152]{1,0:T(8,128)(2,1)} %get-tuple-element.156), channel_id=1, source_target_pairs={{0,3},{1,4},{2,5},{3,6},{4,7},{5,8},{6,9},{7,10},{8,11},{9,12},{10... | collective-permute-start | bytes 884744 | tf_op jit(solution)/shard_map/ppermute | solution.py:23
  820.5 53.2 %collective-permute-start.97 = (f32[128,1152]{0,1:T(8,128)}, f32[128,1152]{0,1:T(8,128)}, u32[]{:S(2)}, u32[]{:S(2)}) collective-permute-start(f32[128,1152]{0,1:T(8,128)} %bitcast.79), channel_id=1, source_target_pairs={{0,1},{1,2},{2,3},{3,4},{4,5},{5,6},{6,7},{7,8},{8,9},{9,10},{10,1... | collective-permute-start | bytes 1769480 | tf_op jit(solution)/shard_map/ppermute | solution.py:23
  828.8 50.1 %collective-permute-start.96 = (f32[128,1152]{0,1:T(8,128)}, f32[128,1152]{0,1:T(8,128)S(1)}, u32[]{:S(2)}, u32[]{:S(2)}) collective-permute-start(f32[128,1152]{0,1:T(8,128)} %bitcast.78), channel_id=1, source_target_pairs={{1,0},{2,1},{3,2},{4,3},{5,4},{6,5},{7,6},{8,7},{9,8},{10,9},{11,1... | collective-permute-start | bytes 1769480 | tf_op jit(solution)/shard_map/ppermute | solution.py:23
  889.3 51.8 %collective-permute-start.88 = (f32[128,1152]{0,1:T(8,128)}, f32[128,1152]{0,1:T(8,128)S(1)}, u32[]{:S(2)}, u32[]{:S(2)}) collective-permute-start(f32[128,1152]{0,1:T(8,128)} %bitcast.856), channel_id=1, source_target_pairs={{0,2},{1,3},{2,4},{3,5},{4,6},{5,7},{6,8},{7,9},{8,10},{9,11},{10,... | collective-permute-start | bytes 1769480 | tf_op jit(solution)/shard_map/ppermute | solution.py:23
  914.6 49.6 %collective-permute-start.85 = (f32[128,1152]{0,1:T(8,128)S(1)}, f32[128,1152]{0,1:T(8,128)}, u32[]{:S(2)}, u32[]{:S(2)}) collective-permute-start(f32[128,1152]{0,1:T(8,128)S(1)} %bitcast.847), channel_id=1, source_target_pairs={{2,0},{3,1},{4,2},{5,3},{6,4},{7,5},{8,6},{9,7},{10,8},{11,9},{12,... | collective-permute-start | bytes 1769480 | tf_op jit(solution)/shard_map/ppermute | solution.py:23
  916.9 48.0 %collective-permute-start.84 = (f32[128,1152]{0,1:T(8,128)S(1)}, f32[128,1152]{0,1:T(8,128)}, u32[]{:S(2)}, u32[]{:S(2)}) collective-permute-start(f32[128,1152]{0,1:T(8,128)S(1)} %bitcast.844), channel_id=1, source_target_pairs={{3,0},{4,1},{5,2},{6,3},{7,4},{8,5},{9,6},{10,7},{11,8},{12,9},{13... | collective-permute-start | bytes 1769480 | tf_op jit(solution)/shard_map/ppermute | solution.py:23
  981.6 64.0 %collective-permute-start.103 = (bf16[128,1152]{1,0:T(8,128)(2,1)}, bf16[128,1152]{1,0:T(8,128)(2,1)}, u32[]{:S(2)}, u32[]{:S(2)}) collective-permute-start(bf16[128,1152]{1,0:T(8,128)(2,1)} %get-tuple-element.154), channel_id=1, source_target_pairs={{0,5},{1,6},{2,7},{3,8},{4,9},{5,10},{6,11},{7,12},{8,13},{9,14},{... | collective-permute-start | bytes 884744 | tf_op jit(solution)/shard_map/ppermute | solution.py:23
  990.9 60.9 %collective-permute-start.104 = (bf16[128,1152]{1,0:T(8,128)(2,1)}, bf16[128,1152]{1,0:T(8,128)(2,1)}, u32[]{:S(2)}, u32[]{:S(2)}) collective-permute-start(bf16[128,1152]{1,0:T(8,128)(2,1)} %get-tuple-element.154), channel_id=1, source_target_pairs={{0,4},{1,5},{2,6},{3,7},{4,8},{5,9},{6,10},{7,11},{8,12},{9,13},{1... | collective-permute-start | bytes 884744 | tf_op jit(solution)/shard_map/ppermute | solution.py:23
  994.6 61.5 %collective-permute-start.105 = (bf16[128,1152]{1,0:T(8,128)(2,1)}, bf16[128,1152]{1,0:T(8,128)(2,1)}, u32[]{:S(2)}, u32[]{:S(2)}) collective-permute-start(bf16[128,1152]{1,0:T(8,128)(2,1)} %get-tuple-element.154), channel_id=1, source_target_pairs={{0,3},{1,4},{2,5},{3,6},{4,7},{5,8},{6,9},{7,10},{8,11},{9,12},{10... | collective-permute-start | bytes 884744 | tf_op jit(solution)/shard_map/ppermute | solution.py:23
  1086.9 59.7 %collective-permute-start.102 = (bf16[128,1152]{1,0:T(8,128)(2,1)}, bf16[128,1152]{1,0:T(8,128)(2,1)}, u32[]{:S(2)}, u32[]{:S(2)}) collective-permute-start(bf16[128,1152]{1,0:T(8,128)(2,1)} %get-tuple-element.77), channel_id=1, source_target_pairs={{16,0},{17,1},{18,2},{19,3},{20,4},{21,5},{22,6},{23,7},{24,8},{25... | collective-permute-start | bytes 884744 | tf_op jit(solution)/shard_map/ppermute | solution.py:23
  1199.3 53.0 %collective-permute-start.138 = (f32[128,1152]{0,1:T(8,128)S(1)}, f32[128,1152]{0,1:T(8,128)S(1)}, u32[]{:S(2)}, u32[]{:S(2)}) collective-permute-start(f32[128,1152]{0,1:T(8,128)S(1)} %bitcast.858), channel_id=1, source_target_pairs={{0,1},{1,2},{2,3},{3,4},{4,5},{5,6},{6,7},{7,8},{8,9},{9,10},{10,1... | collective-permute-start | bytes 1769480 | tf_op jit(solution)/shard_map/ppermute | solution.py:23
  1207.1 49.4 %collective-permute-start.137 = (f32[128,1152]{0,1:T(8,128)}, f32[128,1152]{0,1:T(8,128)S(1)}, u32[]{:S(2)}, u32[]{:S(2)}) collective-permute-start(f32[128,1152]{0,1:T(8,128)} %bitcast.116), channel_id=1, source_target_pairs={{1,0},{2,1},{3,2},{4,3},{5,4},{6,5},{7,6},{8,7},{9,8},{10,9},{11,1... | collective-permute-start | bytes 1769480 | tf_op jit(solution)/shard_map/ppermute | solution.py:23
  1268.2 46.3 %collective-permute-start.129 = (f32[128,1152]{0,1:T(8,128)}, f32[128,1152]{0,1:T(8,128)}, u32[]{:S(2)}, u32[]{:S(2)}) collective-permute-start(f32[128,1152]{0,1:T(8,128)} %bitcast.106), channel_id=1, source_target_pairs={{0,2},{1,3},{2,4},{3,5},{4,6},{5,7},{6,8},{7,9},{8,10},{9,11},{10,... | collective-permute-start | bytes 1769480 | tf_op jit(solution)/shard_map/ppermute | solution.py:23
  1292.8 49.1 %collective-permute-start.126 = (f32[128,1152]{0,1:T(8,128)S(1)}, f32[128,1152]{0,1:T(8,128)S(1)}, u32[]{:S(2)}, u32[]{:S(2)}) collective-permute-start(f32[128,1152]{0,1:T(8,128)S(1)} %bitcast.848), channel_id=1, source_target_pairs={{2,0},{3,1},{4,2},{5,3},{6,4},{7,5},{8,6},{9,7},{10,8},{11,9},{12,... | collective-permute-start | bytes 1769480 | tf_op jit(solution)/shard_map/ppermute | solution.py:23
  1295.1 47.5 %collective-permute-start.125 = (f32[128,1152]{0,1:T(8,128)S(1)}, f32[128,1152]{0,1:T(8,128)S(1)}, u32[]{:S(2)}, u32[]{:S(2)}) collective-permute-start(f32[128,1152]{0,1:T(8,128)S(1)} %bitcast.845), channel_id=1, source_target_pairs={{3,0},{4,1},{5,2},{6,3},{7,4},{8,5},{9,6},{10,7},{11,8},{12,9},{13... | collective-permute-start | bytes 1769480 | tf_op jit(solution)/shard_map/ppermute | solution.py:23
  1356.6 66.2 %collective-permute-start.144 = (bf16[128,1152]{1,0:T(8,128)(2,1)}, bf16[128,1152]{1,0:T(8,128)(2,1)}, u32[]{:S(2)}, u32[]{:S(2)}) collective-permute-start(bf16[128,1152]{1,0:T(8,128)(2,1)} %get-tuple-element.164), channel_id=1, source_target_pairs={{0,5},{1,6},{2,7},{3,8},{4,9},{5,10},{6,11},{7,12},{8,13},{9,14},{... | collective-permute-start | bytes 884744 | tf_op jit(solution)/shard_map/ppermute | solution.py:23
  1368.7 60.3 %collective-permute-start.145 = (bf16[128,1152]{1,0:T(8,128)(2,1)}, bf16[128,1152]{1,0:T(8,128)(2,1)}, u32[]{:S(2)}, u32[]{:S(2)}) collective-permute-start(bf16[128,1152]{1,0:T(8,128)(2,1)} %get-tuple-element.164), channel_id=1, source_target_pairs={{0,4},{1,5},{2,6},{3,7},{4,8},{5,9},{6,10},{7,11},{8,12},{9,13},{1... | collective-permute-start | bytes 884744 | tf_op jit(solution)/shard_map/ppermute | solution.py:23
  1372.4 60.2 %collective-permute-start.146 = (bf16[128,1152]{1,0:T(8,128)(2,1)}, bf16[128,1152]{1,0:T(8,128)(2,1)}, u32[]{:S(2)}, u32[]{:S(2)}) collective-permute-start(bf16[128,1152]{1,0:T(8,128)(2,1)} %get-tuple-element.164), channel_id=1, source_target_pairs={{0,3},{1,4},{2,5},{3,6},{4,7},{5,8},{6,9},{7,10},{8,11},{9,12},{10... | collective-permute-start | bytes 884744 | tf_op jit(solution)/shard_map/ppermute | solution.py:23
  1463.8 60.3 %collective-permute-start.143 = (bf16[128,1152]{1,0:T(8,128)(2,1)}, bf16[128,1152]{1,0:T(8,128)(2,1)}, u32[]{:S(2)}, u32[]{:S(2)}) collective-permute-start(bf16[128,1152]{1,0:T(8,128)(2,1)} %fusion.490), channel_id=1, source_target_pairs={{16,0},{17,1},{18,2},{19,3},{20,4},{21,5},{22,6},{23,7},{24,8},{25... | collective-permute-start | bytes 884744 | tf_op jit(solution)/shard_map/ppermute | solution.py:23
  1564.2 59.2 %collective-permute-start.179 = (f32[128,1152]{0,1:T(8,128)}, f32[128,1152]{0,1:T(8,128)}, u32[]{:S(2)}, u32[]{:S(2)}) collective-permute-start(f32[128,1152]{0,1:T(8,128)} %bitcast.157), channel_id=1, source_target_pairs={{0,1},{1,2},{2,3},{3,4},{4,5},{5,6},{6,7},{7,8},{8,9},{9,10},{10,1... | collective-permute-start | bytes 1769480 | tf_op jit(solution)/shard_map/ppermute | solution.py:23
  1569.5 549.8 %reduce-scatter.14.cloned.1.call-start = ((), (), s32[]{:S(2)}) async-start(), calls=%async_computation.10 | async-start | bytes 16920576
  1589.0 61.7 %collective-permute-start.177 = (f32[128,1152]{0,1:T(8,128)S(1)}, f32[128,1152]{0,1:T(8,128)S(1)}, u32[]{:S(2)}, u32[]{:S(2)}) collective-permute-start(f32[128,1152]{0,1:T(8,128)S(1)} %bitcast.852), channel_id=1, source_target_pairs={{2,0},{3,1},{4,2},{5,3},{6,4},{7,5},{8,6},{9,7},{10,8},{11,9},{12,... | collective-permute-start | bytes 1769480 | tf_op jit(solution)/shard_map/ppermute | solution.py:23
  1593.4 62.4 %collective-permute-start.176 = (f32[128,1152]{0,1:T(8,128)S(1)}, f32[128,1152]{0,1:T(8,128)S(1)}, u32[]{:S(2)}, u32[]{:S(2)}) collective-permute-start(f32[128,1152]{0,1:T(8,128)S(1)} %bitcast.842), channel_id=1, source_target_pairs={{3,0},{4,1},{5,2},{6,3},{7,4},{8,5},{9,6},{10,7},{11,8},{12,9},{13... | collective-permute-start | bytes 1769480 | tf_op jit(solution)/shard_map/ppermute | solution.py:23
  1603.2 58.2 %collective-permute-start.175 = (f32[128,1152]{0,1:T(8,128)S(1)}, f32[128,1152]{0,1:T(8,128)S(1)}, u32[]{:S(2)}, u32[]{:S(2)}) collective-permute-start(f32[128,1152]{0,1:T(8,128)S(1)} %bitcast.835), channel_id=1, source_target_pairs={{4,0},{5,1},{6,2},{7,3},{8,4},{9,5},{10,6},{11,7},{12,8},{13,9},{1... | collective-permute-start | bytes 1769480 | tf_op jit(solution)/shard_map/ppermute | solution.py:23
  1623.4 47.0 %collective-permute-start.174 = (f32[128,1152]{0,1:T(8,128)S(1)}, f32[128,1152]{0,1:T(8,128)S(1)}, u32[]{:S(2)}, u32[]{:S(2)}) collective-permute-start(f32[128,1152]{0,1:T(8,128)S(1)} %bitcast.834), channel_id=1, source_target_pairs={{5,0},{6,1},{7,2},{8,3},{9,4},{10,5},{11,6},{12,7},{13,8},{14,9},{... | collective-permute-start | bytes 1769480 | tf_op jit(solution)/shard_map/ppermute | solution.py:23
  1628.6 53.2 %collective-permute-start.173 = (f32[128,1152]{0,1:T(8,128)}, f32[128,1152]{0,1:T(8,128)}, u32[]{:S(2)}, u32[]{:S(2)}) collective-permute-start(f32[128,1152]{0,1:T(8,128)} %bitcast.149), channel_id=1, source_target_pairs={{0,5},{1,6},{2,7},{3,8},{4,9},{5,10},{6,11},{7,12},{8,13},{9,14},{... | collective-permute-start | bytes 1769480 | tf_op jit(solution)/shard_map/ppermute | solution.py:23
  1703.9 47.3 %collective-permute-start.165 = (f32[128,1152]{0,1:T(8,128)}, f32[128,1152]{0,1:T(8,128)S(1)}, u32[]{:S(2)}, u32[]{:S(2)}) collective-permute-start(f32[128,1152]{0,1:T(8,128)} %bitcast.839), channel_id=1, source_target_pairs={{4,0},{5,1},{6,2},{7,3},{8,4},{9,5},{10,6},{11,7},{12,8},{13,9},{1... | collective-permute-start | bytes 1769480 | tf_op jit(solution)/shard_map/ppermute | solution.py:23
  1764.5 455.4 %reduce-scatter.10.cloned.1.call-start = ((), (), s32[]{:S(2)}) async-start(), calls=%async_computation.4 | async-start | bytes 21307392 | tf_op jit(solution)/shard_map/reduce_scatter | solution.py:366
  1807.6 621.0 %reduce-scatter.12.cloned.1.call-start = ((), (), s32[]{:S(2)}) async-start(), calls=%async_computation.5 | async-start | bytes 21307392 | tf_op jit(solution)/shard_map/reduce_scatter | solution.py:371
  (381 other events, 12276.9 us)
Sparse Core Ops, SparseCore 0:
  10.2 73.7 all-gather.15
  86.1 43.5 all-gather.17
  131.9 109.3 all-gather.21
  243.3 138.5 all-gather.19
  1569.6 134.1 reduce-scatter.15
  1764.6 246.0 reduce-scatter.13
  2015.4 204.4 reduce-scatter.9
  2225.3 203.2 reduce-scatter.11
where the time goes:
time: 2460 us; the launch traced here: 2440 us
  waiting for transfers between devices  924 us (38%)
  starting transfers between devices  570 us (23%)
  matrix products  435 us (18%)
  local copies, waits for them, and re-layouts  261 us (11%)
  blocking collectives  142 us (6%)
  other arithmetic  83.3 us (3%)
    ppermute x184, waiting for transfers between devices, shifted(): lax.ppermute(value, axis, [(source, source + steps) for source in range(i...  612 us
    ppermute x184, starting transfers between devices, shifted(): lax.ppermute(value, axis, [(source, source + steps) for source in range(i...  569 us
    reduce_scatter x1, waiting for transfers between devices, on_device(): lax.psum_scatter(grad_fc2_weight, 'wide', scatter_dimension=1, tiled=True)  209 us
    unnamed x610, local copies, waits for them, and re-layouts  143 us
    unnamed x2, blocking collectives  117 us
    reduce_scatter x1, waiting for transfers between devices, on_device(): lax.psum_scatter(grad_fc1_weight, 'wide', scatter_dimension=0, tiled=True)  101 us
    sub x6, matrix products, attention_probs(): exponent = jnp.exp(scores - row_max)  63.2 us
  transfers between devices with their start and end apart: 192, of which 82 were waited for; matrix products, arithmetic and copies ran while one was open for 22% of the time, Pallas kernels for 0%

commit v1 on v0

--- a/solution.py
+++ b/solution.py
@@ -1,20 +1,567 @@
+import functools
 import math
 
 import jax
 import jax.numpy as jnp
 from jax import lax
+from jax.experimental import pallas as pl
+from jax.experimental.pallas import tpu as pltpu
 from jax.sharding import PartitionSpec as P
 
 D = 1152
 HEADS = 16
 HEAD_DIM = 72
+FF = 4304
 BLOCK = 128
+IMG_BLOCKS = 6
+EPSILON = 1e-06
+MASKED_SCORE = -1e30
+SCALE = 1.0 / math.sqrt(HEAD_DIM)
+MESH = pl.DeviceIdType.MESH
+BF = jnp.bfloat16
+F32 = jnp.float32
+
+
+def place():
+    return lax.axis_index("section"), lax.axis_index("wide")
+
+
+def gather_kernel(count, *refs):
+    ins, outs = refs[:count], refs[count : 2 * count]
+    local_sem, up_send, up_recv, down_send, down_recv, y_send, y_recv, c_send, c_recv = refs[2 * count :]
+    sec, me = place()
+    z = me // 4
+    low = me % 4
+    other_y = me - low + (low + 2) % 4
+    other_c = me - me % 2 + (me + 1) % 2
+
+    barrier = pltpu.get_barrier_semaphore()
+
+    def greet(target):
+        pl.semaphore_signal(barrier, inc=1, device_id=(sec, target), device_id_type=MESH)
+
+    greet(other_y)
+    greet(other_c)
+
+    inside = (z > 0) & (z < 3)
+
+    @pl.when(z > 0)
+    def _():
+        greet(me - 4)
+
+    @pl.when(z < 3)
+    def _():
+        greet(me + 4)
+
+    @pl.when(inside)
+    def _():
+        pl.semaphore_wait(barrier, 4)
+
+    @pl.when(jnp.logical_not(inside))
+    def _():
+        pl.semaphore_wait(barrier, 3)
+
+    def send(piece, origin, sems, slot, target, first=False):
+        return pltpu.make_async_remote_copy(
+            src_ref=ins[piece] if first else outs[piece].at[origin],
+            dst_ref=outs[piece].at[origin],
+            send_sem=sems[0].at[piece, slot],
+            recv_sem=sems[1].at[piece, slot],
+            device_id=(sec, target),
+            device_id_type=MESH,
+        )
+
+    up, down, yy, cc = (up_send, up_recv), (down_send, down_recv), (y_send, y_recv), (c_send, c_recv)
+
+    def mine(piece):
+        return pltpu.make_async_copy(ins[piece], outs[piece].at[me], local_sem.at[piece])
+
+    def along(piece, origin, first, go_up, go_down):
+        zo = origin // 4
+        if go_up:
+
+            @pl.when(z < 3)
+            def _():
+                send(piece, origin, up, zo, me + 4, first).start()
+
+        if go_down:
+
+            @pl.when(z > 0)
+            def _():
+                send(piece, origin, down, zo, me - 4, first).start()
+
+        send(piece, origin, yy, zo, other_y, first).start()
+        send(piece, origin, cc, zo, other_c, first).start()
+
+    for piece in range(count):
+        mine(piece).start()
+        along(piece, me, True, True, True)
+    for step in range(1, 4):
+        for piece in range(count):
+
+            @pl.when(z - step >= 0)
+            def _():
+                origin = me - 4 * step
+                send(piece, origin, up, z - step, me).wait_recv()
+                along(piece, origin, False, True, False)
+
+            @pl.when(z + step <= 3)
+            def _():
+                origin = me + 4 * step
+                send(piece, origin, down, z + step, me).wait_recv()
+                along(piece, origin, False, False, True)
+
+    far = other_y % 4
+    for step in range(4):
+        zo = (z + step) % 4
+        for piece in range(count):
+            origin = zo * 4 + far
+            send(piece, origin, yy, zo, other_y).wait_recv()
+            send(piece, origin, cc, 4 + zo, other_c).start()
+    for zo in range(4):
+        for piece in range(count):
+            send(piece, me, yy, zo, other_y).wait_send()
+            for slot in (zo, 4 + zo):
+                send(piece, me, cc, slot, other_c).wait_send()
+                send(piece, me, cc, slot, other_c).wait_recv()
+
+            @pl.when((zo <= z) & (z < 3))
+            def _():
+                send(piece, me, up, zo, me).wait_send()
+
+            @pl.when((zo >= z) & (z > 0))
+            def _():
+                send(piece, me, down, zo, me).wait_send()
+
+    for piece in range(count):
+        mine(piece).wait()
+
+
+def gather(arrays, cid):
+    count = len(arrays)
+    return pl.pallas_call(
+        functools.partial(gather_kernel, count),
+        out_shape=[jax.ShapeDtypeStruct((16,) + a.shape, a.dtype) for a in arrays],
+        in_specs=[pl.BlockSpec(memory_space=pl.ANY)] * count,
+        out_specs=[pl.BlockSpec(memory_space=pl.ANY)] * count,
+        scratch_shapes=[pltpu.SemaphoreType.DMA((count,))]
+        + [pltpu.SemaphoreType.DMA((count, 4))] * 6
+        + [pltpu.SemaphoreType.DMA((count, 8))] * 2,
+        compiler_params=pltpu.CompilerParams(collective_id=cid, has_side_effects=True),
+    )(*arrays)
+
+
+def exchange_kernel(x_ref, o_ref, local_sem, send_sem, recv_sem):
+    count = x_ref.shape[0]
+    sec, me = place()
+    barrier = pltpu.get_barrier_semaphore()
+    for d in range(1, count):
+        pl.semaphore_signal(barrier, inc=1, device_id=(sec, (me + d) % count), device_id_type=MESH)
+    pl.semaphore_wait(barrier, count - 1)
+    copies = []
+    half = count // 2
+    order = sorted(range(1, count), key=lambda d: abs(d - half))
+    for d in order:
+        target = (me + d) % count
+        copies.append(
+            pltpu.make_async_remote_copy(
+                src_ref=x_ref.at[target],
+                dst_ref=o_ref.at[me],
+                send_sem=send_sem.at[d],
+                recv_sem=recv_sem.at[d],
+                device_id=(sec, target),
+                device_id_type=MESH,
+            )
+        )
+        copies[-1].start()
+    own = pltpu.make_async_copy(x_ref.at[me], o_ref.at[me], local_sem)
+    own.start()
+    own.wait()
+    for copy in copies:
+        copy.wait()
+
+
+def exchange(x, cid):
+    count = x.shape[0]
+    return pl.pallas_call(
+        exchange_kernel,
+        out_shape=jax.ShapeDtypeStruct(x.shape, x.dtype),
+        in_specs=[pl.BlockSpec(memory_space=pl.ANY)],
+        out_specs=pl.BlockSpec(memory_space=pl.ANY),
+        scratch_shapes=[
+            pltpu.SemaphoreType.DMA,
+            pltpu.SemaphoreType.DMA((count,)),
+            pltpu.SemaphoreType.DMA((count,)),
+        ],
+        compiler_params=pltpu.CompilerParams(collective_id=cid, has_side_effects=True),
+    )(x)
+
+
+def dot(a, b):
+    return jnp.dot(a, b, preferred_element_type=F32)
+
+
+def window_bias(img_ref, i, start):
+    own = img_ref[i]
+    return [jnp.where(img_ref[start + j] == own, 0.0, MASKED_SCORE).astype(F32) for j in range(IMG_BLOCKS)]
+
+
+def attn_fwd_kernel(img_ref, first_ref, qkv_ref, o_ref, lse_ref, k_all, vt_all):
+    blocks = qkv_ref.shape[0]
+    for j in range(blocks):
+        part = qkv_ref[j].astype(F32)
+        k_all[j * BLOCK : (j + 1) * BLOCK, :] = part[HEAD_DIM : 2 * HEAD_DIM].T.astype(BF)
+        vt_all[:, j * BLOCK : (j + 1) * BLOCK] = part[2 * HEAD_DIM :].astype(BF)
+
+    def one(i, carry):
+        start = first_ref[i]
+        base = pl.multiple_of(start * BLOCK, BLOCK)
+        qt = qkv_ref[i].astype(F32)[:HEAD_DIM].astype(BF)
+        s = dot(k_all[pl.ds(base, IMG_BLOCKS * BLOCK), :], qt) * SCALE
+        bias = window_bias(img_ref, i, start)
+        parts = [s[j * BLOCK : (j + 1) * BLOCK] + bias[j] for j in range(IMG_BLOCKS)]
+        top = parts[0]
+        for part in parts[1:]:
+            top = jnp.maximum(top, part)
+        top = jnp.max(top, axis=0, keepdims=True)
+        exps = [jnp.exp(part - top) for part in parts]
+        total = exps[0]
+        for part in exps[1:]:
+            total = total + part
+        total = jnp.sum(total, axis=0, keepdims=True)
+        e = jnp.concatenate([part.astype(BF) for part in exps], axis=0)
+        o = dot(vt_all[:, pl.ds(base, IMG_BLOCKS * BLOCK)], e)
+        o_ref[i] = (o / total).astype(BF)
+        lse_ref[i] = top + jnp.log(total)
+        return carry
+
+    lax.fori_loop(0, blocks, one, 0)
+
+
+def window_first(image_row):
+    blocks = image_row.shape[0]
+    first = jnp.argmax(image_row[None, :] == image_row[:, None], axis=1).astype(jnp.int32)
+    return jnp.minimum(first, blocks - IMG_BLOCKS)
+
+
+def attention_fwd(image_row, first, qkv):
+    blocks = qkv.shape[0]
+    return pl.pallas_call(
+        attn_fwd_kernel,
+        out_shape=[
+            jax.ShapeDtypeStruct((blocks, HEAD_DIM, BLOCK), BF),
+            jax.ShapeDtypeStruct((blocks, 1, BLOCK), F32),
+        ],
+        in_specs=[
+            pl.BlockSpec(memory_space=pltpu.SMEM),
+            pl.BlockSpec(memory_space=pltpu.SMEM),
+            pl.BlockSpec(memory_space=pltpu.VMEM),
+        ],
+        out_specs=[pl.BlockSpec(memory_space=pltpu.VMEM)] * 2,
+        scratch_shapes=[
+            pltpu.VMEM((blocks * BLOCK, HEAD_DIM), BF),
+            pltpu.VMEM((HEAD_DIM, blocks * BLOCK), BF),
+        ],
+        compiler_params=pltpu.CompilerParams(vmem_limit_bytes=32 << 20),
+    )(image_row, first, qkv)
+
+
+def attn_bwd_kernel(
+    img_ref, first_ref, qkv_ref, lse_ref, do_ref, o_ref, k_all, kt_all, v_all, q_all, do_all, dk_all, dv_all
+):
+    blocks = qkv_ref.shape[0]
+    for j in range(blocks):
+        part = qkv_ref[j].astype(F32)
+        rows = slice(j * BLOCK, (j + 1) * BLOCK)
+        q_all[rows, :] = part[:HEAD_DIM].T.astype(BF)
+        k_all[rows, :] = part[HEAD_DIM : 2 * HEAD_DIM].T.astype(BF)
+        v_all[rows, :] = part[2 * HEAD_DIM :].T.astype(BF)
+        kt_all[:, rows] = part[HEAD_DIM : 2 * HEAD_DIM].astype(BF)
+        do_all[rows, :] = do_ref[j].astype(F32).T.astype(BF)
+    dk_all[...] = jnp.zeros_like(dk_all)
+    dv_all[...] = jnp.zeros_like(dv_all)
+
+    def one(i, carry):
+        start = first_ref[i]
+        base = pl.multiple_of(start * BLOCK, BLOCK)
+        here = pl.multiple_of(i * BLOCK, BLOCK)
+        near = pl.ds(base, IMG_BLOCKS * BLOCK)
+        qt = qkv_ref[i].astype(F32)[:HEAD_DIM].astype(BF)
+        s = dot(k_all[near, :], qt) * SCALE
+        lse = lse_ref[i]
+        bias = window_bias(img_ref, i, start)
+        probs = [jnp.exp(s[j * BLOCK : (j + 1) * BLOCK] + bias[j] - lse) for j in range(IMG_BLOCKS)]
+        dp = dot(v_all[near, :], do_ref[i])
+        total = probs[0] * dp[:BLOCK]
+        for j in range(1, IMG_BLOCKS):
+            total = total + probs[j] * dp[j * BLOCK : (j + 1) * BLOCK]
+        total = jnp.sum(total, axis=0, keepdims=True)
+        ds = jnp.concatenate(
+            [(probs[j] * (dp[j * BLOCK : (j + 1) * BLOCK] - total)).astype(BF) for j in range(IMG_BLOCKS)], axis=0
+        )
+        p = jnp.concatenate([part.astype(BF) for part in probs], axis=0)
+        dv_all[near, :] += dot(p, do_all[pl.ds(here, BLOCK), :])
+        dk_all[near, :] += dot(ds, q_all[pl.ds(here, BLOCK), :])
+        dq = dot(kt_all[:, near], ds) * SCALE
+        o_ref[i, :HEAD_DIM, :] = dq.astype(BF)
+        return carry
+
+    lax.fori_loop(0, blocks, one, 0)
+    for j in range(blocks):
+        rows = slice(j * BLOCK, (j + 1) * BLOCK)
+        kv = jnp.concatenate([(dk_all[rows, :] * SCALE).T, dv_all[rows, :].T], axis=0)
+        o_ref[j, HEAD_DIM:, :] = kv.astype(BF)
+
+
+def attention_bwd(image_row, first, qkv, lse, grad):
+    blocks = qkv.shape[0]
+    tokens = blocks * BLOCK
+    return pl.pallas_call(
+        attn_bwd_kernel,
+        out_shape=jax.ShapeDtypeStruct((blocks, 3 * HEAD_DIM, BLOCK), BF),
+        in_specs=[
+            pl.BlockSpec(memory_space=pltpu.SMEM),
+            pl.BlockSpec(memory_space=pltpu.SMEM),
+        ]
+        + [pl.BlockSpec(memory_space=pltpu.VMEM)] * 3,
+        out_specs=pl.BlockSpec(memory_space=pltpu.VMEM),
+        scratch_shapes=[
+            pltpu.VMEM((tokens, HEAD_DIM), BF),
+            pltpu.VMEM((HEAD_DIM, tokens), BF),
+            pltpu.VMEM((tokens, HEAD_DIM), BF),
+            pltpu.VMEM((tokens, HEAD_DIM), BF),
+            pltpu.VMEM((tokens, HEAD_DIM), BF),
+            pltpu.VMEM((tokens, HEAD_DIM), F32),
+            pltpu.VMEM((tokens, HEAD_DIM), F32),
+        ],
+        compiler_params=pltpu.CompilerParams(vmem_limit_bytes=32 << 20),
+    )(image_row, first, qkv, lse, grad)
+
+
+def normalised(x):
+    mean = jnp.mean(x, axis=-1, keepdims=True)
+    centred = x - mean
+    rstd = lax.rsqrt(jnp.mean(centred * centred, axis=-1, keepdims=True) + EPSILON)
+    return centred * rstd, rstd
+
+
+def norm_backward(grad, xhat, rstd, gain):
+    g = grad * gain
+    part = g - jnp.mean(g, axis=-1, keepdims=True) - xhat * jnp.mean(g * xhat, axis=-1, keepdims=True)
+    return part * rstd, jnp.sum(grad * xhat, axis=0), jnp.sum(grad, axis=0)
+
+
+def gelu_and_slope(v):
+    c = math.sqrt(2.0 / math.pi)
+    t = jnp.tanh(c * (v + 0.044715 * v * v * v))
+    value = 0.5 * v * (1.0 + t)
+    slope = 0.5 * (1.0 + t) + 0.5 * v * (1.0 - t * t) * c * (1.0 + 3 * 0.044715 * v * v)
+    return value, slope
+
+
+def by_rows(x):
+    return x.T.reshape(HEADS, HEAD_DIM, x.shape[0])
+
+
+def swap(x, bits):
+    return lax.ppermute(x, "wide", [(i, i ^ bits) for i in range(HEADS)])
+
+
+def dw_kernel(count, x_ref, *refs):
+    ys, o_ref = refs[:count], refs[count]
+    for t in range(count):
+        term = dot(x_ref[t], ys[t][...])
+        if t == 0:
+            total = term
+        else:
+            total = total + term
+    o_ref[...] = total.astype(o_ref.dtype)
+
+
+def weight_grad(x, ys, tile):
+    count, rows, block = x.shape
+    cols = ys[0].shape[1]
+    return pl.pallas_call(
+        functools.partial(dw_kernel, count),
+        grid=(pl.cdiv(cols, tile),),
+        out_shape=jax.ShapeDtypeStruct((rows, cols), BF),
+        in_specs=[pl.BlockSpec((count, rows, block), lambda j: (0, 0, 0))]
+        + [pl.BlockSpec((block, tile), lambda j: (0, j))] * count,
+        out_specs=pl.BlockSpec((rows, tile), lambda j: (0, j)),
+        compiler_params=pltpu.CompilerParams(vmem_limit_bytes=48 << 20),
+    )(x, *ys)
+
+
+def on_device(
+    tokens,
+    cotangent,
+    image_of_block,
+    ln1_gain,
+    ln1_bias,
+    qkv_weight,
+    qv_bias,
+    out_weight,
+    out_bias,
+    ln2_gain,
+    ln2_bias,
+    fc1_weight,
+    fc1_bias,
+    fc2_weight,
+    fc2_bias,
+):
+    sec, me = place()
+    micro = tokens.shape[0]
+    low = me % 4
+    own_qkv = qkv_weight[0].reshape(HEAD_DIM, 3, HEADS, HEAD_DIM).transpose(0, 2, 1, 3).reshape(HEAD_DIM, 3 * D)
+    small = jnp.stack(
+        [ln1_gain[0], ln1_bias[0], qv_bias[0, 0], qv_bias[0, 1], out_bias[0], ln2_gain[0], ln2_bias[0], fc2_bias[0]]
+    )
+    small = jnp.pad(small, ((0, 8), (0, BLOCK - HEAD_DIM)))
+    w_qkv, w_out, w_fc1, w_fc2t, small_all = gather(
+        [own_qkv, out_weight[0], fc1_weight[0], fc2_weight[0].T, small], 1
+    )
+    w_qkv = w_qkv.reshape(D, 3 * D)
+    w_out = w_out.reshape(D, D)
+    w_fc1 = w_fc1.reshape(D, FF)
+    w_fc2t = w_fc2t.reshape(D, FF)
+    vectors = small_all[:, :8, :HEAD_DIM].astype(F32)
+    gain1, bias1, _, _, b_out, gain2, bias2, b_fc2 = [vectors[:, i].reshape(D) for i in range(8)]
+    b_qkv = jnp.stack([vectors[:, 2], jnp.zeros_like(vectors[:, 2]), vectors[:, 3]], axis=1).reshape(3 * D, 1)
+    b_fc1 = fc1_bias[0].astype(F32)
+
+    firsts = [window_first(image_of_block[m]) for m in range(micro)]
+
+    def slot_of(batch):
+        return jnp.clip(batch, 0, micro - 1)
+
+    saved = []
+    incoming = jnp.zeros_like(tokens[0])
+    for tick in range(micro + 1):
+        slot = slot_of(tick - sec)
+        image_row = lax.dynamic_index_in_dim(image_of_block, slot, 0, keepdims=False)
+        first = window_first(image_row)
+        x = jnp.where(sec == 0, tokens[min(tick, micro - 1)], incoming).astype(F32)
+        xhat1, rstd1 = normalised(x)
+        n1 = (xhat1 * gain1 + bias1).astype(BF)
+        qkv = jnp.einsum("ck,tc->kt", w_qkv, n1, preferred_element_type=F32) + b_qkv
+        qkv = exchange(qkv.astype(BF).reshape(HEADS, 3 * HEAD_DIM, BLOCK), 2)
+        att, lse = attention_fwd(image_row, first, qkv)
+        att = exchange(att, 3)
+        residual = x + jnp.einsum("ct,cd->td", att.reshape(D, BLOCK), w_out, preferred_element_type=F32) + b_out
+        xhat2, rstd2 = normalised(residual)
+        n2 = (xhat2 * gain2 + bias2).astype(BF)
+        hidden_pre = jnp.einsum("td,df->tf", n2, w_fc1, preferred_element_type=F32) + b_fc1
+        value, _ = gelu_and_slope(hidden_pre)
+        hidden = value.astype(BF)
+        out = residual + jnp.einsum("tf,df->td", hidden, w_fc2t, preferred_element_type=F32) + b_fc2
+        out_low = out.astype(BF)
+        saved.append((x, qkv, lse, att, residual, n2, hidden_pre, hidden, n1, out_low, image_row, first))
+        if tick < micro:
+            incoming = lax.ppermute(out_low, "section", [(0, 1)])
+    outputs = jnp.stack([jnp.where(sec == 0, saved[m][9], saved[m + 1][9]) for m in range(micro)])
+
+    incoming_grad = jnp.zeros(tokens.shape[1:], BF)
+    input_grads = []
+    x_terms, y_terms, small_total, fc1_bias_total = [], [], 0.0, 0.0
+    for tick in range(micro + 1):
+        live = jnp.where(sec == 1, tick < micro, tick >= 1).astype(F32)
+        late, early = min(tick + 1, micro), max(tick - 1, 0)
+        if tick == 0:
+            early = late
+        if tick == micro:
+            late = early
+        if late == early:
+            kept = saved[late]
+        else:
+            kept = tuple(jnp.where(sec == 1, a, b) for a, b in zip(saved[late], saved[early]))
+        x, qkv, lse, att, residual, n2, hidden_pre, hidden, n1, _, image_row, first = kept
+        grad = jnp.where(sec == 1, cotangent[min(tick, micro - 1)], incoming_grad).astype(F32) * live
+        fc_grad = grad.astype(BF)
+        hidden_grad = jnp.einsum("td,df->tf", fc_grad, w_fc2t, preferred_element_type=F32)
+        _, slope = gelu_and_slope(hidden_pre)
+        pre_grad = (hidden_grad * slope).astype(BF)
+        n2_grad = jnp.einsum("tf,df->td", pre_grad, w_fc1, preferred_element_type=F32)
+        xhat2, rstd2 = normalised(residual)
+        part, g_gain2, g_bias2 = norm_backward(n2_grad, xhat2, rstd2, gain2)
+        residual_grad = grad + part
+        branch = residual_grad.astype(BF)
+        att_grad = jnp.einsum("td,cd->ct", branch, w_out, preferred_element_type=F32).astype(BF)
+        att_grad = exchange(att_grad.reshape(HEADS, HEAD_DIM, BLOCK), 3)
+        dqkv = attention_bwd(image_row, first, qkv, lse, att_grad)
+        dqkv = exchange(dqkv, 2)
+        dqkv_rows = dqkv.reshape(3 * D, BLOCK)
+        n1_grad = jnp.einsum("kt,ck->tc", dqkv_rows, w_qkv, preferred_element_type=F32)
+        xhat1, rstd1 = normalised(x)
+        part, g_gain1, g_bias1 = norm_backward(n1_grad, xhat1, rstd1, gain1)
+        input_grad = residual_grad + part
+        input_grads.append(input_grad)
+        if tick < micro:
+            incoming_grad = lax.ppermute(input_grad.astype(BF), "section", [(1, 0)])
+        sums = jnp.sum(dqkv.astype(F32), axis=2)
+        small_total = small_total + jnp.stack(
+            [
+                g_gain1,
+                g_bias1,
+                sums[:, :HEAD_DIM].reshape(D),
+                sums[:, 2 * HEAD_DIM :].reshape(D),
+                jnp.sum(branch.astype(F32), axis=0),
+                g_gain2,
+                g_bias2,
+                jnp.sum(fc_grad.astype(F32), axis=0),
+            ]
+        )
+        fc1_bias_total = fc1_bias_total + jnp.sum(pre_grad.astype(F32), axis=0)
+        xs = jnp.stack([by_rows(n1), att, by_rows(n2), by_rows(fc_grad)]).reshape(4, 4, 4, HEAD_DIM, BLOCK)
+        x_of = [lax.dynamic_index_in_dim(xs, low ^ k, 2, keepdims=False) for k in range(4)]
+        x_all = [x_of[0]] + [swap(x_of[k], k) for k in range(1, 4)]
+        y_own = (dqkv_rows.T, branch, pre_grad, hidden)
+        y_two = tuple(swap(y, 2) for y in y_own)
+        y_one = tuple(swap(y, 1) for y in y_own)
+        y_three = tuple(swap(y, 1) for y in y_two)
+        x_terms += x_all
+        y_terms += [y_own, y_one, y_two, y_three]
+    input_grads = jnp.stack([jnp.where(sec == 0, input_grads[m + 1], input_grads[m]) for m in range(micro)])
+
+    def owned(index, tile):
+        x = jnp.stack([x[index] for x in x_terms]).reshape(len(x_terms), 4 * HEAD_DIM, BLOCK)
+        total = weight_grad(x, [y[index] for y in y_terms], tile)
+        total = total.reshape(4, HEAD_DIM, total.shape[1])
+        z = me // 4
+        result = lax.dynamic_index_in_dim(total, z, 0, keepdims=False).astype(F32)
+        for k in range(1, 4):
+            part = lax.dynamic_index_in_dim(total, z ^ k, 0, keepdims=False)
+            result = result + swap(part, 4 * k).astype(F32)
+        return result
+
+    g_fc2t = owned(3, 512)
+    g_fc1 = owned(2, 512)
+    g_out = owned(1, 384)
+    g_qkv = owned(0, 384)
+    g_qkv = g_qkv.reshape(HEAD_DIM, HEADS, 3, HEAD_DIM).transpose(0, 2, 1, 3).reshape(HEAD_DIM, 3 * D)
+    packed = jnp.concatenate([small_total.reshape(8 * D), fc1_bias_total])
+    packed = lax.psum(packed, "wide")
+    g_small = lax.dynamic_slice_in_dim(packed[: 8 * D].reshape(8, HEADS, HEAD_DIM), me, 1, 1)[:, 0]
+    g_fc1_bias = packed[8 * D :]
+    return (
+        outputs[None],
+        input_grads[None],
+        g_small[0][None],
+        g_small[1][None],
+        g_qkv[None],
+        g_small[2:4][None],
+        g_out[None],
+        g_small[4][None],
+        g_small[5][None],
+        g_small[6][None],
+        g_fc1[None],
+        g_fc1_bias[None],
+        g_fc2t.T[None],
+        g_small[7][None],
+    )
+
+
 BLK_DEV = 1
 REACH = 5
-
-
-EPSILON = 1e-06
-MASKED_SCORE = -1e30
 
 
 def shifted(value, axis, steps):
@@ -241,7 +788,7 @@
     return (input_grad, grad_terms, grad_fc1_bias)
 
 
-def on_device(
+def on_device_near(
     tokens,
     cotangent,
     image_of_block,
@@ -389,8 +936,8 @@
     )
 
 
-def solution(mesh):
-    in_specs = (
+def specs():
+    ins = (
         P(None, "wide", None),
         P(None, "wide", None),
         P(),
@@ -407,7 +954,7 @@
         P("section", None, "wide"),
         P("section", "wide"),
     )
-    out_specs = (
+    outs = (
         P("section", None, "wide", None),
         P("section", None, "wide", None),
         P("section", "wide"),
@@ -423,6 +970,10 @@
         P("section", None, "wide"),
         P("section", "wide"),
     )
-    return jax.shard_map(
-        on_device, mesh=mesh, in_specs=in_specs, out_specs=out_specs, check_vma=False
-    )
+    return ins, outs
+
+
+def solution(mesh):
+    ins, outs = specs()
+    body = on_device if mesh.shape["wide"] == HEADS else on_device_near
+    return jax.shard_map(body, mesh=mesh, in_specs=ins, out_specs=outs, check_vma=False)

time: 2460 us -> 1250 us (0.51)
  waiting for transfers between devices: 924 us -> 264 us
  starting transfers between devices: 570 us -> 65.3 us
  Pallas kernels: 0 us -> 482 us
  matrix products: 435 us -> 141 us
  local copies, waits for them, and re-layouts: 261 us -> 169 us
  blocking collectives: 142 us -> 52.1 us
  other arithmetic: 83.3 us -> 57.4 us
    ppermute x184 -> x58, starting transfers between devices: 569 us -> 65.3 us  [the longest x54 53.5 us: swap(): return lax.ppermute(x, 'wide', [(i, i ^ bits) for i in range(HEADS)])]
    pallas_call x0 -> x23, Pallas kernels: none -> 482 us  [the longest x12 206 us: exchange(): pl.pallas_call(exchange_kernel, out_shape=jax.ShapeDtypeStruct(x.shape, x...]
    ppermute x184 -> x58, waiting for transfers between devices: 612 us -> 264 us  [the longest x54 256 us: swap(): return lax.ppermute(x, 'wide', [(i, i ^ bits) for i in range(HEADS)])]
    reduce_scatter x2 -> x0, waiting for transfers between devices: 309 us -> none  [the longest x1 209 us: on_device(): lax.psum_scatter(grad_fc2_weight, 'wide', scatter_dimension=1, tiled=True)]
    dot_general x60 -> x24, matrix products: 371 us -> 141 us  [the longest x3 23.9 us: on_device(): jnp.einsum('tf,df->td', pre_grad, w_fc1, preferred_element_type=F32)]
    unnamed x2 -> x0, blocking collectives: 117 us -> none
    unnamed x610 -> x378, local copies, waits for them, and re-layouts: 143 us -> 36.2 us
    concatenate x24 -> x0, local copies, waits for them, and re-layouts: 76.3 us -> none  [the longest x12 38.3 us: near_keys(): jnp.concatenate(key_parts, axis=0)]
  transfers between devices with their start and end apart: 192 -> 58, of which waited for: 82 -> 21; matrix products, arithmetic and copies ran while one was open for 22% -> 21% of each run, Pallas kernels for 0% -> 18%
where the time goes in v1:
time: 1250 us; the launch traced here: 1230 us
  Pallas kernels  482 us (39%)
  waiting for transfers between devices  264 us (21%)
  local copies, waits for them, and re-layouts  169 us (14%)
  matrix products  141 us (11%)
  starting transfers between devices  65.3 us (5%)
  other arithmetic  57.4 us (5%)
  blocking collectives  52.1 us (4%)
    ppermute x54, waiting for transfers between devices, swap(): return lax.ppermute(x, 'wide', [(i, i ^ bits) for i in range(HEADS)])  256 us
    pallas_call x12, Pallas kernels, exchange(): pl.pallas_call(exchange_kernel, out_shape=jax.ShapeDtypeStruct(x.shape, x...  206 us
    pallas_call x1, Pallas kernels, gather(): pl.pallas_call(functools.partial(gather_kernel, count), out_shape=[jax.Sh...  175 us
    ppermute x54, starting transfers between devices, swap(): return lax.ppermute(x, 'wide', [(i, i ^ bits) for i in range(HEADS)])  53.5 us
    psum x1, blocking collectives, on_device(): packed = lax.psum(packed, 'wide')  52.1 us
    pallas_call x4, Pallas kernels, weight_grad(): pl.pallas_call(functools.partial(dw_kernel, count), grid=(pl.cdiv(cols, t...  43 us
    unnamed x378, local copies, waits for them, and re-layouts  36.2 us
    ppermute x15, local copies, waits for them, and re-layouts, swap(): return lax.ppermute(x, 'wide', [(i, i ^ bits) for i in range(HEADS)])  35.8 us
  transfers between devices with their start and end apart: 58, of which 21 were waited for; matrix products, arithmetic and copies ran while one was open for 21% of the time, Pallas kernels for 18%

profile of v1, /device:TPU:10, one launch (start us, length us, event | category | flops | bytes accessed | tf_op | source)
XLA Modules:
  0.0 1233.4 jit_solution(13248733080629531317)
XLA Ops:
  9.1 175.3 %shard_map.254 = (bf16[16,72,3456]{2,1,0:T(8,128)(2,1)}, bf16[16,72,1152]{2,1,0:T(8,128)(2,1)}, bf16[16,72,4304]{2,1,0:T(8,128)(2,1)}, bf16[16,72,4304]{2,1,0:T(8,128)(2,1)}, bf16[16,16,128]{2,1,0:T(8,128)(2,1)}) custom-call(bf16[72,3456]{1,0:T(8,128)(2,1)} %copy.200.refs_0_, bf16[72,1152]{1,0:T(8,128)(2,1)} %bitcast.443, bf16[72,4304]{1,0:T(8,128)(2,1)} %bitcast.390, ...), custom_call_target="tpu_custom_call" | custom-call | tf_op jit(solution)/shard_map/pallas_call | solution.py:142
  192.6 25.2 %shard_map.255.qkv_ref = bf16[16,216,128]{2,1,0:T(8,128)(2,1)} custom-call(bf16[16,216,128]{2,1,0:T(8,128)(2,1)} %bitcast.388), custom_call_target="tpu_custom_call" | custom-call | tf_op jit(solution)/shard_map/pallas_call | solution.py:186
  220.5 8.4 shard_map.256
  229.7 11.6 shard_map.257
  250.2 8.0 fusion.15
  261.5 7.7 collective-permute-done
  276.5 22.8 %shard_map.258.qkv_ref = bf16[16,216,128]{2,1,0:T(8,128)(2,1)} custom-call(bf16[16,216,128]{2,1,0:T(8,128)(2,1)} %bitcast.389), custom_call_target="tpu_custom_call" | custom-call | tf_op jit(solution)/shard_map/pallas_call | solution.py:186
  300.5 8.4 shard_map.259
  309.6 11.3 shard_map.260
  323.9 7.3 multiply_convert_fusion
  337.1 7.9 convert_reduce_fusion.2
  345.0 8.5 multiply_reduce_fusion.3
  362.0 10.8 shard_map.264.do_ref
  373.8 10.7 shard_map.265.x_ref
  385.4 22.5 %shard_map.266 = bf16[16,216,128]{2,1,0:T(8,128)(2,1)} custom-call(bf16[16,216,128]{2,1,0:T(8,128)(2,1)} %copy-done.18), custom_call_target="tpu_custom_call" | custom-call | tf_op jit(solution)/shard_map/pallas_call | solution.py:186
  408.0 7.5 fusion.78
  437.7 6.9 fusion.5
  445.6 22.9 %shard_map.261.qkv_ref = bf16[16,216,128]{2,1,0:T(8,128)(2,1)} custom-call(bf16[16,216,128]{2,1,0:T(8,128)(2,1)} %bitcast.387), custom_call_target="tpu_custom_call" | custom-call | tf_op jit(solution)/shard_map/pallas_call | solution.py:186
  469.7 8.4 shard_map.262
  478.8 12.2 shard_map.263
  494.1 7.9 broadcast_select_fusion
  513.3 8.3 multiply_reduce_fusion.1
  527.3 8.0 fusion.19
  535.3 10.4 shard_map.267.do_ref
  547.8 10.7 shard_map.268.x_ref
  559.4 23.1 %shard_map.269 = bf16[16,216,128]{2,1,0:T(8,128)(2,1)} custom-call(bf16[16,216,128]{2,1,0:T(8,128)(2,1)} %copy-done.16), custom_call_target="tpu_custom_call" | custom-call | tf_op jit(solution)/shard_map/pallas_call | solution.py:186
  584.2 6.9 multiply_reduce_fusion.2
  628.6 7.3 convert_reduce_fusion
  636.9 7.1 fusion.147
  649.0 10.5 shard_map.270.do_ref
  660.5 10.7 shard_map.271.x_ref
  672.1 22.6 %shard_map.272 = bf16[16,216,128]{2,1,0:T(8,128)(2,1)} custom-call(bf16[16,216,128]{2,1,0:T(8,128)(2,1)} %copy-done.17), custom_call_target="tpu_custom_call" | custom-call | tf_op jit(solution)/shard_map/pallas_call | solution.py:186
  736.0 52.1 %psum.7 = f32[13520]{0:T(1024)S(1)} all-reduce(f32[13520]{0:T(1024)S(1)} %pad_maximum_fusion.4), channel_id=1, replica_groups=mesh['section'=2,'wide'=16] {'wide'}, use_global_device_ids=true, to_apply=%region_55.56 | all-reduce | flops 13520 | bytes 108160 | tf_op jit(solution)/shard_map/psum | solution.py:542
  836.9 23.1 %collective-permute-done.32.refs_10_ = bf16[128,1152]{1,0:T(8,128)(2,1)S(1)} collective-permute-done((bf16[128,1152]{1,0:T(8,128)(2,1)S(1)}, bf16[128,1152]{1,0:T(8,128)(2,1)S(1)}, u32[]{:S(2)}, u32[]{:S(2)}) %collective-permute-start.32) | collective-permute-done | bytes 294944 | tf_op jit(solution)/shard_map/ppermute | solution.py:367
  866.0 17.6 %collective-permute-done.50 = bf16[128,4304]{0,1:T(8,128)(2,1)S(1)} collective-permute-done((bf16[128,4304]{0,1:T(8,128)(2,1)S(1)}, bf16[128,4304]{0,1:T(8,128)(2,1)S(1)}, u32[]{:S(2)}, u32[]{:S(2)}) %collective-permute-start.50) | collective-permute-done | bytes 1101856 | tf_op jit(solution)/shard_map/ppermute | solution.py:367
  884.6 22.6 %collective-permute-done.38 = bf16[128,4304]{0,1:T(8,128)(2,1)S(1)} collective-permute-done((bf16[128,4304]{0,1:T(8,128)(2,1)S(1)}, bf16[128,4304]{0,1:T(8,128)(2,1)S(1)}, u32[]{:S(2)}, u32[]{:S(2)}) %collective-permute-start.38) | collective-permute-done | bytes 1101856 | tf_op jit(solution)/shard_map/ppermute | solution.py:367
  914.3 12.1 collective-permute-done.17.refs_6_
  927.2 8.5 collective-permute-start.34
  960.9 12.5 %collective-permute-done.41 = bf16[128,4304]{0,1:T(8,128)(2,1)S(1)} collective-permute-done((bf16[128,4304]{0,1:T(8,128)(2,1)S(1)}, bf16[128,4304]{0,1:T(8,128)(2,1)S(1)}, u32[]{:S(2)}, u32[]{:S(2)}) %collective-permute-start.41) | collective-permute-done | bytes 1101856 | tf_op jit(solution)/shard_map/ppermute | solution.py:367
  975.0 41.1 %collective-permute-done.20.refs_10_ = bf16[128,3456]{1,0:T(8,128)(2,1)} collective-permute-done((bf16[128,3456]{1,0:T(8,128)(2,1)}, bf16[128,3456]{1,0:T(8,128)(2,1)}, u32[]{:S(2)}, u32[]{:S(2)}) %collective-permute-start.20) | collective-permute-done | bytes 884768 | tf_op jit(solution)/shard_map/ppermute | solution.py:367
  1055.0 11.4 shard_map.273
  1069.0 8.4 collective-permute-start.22
  1085.0 14.3 %shard_map.276 = bf16[288,4304]{1,0:T(8,128)(2,1)} custom-call(bf16[12,288,128]{2,1,0:T(8,128)(2,1)S(1)} %copy-done.34, bf16[128,4304]{1,0:T(8,128)(2,1)S(1)} %get-tuple-element.200.refs_0_.refs_8_, bf16[128,4304]{1,0:T(8,128)(2,1)S(1)} %copy-done.3, bf16[128,4304]{1,0:T(8,128)(2,1)S(1)} %copy-done.2, bf16[128,4304]{1,0:T(8,128)(2,1)S(1)} %copy-done.4, ...), custom_call_target="tpu_custom_call" | custom-call | tf_op jit(solution)/shard_map/pallas_call | solution.py:384
  1112.3 13.4 %shard_map.275 = bf16[288,4304]{1,0:T(8,128)(2,1)} custom-call(bf16[12,288,128]{2,1,0:T(8,128)(2,1)S(1)} %copy-done.31, bf16[128,4304]{1,0:T(8,128)(2,1)S(1)} %get-tuple-element.211.refs_0_, bf16[128,4304]{1,0:T(8,128)(2,1)S(1)} %copy-done.10, bf16[128,4304]{1,0:T(8,128)(2,1)S(1)} %copy-done.9, bf16[128,4304]{1,0:T(8,128)(2,1)S(1)} %copy-done.11, ...), custom_call_target="tpu_custom_call" | custom-call | tf_op jit(solution)/shard_map/pallas_call | solution.py:384
  1132.9 17.4 %collective-permute-done.24 = bf16[72,3456]{1,0:T(8,128)(2,1)} collective-permute-done((bf16[72,3456]{1,0:T(8,128)(2,1)}, bf16[72,3456]{1,0:T(8,128)(2,1)}, u32[]{:S(2)}, u32[]{:S(2)}) %collective-permute-start.24) | collective-permute-done | bytes 497696 | tf_op jit(solution)/shard_map/ppermute | solution.py:367
  1161.9 42.1 %collective-permute-done.57 = bf16[72,4304]{1,0:T(8,128)(2,1)} collective-permute-done((bf16[72,4304]{1,0:T(8,128)(2,1)}, bf16[72,4304]{1,0:T(8,128)(2,1)}, u32[]{:S(2)}, u32[]{:S(2)}) %collective-permute-start.57) | collective-permute-done | bytes 619808 | tf_op jit(solution)/shard_map/ppermute | solution.py:367
  1207.0 8.6 collective-permute-done.47
  1215.6 14.6 %collective-permute-done.48 = bf16[72,4304]{1,0:T(8,128)(2,1)S(1)} collective-permute-done((bf16[72,4304]{1,0:T(8,128)(2,1)S(1)}, bf16[72,4304]{1,0:T(8,128)(2,1)S(1)}, u32[]{:S(2)}, u32[]{:S(2)}) %collective-permute-start.48) | collective-permute-done | bytes 619808 | tf_op jit(solution)/shard_map/ppermute | solution.py:367
  (682 shorter events, 372.3 us)
Async XLA Ops:
  357.2 460.8 %collective-permute-start.26 = (bf16[128,1152]{1,0:T(8,128)(2,1)S(1)}, bf16[128,1152]{1,0:T(8,128)(2,1)}, u32[]{:S(2)}, u32[]{:S(2)}) collective-permute-start(bf16[128,1152]{1,0:T(8,128)(2,1)S(1)} %get-tuple-element.84.refs_0_), channel_id=1, source_target_pairs={{0,2},{1,3},{2,0},{3,1},{4,6},{5,7},{6,4},{7,5},{8,10},{9,11},{10,... | collective-permute-start | bytes 884744 | tf_op jit(solution)/shard_map/ppermute | solution.py:367
  358.6 468.0 %collective-permute-start.25 = (bf16[128,1152]{1,0:T(8,128)(2,1)S(1)}, bf16[128,1152]{1,0:T(8,128)(2,1)}, u32[]{:S(2)}, u32[]{:S(2)}) collective-permute-start(bf16[128,1152]{1,0:T(8,128)(2,1)S(1)} %get-tuple-element.84.refs_0_), channel_id=1, source_target_pairs={{0,1},{1,0},{2,3},{3,2},{4,5},{5,4},{6,7},{7,6},{8,9},{9,8},{10,11... | collective-permute-start | bytes 884744 | tf_op jit(solution)/shard_map/ppermute | solution.py:367
  423.2 82.2 %collective-permute-start.2 = (bf16[128,1152]{1,0:T(8,128)(2,1)}, bf16[128,1152]{1,0:T(8,128)(2,1)}, u32[]{:S(2)}, u32[]{:S(2)}) collective-permute-start(bf16[128,1152]{1,0:T(8,128)(2,1)} %get-tuple-element.96), channel_id=1, source_target_pairs={{16,0},{17,1},{18,2},{19,3},{20,4},{21,5},{22,6},{23,7},{24,8},{25... | collective-permute-start | bytes 884744 | tf_op jit(solution)/shard_map/ppermute | solution.py:499
  526.1 301.7 %collective-permute-start.29 = (bf16[128,1152]{1,0:T(8,128)(2,1)}, bf16[128,1152]{1,0:T(8,128)(2,1)}, u32[]{:S(2)}, u32[]{:S(2)}) collective-permute-start(bf16[128,1152]{1,0:T(8,128)(2,1)} %get-tuple-element.81.refs_4_), channel_id=1, source_target_pairs={{0,2},{1,3},{2,0},{3,1},{4,6},{5,7},{6,4},{7,5},{8,10},{9,11},{10,... | collective-permute-start | bytes 884744 | tf_op jit(solution)/shard_map/ppermute | solution.py:367
  593.9 30.2 %collective-permute-start.3 = (bf16[128,1152]{1,0:T(8,128)(2,1)}, bf16[128,1152]{1,0:T(8,128)(2,1)}, u32[]{:S(2)}, u32[]{:S(2)}) collective-permute-start(bf16[128,1152]{1,0:T(8,128)(2,1)} %convert_element_type.260), channel_id=1, source_target_pairs={{16,0},{17,1},{18,2},{19,3},{20,4},{21,5},{22,6},{23,7},{24,8},{25... | collective-permute-start | bytes 884744 | tf_op jit(solution)/shard_map/ppermute | solution.py:499
  608.5 123.2 %collective-permute-start.7 = (bf16[4,4,72,128]{3,2,1,0:T(8,128)(2,1)}, bf16[4,4,72,128]{3,2,1,0:T(8,128)(2,1)}, u32[]{:S(2)}, u32[]{:S(2)}) collective-permute-start(bf16[4,4,72,128]{3,2,1,0:T(8,128)(2,1)} %get-tuple-element.127), channel_id=1, source_target_pairs={{0,1},{1,0},{2,3},{3,2},{4,5},{5,4},{6,7},{7,6},{8,9},{9,8},{10,11... | collective-permute-start | bytes 884744 | tf_op jit(solution)/shard_map/ppermute | solution.py:367
  624.1 168.1 %collective-permute-start.8 = (bf16[4,4,72,128]{3,2,1,0:T(8,128)(2,1)}, bf16[4,4,72,128]{3,2,1,0:T(8,128)(2,1)}, u32[]{:S(2)}, u32[]{:S(2)}) collective-permute-start(bf16[4,4,72,128]{3,2,1,0:T(8,128)(2,1)} %get-tuple-element.126), channel_id=1, source_target_pairs={{0,2},{1,3},{2,0},{3,1},{4,6},{5,7},{6,4},{7,5},{8,10},{9,11},{10,... | collective-permute-start | bytes 884744 | tf_op jit(solution)/shard_map/ppermute | solution.py:367
  731.7 62.3 %collective-permute-start.9 = (bf16[4,4,72,128]{3,2,1,0:T(8,128)(2,1)}, bf16[4,4,72,128]{3,2,1,0:T(8,128)(2,1)}, u32[]{:S(2)}, u32[]{:S(2)}) collective-permute-start(bf16[4,4,72,128]{3,2,1,0:T(8,128)(2,1)} %get-tuple-element.125), channel_id=1, source_target_pairs={{0,3},{1,2},{2,1},{3,0},{4,7},{5,6},{6,5},{7,4},{8,11},{9,10},{10,... | collective-permute-start | bytes 884744 | tf_op jit(solution)/shard_map/ppermute | solution.py:367
  804.2 12.4 %collective-permute-start.6 = (bf16[4,4,72,128]{3,2,1,0:T(8,128)(2,1)S(1)}, bf16[4,4,72,128]{3,2,1,0:T(8,128)(2,1)S(1)}, u32[]{:S(2)}, u32[]{:S(2)}) collective-permute-start(bf16[4,4,72,128]{3,2,1,0:T(8,128)(2,1)S(1)} %copy-done.115), channel_id=1, source_target_pairs={{0,3},{1,2},{2,1},{3,0},{4,7},{5,6},{6,5},{7,4},{8,11},{9,10},{10,... | collective-permute-start | bytes 884744 | tf_op jit(solution)/shard_map/ppermute | solution.py:367
  818.0 18.2 %collective-permute-start.28 = (bf16[128,1152]{1,0:T(8,128)(2,1)}, bf16[128,1152]{1,0:T(8,128)(2,1)S(1)}, u32[]{:S(2)}, u32[]{:S(2)}) collective-permute-start(bf16[128,1152]{1,0:T(8,128)(2,1)} %get-tuple-element.81.refs_4_), channel_id=1, source_target_pairs={{0,1},{1,0},{2,3},{3,2},{4,5},{5,4},{6,7},{7,6},{8,9},{9,8},{10,11... | collective-permute-start | bytes 884744 | tf_op jit(solution)/shard_map/ppermute | solution.py:367
  818.0 18.6 %collective-permute-start.27 = (bf16[128,1152]{1,0:T(8,128)(2,1)}, bf16[128,1152]{1,0:T(8,128)(2,1)S(1)}, u32[]{:S(2)}, u32[]{:S(2)}) collective-permute-start(bf16[128,1152]{1,0:T(8,128)(2,1)} %collective-permute-done.26.refs_2_), channel_id=1, source_target_pairs={{0,1},{1,0},{2,3},{3,2},{4,5},{5,4},{6,7},{7,6},{8,9},{9,8},{10,11... | collective-permute-start | bytes 884744 | tf_op jit(solution)/shard_map/ppermute | solution.py:367
  826.7 37.7 %collective-permute-start.14 = (bf16[128,3456]{1,0:T(8,128)(2,1)S(1)}, bf16[128,3456]{1,0:T(8,128)(2,1)}, u32[]{:S(2)}, u32[]{:S(2)}) collective-permute-start(bf16[128,3456]{1,0:T(8,128)(2,1)S(1)} %bitcast.327), channel_id=1, source_target_pairs={{0,2},{1,3},{2,0},{3,1},{4,6},{5,7},{6,4},{7,5},{8,10},{9,11},{10,... | collective-permute-start | bytes 2654216 | tf_op jit(solution)/shard_map/ppermute | solution.py:367
  827.8 32.2 %collective-permute-start.32 = (bf16[128,1152]{1,0:T(8,128)(2,1)S(1)}, bf16[128,1152]{1,0:T(8,128)(2,1)S(1)}, u32[]{:S(2)}, u32[]{:S(2)}) collective-permute-start(bf16[128,1152]{1,0:T(8,128)(2,1)S(1)} %copy-done.21), channel_id=1, source_target_pairs={{0,2},{1,3},{2,0},{3,1},{4,6},{5,7},{6,4},{7,5},{8,10},{9,11},{10,... | collective-permute-start | bytes 884744 | tf_op jit(solution)/shard_map/ppermute | solution.py:367
  835.4 25.4 %collective-permute-start.31 = (bf16[128,1152]{1,0:T(8,128)(2,1)S(1)}, bf16[128,1152]{1,0:T(8,128)(2,1)S(1)}, u32[]{:S(2)}, u32[]{:S(2)}) collective-permute-start(bf16[128,1152]{1,0:T(8,128)(2,1)S(1)} %copy-done.21), channel_id=1, source_target_pairs={{0,1},{1,0},{2,3},{3,2},{4,5},{5,4},{6,7},{7,6},{8,9},{9,8},{10,11... | collective-permute-start | bytes 884744 | tf_op jit(solution)/shard_map/ppermute | solution.py:367
  836.1 28.5 %collective-permute-start.13 = (bf16[128,3456]{1,0:T(8,128)(2,1)S(1)}, bf16[128,3456]{1,0:T(8,128)(2,1)S(1)}, u32[]{:S(2)}, u32[]{:S(2)}) collective-permute-start(bf16[128,3456]{1,0:T(8,128)(2,1)S(1)} %bitcast.328), channel_id=1, source_target_pairs={{0,1},{1,0},{2,3},{3,2},{4,5},{5,4},{6,7},{7,6},{8,9},{9,8},{10,11... | collective-permute-start | bytes 2654216 | tf_op jit(solution)/shard_map/ppermute | solution.py:367
  836.6 47.0 %collective-permute-start.50 = (bf16[128,4304]{0,1:T(8,128)(2,1)S(1)}, bf16[128,4304]{0,1:T(8,128)(2,1)S(1)}, u32[]{:S(2)}, u32[]{:S(2)}) collective-permute-start(bf16[128,4304]{0,1:T(8,128)(2,1)S(1)} %copy-done.75), channel_id=1, source_target_pairs={{0,2},{1,3},{2,0},{3,1},{4,6},{5,7},{6,4},{7,5},{8,10},{9,11},{10,... | collective-permute-start | bytes 3305480 | tf_op jit(solution)/shard_map/ppermute | solution.py:367
  860.0 24.4 %collective-permute-start.49 = (bf16[128,4304]{0,1:T(8,128)(2,1)S(1)}, bf16[128,4304]{0,1:T(8,128)(2,1)S(1)}, u32[]{:S(2)}, u32[]{:S(2)}) collective-permute-start(bf16[128,4304]{0,1:T(8,128)(2,1)S(1)} %copy-done.75), channel_id=1, source_target_pairs={{0,1},{1,0},{2,3},{3,2},{4,5},{5,4},{6,7},{7,6},{8,9},{9,8},{10,11... | collective-permute-start | bytes 3305480 | tf_op jit(solution)/shard_map/ppermute | solution.py:367
  863.7 43.6 %collective-permute-start.38 = (bf16[128,4304]{0,1:T(8,128)(2,1)S(1)}, bf16[128,4304]{0,1:T(8,128)(2,1)S(1)}, u32[]{:S(2)}, u32[]{:S(2)}) collective-permute-start(bf16[128,4304]{0,1:T(8,128)(2,1)S(1)} %copy-done.74), channel_id=1, source_target_pairs={{0,2},{1,3},{2,0},{3,1},{4,6},{5,7},{6,4},{7,5},{8,10},{9,11},{10,... | collective-permute-start | bytes 3305480 | tf_op jit(solution)/shard_map/ppermute | solution.py:367
  864.4 48.4 %collective-permute-start.37 = (bf16[128,4304]{0,1:T(8,128)(2,1)S(1)}, bf16[128,4304]{0,1:T(8,128)(2,1)}, u32[]{:S(2)}, u32[]{:S(2)}) collective-permute-start(bf16[128,4304]{0,1:T(8,128)(2,1)S(1)} %copy-done.74), channel_id=1, source_target_pairs={{0,1},{1,0},{2,3},{3,2},{4,5},{5,4},{6,7},{7,6},{8,9},{9,8},{10,11... | collective-permute-start | bytes 3305480 | tf_op jit(solution)/shard_map/ppermute | solution.py:367
  864.6 61.7 %collective-permute-start.17 = (bf16[128,3456]{1,0:T(8,128)(2,1)S(1)}, bf16[128,3456]{1,0:T(8,128)(2,1)}, u32[]{:S(2)}, u32[]{:S(2)}) collective-permute-start(bf16[128,3456]{1,0:T(8,128)(2,1)S(1)} %bitcast.330), channel_id=1, source_target_pairs={{0,2},{1,3},{2,0},{3,1},{4,6},{5,7},{6,4},{7,5},{8,10},{9,11},{10,... | collective-permute-start | bytes 2654216 | tf_op jit(solution)/shard_map/ppermute | solution.py:367
  883.6 43.5 %collective-permute-start.16 = (bf16[128,3456]{1,0:T(8,128)(2,1)S(1)}, bf16[128,3456]{1,0:T(8,128)(2,1)S(1)}, u32[]{:S(2)}, u32[]{:S(2)}) collective-permute-start(bf16[128,3456]{1,0:T(8,128)(2,1)S(1)} %bitcast.331), channel_id=1, source_target_pairs={{0,1},{1,0},{2,3},{3,2},{4,5},{5,4},{6,7},{7,6},{8,9},{9,8},{10,11... | collective-permute-start | bytes 2654216 | tf_op jit(solution)/shard_map/ppermute | solution.py:367
  884.5 24.1 %collective-permute-start.33 = (bf16[128,1152]{1,0:T(8,128)(2,1)S(1)}, bf16[128,1152]{1,0:T(8,128)(2,1)S(1)}, u32[]{:S(2)}, u32[]{:S(2)}) collective-permute-start(bf16[128,1152]{1,0:T(8,128)(2,1)S(1)} %collective-permute-done.32.refs_10_), channel_id=1, source_target_pairs={{0,1},{1,0},{2,3},{3,2},{4,5},{5,4},{6,7},{7,6},{8,9},{9,8},{10,11... | collective-permute-start | bytes 884744 | tf_op jit(solution)/shard_map/ppermute | solution.py:367
  907.3 51.3 %collective-permute-start.53 = (bf16[128,4304]{0,1:T(8,128)(2,1)S(1)}, bf16[128,4304]{0,1:T(8,128)(2,1)}, u32[]{:S(2)}, u32[]{:S(2)}) collective-permute-start(bf16[128,4304]{0,1:T(8,128)(2,1)S(1)} %copy-done.77), channel_id=1, source_target_pairs={{0,2},{1,3},{2,0},{3,1},{4,6},{5,7},{6,4},{7,5},{8,10},{9,11},{10,... | collective-permute-start | bytes 3305480 | tf_op jit(solution)/shard_map/ppermute | solution.py:367
  908.6 50.0 %collective-permute-start.52 = (bf16[128,4304]{0,1:T(8,128)(2,1)S(1)}, bf16[128,4304]{0,1:T(8,128)(2,1)}, u32[]{:S(2)}, u32[]{:S(2)}) collective-permute-start(bf16[128,4304]{0,1:T(8,128)(2,1)S(1)} %copy-done.77), channel_id=1, source_target_pairs={{0,1},{1,0},{2,3},{3,2},{4,5},{5,4},{6,7},{7,6},{8,9},{9,8},{10,11... | collective-permute-start | bytes 3305480 | tf_op jit(solution)/shard_map/ppermute | solution.py:367
  912.9 60.5 %collective-permute-start.41 = (bf16[128,4304]{0,1:T(8,128)(2,1)S(1)}, bf16[128,4304]{0,1:T(8,128)(2,1)S(1)}, u32[]{:S(2)}, u32[]{:S(2)}) collective-permute-start(bf16[128,4304]{0,1:T(8,128)(2,1)S(1)} %copy-done.76), channel_id=1, source_target_pairs={{0,2},{1,3},{2,0},{3,1},{4,6},{5,7},{6,4},{7,5},{8,10},{9,11},{10,... | collective-permute-start | bytes 3305480 | tf_op jit(solution)/shard_map/ppermute | solution.py:367
  926.3 48.4 %collective-permute-start.40 = (bf16[128,4304]{0,1:T(8,128)(2,1)S(1)}, bf16[128,4304]{0,1:T(8,128)(2,1)S(1)}, u32[]{:S(2)}, u32[]{:S(2)}) collective-permute-start(bf16[128,4304]{0,1:T(8,128)(2,1)S(1)} %copy-done.76), channel_id=1, source_target_pairs={{0,1},{1,0},{2,3},{3,2},{4,5},{5,4},{6,7},{7,6},{8,9},{9,8},{10,11... | collective-permute-start | bytes 3305480 | tf_op jit(solution)/shard_map/ppermute | solution.py:367
  927.2 12.9 %collective-permute-start.34 = (bf16[72,1152]{1,0:T(8,128)(2,1)S(1)}, bf16[72,1152]{1,0:T(8,128)(2,1)S(1)}, u32[]{:S(2)}, u32[]{:S(2)}) collective-permute-start(bf16[72,1152]{1,0:T(8,128)(2,1)S(1)} %get-tuple-element.133), channel_id=1, source_target_pairs={{0,4},{1,5},{2,6},{3,7},{4,0},{5,1},{6,2},{7,3},{8,12},{9,13},{10,... | collective-permute-start | bytes 497672 | tf_op jit(solution)/shard_map/ppermute | solution.py:367
  957.0 59.3 %collective-permute-start.44 = (bf16[128,4304]{0,1:T(8,128)(2,1)S(1)}, bf16[128,4304]{0,1:T(8,128)(2,1)S(1)}, u32[]{:S(2)}, u32[]{:S(2)}) collective-permute-start(bf16[128,4304]{0,1:T(8,128)(2,1)S(1)} %copy-done.78), channel_id=1, source_target_pairs={{0,2},{1,3},{2,0},{3,1},{4,6},{5,7},{6,4},{7,5},{8,10},{9,11},{10,... | collective-permute-start | bytes 3305480 | tf_op jit(solution)/shard_map/ppermute | solution.py:367
  958.6 58.0 %collective-permute-start.43 = (bf16[128,4304]{0,1:T(8,128)(2,1)S(1)}, bf16[128,4304]{0,1:T(8,128)(2,1)S(1)}, u32[]{:S(2)}, u32[]{:S(2)}) collective-permute-start(bf16[128,4304]{0,1:T(8,128)(2,1)S(1)} %copy-done.78), channel_id=1, source_target_pairs={{0,1},{1,0},{2,3},{3,2},{4,5},{5,4},{6,7},{7,6},{8,9},{9,8},{10,11... | collective-permute-start | bytes 3305480 | tf_op jit(solution)/shard_map/ppermute | solution.py:367
  958.6 58.2 %collective-permute-start.51 = (bf16[128,4304]{0,1:T(8,128)(2,1)}, bf16[128,4304]{0,1:T(8,128)(2,1)S(1)}, u32[]{:S(2)}, u32[]{:S(2)}) collective-permute-start(bf16[128,4304]{0,1:T(8,128)(2,1)} %copy-done.79), channel_id=1, source_target_pairs={{0,1},{1,0},{2,3},{3,2},{4,5},{5,4},{6,7},{7,6},{8,9},{9,8},{10,11... | collective-permute-start | bytes 3305480 | tf_op jit(solution)/shard_map/ppermute | solution.py:367
  973.4 42.7 %collective-permute-start.20 = (bf16[128,3456]{1,0:T(8,128)(2,1)}, bf16[128,3456]{1,0:T(8,128)(2,1)}, u32[]{:S(2)}, u32[]{:S(2)}) collective-permute-start(bf16[128,3456]{1,0:T(8,128)(2,1)} %bitcast.80.refs_8_), channel_id=1, source_target_pairs={{0,2},{1,3},{2,0},{3,1},{4,6},{5,7},{6,4},{7,5},{8,10},{9,11},{10,... | collective-permute-start | bytes 2654216 | tf_op jit(solution)/shard_map/ppermute | solution.py:367
  974.8 42.4 %collective-permute-start.39 = (bf16[128,4304]{0,1:T(8,128)(2,1)}, bf16[128,4304]{0,1:T(8,128)(2,1)S(1)}, u32[]{:S(2)}, u32[]{:S(2)}) collective-permute-start(bf16[128,4304]{0,1:T(8,128)(2,1)} %copy-done.81), channel_id=1, source_target_pairs={{0,1},{1,0},{2,3},{3,2},{4,5},{5,4},{6,7},{7,6},{8,9},{9,8},{10,11... | collective-permute-start | bytes 3305480 | tf_op jit(solution)/shard_map/ppermute | solution.py:367
  1016.1 33.7 %collective-permute-start.19 = (bf16[128,3456]{1,0:T(8,128)(2,1)}, bf16[128,3456]{1,0:T(8,128)(2,1)}, u32[]{:S(2)}, u32[]{:S(2)}) collective-permute-start(bf16[128,3456]{1,0:T(8,128)(2,1)} %bitcast.80.refs_8_), channel_id=1, source_target_pairs={{0,1},{1,0},{2,3},{3,2},{4,5},{5,4},{6,7},{7,6},{8,9},{9,8},{10,11... | collective-permute-start | bytes 2654216 | tf_op jit(solution)/shard_map/ppermute | solution.py:367
  1016.3 33.9 %collective-permute-start.15 = (bf16[128,3456]{1,0:T(8,128)(2,1)}, bf16[128,3456]{1,0:T(8,128)(2,1)}, u32[]{:S(2)}, u32[]{:S(2)}) collective-permute-start(bf16[128,3456]{1,0:T(8,128)(2,1)} %collective-permute-done.14.refs_2_), channel_id=1, source_target_pairs={{0,1},{1,0},{2,3},{3,2},{4,5},{5,4},{6,7},{7,6},{8,9},{9,8},{10,11... | collective-permute-start | bytes 2654216 | tf_op jit(solution)/shard_map/ppermute | solution.py:367
  1016.6 33.7 %collective-permute-start.18 = (bf16[128,3456]{1,0:T(8,128)(2,1)}, bf16[128,3456]{1,0:T(8,128)(2,1)}, u32[]{:S(2)}, u32[]{:S(2)}) collective-permute-start(bf16[128,3456]{1,0:T(8,128)(2,1)} %collective-permute-done.17.refs_6_), channel_id=1, source_target_pairs={{0,1},{1,0},{2,3},{3,2},{4,5},{5,4},{6,7},{7,6},{8,9},{9,8},{10,11... | collective-permute-start | bytes 2654216 | tf_op jit(solution)/shard_map/ppermute | solution.py:367
  1016.8 33.5 %collective-permute-start.21 = (bf16[128,3456]{1,0:T(8,128)(2,1)}, bf16[128,3456]{1,0:T(8,128)(2,1)}, u32[]{:S(2)}, u32[]{:S(2)}) collective-permute-start(bf16[128,3456]{1,0:T(8,128)(2,1)} %collective-permute-done.20.refs_10_), channel_id=1, source_target_pairs={{0,1},{1,0},{2,3},{3,2},{4,5},{5,4},{6,7},{7,6},{8,9},{9,8},{10,11... | collective-permute-start | bytes 2654216 | tf_op jit(solution)/shard_map/ppermute | solution.py:367
  1017.2 60.2 %collective-permute-start.54 = (bf16[128,4304]{0,1:T(8,128)(2,1)}, bf16[128,4304]{0,1:T(8,128)(2,1)}, u32[]{:S(2)}, u32[]{:S(2)}) collective-permute-start(bf16[128,4304]{0,1:T(8,128)(2,1)} %collective-permute-done.53), channel_id=1, source_target_pairs={{0,1},{1,0},{2,3},{3,2},{4,5},{5,4},{6,7},{7,6},{8,9},{9,8},{10,11... | collective-permute-start | bytes 3305480 | tf_op jit(solution)/shard_map/ppermute | solution.py:367
  1049.8 52.2 %collective-permute-start.42 = (bf16[128,4304]{0,1:T(8,128)(2,1)}, bf16[128,4304]{0,1:T(8,128)(2,1)}, u32[]{:S(2)}, u32[]{:S(2)}) collective-permute-start(bf16[128,4304]{0,1:T(8,128)(2,1)} %copy-done.82), channel_id=1, source_target_pairs={{0,1},{1,0},{2,3},{3,2},{4,5},{5,4},{6,7},{7,6},{8,9},{9,8},{10,11... | collective-permute-start | bytes 3305480 | tf_op jit(solution)/shard_map/ppermute | solution.py:367
  1050.2 57.2 %collective-permute-start.45 = (bf16[128,4304]{0,1:T(8,128)(2,1)}, bf16[128,4304]{0,1:T(8,128)(2,1)}, u32[]{:S(2)}, u32[]{:S(2)}) collective-permute-start(bf16[128,4304]{0,1:T(8,128)(2,1)} %copy-done.83), channel_id=1, source_target_pairs={{0,1},{1,0},{2,3},{3,2},{4,5},{5,4},{6,7},{7,6},{8,9},{9,8},{10,11... | collective-permute-start | bytes 3305480 | tf_op jit(solution)/shard_map/ppermute | solution.py:367
  1069.0 59.5 %collective-permute-start.22 = (bf16[72,3456]{1,0:T(8,128)(2,1)}, bf16[72,3456]{1,0:T(8,128)(2,1)}, u32[]{:S(2)}, u32[]{:S(2)}) collective-permute-start(bf16[72,3456]{1,0:T(8,128)(2,1)} %get-tuple-element.107), channel_id=1, source_target_pairs={{0,4},{1,5},{2,6},{3,7},{4,0},{5,1},{6,2},{7,3},{8,12},{9,13},{10,... | collective-permute-start | bytes 1493000 | tf_op jit(solution)/shard_map/ppermute | solution.py:367
  1077.4 52.7 %collective-permute-start.23 = (bf16[72,3456]{1,0:T(8,128)(2,1)}, bf16[72,3456]{1,0:T(8,128)(2,1)}, u32[]{:S(2)}, u32[]{:S(2)}) collective-permute-start(bf16[72,3456]{1,0:T(8,128)(2,1)} %get-tuple-element.109), channel_id=1, source_target_pairs={{0,8},{1,9},{2,10},{3,11},{4,12},{5,13},{6,14},{7,15},{8,0},{9,1},... | collective-permute-start | bytes 1493000 | tf_op jit(solution)/shard_map/ppermute | solution.py:367
  1077.4 72.9 %collective-permute-start.24 = (bf16[72,3456]{1,0:T(8,128)(2,1)}, bf16[72,3456]{1,0:T(8,128)(2,1)}, u32[]{:S(2)}, u32[]{:S(2)}) collective-permute-start(bf16[72,3456]{1,0:T(8,128)(2,1)} %get-tuple-element.108), channel_id=1, source_target_pairs={{0,12},{1,13},{2,14},{3,15},{4,8},{5,9},{6,10},{7,11},{8,4},{9,5},... | collective-permute-start | bytes 1493000 | tf_op jit(solution)/shard_map/ppermute | solution.py:367
  1102.1 55.2 %collective-permute-start.55 = (bf16[72,4304]{1,0:T(8,128)(2,1)}, bf16[72,4304]{1,0:T(8,128)(2,1)}, u32[]{:S(2)}, u32[]{:S(2)}) collective-permute-start(bf16[72,4304]{1,0:T(8,128)(2,1)} %get-tuple-element.101), channel_id=1, source_target_pairs={{0,4},{1,5},{2,6},{3,7},{4,0},{5,1},{6,2},{7,3},{8,12},{9,13},{10,... | collective-permute-start | bytes 1859336 | tf_op jit(solution)/shard_map/ppermute | solution.py:367
  1107.4 54.5 %collective-permute-start.56 = (bf16[72,4304]{1,0:T(8,128)(2,1)}, bf16[72,4304]{1,0:T(8,128)(2,1)}, u32[]{:S(2)}, u32[]{:S(2)}) collective-permute-start(bf16[72,4304]{1,0:T(8,128)(2,1)} %get-tuple-element.103), channel_id=1, source_target_pairs={{0,8},{1,9},{2,10},{3,11},{4,12},{5,13},{6,14},{7,15},{8,0},{9,1},... | collective-permute-start | bytes 1859336 | tf_op jit(solution)/shard_map/ppermute | solution.py:367
  1128.5 75.5 %collective-permute-start.57 = (bf16[72,4304]{1,0:T(8,128)(2,1)}, bf16[72,4304]{1,0:T(8,128)(2,1)}, u32[]{:S(2)}, u32[]{:S(2)}) collective-permute-start(bf16[72,4304]{1,0:T(8,128)(2,1)} %get-tuple-element.102), channel_id=1, source_target_pairs={{0,12},{1,13},{2,14},{3,15},{4,8},{5,9},{6,10},{7,11},{8,4},{9,5},... | collective-permute-start | bytes 1859336 | tf_op jit(solution)/shard_map/ppermute | solution.py:367
  1130.1 76.9 %collective-permute-start.46 = (bf16[72,4304]{1,0:T(8,128)(2,1)}, bf16[72,4304]{1,0:T(8,128)(2,1)}, u32[]{:S(2)}, u32[]{:S(2)}) collective-permute-start(bf16[72,4304]{1,0:T(8,128)(2,1)} %get-tuple-element.104), channel_id=1, source_target_pairs={{0,4},{1,5},{2,6},{3,7},{4,0},{5,1},{6,2},{7,3},{8,12},{9,13},{10,... | collective-permute-start | bytes 1859336 | tf_op jit(solution)/shard_map/ppermute | solution.py:367
  1150.3 65.3 %collective-permute-start.47 = (bf16[72,4304]{1,0:T(8,128)(2,1)}, bf16[72,4304]{1,0:T(8,128)(2,1)}, u32[]{:S(2)}, u32[]{:S(2)}) collective-permute-start(bf16[72,4304]{1,0:T(8,128)(2,1)} %get-tuple-element.106), channel_id=1, source_target_pairs={{0,8},{1,9},{2,10},{3,11},{4,12},{5,13},{6,14},{7,15},{8,0},{9,1},... | collective-permute-start | bytes 1859336 | tf_op jit(solution)/shard_map/ppermute | solution.py:367
  1157.3 72.9 %collective-permute-start.48 = (bf16[72,4304]{1,0:T(8,128)(2,1)S(1)}, bf16[72,4304]{1,0:T(8,128)(2,1)S(1)}, u32[]{:S(2)}, u32[]{:S(2)}) collective-permute-start(bf16[72,4304]{1,0:T(8,128)(2,1)S(1)} %copy-done.88), channel_id=1, source_target_pairs={{0,12},{1,13},{2,14},{3,15},{4,8},{5,9},{6,10},{7,11},{8,4},{9,5},... | collective-permute-start | bytes 1859336 | tf_op jit(solution)/shard_map/ppermute | solution.py:367
  (177 other events, 4393.8 us)

commit v2 on v1

--- a/solution.py
+++ b/solution.py
@@ -12,6 +12,8 @@
 HEADS = 16
 HEAD_DIM = 72
 FF = 4304
+FFP = -(-FF // 256) * 256
+SPLIT = 9 * 256
 BLOCK = 128
 IMG_BLOCKS = 6
 EPSILON = 1e-06
@@ -151,13 +153,98 @@
     )(*arrays)
 
 
-def exchange_kernel(x_ref, o_ref, local_sem, send_sem, recv_sem):
-    count = x_ref.shape[0]
-    sec, me = place()
+def flip(low, k):
+    return [low, low + 1 - 2 * (low % 2), (low + 2) % 4, 3 - low][k]
+
+
+def greet_all(count, sec, me):
     barrier = pltpu.get_barrier_semaphore()
     for d in range(1, count):
         pl.semaphore_signal(barrier, inc=1, device_id=(sec, (me + d) % count), device_id_type=MESH)
     pl.semaphore_wait(barrier, count - 1)
+
+
+class Whole:
+    def __init__(self, zero, one, cols=None):
+        self.sources, self.cols = (zero, one), cols
+
+    def shape(self):
+        rows, cols = self.sources[0].shape
+        return (4, rows, cols if self.cols is None else self.cols[1] - self.cols[0])
+
+    def source(self, ref, low, k):
+        return ref if self.cols is None else ref.at[:, self.cols[0] : self.cols[1]]
+
+    forwarded = True
+
+
+class Rows:
+    def __init__(self, zero, one):
+        self.sources = (zero, one)
+
+    def shape(self):
+        return self.sources[0].shape
+
+    def source(self, ref, low, k):
+        return ref.at[flip(low, k)]
+
+    forwarded = False
+
+
+class PlaneCopies:
+    def __init__(self, item, zero_ref, one_ref, slot, local_sem, send_sem, recv_sem):
+        self.item, self.refs, self.slot = item, (zero_ref, one_ref), slot
+        self.local_sem, self.send_sem, self.recv_sem = local_sem, send_sem, recv_sem
+        self.sec, self.me = place()
+        self.low = self.me % 4
+
+    def remote(self, src, k, to):
+        return pltpu.make_async_remote_copy(
+            src_ref=src,
+            dst_ref=self.slot(k),
+            send_sem=self.send_sem.at[k],
+            recv_sem=self.recv_sem.at[k],
+            device_id=(self.sec, self.me - self.low + flip(self.low, to)),
+            device_id_type=MESH,
+        )
+
+    def local(self, ref):
+        return pltpu.make_async_copy(self.item.source(ref, self.low, 0), self.slot(0), self.local_sem)
+
+    def start(self):
+        def go(ref):
+            self.local(ref).start()
+            for k in (2, 1) if self.item.forwarded else (2, 3, 1):
+                self.remote(self.item.source(ref, self.low, k), k, k).start()
+
+        @pl.when(self.sec == 0)
+        def _():
+            go(self.refs[0])
+
+        @pl.when(self.sec == 1)
+        def _():
+            go(self.refs[1])
+
+    def forward(self):
+        if self.item.forwarded:
+            self.remote(self.slot(2), 2, 2).wait_recv()
+            self.remote(self.slot(2), 3, 1).start()
+
+    def finish(self):
+        self.local(self.refs[0]).wait()
+        for k in (1, 2, 3):
+            self.remote(self.slot(k), k, k).wait_send()
+            if k != 2 or not self.item.forwarded:
+                self.remote(self.slot(k), k, k).wait_recv()
+
+
+def exchange_kernel(items, x_ref, *refs):
+    n = len(items)
+    sources, o_ref, outs = refs[: 2 * n], refs[2 * n], refs[2 * n + 1 : 3 * n + 1]
+    local_sem, send_sem, recv_sem = refs[3 * n + 1 : 3 * n + 4]
+    count = x_ref.shape[0]
+    sec, me = place()
+    greet_all(count, sec, me)
     copies = []
     half = count // 2
     order = sorted(range(1, count), key=lambda d: abs(d - half))
@@ -176,25 +263,41 @@
         copies[-1].start()
     own = pltpu.make_async_copy(x_ref.at[me], o_ref.at[me], local_sem)
     own.start()
+    behind = []
+    for i, item in enumerate(items):
+        sems = refs[3 * n + 4 + 3 * i : 3 * n + 7 + 3 * i]
+        behind.append(
+            PlaneCopies(item, sources[2 * i], sources[2 * i + 1], lambda k, i=i: outs[i].at[k], *sems)
+        )
+        behind[-1].start()
     own.wait()
+    for one in behind:
+        one.forward()
     for copy in copies:
         copy.wait()
-
-
-def exchange(x, cid):
+    for one in behind:
+        one.finish()
+
+
+def exchange(x, cid, items=()):
     count = x.shape[0]
-    return pl.pallas_call(
-        exchange_kernel,
-        out_shape=jax.ShapeDtypeStruct(x.shape, x.dtype),
-        in_specs=[pl.BlockSpec(memory_space=pl.ANY)],
-        out_specs=pl.BlockSpec(memory_space=pl.ANY),
+    sources = [source for item in items for source in item.sources]
+    anywhere = pl.BlockSpec(memory_space=pl.ANY)
+    out = pl.pallas_call(
+        functools.partial(exchange_kernel, list(items)),
+        out_shape=[jax.ShapeDtypeStruct(x.shape, x.dtype)]
+        + [jax.ShapeDtypeStruct(item.shape(), item.sources[0].dtype) for item in items],
+        in_specs=[anywhere] * (1 + len(sources)),
+        out_specs=[anywhere] * (1 + len(items)),
         scratch_shapes=[
             pltpu.SemaphoreType.DMA,
             pltpu.SemaphoreType.DMA((count,)),
             pltpu.SemaphoreType.DMA((count,)),
-        ],
+        ]
+        + [pltpu.SemaphoreType.DMA, pltpu.SemaphoreType.DMA((4,)), pltpu.SemaphoreType.DMA((4,))] * len(items),
         compiler_params=pltpu.CompilerParams(collective_id=cid, has_side_effects=True),
-    )(x)
+    )(x, *sources)
+    return out if items else out[0]
 
 
 def dot(a, b):
@@ -363,33 +466,211 @@
     return x.T.reshape(HEADS, HEAD_DIM, x.shape[0])
 
 
-def swap(x, bits):
-    return lax.ppermute(x, "wide", [(i, i ^ bits) for i in range(HEADS)])
-
-
-def dw_kernel(count, x_ref, *refs):
-    ys, o_ref = refs[:count], refs[count]
-    for t in range(count):
-        term = dot(x_ref[t], ys[t][...])
-        if t == 0:
-            total = term
+def pad_ff(x):
+    return jnp.pad(x, ((0, 0),) * (x.ndim - 1) + ((0, FFP - FF),))
+
+
+def owners(x):
+    return x.reshape(4, 4, HEAD_DIM, BLOCK).swapaxes(0, 1)
+
+
+TENSORS = ("fc2", "fc1", "out", "qkv")
+
+
+def final_kernel(tiles, early, late, *refs):
+    refs = list(refs)
+
+    def take(n):
+        part = refs[:n]
+        del refs[:n]
+        return part
+
+    small_ref = take(1)[0]
+    x_refs = {name: take(2) for name in TENSORS}
+    early_refs = take(len(early))
+    late_refs = take(2 * len(late))
+    small_out = take(1)[0]
+    out_refs = dict(zip(TENSORS, take(4)))
+    y_bufs = dict(zip(TENSORS, take(4)))
+    x_buf = take(1)[0]
+    g_bufs, one_bufs, two_bufs = [dict(zip(TENSORS, take(4))) for _ in range(3)]
+    small_got = take(1)[0]
+    early_sem, small_send, small_recv = take(3)
+    sems = {name: take(4) for name in TENSORS}
+    late_sems = [take(3) for _ in late]
+
+    sec, me = place()
+    z, low = me // 4, me % 4
+    pair = z + 1 - 2 * (z % 2)
+    count = small_ref.shape[0]
+    greet_all(count, sec, me)
+
+    loads = []
+    for i, (name, batch, cols) in enumerate(early):
+        dst = y_bufs[name].at[4 * batch : 4 * batch + 4]
+        if cols is not None:
+            dst = dst.at[:, :, cols[0] : cols[1]]
+        loads.append((name, pltpu.make_async_copy(early_refs[i], dst, early_sem.at[i])))
+        loads[-1][1].start()
+    behind = []
+    for i, (name, batch, item) in enumerate(late):
+
+        def slot(k, name=name, batch=batch, item=item):
+            ref = y_bufs[name].at[4 * batch + k]
+            return ref if item.cols is None else ref.at[:, item.cols[0] : item.cols[1]]
+
+        behind.append((name, PlaneCopies(item, late_refs[2 * i], late_refs[2 * i + 1], slot, *late_sems[i])))
+        behind[-1][1].start()
+    smalls = []
+    for d in range(1, count):
+        target = (me + d) % count
+        smalls.append(
+            pltpu.make_async_remote_copy(
+                src_ref=small_ref.at[target],
+                dst_ref=small_got.at[d],
+                send_sem=small_send.at[d],
+                recv_sem=small_recv.at[d],
+                device_id=(sec, target),
+                device_id_type=MESH,
+            )
+        )
+        smalls[-1].start()
+
+    def first(name, i):
+        send, recv = sems[name][0], sems[name][1]
+        return pltpu.make_async_remote_copy(
+            src_ref=g_bufs[name].at[i, 2:4],
+            dst_ref=one_bufs[name].at[i],
+            send_sem=send.at[i],
+            recv_sem=recv.at[i],
+            device_id=(sec, pair * 4 + low),
+            device_id_type=MESH,
+        )
+
+    def second(name, i):
+        send, recv = sems[name][2], sems[name][3]
+        return pltpu.make_async_remote_copy(
+            src_ref=g_bufs[name].at[i, 1],
+            dst_ref=two_bufs[name].at[i],
+            send_sem=send.at[i],
+            recv_sem=recv.at[i],
+            device_id=(sec, (3 - z) * 4 + low),
+            device_id_type=MESH,
+        )
+
+    def ready(name):
+        for other, one in behind:
+            if other == name:
+                one.forward()
+        for other, load in loads:
+            if other == name:
+                load.wait()
+        for other, one in behind:
+            if other == name:
+                one.finish()
+        rows = []
+        for owner in (z, 3 - z, pair, 3 - pair):
+            rows.append(
+                jnp.concatenate(
+                    [x_refs[name][batch][k, owner].astype(F32) for batch in range(2) for k in range(4)], axis=1
+                )
+            )
+        x_buf[...] = jnp.concatenate(rows, axis=0).astype(BF)
+
+    def columns(name, i):
+        width = tiles[name][1]
+        return pl.ds(pl.multiple_of(i * width, 128), width)
+
+    def compute(name, i):
+        width = tiles[name][1]
+        buf = y_bufs[name]
+        if name == "qkv":
+            rows = pl.ds(pl.multiple_of(i * width, 128), width)
+            y = jnp.concatenate([buf[part, rows, :] for part in range(8)], axis=1)
+            total = lax.dot_general(x_buf[...], y, (((1,), (1,)), ((), ())), preferred_element_type=F32)
         else:
-            total = total + term
-    o_ref[...] = total.astype(o_ref.dtype)
-
-
-def weight_grad(x, ys, tile):
-    count, rows, block = x.shape
-    cols = ys[0].shape[1]
-    return pl.pallas_call(
-        functools.partial(dw_kernel, count),
-        grid=(pl.cdiv(cols, tile),),
-        out_shape=jax.ShapeDtypeStruct((rows, cols), BF),
-        in_specs=[pl.BlockSpec((count, rows, block), lambda j: (0, 0, 0))]
-        + [pl.BlockSpec((block, tile), lambda j: (0, j))] * count,
-        out_specs=pl.BlockSpec((rows, tile), lambda j: (0, j)),
-        compiler_params=pltpu.CompilerParams(vmem_limit_bytes=48 << 20),
-    )(x, *ys)
+            y = jnp.concatenate([buf[part, :, columns(name, i)] for part in range(8)], axis=0)
+            total = dot(x_buf[...], y)
+        g_bufs[name][i] = total.reshape(4, HEAD_DIM, width).astype(BF)
+        first(name, i).start()
+
+    def middle(name, i):
+        first(name, i).wait_recv()
+        out_refs[name][:, columns(name, i)] = g_bufs[name][i, 0].astype(F32) + one_bufs[name][i, 0].astype(F32)
+        g_bufs[name][i, 1] = (g_bufs[name][i, 1].astype(F32) + one_bufs[name][i, 1].astype(F32)).astype(BF)
+        second(name, i).start()
+
+    def finish(name, i):
+        second(name, i).wait_recv()
+        out_refs[name][:, columns(name, i)] += two_bufs[name][i].astype(F32)
+        first(name, i).wait_send()
+        second(name, i).wait_send()
+
+    def loop(name, *steps):
+        def body(i, carry):
+            for step, which in steps:
+                step(which, i)
+            return carry
+
+        lax.fori_loop(0, tiles[name][0], body, 0)
+
+    ready("fc2")
+    loop("fc2", (compute, "fc2"))
+    ready("fc1")
+    loop("fc1", (compute, "fc1"), (middle, "fc2"))
+    ready("out")
+    loop("out", (compute, "out"))
+    loop("fc1", (middle, "fc1"), (finish, "fc2"))
+    ready("qkv")
+    loop("qkv", (compute, "qkv"))
+    loop("out", (middle, "out"))
+    loop("fc1", (finish, "fc1"))
+    loop("qkv", (middle, "qkv"))
+    loop("out", (finish, "out"))
+    for copy in smalls:
+        copy.wait()
+    total = small_ref[me]
+    for d in range(1, count):
+        total = total + small_got[d]
+    small_out[...] = total
+    loop("qkv", (finish, "qkv"))
+
+
+def final(small, xs, early, late, cid):
+    count = small.shape[0]
+    tokens = xs["qkv"][0].shape[-1]
+    widths = {"fc2": FFP, "fc1": FFP, "out": D, "qkv": 3 * D}
+    tiles = {name: (w // (256 if name[0] == "f" else 384), 256 if name[0] == "f" else 384) for name, w in widths.items()}
+    anywhere, vmem = pl.BlockSpec(memory_space=pl.ANY), pl.BlockSpec(memory_space=pltpu.VMEM)
+    args = [small] + [x for name in TENSORS for x in xs[name]]
+    n_vmem = len(args)
+    args += [e[3] for e in early] + [source for _, _, item in late for source in item.sources]
+    dma = pltpu.SemaphoreType.DMA
+    scratch = []
+    for name in TENSORS:
+        shape = (8, widths[name], tokens) if name == "qkv" else (8, tokens, widths[name])
+        scratch.append(pltpu.VMEM(shape, BF))
+    scratch.append(pltpu.VMEM((4 * HEAD_DIM, 8 * tokens), BF))
+    for lead in ((4,), (2,), ()):
+        for name in TENSORS:
+            scratch.append(pltpu.VMEM((tiles[name][0],) + lead + (HEAD_DIM, tiles[name][1]), BF))
+    scratch.append(pltpu.VMEM(small.shape, F32))
+    scratch += [dma((len(early),)), dma((count,)), dma((count,))]
+    for name in TENSORS:
+        scratch += [dma((tiles[name][0],))] * 4
+    scratch += [dma, dma((4,)), dma((4,))] * len(late)
+    out = pl.pallas_call(
+        functools.partial(final_kernel, tiles, [e[:3] for e in early], late),
+        out_shape=[jax.ShapeDtypeStruct(small.shape[1:], F32)]
+        + [jax.ShapeDtypeStruct((HEAD_DIM, widths[name]), F32) for name in TENSORS],
+        in_specs=[vmem] * n_vmem + [anywhere] * (len(args) - n_vmem),
+        out_specs=[vmem] * 5,
+        scratch_shapes=scratch,
+        compiler_params=pltpu.CompilerParams(
+            collective_id=cid, has_side_effects=True, vmem_limit_bytes=60 << 20
+        ),
+    )(*args)
+    return out[0], dict(zip(TENSORS, out[1:]))
 
 
 def on_device(
@@ -410,95 +691,113 @@
     fc2_bias,
 ):
     sec, me = place()
-    micro = tokens.shape[0]
-    low = me % 4
     own_qkv = qkv_weight[0].reshape(HEAD_DIM, 3, HEADS, HEAD_DIM).transpose(0, 2, 1, 3).reshape(HEAD_DIM, 3 * D)
     small = jnp.stack(
         [ln1_gain[0], ln1_bias[0], qv_bias[0, 0], qv_bias[0, 1], out_bias[0], ln2_gain[0], ln2_bias[0], fc2_bias[0]]
     )
     small = jnp.pad(small, ((0, 8), (0, BLOCK - HEAD_DIM)))
     w_qkv, w_out, w_fc1, w_fc2t, small_all = gather(
-        [own_qkv, out_weight[0], fc1_weight[0], fc2_weight[0].T, small], 1
+        [own_qkv, out_weight[0], pad_ff(fc1_weight[0]), pad_ff(fc2_weight[0].T), small], 1
     )
     w_qkv = w_qkv.reshape(D, 3 * D)
     w_out = w_out.reshape(D, D)
-    w_fc1 = w_fc1.reshape(D, FF)
-    w_fc2t = w_fc2t.reshape(D, FF)
+    w_fc1 = w_fc1.reshape(D, FFP)
+    w_fc2t = w_fc2t.reshape(D, FFP)
     vectors = small_all[:, :8, :HEAD_DIM].astype(F32)
     gain1, bias1, _, _, b_out, gain2, bias2, b_fc2 = [vectors[:, i].reshape(D) for i in range(8)]
     b_qkv = jnp.stack([vectors[:, 2], jnp.zeros_like(vectors[:, 2]), vectors[:, 3]], axis=1).reshape(3 * D, 1)
-    b_fc1 = fc1_bias[0].astype(F32)
-
-    firsts = [window_first(image_of_block[m]) for m in range(micro)]
-
-    def slot_of(batch):
-        return jnp.clip(batch, 0, micro - 1)
+    b_fc1 = pad_ff(fc1_bias[0]).astype(F32)
+
+    def choose(at_zero, at_one):
+        return jax.tree.map(lambda a, b: jnp.where(sec == 0, a, b), at_zero, at_one)
 
     saved = []
     incoming = jnp.zeros_like(tokens[0])
-    for tick in range(micro + 1):
-        slot = slot_of(tick - sec)
+    sent = {}
+    for tick in range(3):
+        slot = jnp.clip(tick - sec, 0, 1)
         image_row = lax.dynamic_index_in_dim(image_of_block, slot, 0, keepdims=False)
         first = window_first(image_row)
-        x = jnp.where(sec == 0, tokens[min(tick, micro - 1)], incoming).astype(F32)
-        xhat1, rstd1 = normalised(x)
+        x = jnp.where(sec == 0, tokens[min(tick, 1)], incoming).astype(F32)
+        xhat1, _ = normalised(x)
         n1 = (xhat1 * gain1 + bias1).astype(BF)
         qkv = jnp.einsum("ck,tc->kt", w_qkv, n1, preferred_element_type=F32) + b_qkv
-        qkv = exchange(qkv.astype(BF).reshape(HEADS, 3 * HEAD_DIM, BLOCK), 2)
-        att, lse = attention_fwd(image_row, first, qkv)
-        att = exchange(att, 3)
+        qkv = qkv.astype(BF).reshape(HEADS, 3 * HEAD_DIM, BLOCK)
+        if tick < 2:
+            qkv = exchange(qkv, 2)
+            att, lse = attention_fwd(image_row, first, qkv)
+            att = exchange(att, 3)
+        else:
+            old = [saved[0], saved[1]]
+            qkv, sent["h0a"] = exchange(qkv, 4, [Whole(old[0]["hidden"], old[1]["hidden"], (0, SPLIT))])
+            att, lse = attention_fwd(image_row, first, qkv)
+            att, sent["n1_0"], sent["att_0"], sent["n2_0"] = exchange(
+                att, 5, [Rows(old[0][name], old[1][name]) for name in ("n1", "att_rows", "n2")]
+            )
         residual = x + jnp.einsum("ct,cd->td", att.reshape(D, BLOCK), w_out, preferred_element_type=F32) + b_out
-        xhat2, rstd2 = normalised(residual)
+        xhat2, _ = normalised(residual)
         n2 = (xhat2 * gain2 + bias2).astype(BF)
         hidden_pre = jnp.einsum("td,df->tf", n2, w_fc1, preferred_element_type=F32) + b_fc1
         value, _ = gelu_and_slope(hidden_pre)
         hidden = value.astype(BF)
         out = residual + jnp.einsum("tf,df->td", hidden, w_fc2t, preferred_element_type=F32) + b_fc2
         out_low = out.astype(BF)
-        saved.append((x, qkv, lse, att, residual, n2, hidden_pre, hidden, n1, out_low, image_row, first))
-        if tick < micro:
+        saved.append(
+            dict(
+                x=x, qkv=qkv, lse=lse, residual=residual, hidden_pre=hidden_pre, hidden=hidden, low=out_low,
+                att_rows=owners(att), n1=owners(by_rows(n1)), n2=owners(by_rows(n2)), image=image_row, first=first,
+            )
+        )
+        if tick < 2:
             incoming = lax.ppermute(out_low, "section", [(0, 1)])
-    outputs = jnp.stack([jnp.where(sec == 0, saved[m][9], saved[m + 1][9]) for m in range(micro)])
+    outputs = jnp.stack([choose(saved[m]["low"], saved[m + 1]["low"]) for m in range(2)])
 
     incoming_grad = jnp.zeros(tokens.shape[1:], BF)
-    input_grads = []
-    x_terms, y_terms, small_total, fc1_bias_total = [], [], 0.0, 0.0
-    for tick in range(micro + 1):
-        live = jnp.where(sec == 1, tick < micro, tick >= 1).astype(F32)
-        late, early = min(tick + 1, micro), max(tick - 1, 0)
-        if tick == 0:
-            early = late
-        if tick == micro:
-            late = early
-        if late == early:
-            kept = saved[late]
+    input_grads, done, back = [], [], []
+    needed = ("x", "qkv", "lse", "residual", "hidden_pre", "image", "first")
+    for tick in range(3):
+        if tick == 1:
+            k = choose({name: saved[0][name] for name in needed}, {name: saved[2][name] for name in needed})
         else:
-            kept = tuple(jnp.where(sec == 1, a, b) for a, b in zip(saved[late], saved[early]))
-        x, qkv, lse, att, residual, n2, hidden_pre, hidden, n1, _, image_row, first = kept
-        grad = jnp.where(sec == 1, cotangent[min(tick, micro - 1)], incoming_grad).astype(F32) * live
+            k = saved[1]
+        grad = jnp.where(sec == 1, cotangent[min(tick, 1)], incoming_grad).astype(F32)
         fc_grad = grad.astype(BF)
         hidden_grad = jnp.einsum("td,df->tf", fc_grad, w_fc2t, preferred_element_type=F32)
-        _, slope = gelu_and_slope(hidden_pre)
+        _, slope = gelu_and_slope(k["hidden_pre"])
         pre_grad = (hidden_grad * slope).astype(BF)
         n2_grad = jnp.einsum("tf,df->td", pre_grad, w_fc1, preferred_element_type=F32)
-        xhat2, rstd2 = normalised(residual)
+        xhat2, rstd2 = normalised(k["residual"])
         part, g_gain2, g_bias2 = norm_backward(n2_grad, xhat2, rstd2, gain2)
         residual_grad = grad + part
         branch = residual_grad.astype(BF)
         att_grad = jnp.einsum("td,cd->ct", branch, w_out, preferred_element_type=F32).astype(BF)
-        att_grad = exchange(att_grad.reshape(HEADS, HEAD_DIM, BLOCK), 3)
-        dqkv = attention_bwd(image_row, first, qkv, lse, att_grad)
-        dqkv = exchange(dqkv, 2)
-        dqkv_rows = dqkv.reshape(3 * D, BLOCK)
-        n1_grad = jnp.einsum("kt,ck->tc", dqkv_rows, w_qkv, preferred_element_type=F32)
-        xhat1, rstd1 = normalised(x)
+        att_grad = att_grad.reshape(HEADS, HEAD_DIM, BLOCK)
+        back.append(dict(fc=owners(by_rows(fc_grad)), pre=pre_grad, branch=branch))
+        if tick == 0:
+            att_grad, sent["h0b"] = exchange(att_grad, 6, [Whole(saved[0]["hidden"], saved[1]["hidden"], (SPLIT, FFP))])
+        elif tick == 1:
+            att_grad, sent["n1_1"], sent["att_1"], sent["n2_1"] = exchange(
+                att_grad, 8, [Rows(saved[1][name], saved[2][name]) for name in ("n1", "att_rows", "n2")]
+            )
+        else:
+            att_grad, sent["fc_0"], sent["fc_1"] = exchange(
+                att_grad, 10, [Rows(back[1]["fc"], back[0]["fc"]), Rows(back[2]["fc"], back[1]["fc"])]
+            )
+        dqkv = attention_bwd(k["image"], k["first"], k["qkv"], k["lse"], att_grad)
+        if tick == 0:
+            dqkv, sent["h1a"] = exchange(dqkv, 7, [Whole(saved[1]["hidden"], saved[2]["hidden"], (0, SPLIT))])
+        elif tick == 1:
+            dqkv, sent["h1b"] = exchange(dqkv, 9, [Whole(saved[1]["hidden"], saved[2]["hidden"], (SPLIT, FFP))])
+        else:
+            dqkv, sent["pre_0a"] = exchange(dqkv, 11, [Whole(back[1]["pre"], back[0]["pre"], (0, SPLIT))])
+        back[-1]["dqkv"] = dqkv.reshape(3 * D, BLOCK)
+        n1_grad = jnp.einsum("kt,ck->tc", back[-1]["dqkv"], w_qkv, preferred_element_type=F32)
+        xhat1, rstd1 = normalised(k["x"])
         part, g_gain1, g_bias1 = norm_backward(n1_grad, xhat1, rstd1, gain1)
         input_grad = residual_grad + part
         input_grads.append(input_grad)
-        if tick < micro:
-            incoming_grad = lax.ppermute(input_grad.astype(BF), "section", [(1, 0)])
         sums = jnp.sum(dqkv.astype(F32), axis=2)
-        small_total = small_total + jnp.stack(
+        done.append(
             [
                 g_gain1,
                 g_bias1,
@@ -508,40 +807,44 @@
                 g_gain2,
                 g_bias2,
                 jnp.sum(fc_grad.astype(F32), axis=0),
+                jnp.sum(pre_grad.astype(F32), axis=0),
             ]
         )
-        fc1_bias_total = fc1_bias_total + jnp.sum(pre_grad.astype(F32), axis=0)
-        xs = jnp.stack([by_rows(n1), att, by_rows(n2), by_rows(fc_grad)]).reshape(4, 4, 4, HEAD_DIM, BLOCK)
-        x_of = [lax.dynamic_index_in_dim(xs, low ^ k, 2, keepdims=False) for k in range(4)]
-        x_all = [x_of[0]] + [swap(x_of[k], k) for k in range(1, 4)]
-        y_own = (dqkv_rows.T, branch, pre_grad, hidden)
-        y_two = tuple(swap(y, 2) for y in y_own)
-        y_one = tuple(swap(y, 1) for y in y_own)
-        y_three = tuple(swap(y, 1) for y in y_two)
-        x_terms += x_all
-        y_terms += [y_own, y_one, y_two, y_three]
-    input_grads = jnp.stack([jnp.where(sec == 0, input_grads[m + 1], input_grads[m]) for m in range(micro)])
-
-    def owned(index, tile):
-        x = jnp.stack([x[index] for x in x_terms]).reshape(len(x_terms), 4 * HEAD_DIM, BLOCK)
-        total = weight_grad(x, [y[index] for y in y_terms], tile)
-        total = total.reshape(4, HEAD_DIM, total.shape[1])
-        z = me // 4
-        result = lax.dynamic_index_in_dim(total, z, 0, keepdims=False).astype(F32)
-        for k in range(1, 4):
-            part = lax.dynamic_index_in_dim(total, z ^ k, 0, keepdims=False)
-            result = result + swap(part, 4 * k).astype(F32)
-        return result
-
-    g_fc2t = owned(3, 512)
-    g_fc1 = owned(2, 512)
-    g_out = owned(1, 384)
-    g_qkv = owned(0, 384)
-    g_qkv = g_qkv.reshape(HEAD_DIM, HEADS, 3, HEAD_DIM).transpose(0, 2, 1, 3).reshape(HEAD_DIM, 3 * D)
-    packed = jnp.concatenate([small_total.reshape(8 * D), fc1_bias_total])
-    packed = lax.psum(packed, "wide")
-    g_small = lax.dynamic_slice_in_dim(packed[: 8 * D].reshape(8, HEADS, HEAD_DIM), me, 1, 1)[:, 0]
-    g_fc1_bias = packed[8 * D :]
+        if tick < 2:
+            incoming_grad = lax.ppermute(input_grad.astype(BF), "section", [(1, 0)])
+    input_grads = jnp.stack([choose(input_grads[m + 1], input_grads[m]) for m in range(2)])
+
+    sums = [choose(done[1][i] + done[2][i], done[0][i] + done[1][i]) for i in range(9)]
+    by_owner = jnp.stack(sums[:8]).reshape(8, HEADS, HEAD_DIM).transpose(1, 0, 2)
+    by_owner = jnp.pad(by_owner, ((0, 0), (0, 0), (0, BLOCK - HEAD_DIM)))
+    lines = FFP // BLOCK
+    to_all = jnp.broadcast_to(sums[8].reshape(1, lines, BLOCK), (HEADS, lines, BLOCK))
+    to_all = jnp.pad(to_all, ((0, 0), (0, 40 - lines), (0, 0)))
+    xs = {
+        "fc2": [sent["fc_0"], sent["fc_1"]],
+        "fc1": [sent["n2_0"], sent["n2_1"]],
+        "out": [sent["att_0"], sent["att_1"]],
+        "qkv": [sent["n1_0"], sent["n1_1"]],
+    }
+    early = [
+        ("fc2", 0, (0, SPLIT), sent["h0a"]),
+        ("fc2", 0, (SPLIT, FFP), sent["h0b"]),
+        ("fc2", 1, (0, SPLIT), sent["h1a"]),
+        ("fc2", 1, (SPLIT, FFP), sent["h1b"]),
+        ("fc1", 0, (0, SPLIT), sent["pre_0a"]),
+    ]
+    late = [
+        ("fc1", 0, Whole(back[1]["pre"], back[0]["pre"], (SPLIT, FFP))),
+        ("fc1", 1, Whole(back[2]["pre"], back[1]["pre"])),
+        ("out", 0, Whole(back[1]["branch"], back[0]["branch"])),
+        ("out", 1, Whole(back[2]["branch"], back[1]["branch"])),
+        ("qkv", 0, Whole(back[1]["dqkv"], back[0]["dqkv"])),
+        ("qkv", 1, Whole(back[2]["dqkv"], back[1]["dqkv"])),
+    ]
+    packed, grads = final(jnp.concatenate([by_owner, to_all], axis=1), xs, early, late, 12)
+    g_small = packed[:8, :HEAD_DIM]
+    g_fc1_bias = packed[8 : 8 + lines].reshape(FFP)[:FF]
+    g_qkv = grads["qkv"].reshape(HEAD_DIM, HEADS, 3, HEAD_DIM).transpose(0, 2, 1, 3).reshape(HEAD_DIM, 3 * D)
     return (
         outputs[None],
         input_grads[None],
@@ -549,13 +852,13 @@
         g_small[1][None],
         g_qkv[None],
         g_small[2:4][None],
-        g_out[None],
+        grads["out"][None],
         g_small[4][None],
         g_small[5][None],
         g_small[6][None],
-        g_fc1[None],
+        grads["fc1"][:, :FF][None],
         g_fc1_bias[None],
-        g_fc2t.T[None],
+        grads["fc2"].T[:FF][None],
         g_small[7][None],
     )
 

time: 1250 us -> 887 us (0.71)
  waiting for transfers between devices: 264 us -> 8.51 us
  Pallas kernels: 482 us -> 644 us
  local copies, waits for them, and re-layouts: 169 us -> 51.1 us
  starting transfers between devices: 65.3 us -> 12.6 us
  blocking collectives: 52.1 us -> 0 us
  other arithmetic: 57.4 us -> 33.6 us
  matrix products: 141 us -> 127 us
    ppermute x54 -> x0, waiting for transfers between devices: 256 us -> none  [swap(): return lax.ppermute(x, 'wide', [(i, i ^ bits) for i in range(HEADS)])]
    pallas_call x16 -> x13, Pallas kernels: 249 us -> 410 us  [the longest x12 257 us: exchange(): pl.pallas_call(functools.partial(exchange_kernel, list(items)), out_shape...]
    ppermute x54 -> x0, starting transfers between devices: 53.5 us -> none  [swap(): return lax.ppermute(x, 'wide', [(i, i ^ bits) for i in range(HEADS)])]
    psum x1 -> x0, blocking collectives: 52.1 us -> none  [on_device(): packed = lax.psum(packed, 'wide')]
    ppermute x15 -> x0, local copies, waits for them, and re-layouts: 35.8 us -> none  [swap(): return lax.ppermute(x, 'wide', [(i, i ^ bits) for i in range(HEADS)])]
    unnamed x378 -> x253, local copies, waits for them, and re-layouts: 36.2 us -> 11.5 us
    another operation x31 -> x10, local copies, waits for them, and re-layouts: 24.6 us -> 7.97 us  [the longest x9 7.87 us: owners(): return x.reshape(4, 4, HEAD_DIM, BLOCK).swapaxes(0, 1)]
    slice x18 -> x0, local copies, waits for them, and re-layouts: 15.6 us -> none  [the longest x12 12.4 us: owned(): x[index]]
  transfers between devices with their start and end apart: 58 -> 4, of which waited for: 21 -> 2; matrix products, arithmetic and copies ran while one was open for 21% -> 3% of each run, Pallas kernels for 18% -> 4%
where the time goes in v2:
time: 887 us; the launch traced here: 879 us
  Pallas kernels  644 us (73%)
  matrix products  127 us (14%)
  local copies, waits for them, and re-layouts  51.1 us (6%)
  other arithmetic  33.6 us (4%)
  starting transfers between devices  12.6 us (1%)
    pallas_call x12, Pallas kernels, exchange(): pl.pallas_call(functools.partial(exchange_kernel, list(items)), out_shape...  257 us
    pallas_call x1, Pallas kernels, gather(): pl.pallas_call(functools.partial(gather_kernel, count), out_shape=[jax.Sh...  176 us
    pallas_call x1, Pallas kernels, final(): pl.pallas_call(functools.partial(final_kernel, tiles, [e[:3] for e in ear...  153 us
    pallas_call x3, Pallas kernels, attention_bwd(): pl.pallas_call(attn_bwd_kernel, out_shape=jax.ShapeDtypeStruct((blocks, 3...  32.4 us
    pallas_call x3, Pallas kernels, attention_fwd(): pl.pallas_call(attn_fwd_kernel, out_shape=[jax.ShapeDtypeStruct((blocks,...  25.7 us
    dot_general x3, matrix products, on_device(): jnp.einsum('td,df->tf', n2, w_fc1, preferred_element_type=F32) + b_fc1  22.8 us
    dot_general x3, matrix products, on_device(): qkv = jnp.einsum('ck,tc->kt', w_qkv, n1, preferred_element_type=F32) + b_qkv  20.6 us
    dot_general x3, matrix products, on_device(): jnp.einsum('td,df->tf', fc_grad, w_fc2t, preferred_element_type=F32)  20.2 us
  transfers between devices with their start and end apart: 4, of which 2 were waited for; matrix products, arithmetic and copies ran while one was open for 3% of the time, Pallas kernels for 4%

profile of v2, /device:TPU:10, one launch (start us, length us, event | category | flops | bytes accessed | tf_op | source)
XLA Modules:
  0.0 879.1 jit_solution(12422188875282759975)
XLA Ops:
  15.0 175.8 %shard_map.254 = (bf16[16,72,3456]{2,1,0:T(8,128)(2,1)}, bf16[16,72,1152]{2,1,0:T(8,128)(2,1)}, bf16[16,72,4352]{2,1,0:T(8,128)(2,1)}, bf16[16,72,4352]{2,1,0:T(8,128)(2,1)}, bf16[16,16,128]{2,1,0:T(8,128)(2,1)}) custom-call(bf16[72,3456]{1,0:T(8,128)(2,1)} %copy.93.refs_0_, bf16[72,1152]{1,0:T(8,128)(2,1)} %bitcast.338, bf16[72,4352]{1,0:T(8,128)(2,1)} %pad.23.refs_2_, ...), custom_call_target="tpu_custom_call" | custom-call | tf_op jit(solution)/shard_map/pallas_call | solution.py:144
  192.5 6.9 fusion.3
  199.4 25.2 %shard_map.255.qkv_ref = bf16[16,216,128]{2,1,0:T(8,128)(2,1)} custom-call(bf16[16,216,128]{2,1,0:T(8,128)(2,1)} %bitcast.329), custom_call_target="tpu_custom_call" | custom-call | tf_op jit(solution)/shard_map/pallas_call | solution.py:286
  226.3 8.4 shard_map.256
  235.5 11.7 %shard_map.257 = bf16[16,72,128]{2,1,0:T(8,128)(2,1)} custom-call(bf16[16,72,128]{2,1,0:T(8,128)(2,1)} %copy-done.12), custom_call_target="tpu_custom_call" | custom-call | tf_op jit(solution)/shard_map/pallas_call | solution.py:286
  247.1 2.6 fusion.112
  250.0 7.5 fusion.24
  257.6 3.3 fusion.15
  264.8 7.0 collective-permute-done
  272.2 6.9 fusion.4
  279.1 22.8 %shard_map.258.qkv_ref = bf16[16,216,128]{2,1,0:T(8,128)(2,1)} custom-call(bf16[16,216,128]{2,1,0:T(8,128)(2,1)} %bitcast.330), custom_call_target="tpu_custom_call" | custom-call | tf_op jit(solution)/shard_map/pallas_call | solution.py:286
  303.0 8.4 shard_map.259
  312.2 11.3 %shard_map.260 = bf16[16,72,128]{2,1,0:T(8,128)(2,1)} custom-call(bf16[16,72,128]{2,1,0:T(8,128)(2,1)} %copy-done.13), custom_call_target="tpu_custom_call" | custom-call | tf_op jit(solution)/shard_map/pallas_call | solution.py:286
  323.5 2.6 fusion.113
  327.2 7.8 multiply_convert_fusion
  335.0 3.3 fusion.16
  339.8 4.9 convert_reduce_fusion
  344.7 3.9 multiply_reduce_fusion
  352.5 3.3 convolution_convert_fusion.2
  355.9 21.7 %shard_map.264 = (bf16[16,72,128]{2,1,0:T(8,128)(2,1)}, bf16[4,128,2048]{2,1,0:T(8,128)(2,1)}) custom-call(bf16[16,72,128]{2,1,0:T(8,128)(2,1)} %bitcast.334, bf16[128,4352]{1,0:T(8,128)(2,1)} %copy-done.31, bf16[128,4352]{1,0:T(8,128)(2,1)} %copy-done.23), custom_call_target="tpu_custom_call" | custom-call | tf_op jit(solution)/shard_map/pallas_call | solution.py:286
  378.6 10.7 %shard_map.265.x_ref = bf16[16,216,128]{2,1,0:T(8,128)(2,1)S(1)} custom-call(s32[16]{0:T(128)S(1)} %fusion.97.img_ref, s32[16]{0:T(128)S(1)} %broadcast_minimum_fusion.1.first_ref, bf16[16,216,128]{2,1,0:T(8,128)(2,1)S(1)} %copy-done.1, f32[16,1,128]{2,1,0:T(1,128)S(1)} %get-tuple-element.67.lse_ref, bf16[16,72,128]{2,1,0:T(8,128)(2,1)S(1)} %copy-done.11), custom_call_target="tpu_custom_call" | custom-call | tf_op jit(solution)/shard_map/pallas_call | solution.py:422
  392.7 6.9 fusion.5
  401.6 29.0 %shard_map.261 = (bf16[16,216,128]{2,1,0:T(8,128)(2,1)}, bf16[4,128,2304]{2,1,0:T(8,128)(2,1)}) custom-call(bf16[16,216,128]{2,1,0:T(8,128)(2,1)} %bitcast.328, bf16[128,4352]{1,0:T(8,128)(2,1)} %copy-done.31, bf16[128,4352]{1,0:T(8,128)(2,1)} %copy-done.23), custom_call_target="tpu_custom_call" | custom-call | tf_op jit(solution)/shard_map/pallas_call | solution.py:286
  431.7 8.9 %shard_map.262 = (bf16[16,72,128]{2,1,0:T(8,128)(2,1)S(1)}, f32[16,1,128]{2,1,0:T(1,128)S(1)}) custom-call(s32[16]{0:T(128)S(1)} %get-tuple-element.144.img_ref, s32[16]{0:T(128)S(1)} %get-tuple-element.171.first_ref, bf16[16,216,128]{2,1,0:T(8,128)(2,1)S(1)} %copy-done.7), custom_call_target="tpu_custom_call" | custom-call | tf_op jit(solution)/shard_map/pallas_call | solution.py:352
  441.3 17.6 %shard_map.263 = (bf16[16,72,128]{2,1,0:T(8,128)(2,1)}, bf16[4,4,72,128]{3,2,1,0:T(8,128)(2,1)}, bf16[4,4,72,128]{3,2,1,0:T(8,128)(2,1)}, bf16[4,4,72,128]{3,2,1,0:T(8,128)(2,1)}) custom-call(bf16[16,72,128]{2,1,0:T(8,128)(2,1)} %copy-done.14, bf16[4,4,72,128]{3,2,1,0:T(8,128)(2,1)} %bitcast.326, bf16[4,4,72,128]{3,2,1,0:T(8,128)(2,1)} %bitcast.304, ...), custom_call_target="tpu_custom_call" | custom-call | tf_op jit(solution)/shard_map/pallas_call | solution.py:286
  458.9 2.6 fusion.114
  462.8 7.5 fusion.31
  471.4 4.0 fusion.19
  475.4 29.1 %shard_map.266 = (bf16[16,216,128]{2,1,0:T(8,128)(2,1)}, bf16[4,128,2304]{2,1,0:T(8,128)(2,1)}) custom-call(bf16[16,216,128]{2,1,0:T(8,128)(2,1)} %copy-done.4, bf16[128,4352]{1,0:T(8,128)(2,1)} %copy-done.23, bf16[128,4352]{1,0:T(8,128)(2,1)} %copy-done.32), custom_call_target="tpu_custom_call" | custom-call | tf_op jit(solution)/shard_map/pallas_call | solution.py:286
  504.4 6.8 fusion.71
  512.6 5.3 collective-permute-start.2
  526.2 8.1 convert_reduce_fusion.2
  534.3 3.9 multiply_reduce_fusion.2
  541.5 17.9 %shard_map.267 = (bf16[16,72,128]{2,1,0:T(8,128)(2,1)}, bf16[4,4,72,128]{3,2,1,0:T(8,128)(2,1)}, bf16[4,4,72,128]{3,2,1,0:T(8,128)(2,1)}, bf16[4,4,72,128]{3,2,1,0:T(8,128)(2,1)}) custom-call(bf16[16,72,128]{2,1,0:T(8,128)(2,1)} %bitcast.336, bf16[4,4,72,128]{3,2,1,0:T(8,128)(2,1)} %bitcast.305, bf16[4,4,72,128]{3,2,1,0:T(8,128)(2,1)} %bitcast.323, ...), custom_call_target="tpu_custom_call" | custom-call | tf_op jit(solution)/shard_map/pallas_call | solution.py:286
  560.4 10.7 %shard_map.268.x_ref = bf16[16,216,128]{2,1,0:T(8,128)(2,1)S(1)} custom-call(s32[16]{0:T(128)S(1)} %copy-done.20, s32[16]{0:T(128)S(1)} %copy-done.19, bf16[16,216,128]{2,1,0:T(8,128)(2,1)S(1)} %broadcast_select_fusion.qkv_ref, f32[16,1,128]{2,1,0:T(1,128)S(1)} %bitcast.254, bf16[16,72,128]{2,1,0:T(8,128)(2,1)S(1)} %copy-done.9), custom_call_target="tpu_custom_call" | custom-call | tf_op jit(solution)/shard_map/pallas_call | solution.py:422
  572.0 27.4 %shard_map.269 = (bf16[16,216,128]{2,1,0:T(8,128)(2,1)}, bf16[4,128,2048]{2,1,0:T(8,128)(2,1)}) custom-call(bf16[16,216,128]{2,1,0:T(8,128)(2,1)} %copy-done.5, bf16[128,4352]{1,0:T(8,128)(2,1)} %copy-done.23, bf16[128,4352]{1,0:T(8,128)(2,1)} %copy-done.32), custom_call_target="tpu_custom_call" | custom-call | tf_op jit(solution)/shard_map/pallas_call | solution.py:286
  599.5 6.8 multiply_reduce_fusion.3
  608.3 4.4 collective-permute-start.3
  619.1 7.2 convert_reduce_fusion.1
  626.3 8.9 %multiply_reduce_fusion.1 = (f32[1152]{0:T(1024)}, f32[128]{0:T(128)}, f32[128]{0:T(128)}, f32[1152]{0:T(1024)S(1)}, f32[128,1152]{1,0:T(8,128)}) fusion(f32[128]{0:T(128)S(1)} %copy-done.99, f32[128,1152]{1,0:T(8,128)S(1)} %copy-done.22, f32[128]{0:T(128)S(1)} %copy-done.95, f32[1152]{0:T(1024)S(1)} %copy-done.71, ...), kind=kOutput, calls=%fused_computation.132 | convolution fusion | flops 1284781568 | bytes 12336640 | tf_op jit(solution)/shard_map/tf,df->td/dot_general | solution.py:768
  638.9 3.5 convolution_convert_fusion
  643.7 14.7 %shard_map.270 = (bf16[16,72,128]{2,1,0:T(8,128)(2,1)}, bf16[4,4,72,128]{3,2,1,0:T(8,128)(2,1)}, bf16[4,4,72,128]{3,2,1,0:T(8,128)(2,1)}) custom-call(bf16[16,72,128]{2,1,0:T(8,128)(2,1)} %bitcast.335, bf16[4,4,72,128]{3,2,1,0:T(8,128)(2,1)} %bitcast.306, bf16[4,4,72,128]{3,2,1,0:T(8,128)(2,1)} %bitcast.320, bf16[4,4,72,128]{3,2,1,0:T(8,128)(2,1)} %bitcast.327, ...), custom_call_target="tpu_custom_call" | custom-call | tf_op jit(solution)/shard_map/pallas_call | solution.py:286
  659.4 11.0 %shard_map.271.x_ref = bf16[16,216,128]{2,1,0:T(8,128)(2,1)S(1)} custom-call(s32[16]{0:T(128)S(1)} %copy-done.16, s32[16]{0:T(128)S(1)} %copy-done.18, bf16[16,216,128]{2,1,0:T(8,128)(2,1)S(1)} %copy-done.1, f32[16,1,128]{2,1,0:T(1,128)S(1)} %get-tuple-element.67.lse_ref, bf16[16,72,128]{2,1,0:T(8,128)(2,1)S(1)} %copy-done.10), custom_call_target="tpu_custom_call" | custom-call | tf_op jit(solution)/shard_map/pallas_call | solution.py:422
  671.3 28.8 %shard_map.272 = (bf16[16,216,128]{2,1,0:T(8,128)(2,1)}, bf16[4,128,2304]{2,1,0:T(8,128)(2,1)}) custom-call(bf16[16,216,128]{2,1,0:T(8,128)(2,1)} %copy-done.6, bf16[128,4352]{1,0:T(8,128)(2,1)} %copy-done.27, bf16[128,4352]{1,0:T(8,128)(2,1)} %copy-done.30), custom_call_target="tpu_custom_call" | custom-call | tf_op jit(solution)/shard_map/pallas_call | solution.py:286
  702.1 6.2 fusion.70
  709.6 153.0 %shard_map.273 = (f32[48,128]{1,0:T(8,128)}, f32[72,4352]{1,0:T(8,128)}, f32[72,4352]{1,0:T(8,128)}, f32[72,1152]{1,0:T(8,128)}, f32[72,3456]{1,0:T(8,128)}) custom-call(f32[16,48,128]{2,1,0:T(8,128)} %select_maximum_fusion.refs_0_, bf16[4,4,72,128]{3,2,1,0:T(8,128)(2,1)} %get-tuple-element.76.refs_1_, bf16[4,4,72,128]{3,2,1,0:T(8,128)(2,1)} %get-tuple-element.77.refs_2_, ...), custom_call_target="tpu_custom_call" | custom-call | tf_op jit(solution)/shard_map/pallas_call | solution.py:662
  870.0 3.0 broadcast_in_dim_reshape.3
  873.0 2.5 slice_bitcast_fusion.1
  (390 shorter events, 85.3 us)
Async XLA Ops:
  0.6 9.9 %copy-start.65 = (bf16[1,4304,72]{1,2,0:T(8,128)(2,1)S(1)}, bf16[1,4304,72]{1,2,0:T(8,128)(2,1)}, u32[]{:S(2)}) copy-start(bf16[1,4304,72]{1,2,0:T(8,128)(2,1)} %param.28) | copy-start | bytes 1859332
  0.7 10.8 %copy-start.72 = (bf16[1,72,3456]{2,1,0:T(8,128)(2,1)S(1)}, bf16[1,72,3456]{2,1,0:T(8,128)(2,1)}, u32[]{:S(2)}) copy-start(bf16[1,72,3456]{2,1,0:T(8,128)(2,1)} %param.20) | copy-start | bytes 1492996
  7.2 242.7 %copy-start.88 = (f32[4352]{0:T(1024)}, f32[4352]{0:T(1024)S(1)}, u32[]{:S(2)}) copy-start(f32[4352]{0:T(1024)S(1)} %pad_convert_fusion) | copy-start | bytes 52228
  13.9 178.6 %copy-start.33 = (bf16[2,128,1152]{2,1,0:T(8,128)(2,1)S(1)}, bf16[2,128,1152]{2,1,0:T(8,128)(2,1)}, u32[]{:S(2)}) copy-start(bf16[2,128,1152]{2,1,0:T(8,128)(2,1)} %param.15) | copy-start | bytes 1769476
  191.9 319.4 %copy-start.66 = (f32[1152]{0:T(1024)}, f32[1152]{0:T(1024)S(1)}, u32[]{:S(2)}) copy-start(f32[1152]{0:T(1024)S(1)} %mul.458) | copy-start | bytes 13828
  192.0 270.8 %copy-start.69 = (f32[1152]{0:T(1024)}, f32[1152]{0:T(1024)S(1)}, u32[]{:S(2)}) copy-start(f32[1152]{0:T(1024)S(1)} %mul.464) | copy-start | bytes 13828
  249.7 98.9 %copy-start.28 = (f32[128,1152]{1,0:T(8,128)}, f32[128,1152]{1,0:T(8,128)S(1)}, u32[]{:S(2)}) copy-start(f32[128,1152]{1,0:T(8,128)S(1)} %get-tuple-element.176) | copy-start | bytes 1769476
  260.8 18.3 %copy-start.59 = (bf16[128,1152]{1,0:T(8,128)(2,1)}, bf16[128,1152]{1,0:T(8,128)(2,1)S(1)}, u32[]{:S(2)}) copy-start(bf16[128,1152]{1,0:T(8,128)(2,1)S(1)} %fusion.15) | copy-start | bytes 884740
  260.8 10.9 %collective-permute-start = (bf16[128,1152]{1,0:T(8,128)(2,1)S(1)}, bf16[128,1152]{1,0:T(8,128)(2,1)S(1)}, u32[]{:S(2)}, u32[]{:S(2)}) collective-permute-start(bf16[128,1152]{1,0:T(8,128)(2,1)S(1)} %fusion.15), channel_id=1, source_target_pairs={{0,16},{1,17},{2,18},{3,19},{4,20},{5,21},{6,22},{7,23},{8,24},{9,... | collective-permute-start | bytes 884744 | tf_op jit(solution)/shard_map/ppermute | solution.py:752
  262.4 115.2 %copy-start.15 = (s32[16]{0:T(128)}, s32[16]{0:T(128)S(1)}, u32[]{:S(2)}) copy-start(s32[16]{0:T(128)S(1)} %fusion.97.img_ref) | copy-start | bytes 196
  264.8 112.7 %copy-start.17 = (s32[16]{0:T(128)}, s32[16]{0:T(128)S(1)}, u32[]{:S(2)}) copy-start(s32[16]{0:T(128)S(1)} %broadcast_minimum_fusion.1.first_ref) | copy-start | bytes 196
  272.0 239.3 %copy-start.25 = (bf16[128,1152]{1,0:T(8,128)(2,1)}, bf16[128,1152]{1,0:T(8,128)(2,1)S(1)}, u32[]{:S(2)}) copy-start(bf16[128,1152]{1,0:T(8,128)(2,1)S(1)} %get-tuple-element.152) | copy-start | bytes 884740
  272.0 239.3 %copy-start.90 = (f32[128]{0:T(128)}, f32[128]{0:T(128)S(1)}, u32[]{:S(2)}) copy-start(f32[128]{0:T(128)S(1)} %broadcast_multiply_fusion.17) | copy-start | bytes 1540
  272.2 239.1 %copy-start.92 = (f32[128]{0:T(128)}, f32[128]{0:T(128)S(1)}, u32[]{:S(2)}) copy-start(f32[128]{0:T(128)S(1)} %add_rsqrt_fusion.5) | copy-start | bytes 1540
  326.1 22.5 %copy-start.21 = (f32[128,1152]{1,0:T(8,128)}, f32[128,1152]{1,0:T(8,128)S(1)}, u32[]{:S(2)}) copy-start(f32[128,1152]{1,0:T(8,128)S(1)} %get-tuple-element.180) | copy-start | bytes 1769476
  326.9 21.8 %copy-start.94 = (f32[128]{0:T(128)}, f32[128]{0:T(128)S(1)}, u32[]{:S(2)}) copy-start(f32[128]{0:T(128)S(1)} %broadcast_multiply_fusion.16) | copy-start | bytes 1540
  327.1 21.5 %copy-start.98 = (f32[128]{0:T(128)}, f32[128]{0:T(128)S(1)}, u32[]{:S(2)}) copy-start(f32[128]{0:T(128)S(1)} %add_rsqrt_fusion.4) | copy-start | bytes 1540
  334.9 9.8 %slice-start.9 = ((s8[10027008]{0:T(1024)(128)(4,1)}), s8[4194304]{0:T(1024)(128)(4,1)S(1)}, s32[]{:S(2)}) async-start(s8[10027008]{0:T(1024)(128)(4,1)} %bitcast.273), calls=%async_computation.9 | async-start | bytes 8388608
  335.0 9.8 %slice-start.10 = ((s8[10027008]{0:T(1024)(128)(4,1)}), s8[4194304]{0:T(1024)(128)(4,1)S(1)}, s32[]{:S(2)}) async-start(s8[10027008]{0:T(1024)(128)(4,1)} %bitcast.273), calls=%async_computation.10 | async-start | bytes 8388608
  338.2 51.0 %copy-start.46 = (bf16[128,1152]{1,0:T(8,128)(2,1)}, bf16[128,1152]{1,0:T(8,128)(2,1)S(1)}, u32[]{:S(2)}) copy-start(bf16[128,1152]{1,0:T(8,128)(2,1)S(1)} %fusion.16) | copy-start | bytes 884740
  338.3 51.9 %collective-permute-start.1 = (bf16[128,1152]{1,0:T(8,128)(2,1)S(1)}, bf16[128,1152]{1,0:T(8,128)(2,1)}, u32[]{:S(2)}, u32[]{:S(2)}) collective-permute-start(bf16[128,1152]{1,0:T(8,128)(2,1)S(1)} %fusion.16), channel_id=1, source_target_pairs={{0,16},{1,17},{2,18},{3,19},{4,20},{5,21},{6,22},{7,23},{8,24},{9,... | collective-permute-start | bytes 884744 | tf_op jit(solution)/shard_map/ppermute | solution.py:752
  355.8 21.7 %copy-start.1 = (bf16[16,216,128]{2,1,0:T(8,128)(2,1)S(1)}, bf16[16,216,128]{2,1,0:T(8,128)(2,1)}, u32[]{:S(2)}) copy-start(bf16[16,216,128]{2,1,0:T(8,128)(2,1)} %shard_map.258.qkv_ref) | copy-start | bytes 2654212
  355.8 33.4 %copy-start.60 = (bf16[128,1152]{1,0:T(8,128)(2,1)S(1)}, bf16[128,1152]{1,0:T(8,128)(2,1)}, u32[]{:S(2)}) copy-start(bf16[128,1152]{1,0:T(8,128)(2,1)} %copy-done.59) | copy-start | bytes 884740
  355.8 34.3 %copy-start.34 = (bf16[2,128,1152]{2,1,0:T(8,128)(2,1)S(1)}, bf16[2,128,1152]{2,1,0:T(8,128)(2,1)}, u32[]{:S(2)}) copy-start(bf16[2,128,1152]{2,1,0:T(8,128)(2,1)} %param.15) | copy-start | bytes 1769476
  389.3 10.3 %copy-start.4 = (bf16[16,216,128]{2,1,0:T(8,128)(2,1)}, bf16[16,216,128]{2,1,0:T(8,128)(2,1)S(1)}, u32[]{:S(2)}) copy-start(bf16[16,216,128]{2,1,0:T(8,128)(2,1)S(1)} %shard_map.265.x_ref) | copy-start | bytes 2654212
  391.4 67.5 %copy-start.40 = (bf16[128,1152]{1,0:T(8,128)(2,1)}, bf16[128,1152]{1,0:T(8,128)(2,1)S(1)}, u32[]{:S(2)}) copy-start(bf16[128,1152]{1,0:T(8,128)(2,1)S(1)} %get-tuple-element.150) | copy-start | bytes 884740
  461.5 9.8 %slice-start.6 = ((s8[10027008]{0:T(1024)(128)(4,1)}), s8[4194304]{0:T(1024)(128)(4,1)S(1)}, s32[]{:S(2)}) async-start(s8[10027008]{0:T(1024)(128)(4,1)} %bitcast.266), calls=%async_computation.6 | async-start | bytes 8388608
  512.6 11.6 %copy-start.3 = (bf16[16,216,128]{2,1,0:T(8,128)(2,1)S(1)}, bf16[16,216,128]{2,1,0:T(8,128)(2,1)}, u32[]{:S(2)}) copy-start(bf16[16,216,128]{2,1,0:T(8,128)(2,1)} %shard_map.255.qkv_ref) | copy-start | bytes 2654212
  512.6 11.6 %copy-start.8 = (bf16[16,216,128]{2,1,0:T(8,128)(2,1)S(1)}, bf16[16,216,128]{2,1,0:T(8,128)(2,1)}, u32[]{:S(2)}) copy-start(bf16[16,216,128]{2,1,0:T(8,128)(2,1)} %get-tuple-element.64.qkv_ref) | copy-start | bytes 2654212
  512.6 11.7 %collective-permute-start.2 = (bf16[128,1152]{1,0:T(8,128)(2,1)}, bf16[128,1152]{1,0:T(8,128)(2,1)}, u32[]{:S(2)}, u32[]{:S(2)}) collective-permute-start(bf16[128,1152]{1,0:T(8,128)(2,1)} %get-tuple-element.148), channel_id=1, source_target_pairs={{16,0},{17,1},{18,2},{19,3},{20,4},{21,5},{22,6},{23,7},{24,8},{25... | collective-permute-start | bytes 884744 | tf_op jit(solution)/shard_map/ppermute | solution.py:814
  524.2 10.1 %slice-start.12 = ((s8[10027008]{0:T(1024)(128)(4,1)}), s8[4194304]{0:T(1024)(128)(4,1)S(1)}, s32[]{:S(2)}) async-start(s8[10027008]{0:T(1024)(128)(4,1)} %bitcast.276), calls=%async_computation.12 | async-start | bytes 8388608
  526.1 12.1 %copy-start.50 = (bf16[128,1152]{1,0:T(8,128)(2,1)}, bf16[128,1152]{1,0:T(8,128)(2,1)S(1)}, u32[]{:S(2)}) copy-start(bf16[128,1152]{1,0:T(8,128)(2,1)S(1)} %get-tuple-element.131) | copy-start | bytes 884740
  539.9 19.5 %copy-start.19 = (s32[16]{0:T(128)S(1)}, s32[16]{0:T(128)}, u32[]{:S(2)}) copy-start(s32[16]{0:T(128)} %get-tuple-element.170.first_ref) | copy-start | bytes 196
  539.9 19.5 %copy-start.20 = (s32[16]{0:T(128)S(1)}, s32[16]{0:T(128)}, u32[]{:S(2)}) copy-start(s32[16]{0:T(128)} %get-tuple-element.143.img_ref) | copy-start | bytes 196
  560.4 39.0 %copy-start.35 = (bf16[2,128,1152]{2,1,0:T(8,128)(2,1)S(1)}, bf16[2,128,1152]{2,1,0:T(8,128)(2,1)}, u32[]{:S(2)}) copy-start(bf16[2,128,1152]{2,1,0:T(8,128)(2,1)} %param.15) | copy-start | bytes 1769476
  560.4 39.0 %copy-start.41 = (bf16[128,1152]{1,0:T(8,128)(2,1)S(1)}, bf16[128,1152]{1,0:T(8,128)(2,1)}, u32[]{:S(2)}) copy-start(bf16[128,1152]{1,0:T(8,128)(2,1)} %copy-done.40) | copy-start | bytes 884740
  560.4 39.0 %copy-start.67 = (f32[1152]{0:T(1024)S(1)}, f32[1152]{0:T(1024)}, u32[]{:S(2)}) copy-start(f32[1152]{0:T(1024)} %copy-done.66) | copy-start | bytes 13828
  560.4 39.0 %copy-start.103 = (f32[128]{0:T(128)S(1)}, f32[128]{0:T(128)}, u32[]{:S(2)}) copy-start(f32[128]{0:T(128)} %copy-done.102) | copy-start | bytes 1540
  560.4 39.0 %copy-start.107 = (f32[128]{0:T(128)S(1)}, f32[128]{0:T(128)}, u32[]{:S(2)}) copy-start(f32[128]{0:T(128)} %add_rsqrt_fusion) | copy-start | bytes 1540
  607.6 11.3 %copy-start.45 = (bf16[2,128,1152]{2,1,0:T(8,128)(2,1)S(1)}, bf16[2,128,1152]{2,1,0:T(8,128)(2,1)}, u32[]{:S(2)}) copy-start(bf16[2,128,1152]{2,1,0:T(8,128)(2,1)} %param.16) | copy-start | bytes 1769476
  608.3 10.5 %collective-permute-start.3 = (bf16[128,1152]{1,0:T(8,128)(2,1)}, bf16[128,1152]{1,0:T(8,128)(2,1)}, u32[]{:S(2)}, u32[]{:S(2)}) collective-permute-start(bf16[128,1152]{1,0:T(8,128)(2,1)} %convert_element_type.187), channel_id=1, source_target_pairs={{16,0},{17,1},{18,2},{19,3},{20,4},{21,5},{22,6},{23,7},{24,8},{25... | collective-permute-start | bytes 884744 | tf_op jit(solution)/shard_map/ppermute | solution.py:814
  626.3 9.0 %copy-start.42 = (bf16[128,4352]{1,0:T(8,128)(2,1)}, bf16[128,4352]{1,0:T(8,128)(2,1)S(1)}, u32[]{:S(2)}) copy-start(bf16[128,4352]{1,0:T(8,128)(2,1)S(1)} %get-tuple-element.198.refs_16_) | copy-start | bytes 3342340
  642.4 16.0 %copy-start.16 = (s32[16]{0:T(128)S(1)}, s32[16]{0:T(128)}, u32[]{:S(2)}) copy-start(s32[16]{0:T(128)} %copy-done.15) | copy-start | bytes 196
  642.4 16.0 %copy-start.18 = (s32[16]{0:T(128)S(1)}, s32[16]{0:T(128)}, u32[]{:S(2)}) copy-start(s32[16]{0:T(128)} %copy-done.17) | copy-start | bytes 196
  659.4 40.7 %copy-start.38 = (bf16[16,216,128]{2,1,0:T(8,128)(2,1)S(1)}, bf16[16,216,128]{2,1,0:T(8,128)(2,1)}, u32[]{:S(2)}) copy-start(bf16[16,216,128]{2,1,0:T(8,128)(2,1)} %get-tuple-element.69) | copy-start | bytes 2654212
  671.3 30.7 %copy-start.26 = (bf16[128,1152]{1,0:T(8,128)(2,1)S(1)}, bf16[128,1152]{1,0:T(8,128)(2,1)}, u32[]{:S(2)}) copy-start(bf16[128,1152]{1,0:T(8,128)(2,1)} %copy-done.25) | copy-start | bytes 884740
  671.3 30.7 %copy-start.91 = (f32[128]{0:T(128)S(1)}, f32[128]{0:T(128)}, u32[]{:S(2)}) copy-start(f32[128]{0:T(128)} %copy-done.90) | copy-start | bytes 1540
  671.3 30.7 %copy-start.93 = (f32[128]{0:T(128)S(1)}, f32[128]{0:T(128)}, u32[]{:S(2)}) copy-start(f32[128]{0:T(128)} %copy-done.92) | copy-start | bytes 1540
  (82 other events, 434.8 us)

commit v3 on v2

--- a/solution.py
+++ b/solution.py
@@ -28,115 +28,109 @@
     return lax.axis_index("section"), lax.axis_index("wide")
 
 
-def gather_kernel(count, *refs):
-    ins, outs = refs[:count], refs[count : 2 * count]
-    local_sem, up_send, up_recv, down_send, down_recv, y_send, y_recv, c_send, c_recv = refs[2 * count :]
-    sec, me = place()
-    z = me // 4
-    low = me % 4
-    other_y = me - low + (low + 2) % 4
-    other_c = me - me % 2 + (me + 1) % 2
-
-    barrier = pltpu.get_barrier_semaphore()
-
-    def greet(target):
-        pl.semaphore_signal(barrier, inc=1, device_id=(sec, target), device_id_type=MESH)
-
-    greet(other_y)
-    greet(other_c)
-
-    inside = (z > 0) & (z < 3)
-
-    @pl.when(z > 0)
-    def _():
-        greet(me - 4)
-
-    @pl.when(z < 3)
-    def _():
-        greet(me + 4)
-
-    @pl.when(inside)
-    def _():
-        pl.semaphore_wait(barrier, 4)
-
-    @pl.when(jnp.logical_not(inside))
-    def _():
-        pl.semaphore_wait(barrier, 3)
-
-    def send(piece, origin, sems, slot, target, first=False):
+class Gather:
+    def __init__(self, ins, outs, sems):
+        self.ins, self.outs, self.count = ins, outs, len(ins)
+        self.local_sem = sems[0]
+        self.up, self.down, self.yy, self.cc = [(sems[1 + 2 * i], sems[2 + 2 * i]) for i in range(4)]
+        self.sec, self.me = place()
+        self.z, self.low = self.me // 4, self.me % 4
+        self.other_y = self.me - self.low + flip(self.low, 2)
+        self.other_c = self.me - self.low + flip(self.low, 1)
+
+    @staticmethod
+    def semaphores(count):
+        dma = pltpu.SemaphoreType.DMA
+        return [dma((count,))] + [dma((count, 4))] * 6 + [dma((count, 8))] * 2
+
+    def send(self, piece, origin, sems, slot, target, first=False):
         return pltpu.make_async_remote_copy(
-            src_ref=ins[piece] if first else outs[piece].at[origin],
-            dst_ref=outs[piece].at[origin],
+            src_ref=self.ins[piece] if first else self.outs[piece].at[origin],
+            dst_ref=self.outs[piece].at[origin],
             send_sem=sems[0].at[piece, slot],
             recv_sem=sems[1].at[piece, slot],
-            device_id=(sec, target),
+            device_id=(self.sec, target),
             device_id_type=MESH,
         )
 
-    up, down, yy, cc = (up_send, up_recv), (down_send, down_recv), (y_send, y_recv), (c_send, c_recv)
-
-    def mine(piece):
-        return pltpu.make_async_copy(ins[piece], outs[piece].at[me], local_sem.at[piece])
-
-    def along(piece, origin, first, go_up, go_down):
+    def mine(self, piece):
+        return pltpu.make_async_copy(self.ins[piece], self.outs[piece].at[self.me], self.local_sem.at[piece])
+
+    def along(self, piece, origin, first, go_up, go_down):
         zo = origin // 4
         if go_up:
 
-            @pl.when(z < 3)
+            @pl.when(self.z < 3)
             def _():
-                send(piece, origin, up, zo, me + 4, first).start()
+                self.send(piece, origin, self.up, zo, self.me + 4, first).start()
 
         if go_down:
 
-            @pl.when(z > 0)
+            @pl.when(self.z > 0)
             def _():
-                send(piece, origin, down, zo, me - 4, first).start()
-
-        send(piece, origin, yy, zo, other_y, first).start()
-        send(piece, origin, cc, zo, other_c, first).start()
-
-    for piece in range(count):
-        mine(piece).start()
-        along(piece, me, True, True, True)
+                self.send(piece, origin, self.down, zo, self.me - 4, first).start()
+
+        self.send(piece, origin, self.yy, zo, self.other_y, first).start()
+        self.send(piece, origin, self.cc, zo, self.other_c, first).start()
+
+    def start(self):
+        for piece in range(self.count):
+            self.mine(piece).start()
+            self.along(piece, self.me, True, True, True)
+
+    def step(self, step):
+        for piece in range(self.count):
+
+            @pl.when(self.z - step >= 0)
+            def _():
+                origin = self.me - 4 * step
+                self.send(piece, origin, self.up, self.z - step, self.me).wait_recv()
+                self.along(piece, origin, False, True, False)
+
+            @pl.when(self.z + step <= 3)
+            def _():
+                origin = self.me + 4 * step
+                self.send(piece, origin, self.down, self.z + step, self.me).wait_recv()
+                self.along(piece, origin, False, False, True)
+
+    def across(self):
+        far = self.other_y % 4
+        for step in range(4):
+            zo = (self.z + step) % 4
+            for piece in range(self.count):
+                origin = zo * 4 + far
+                self.send(piece, origin, self.yy, zo, self.other_y).wait_recv()
+                self.send(piece, origin, self.cc, 4 + zo, self.other_c).start()
+
+    def finish(self):
+        for zo in range(4):
+            for piece in range(self.count):
+                self.send(piece, self.me, self.yy, zo, self.other_y).wait_send()
+                for slot in (zo, 4 + zo):
+                    self.send(piece, self.me, self.cc, slot, self.other_c).wait_send()
+                    self.send(piece, self.me, self.cc, slot, self.other_c).wait_recv()
+
+                @pl.when((zo <= self.z) & (self.z < 3))
+                def _():
+                    self.send(piece, self.me, self.up, zo, self.me).wait_send()
+
+                @pl.when((zo >= self.z) & (self.z > 0))
+                def _():
+                    self.send(piece, self.me, self.down, zo, self.me).wait_send()
+
+        for piece in range(self.count):
+            self.mine(piece).wait()
+
+
+def gather_kernel(count, *refs):
+    sec, me = place()
+    greet_all(16, sec, me)
+    work = Gather(refs[:count], refs[count : 2 * count], refs[2 * count :])
+    work.start()
     for step in range(1, 4):
-        for piece in range(count):
-
-            @pl.when(z - step >= 0)
-            def _():
-                origin = me - 4 * step
-                send(piece, origin, up, z - step, me).wait_recv()
-                along(piece, origin, False, True, False)
-
-            @pl.when(z + step <= 3)
-            def _():
-                origin = me + 4 * step
-                send(piece, origin, down, z + step, me).wait_recv()
-                along(piece, origin, False, False, True)
-
-    far = other_y % 4
-    for step in range(4):
-        zo = (z + step) % 4
-        for piece in range(count):
-            origin = zo * 4 + far
-            send(piece, origin, yy, zo, other_y).wait_recv()
-            send(piece, origin, cc, 4 + zo, other_c).start()
-    for zo in range(4):
-        for piece in range(count):
-            send(piece, me, yy, zo, other_y).wait_send()
-            for slot in (zo, 4 + zo):
-                send(piece, me, cc, slot, other_c).wait_send()
-                send(piece, me, cc, slot, other_c).wait_recv()
-
-            @pl.when((zo <= z) & (z < 3))
-            def _():
-                send(piece, me, up, zo, me).wait_send()
-
-            @pl.when((zo >= z) & (z > 0))
-            def _():
-                send(piece, me, down, zo, me).wait_send()
-
-    for piece in range(count):
-        mine(piece).wait()
+        work.step(step)
+    work.across()
+    work.finish()
 
 
 def gather(arrays, cid):
@@ -146,9 +140,7 @@
         out_shape=[jax.ShapeDtypeStruct((16,) + a.shape, a.dtype) for a in arrays],
         in_specs=[pl.BlockSpec(memory_space=pl.ANY)] * count,
         out_specs=[pl.BlockSpec(memory_space=pl.ANY)] * count,
-        scratch_shapes=[pltpu.SemaphoreType.DMA((count,))]
-        + [pltpu.SemaphoreType.DMA((count, 4))] * 6
-        + [pltpu.SemaphoreType.DMA((count, 8))] * 2,
+        scratch_shapes=Gather.semaphores(count),
         compiler_params=pltpu.CompilerParams(collective_id=cid, has_side_effects=True),
     )(*arrays)
 
@@ -238,91 +230,101 @@
                 self.remote(self.slot(k), k, k).wait_recv()
 
 
-def exchange_kernel(items, x_ref, *refs):
+def dot(a, b):
+    return jnp.dot(a, b, preferred_element_type=F32)
+
+
+def window(image_row):
+    blocks = image_row.shape[0]
+    first = jnp.argmax(image_row[None, :] == image_row[:, None], axis=1).astype(jnp.int32)
+    first = jnp.minimum(first, blocks - IMG_BLOCKS)
+    near = image_row[first[:, None] + jnp.arange(IMG_BLOCKS)[None, :]]
+    bias = jnp.where(near == image_row[:, None], 0.0, MASKED_SCORE).astype(F32)
+    return first, jnp.broadcast_to(bias[:, :, None], (blocks, IMG_BLOCKS, BLOCK))
+
+
+def near_rows(ref, start):
+    return jnp.concatenate([ref[start + j] for j in range(IMG_BLOCKS)], axis=0)
+
+
+def near_columns(ref, start):
+    return jnp.concatenate([ref[start + j] for j in range(IMG_BLOCKS)], axis=1)
+
+
+def attend_kernel(items, pieces, first_ref, bias_ref, x_ref, *refs):
+    refs = list(refs)
+
+    def take(n):
+        part = refs[:n]
+        del refs[:n]
+        return part
+
     n = len(items)
-    sources, o_ref, outs = refs[: 2 * n], refs[2 * n], refs[2 * n + 1 : 3 * n + 1]
-    local_sem, send_sem, recv_sem = refs[3 * n + 1 : 3 * n + 4]
-    count = x_ref.shape[0]
+    sources, shards = take(2 * n), take(pieces)
+    qkv_ref, lse_ref, att_ref = take(3)
+    outs, whole = take(n), take(pieces)
+    k_all, vt_all, o_buf, local_sem, send_sem, recv_sem, att_send, att_recv = take(8)
+    blocks = x_ref.shape[0]
     sec, me = place()
-    greet_all(count, sec, me)
-    copies = []
-    half = count // 2
-    order = sorted(range(1, count), key=lambda d: abs(d - half))
-    for d in order:
-        target = (me + d) % count
-        copies.append(
-            pltpu.make_async_remote_copy(
-                src_ref=x_ref.at[target],
-                dst_ref=o_ref.at[me],
-                send_sem=send_sem.at[d],
-                recv_sem=recv_sem.at[d],
-                device_id=(sec, target),
-                device_id_type=MESH,
-            )
-        )
-        copies[-1].start()
-    own = pltpu.make_async_copy(x_ref.at[me], o_ref.at[me], local_sem)
+    greet_all(blocks, sec, me)
+
+    def incoming(d):
+        target = (me + d) % blocks
+        return pltpu.make_async_remote_copy(
+            src_ref=x_ref.at[target],
+            dst_ref=qkv_ref.at[me],
+            send_sem=send_sem.at[d],
+            recv_sem=recv_sem.at[d],
+            device_id=(sec, target),
+            device_id_type=MESH,
+        )
+
+    def outgoing(d):
+        target = (me + d) % blocks
+        return pltpu.make_async_remote_copy(
+            src_ref=o_buf.at[d],
+            dst_ref=att_ref.at[me],
+            send_sem=att_send.at[d],
+            recv_sem=att_recv.at[d],
+            device_id=(sec, target),
+            device_id_type=MESH,
+        )
+
+    for d in sorted(range(1, blocks), key=lambda d: abs(d - blocks // 2)):
+        incoming(d).start()
+    own = pltpu.make_async_copy(x_ref.at[me], qkv_ref.at[me], local_sem)
     own.start()
+    behind_sems = [take(3) for _ in items]
+    work = None
+    if pieces:
+        work = Gather(shards, whole, take(9))
+        work.start()
+    own.wait()
+    for d in range(1, blocks):
+        incoming(d).wait()
+    if work:
+        work.step(1)
     behind = []
     for i, item in enumerate(items):
-        sems = refs[3 * n + 4 + 3 * i : 3 * n + 7 + 3 * i]
-        behind.append(
-            PlaneCopies(item, sources[2 * i], sources[2 * i + 1], lambda k, i=i: outs[i].at[k], *sems)
-        )
+        slot = lambda k, i=i: outs[i].at[k]
+        behind.append(PlaneCopies(item, sources[2 * i], sources[2 * i + 1], slot, *behind_sems[i]))
         behind[-1].start()
-    own.wait()
-    for one in behind:
-        one.forward()
-    for copy in copies:
-        copy.wait()
-    for one in behind:
-        one.finish()
-
-
-def exchange(x, cid, items=()):
-    count = x.shape[0]
-    sources = [source for item in items for source in item.sources]
-    anywhere = pl.BlockSpec(memory_space=pl.ANY)
-    out = pl.pallas_call(
-        functools.partial(exchange_kernel, list(items)),
-        out_shape=[jax.ShapeDtypeStruct(x.shape, x.dtype)]
-        + [jax.ShapeDtypeStruct(item.shape(), item.sources[0].dtype) for item in items],
-        in_specs=[anywhere] * (1 + len(sources)),
-        out_specs=[anywhere] * (1 + len(items)),
-        scratch_shapes=[
-            pltpu.SemaphoreType.DMA,
-            pltpu.SemaphoreType.DMA((count,)),
-            pltpu.SemaphoreType.DMA((count,)),
-        ]
-        + [pltpu.SemaphoreType.DMA, pltpu.SemaphoreType.DMA((4,)), pltpu.SemaphoreType.DMA((4,))] * len(items),
-        compiler_params=pltpu.CompilerParams(collective_id=cid, has_side_effects=True),
-    )(x, *sources)
-    return out if items else out[0]
-
-
-def dot(a, b):
-    return jnp.dot(a, b, preferred_element_type=F32)
-
-
-def window_bias(img_ref, i, start):
-    own = img_ref[i]
-    return [jnp.where(img_ref[start + j] == own, 0.0, MASKED_SCORE).astype(F32) for j in range(IMG_BLOCKS)]
-
-
-def attn_fwd_kernel(img_ref, first_ref, qkv_ref, o_ref, lse_ref, k_all, vt_all):
-    blocks = qkv_ref.shape[0]
-    for j in range(blocks):
+
+    def arrange(j, carry):
         part = qkv_ref[j].astype(F32)
-        k_all[j * BLOCK : (j + 1) * BLOCK, :] = part[HEAD_DIM : 2 * HEAD_DIM].T.astype(BF)
-        vt_all[:, j * BLOCK : (j + 1) * BLOCK] = part[2 * HEAD_DIM :].astype(BF)
-
-    def one(i, carry):
+        k_all[j] = part[HEAD_DIM : 2 * HEAD_DIM].T.astype(BF)
+        vt_all[j] = part[2 * HEAD_DIM :].astype(BF)
+        return carry
+
+    lax.fori_loop(0, blocks, arrange, 0)
+
+    def one_block(d, carry):
+        i = (me + d) % blocks
         start = first_ref[i]
-        base = pl.multiple_of(start * BLOCK, BLOCK)
         qt = qkv_ref[i].astype(F32)[:HEAD_DIM].astype(BF)
-        s = dot(k_all[pl.ds(base, IMG_BLOCKS * BLOCK), :], qt) * SCALE
-        bias = window_bias(img_ref, i, start)
-        parts = [s[j * BLOCK : (j + 1) * BLOCK] + bias[j] for j in range(IMG_BLOCKS)]
+        s = dot(near_rows(k_all, start), qt) * SCALE
+        bias = bias_ref[i]
+        parts = [s[j * BLOCK : (j + 1) * BLOCK] + bias[j : j + 1] for j in range(IMG_BLOCKS)]
         top = parts[0]
         for part in parts[1:]:
             top = jnp.maximum(top, part)
@@ -333,68 +335,139 @@
             total = total + part
         total = jnp.sum(total, axis=0, keepdims=True)
         e = jnp.concatenate([part.astype(BF) for part in exps], axis=0)
-        o = dot(vt_all[:, pl.ds(base, IMG_BLOCKS * BLOCK)], e)
-        o_ref[i] = (o / total).astype(BF)
+        o = dot(near_columns(vt_all, start), e)
+        o_buf[d] = (o / total).astype(BF)
         lse_ref[i] = top + jnp.log(total)
+
+        @pl.when(d > 0)
+        def _():
+            outgoing(d).start()
+
         return carry
 
-    lax.fori_loop(0, blocks, one, 0)
-
-
-def window_first(image_row):
-    blocks = image_row.shape[0]
-    first = jnp.argmax(image_row[None, :] == image_row[:, None], axis=1).astype(jnp.int32)
-    return jnp.minimum(first, blocks - IMG_BLOCKS)
-
-
-def attention_fwd(image_row, first, qkv):
+    lax.fori_loop(0, blocks, one_block, 0)
+    att_ref[me] = o_buf[0]
+    if work:
+        work.step(2)
+    for one in behind:
+        one.forward()
+    for d in range(1, blocks):
+        outgoing(d).wait()
+    if work:
+        work.step(3)
+        work.across()
+        work.finish()
+    for one in behind:
+        one.finish()
+
+
+def attend(qkv, near, cid, items=(), shards=()):
     blocks = qkv.shape[0]
-    return pl.pallas_call(
-        attn_fwd_kernel,
+    n = len(items)
+    sources = [source for item in items for source in item.sources]
+    anywhere, vmem, smem = [pl.BlockSpec(memory_space=m) for m in (pl.ANY, pltpu.VMEM, pltpu.SMEM)]
+    dma = pltpu.SemaphoreType.DMA
+    scratch = [
+        pltpu.VMEM((blocks, BLOCK, HEAD_DIM), BF),
+        pltpu.VMEM((blocks, HEAD_DIM, BLOCK), BF),
+        pltpu.VMEM((blocks, HEAD_DIM, BLOCK), BF),
+        dma,
+    ] + [dma((blocks,))] * 4
+    scratch += [dma, dma((4,)), dma((4,))] * n
+    if shards:
+        scratch += Gather.semaphores(len(shards))
+    out = pl.pallas_call(
+        functools.partial(attend_kernel, list(items), len(shards)),
         out_shape=[
+            jax.ShapeDtypeStruct(qkv.shape, BF),
+            jax.ShapeDtypeStruct((blocks, 1, BLOCK), F32),
             jax.ShapeDtypeStruct((blocks, HEAD_DIM, BLOCK), BF),
-            jax.ShapeDtypeStruct((blocks, 1, BLOCK), F32),
-        ],
-        in_specs=[
-            pl.BlockSpec(memory_space=pltpu.SMEM),
-            pl.BlockSpec(memory_space=pltpu.SMEM),
-            pl.BlockSpec(memory_space=pltpu.VMEM),
-        ],
-        out_specs=[pl.BlockSpec(memory_space=pltpu.VMEM)] * 2,
-        scratch_shapes=[
-            pltpu.VMEM((blocks * BLOCK, HEAD_DIM), BF),
-            pltpu.VMEM((HEAD_DIM, blocks * BLOCK), BF),
-        ],
-        compiler_params=pltpu.CompilerParams(vmem_limit_bytes=32 << 20),
-    )(image_row, first, qkv)
-
-
-def attn_bwd_kernel(
-    img_ref, first_ref, qkv_ref, lse_ref, do_ref, o_ref, k_all, kt_all, v_all, q_all, do_all, dk_all, dv_all
-):
-    blocks = qkv_ref.shape[0]
-    for j in range(blocks):
+        ]
+        + [jax.ShapeDtypeStruct(item.shape(), BF) for item in items]
+        + [jax.ShapeDtypeStruct((blocks,) + shard.shape, BF) for shard in shards],
+        in_specs=[smem, vmem] + [anywhere] * (1 + len(sources) + len(shards)),
+        out_specs=[vmem] * 3 + [anywhere] * (n + len(shards)),
+        scratch_shapes=scratch,
+        compiler_params=pltpu.CompilerParams(collective_id=cid, has_side_effects=True, vmem_limit_bytes=32 << 20),
+    )(*near, qkv, *sources, *shards)
+    return out[0], out[1], out[2], out[3 : 3 + n], out[3 + n :]
+
+
+def attend_back_kernel(items, first_ref, bias_ref, qkv_ref, lse_ref, x_ref, *refs):
+    refs = list(refs)
+
+    def take(n):
+        part = refs[:n]
+        del refs[:n]
+        return part
+
+    n = len(items)
+    sources = take(2 * n)
+    dq_ref, dkv_ref = take(2)
+    outs = take(n)
+    do_ref, k_all, kt_all, v_all, q_all, do_all, p_all, s_all, dq_buf, dkv_buf = take(10)
+    local_sem, send_sem, recv_sem, q_send, q_recv, kv_send, kv_recv = take(7)
+    blocks = x_ref.shape[0]
+    sec, me = place()
+    greet_all(blocks, sec, me)
+
+    def remote(src, dst, send, recv, d):
+        return pltpu.make_async_remote_copy(
+            src_ref=src,
+            dst_ref=dst,
+            send_sem=send.at[d],
+            recv_sem=recv.at[d],
+            device_id=(sec, (me + d) % blocks),
+            device_id_type=MESH,
+        )
+
+    def incoming(d):
+        return remote(x_ref.at[(me + d) % blocks], do_ref.at[me], send_sem, recv_sem, d)
+
+    def send_q(d):
+        return remote(dq_buf.at[d], dq_ref.at[me], q_send, q_recv, d)
+
+    def send_kv(d):
+        return remote(dkv_buf.at[d], dkv_ref.at[me], kv_send, kv_recv, d)
+
+    for d in sorted(range(1, blocks), key=lambda d: abs(d - blocks // 2)):
+        incoming(d).start()
+    own = pltpu.make_async_copy(x_ref.at[me], do_ref.at[me], local_sem)
+    own.start()
+
+    def arrange(j, carry):
         part = qkv_ref[j].astype(F32)
-        rows = slice(j * BLOCK, (j + 1) * BLOCK)
-        q_all[rows, :] = part[:HEAD_DIM].T.astype(BF)
-        k_all[rows, :] = part[HEAD_DIM : 2 * HEAD_DIM].T.astype(BF)
-        v_all[rows, :] = part[2 * HEAD_DIM :].T.astype(BF)
-        kt_all[:, rows] = part[HEAD_DIM : 2 * HEAD_DIM].astype(BF)
-        do_all[rows, :] = do_ref[j].astype(F32).T.astype(BF)
-    dk_all[...] = jnp.zeros_like(dk_all)
-    dv_all[...] = jnp.zeros_like(dv_all)
-
-    def one(i, carry):
+        q_all[j] = part[:HEAD_DIM].T.astype(BF)
+        k_all[j] = part[HEAD_DIM : 2 * HEAD_DIM].T.astype(BF)
+        v_all[j] = part[2 * HEAD_DIM :].T.astype(BF)
+        kt_all[j] = part[HEAD_DIM : 2 * HEAD_DIM].astype(BF)
+        return carry
+
+    lax.fori_loop(0, blocks, arrange, 0)
+    own.wait()
+    for d in range(1, blocks):
+        incoming(d).wait()
+    behind = []
+    for i, item in enumerate(items):
+        behind.append(
+            PlaneCopies(item, sources[2 * i], sources[2 * i + 1], lambda k, i=i: outs[i].at[k], *take(3))
+        )
+        behind[-1].start()
+
+    def arrange_grad(j, carry):
+        do_all[j] = do_ref[j].astype(F32).T.astype(BF)
+        return carry
+
+    lax.fori_loop(0, blocks, arrange_grad, 0)
+
+    def by_query(d, carry):
+        i = (me + d) % blocks
         start = first_ref[i]
-        base = pl.multiple_of(start * BLOCK, BLOCK)
-        here = pl.multiple_of(i * BLOCK, BLOCK)
-        near = pl.ds(base, IMG_BLOCKS * BLOCK)
         qt = qkv_ref[i].astype(F32)[:HEAD_DIM].astype(BF)
-        s = dot(k_all[near, :], qt) * SCALE
-        lse = lse_ref[i]
-        bias = window_bias(img_ref, i, start)
-        probs = [jnp.exp(s[j * BLOCK : (j + 1) * BLOCK] + bias[j] - lse) for j in range(IMG_BLOCKS)]
-        dp = dot(v_all[near, :], do_ref[i])
+        s = dot(near_rows(k_all, start), qt) * SCALE
+        shift = bias_ref[i] - lse_ref[i]
+        probs = [jnp.exp(s[j * BLOCK : (j + 1) * BLOCK] + shift[j : j + 1]) for j in range(IMG_BLOCKS)]
+        dp = dot(near_rows(v_all, start), do_ref[i])
         total = probs[0] * dp[:BLOCK]
         for j in range(1, IMG_BLOCKS):
             total = total + probs[j] * dp[j * BLOCK : (j + 1) * BLOCK]
@@ -402,43 +475,83 @@
         ds = jnp.concatenate(
             [(probs[j] * (dp[j * BLOCK : (j + 1) * BLOCK] - total)).astype(BF) for j in range(IMG_BLOCKS)], axis=0
         )
-        p = jnp.concatenate([part.astype(BF) for part in probs], axis=0)
-        dv_all[near, :] += dot(p, do_all[pl.ds(here, BLOCK), :])
-        dk_all[near, :] += dot(ds, q_all[pl.ds(here, BLOCK), :])
-        dq = dot(kt_all[:, near], ds) * SCALE
-        o_ref[i, :HEAD_DIM, :] = dq.astype(BF)
+        for j in range(IMG_BLOCKS):
+            p_all[i, j] = probs[j].astype(BF)
+            s_all[i, j] = ds[j * BLOCK : (j + 1) * BLOCK]
+        dq_buf[d] = (dot(near_columns(kt_all, start), ds) * SCALE).astype(BF)
+
+        @pl.when(d > 0)
+        def _():
+            send_q(d).start()
+
         return carry
 
-    lax.fori_loop(0, blocks, one, 0)
-    for j in range(blocks):
-        rows = slice(j * BLOCK, (j + 1) * BLOCK)
-        kv = jnp.concatenate([(dk_all[rows, :] * SCALE).T, dv_all[rows, :].T], axis=0)
-        o_ref[j, HEAD_DIM:, :] = kv.astype(BF)
-
-
-def attention_bwd(image_row, first, qkv, lse, grad):
+    lax.fori_loop(0, blocks, by_query, 0)
+    for one in behind:
+        one.forward()
+
+    def by_key(d, carry):
+        j = (me + d) % blocks
+        start = first_ref[j]
+        place_in = jnp.clip(j - start, 0, IMG_BLOCKS - 1)
+        same = (bias_ref[j] == 0.0).astype(F32).astype(BF)
+        p, ds = [], []
+        for m in range(IMG_BLOCKS):
+            p.append(p_all[start + m, place_in] * same[m : m + 1])
+            ds.append(s_all[start + m, place_in] * same[m : m + 1])
+        dv = dot(jnp.concatenate(p, axis=1), near_rows(do_all, start))
+        dk = dot(jnp.concatenate(ds, axis=1), near_rows(q_all, start)) * SCALE
+        dkv_buf[d] = jnp.concatenate([dk.T, dv.T], axis=0).astype(BF)
+
+        @pl.when(d > 0)
+        def _():
+            send_kv(d).start()
+
+        return carry
+
+    lax.fori_loop(0, blocks, by_key, 0)
+    dq_ref[me] = dq_buf[0]
+    dkv_ref[me] = dkv_buf[0]
+    for d in range(1, blocks):
+        send_q(d).wait()
+        send_kv(d).wait()
+    for one in behind:
+        one.finish()
+
+
+def attend_back(att_grad, near, qkv, lse, cid, items=()):
     blocks = qkv.shape[0]
-    tokens = blocks * BLOCK
-    return pl.pallas_call(
-        attn_bwd_kernel,
-        out_shape=jax.ShapeDtypeStruct((blocks, 3 * HEAD_DIM, BLOCK), BF),
-        in_specs=[
-            pl.BlockSpec(memory_space=pltpu.SMEM),
-            pl.BlockSpec(memory_space=pltpu.SMEM),
+    n = len(items)
+    sources = [source for item in items for source in item.sources]
+    anywhere, vmem, smem = [pl.BlockSpec(memory_space=m) for m in (pl.ANY, pltpu.VMEM, pltpu.SMEM)]
+    dma = pltpu.SemaphoreType.DMA
+    scratch = [
+        pltpu.VMEM((blocks, HEAD_DIM, BLOCK), BF),
+        pltpu.VMEM((blocks, BLOCK, HEAD_DIM), BF),
+        pltpu.VMEM((blocks, HEAD_DIM, BLOCK), BF),
+        pltpu.VMEM((blocks, BLOCK, HEAD_DIM), BF),
+        pltpu.VMEM((blocks, BLOCK, HEAD_DIM), BF),
+        pltpu.VMEM((blocks, BLOCK, HEAD_DIM), BF),
+        pltpu.VMEM((blocks, IMG_BLOCKS, BLOCK, BLOCK), BF),
+        pltpu.VMEM((blocks, IMG_BLOCKS, BLOCK, BLOCK), BF),
+        pltpu.VMEM((blocks, HEAD_DIM, BLOCK), BF),
+        pltpu.VMEM((blocks, 2 * HEAD_DIM, BLOCK), BF),
+        dma,
+    ] + [dma((blocks,))] * 6
+    scratch += [dma, dma((4,)), dma((4,))] * n
+    out = pl.pallas_call(
+        functools.partial(attend_back_kernel, list(items)),
+        out_shape=[
+            jax.ShapeDtypeStruct((blocks, HEAD_DIM, BLOCK), BF),
+            jax.ShapeDtypeStruct((blocks, 2 * HEAD_DIM, BLOCK), BF),
         ]
-        + [pl.BlockSpec(memory_space=pltpu.VMEM)] * 3,
-        out_specs=pl.BlockSpec(memory_space=pltpu.VMEM),
-        scratch_shapes=[
-            pltpu.VMEM((tokens, HEAD_DIM), BF),
-            pltpu.VMEM((HEAD_DIM, tokens), BF),
-            pltpu.VMEM((tokens, HEAD_DIM), BF),
-            pltpu.VMEM((tokens, HEAD_DIM), BF),
-            pltpu.VMEM((tokens, HEAD_DIM), BF),
-            pltpu.VMEM((tokens, HEAD_DIM), F32),
-            pltpu.VMEM((tokens, HEAD_DIM), F32),
-        ],
-        compiler_params=pltpu.CompilerParams(vmem_limit_bytes=32 << 20),
-    )(image_row, first, qkv, lse, grad)
+        + [jax.ShapeDtypeStruct(item.shape(), BF) for item in items],
+        in_specs=[smem, vmem, vmem, vmem] + [anywhere] * (1 + len(sources)),
+        out_specs=[vmem] * 2 + [anywhere] * n,
+        scratch_shapes=scratch,
+        compiler_params=pltpu.CompilerParams(collective_id=cid, has_side_effects=True, vmem_limit_bytes=40 << 20),
+    )(*near, qkv, lse, att_grad, *sources)
+    return jnp.concatenate(out[:2], axis=1), out[2:]
 
 
 def normalised(x):
@@ -696,13 +809,10 @@
         [ln1_gain[0], ln1_bias[0], qv_bias[0, 0], qv_bias[0, 1], out_bias[0], ln2_gain[0], ln2_bias[0], fc2_bias[0]]
     )
     small = jnp.pad(small, ((0, 8), (0, BLOCK - HEAD_DIM)))
-    w_qkv, w_out, w_fc1, w_fc2t, small_all = gather(
-        [own_qkv, out_weight[0], pad_ff(fc1_weight[0]), pad_ff(fc2_weight[0].T), small], 1
-    )
+    w_qkv, w_out, small_all = gather([own_qkv, out_weight[0], small], 1)
+    ff_shards = [pad_ff(fc1_weight[0]), pad_ff(fc2_weight[0].T)]
     w_qkv = w_qkv.reshape(D, 3 * D)
     w_out = w_out.reshape(D, D)
-    w_fc1 = w_fc1.reshape(D, FFP)
-    w_fc2t = w_fc2t.reshape(D, FFP)
     vectors = small_all[:, :8, :HEAD_DIM].astype(F32)
     gain1, bias1, _, _, b_out, gain2, bias2, b_fc2 = [vectors[:, i].reshape(D) for i in range(8)]
     b_qkv = jnp.stack([vectors[:, 2], jnp.zeros_like(vectors[:, 2]), vectors[:, 3]], axis=1).reshape(3 * D, 1)
@@ -717,23 +827,23 @@
     for tick in range(3):
         slot = jnp.clip(tick - sec, 0, 1)
         image_row = lax.dynamic_index_in_dim(image_of_block, slot, 0, keepdims=False)
-        first = window_first(image_row)
+        near = window(image_row)
         x = jnp.where(sec == 0, tokens[min(tick, 1)], incoming).astype(F32)
         xhat1, _ = normalised(x)
         n1 = (xhat1 * gain1 + bias1).astype(BF)
         qkv = jnp.einsum("ck,tc->kt", w_qkv, n1, preferred_element_type=F32) + b_qkv
         qkv = qkv.astype(BF).reshape(HEADS, 3 * HEAD_DIM, BLOCK)
-        if tick < 2:
-            qkv = exchange(qkv, 2)
-            att, lse = attention_fwd(image_row, first, qkv)
-            att = exchange(att, 3)
+        if tick == 0:
+            qkv, lse, att, _, whole = attend(qkv, near, 2, shards=ff_shards)
+            w_fc1, w_fc2t = [w.reshape(D, FFP) for w in whole]
+        elif tick == 1:
+            qkv, lse, att, _, _ = attend(qkv, near, 3)
         else:
-            old = [saved[0], saved[1]]
-            qkv, sent["h0a"] = exchange(qkv, 4, [Whole(old[0]["hidden"], old[1]["hidden"], (0, SPLIT))])
-            att, lse = attention_fwd(image_row, first, qkv)
-            att, sent["n1_0"], sent["att_0"], sent["n2_0"] = exchange(
-                att, 5, [Rows(old[0][name], old[1][name]) for name in ("n1", "att_rows", "n2")]
-            )
+            old = saved
+            items = [Rows(old[0][name], old[1][name]) for name in ("n1", "att_rows", "n2")]
+            items.append(Whole(old[0]["hidden"], old[1]["hidden"], (0, SPLIT)))
+            qkv, lse, att, got, _ = attend(qkv, near, 4, items)
+            sent["n1_0"], sent["att_0"], sent["n2_0"], sent["h0a"] = got
         residual = x + jnp.einsum("ct,cd->td", att.reshape(D, BLOCK), w_out, preferred_element_type=F32) + b_out
         xhat2, _ = normalised(residual)
         n2 = (xhat2 * gain2 + bias2).astype(BF)
@@ -745,7 +855,7 @@
         saved.append(
             dict(
                 x=x, qkv=qkv, lse=lse, residual=residual, hidden_pre=hidden_pre, hidden=hidden, low=out_low,
-                att_rows=owners(att), n1=owners(by_rows(n1)), n2=owners(by_rows(n2)), image=image_row, first=first,
+                att_rows=owners(att), n1=owners(by_rows(n1)), n2=owners(by_rows(n2)), near=near,
             )
         )
         if tick < 2:
@@ -754,7 +864,7 @@
 
     incoming_grad = jnp.zeros(tokens.shape[1:], BF)
     input_grads, done, back = [], [], []
-    needed = ("x", "qkv", "lse", "residual", "hidden_pre", "image", "first")
+    needed = ("x", "qkv", "lse", "residual", "hidden_pre", "near")
     for tick in range(3):
         if tick == 1:
             k = choose({name: saved[0][name] for name in needed}, {name: saved[2][name] for name in needed})
@@ -774,22 +884,21 @@
         att_grad = att_grad.reshape(HEADS, HEAD_DIM, BLOCK)
         back.append(dict(fc=owners(by_rows(fc_grad)), pre=pre_grad, branch=branch))
         if tick == 0:
-            att_grad, sent["h0b"] = exchange(att_grad, 6, [Whole(saved[0]["hidden"], saved[1]["hidden"], (SPLIT, FFP))])
+            items = [
+                Whole(saved[0]["hidden"], saved[1]["hidden"], (SPLIT, FFP)),
+                Whole(saved[1]["hidden"], saved[2]["hidden"], (0, SPLIT)),
+            ]
+            names = ["h0b", "h1a"]
         elif tick == 1:
-            att_grad, sent["n1_1"], sent["att_1"], sent["n2_1"] = exchange(
-                att_grad, 8, [Rows(saved[1][name], saved[2][name]) for name in ("n1", "att_rows", "n2")]
-            )
+            items = [Rows(saved[1][name], saved[2][name]) for name in ("n1", "att_rows", "n2")]
+            items.append(Whole(saved[1]["hidden"], saved[2]["hidden"], (SPLIT, FFP)))
+            names = ["n1_1", "att_1", "n2_1", "h1b"]
         else:
-            att_grad, sent["fc_0"], sent["fc_1"] = exchange(
-                att_grad, 10, [Rows(back[1]["fc"], back[0]["fc"]), Rows(back[2]["fc"], back[1]["fc"])]
-            )
-        dqkv = attention_bwd(k["image"], k["first"], k["qkv"], k["lse"], att_grad)
-        if tick == 0:
-            dqkv, sent["h1a"] = exchange(dqkv, 7, [Whole(saved[1]["hidden"], saved[2]["hidden"], (0, SPLIT))])
-        elif tick == 1:
-            dqkv, sent["h1b"] = exchange(dqkv, 9, [Whole(saved[1]["hidden"], saved[2]["hidden"], (SPLIT, FFP))])
-        else:
-            dqkv, sent["pre_0a"] = exchange(dqkv, 11, [Whole(back[1]["pre"], back[0]["pre"], (0, SPLIT))])
+            items = [Rows(back[1]["fc"], back[0]["fc"]), Rows(back[2]["fc"], back[1]["fc"])]
+            items.append(Whole(back[1]["pre"], back[0]["pre"], (0, SPLIT)))
+            names = ["fc_0", "fc_1", "pre_0a"]
+        dqkv, got = attend_back(att_grad, k["near"], k["qkv"], k["lse"], 5 + tick, items)
+        sent.update(zip(names, got))
         back[-1]["dqkv"] = dqkv.reshape(3 * D, BLOCK)
         n1_grad = jnp.einsum("kt,ck->tc", back[-1]["dqkv"], w_qkv, preferred_element_type=F32)
         xhat1, rstd1 = normalised(k["x"])

time: 887 us -> 849 us (0.957)
  Pallas kernels: 644 us -> 598 us
  matrix products: 127 us -> 111 us
  local copies, waits for them, and re-layouts: 51.1 us -> 66.5 us
    pallas_call x1, Pallas kernels: 176 us -> 66.2 us  [gather(): pl.pallas_call(functools.partial(gather_kernel, count), out_shape=[jax.Sh...]
    pallas_call x18 -> x6, Pallas kernels: 315 us -> 378 us  [the longest x3 220 us: attend(): pl.pallas_call(functools.partial(attend_kernel, list(items), len(shards))...]
  transfers between devices with their start and end apart: 4 -> 4, of which waited for: 2 -> 3; matrix products, arithmetic and copies ran while one was open for 3% -> 4% of each run, Pallas kernels for 4% -> 0%
where the time goes in v3:
time: 849 us; the launch traced here: 838 us
  Pallas kernels  598 us (70%)
  matrix products  111 us (13%)
  local copies, waits for them, and re-layouts  66.5 us (8%)
  other arithmetic  35.3 us (4%)
  starting transfers between devices  14.9 us (2%)
  waiting for transfers between devices  9.55 us (1%)
    pallas_call x3, Pallas kernels, attend(): pl.pallas_call(functools.partial(attend_kernel, list(items), len(shards))...  220 us
    pallas_call x3, Pallas kernels, attend_back(): pl.pallas_call(functools.partial(attend_back_kernel, list(items)), out_sh...  158 us
    pallas_call x1, Pallas kernels, final(): pl.pallas_call(functools.partial(final_kernel, tiles, [e[:3] for e in ear...  153 us
    pallas_call x1, Pallas kernels, gather(): pl.pallas_call(functools.partial(gather_kernel, count), out_shape=[jax.Sh...  66.2 us
    dot_general x3, matrix products, on_device(): jnp.einsum('td,df->tf', fc_grad, w_fc2t, preferred_element_type=F32)  24.1 us
    dot_general x3, matrix products, on_device(): qkv = jnp.einsum('ck,tc->kt', w_qkv, n1, preferred_element_type=F32) + b_qkv  19.1 us
    dot_general x3, matrix products, on_device(): jnp.einsum('kt,ck->tc', back[-1]['dqkv'], w_qkv, preferred_element_type=F32)  17 us
  transfers between devices with their start and end apart: 4, of which 3 were waited for; matrix products, arithmetic and copies ran while one was open for 4% of the time, Pallas kernels for 0%

profile of v3, /device:TPU:10, one launch (start us, length us, event | category | flops | bytes accessed | tf_op | source)
XLA Modules:
  0.0 837.9 jit_solution(13035495073128806978)
XLA Ops:
  12.2 2.5 reshape_squeeze.3
  17.5 66.2 %shard_map.254 = (bf16[16,72,3456]{2,1,0:T(8,128)(2,1)}, bf16[16,72,1152]{2,1,0:T(8,128)(2,1)}, bf16[16,16,128]{2,1,0:T(8,128)(2,1)}) custom-call(bf16[72,3456]{1,0:T(8,128)(2,1)} %copy.93.refs_0_, bf16[72,1152]{1,0:T(8,128)(2,1)} %bitcast.346, bf16[16,128]{1,0:T(8,128)(2,1)} %pad.23.refs_2_), custom_call_target="tpu_custom_call" | custom-call | tf_op jit(solution)/shard_map/pallas_call | solution.py:138
  86.1 6.1 fusion.3
  92.3 129.9 %shard_map.255 = (bf16[16,216,128]{2,1,0:T(8,128)(2,1)S(1)}, f32[16,1,128]{2,1,0:T(1,128)S(1)}, bf16[16,72,128]{2,1,0:T(8,128)(2,1)S(1)}, bf16[16,72,4352]{2,1,0:T(8,128)(2,1)S(1)}, bf16[16,72,4352]{2,1,0:T(8,128)(2,1)}) custom-call(s32[16]{0:T(128)S(1)} %get-tuple-element.177.first_ref, f32[16,6,128]{2,1,0:T(8,128)S(1)} %broadcast_in_dim.38.bias_ref, ...), custom_call_target="tpu_custom_call" | custom-call | tf_op jit(solution)/shard_map/pallas_call | solution.py:379
  224.2 3.3 fusion.24
  229.2 1.9 slice-done.10
  231.5 3.2 fusion.15
  238.0 8.2 collective-permute-done
  247.8 6.1 fusion.4
  254.0 37.1 %shard_map.256 = (bf16[16,216,128]{2,1,0:T(8,128)(2,1)S(1)}, f32[16,1,128]{2,1,0:T(1,128)S(1)}, bf16[16,72,128]{2,1,0:T(8,128)(2,1)S(1)}) custom-call(s32[16]{0:T(128)S(1)} %broadcast_minimum_fusion.1.first_ref, f32[16,6,128]{2,1,0:T(8,128)S(1)} %broadcast_in_dim.39.bias_ref, bf16[16,216,128]{2,1,0:T(8,128)(2,1)S(1)} %bitcast.291), custom_call_target="tpu_custom_call" | custom-call | tf_op jit(solution)/shard_map/pallas_call | solution.py:379
  292.3 3.3 multiply_convert_fusion
  296.6 5.1 fusion.16
  301.6 1.7 select_bitcast_fusion.1
  305.1 8.0 convert_reduce_fusion
  313.2 3.9 multiply_reduce_fusion
  317.1 2.2 convert_reduce_fusion.12
  319.3 1.8 copy.102
  322.8 1.8 copy.100
  324.7 1.7 copy.137
  326.4 3.4 convolution_convert_fusion.2
  329.8 2.0 fusion.82
  333.9 6.9 fusion.5
  340.7 1.9 copy.94
  344.3 1.8 copy.96
  352.3 53.4 %shard_map.257 = (bf16[16,216,128]{2,1,0:T(8,128)(2,1)S(1)}, f32[16,1,128]{2,1,0:T(1,128)S(1)}, bf16[16,72,128]{2,1,0:T(8,128)(2,1)S(1)}, bf16[4,4,72,128]{3,2,1...) custom-call(s32[16]{0:T(128)S(1)} %get-tuple-element.176.first_ref, ...), custom_call_target="tpu_custom_call" | custom-call | tf_op jit(solution)/shard_map/pallas_call | solution.py:379
  408.2 8.0 fusion.31
  416.8 3.3 fusion.19
  420.1 53.5 %shard_map.258 = (bf16[16,72,128]{2,1,0:T(8,128)(2,1)S(1)}, bf16[16,144,128]{2,1,0:T(8,128)(2,1)S(1)}, bf16[4,128,2048]{2,1,0:T(8,128)(2,1)S(1)}, bf16[4,128,2304]{2,1,0:T(8,128)(2,1)S(1)}) custom-call(s32[16]{0:T(128)S(1)} %broadcast_minimum_fusion.1.first_ref, f32[16,6,128]{2,1,0:T(8,128)S(1)} %broadcast_in_dim.39.bias_ref, ...), custom_call_target="tpu_custom_call" | custom-call | tf_op jit(solution)/shard_map/pallas_call | solution.py:542
  473.8 7.6 fusion.71
  482.7 6.1 collective-permute-start.2
  495.1 8.1 convert_reduce_fusion.2
  503.3 4.7 multiply_reduce_fusion.2
  509.5 2.7 convolution_convert_fusion.1
  512.4 53.0 %shard_map.259 = (bf16[16,72,128]{2,1,0:T(8,128)(2,1)S(1)}, bf16[16,144,128]{2,1,0:T(8,128)(2,1)S(1)}, bf16[4,4,72,128]{3,2,1,0:T(8,128)(2,1)S(1)}, bf16[4,4,72,...) custom-call(s32[16]{0:T(128)S(1)} %get-tuple-element.175.first_ref, ...), custom_call_target="tpu_custom_call" | custom-call | tf_op jit(solution)/shard_map/pallas_call | solution.py:542
  565.6 3.2 multiply_reduce_fusion.3
  570.9 5.7 collective-permute-start.3
  577.0 2.0 copy.109
  583.5 8.0 convert_reduce_fusion.1
  591.6 4.7 multiply_reduce_fusion.1
  598.6 2.4 convert_reduce_fusion.13
  601.1 2.7 convolution_convert_fusion
  603.9 1.9 copy.113
  608.0 51.5 %shard_map.260 = (bf16[16,72,128]{2,1,0:T(8,128)(2,1)S(1)}, bf16[16,144,128]{2,1,0:T(8,128)(2,1)S(1)}, bf16[4,4,72,128]{3,2,1,0:T(8,128)(2,1)S(1)}, bf16[4,4,72,...) custom-call(s32[16]{0:T(128)S(1)} %broadcast_minimum_fusion.1.first_ref, f32[16,6,128]{2,1,0:T(8,128)S(1)} %broadcast_in_dim.39.bias_ref, ...), custom_call_target="tpu_custom_call" | custom-call | tf_op jit(solution)/shard_map/pallas_call | solution.py:542
  660.7 6.1 fusion.70
  668.1 153.0 %shard_map.261 = (f32[48,128]{1,0:T(8,128)}, f32[72,4352]{1,0:T(8,128)}, f32[72,4352]{1,0:T(8,128)}, f32[72,1152]{1,0:T(8,128)}, f32[72,3456]{1,0:T(8,128)}) custom-call(f32[16,48,128]{2,1,0:T(8,128)} %select_maximum_fusion.refs_0_, bf16[4,4,72,128]{3,2,1,0:T(8,128)(2,1)} %copy-done.36, bf16[4,4,72,128]{3,2,1,0:T(8,128)(2,1)} %copy-done.37, ...), custom_call_target="tpu_custom_call" | custom-call | tf_op jit(solution)/shard_map/pallas_call | solution.py:775
  825.1 1.7 copy.116
  828.5 3.0 broadcast_in_dim_reshape.3
  831.5 2.6 slice_bitcast_fusion.1
  (464 shorter events, 75.4 us)
Async XLA Ops:
  1.8 84.3 %copy-start.114 = (f32[128]{0:T(128)}, f32[128]{0:T(128)S(1)}, u32[]{:S(2)}) copy-start(f32[128]{0:T(128)S(1)} %broadcast_multiply_fusion.19) | copy-start | bytes 1540
  3.0 83.1 %copy-start.120 = (f32[128]{0:T(128)}, f32[128]{0:T(128)S(1)}, u32[]{:S(2)}) copy-start(f32[128]{0:T(128)S(1)} %add_rsqrt_fusion.7) | copy-start | bytes 1540
  11.3 212.8 %copy-start.97 = (f32[4352]{0:T(1024)}, f32[4352]{0:T(1024)S(1)}, u32[]{:S(2)}) copy-start(f32[4352]{0:T(1024)S(1)} %pad_convert_fusion) | copy-start | bytes 52228
  14.7 71.4 %copy-start.55 = (bf16[2,128,1152]{2,1,0:T(8,128)(2,1)S(1)}, bf16[2,128,1152]{2,1,0:T(8,128)(2,1)}, u32[]{:S(2)}) copy-start(bf16[2,128,1152]{2,1,0:T(8,128)(2,1)} %param.15) | copy-start | bytes 1769476
  85.4 162.4 %copy-start.101 = (f32[3456]{0:T(1024)}, f32[3456]{0:T(1024)S(1)}, u32[]{:S(2)}) copy-start(f32[3456]{0:T(1024)S(1)} %add.579) | copy-start | bytes 41476
  86.1 137.1 %copy-start.41 = (bf16[16,72,1152]{2,1,0:T(8,128)(2,1)S(1)}, bf16[16,72,1152]{2,1,0:T(8,128)(2,1)}, u32[]{:S(2)}) copy-start(bf16[16,72,1152]{2,1,0:T(8,128)(2,1)} %get-tuple-element.59) | copy-start | bytes 7962628
  92.2 130.9 %copy-start.56 = (bf16[2,128,1152]{2,1,0:T(8,128)(2,1)S(1)}, bf16[2,128,1152]{2,1,0:T(8,128)(2,1)}, u32[]{:S(2)}) copy-start(bf16[2,128,1152]{2,1,0:T(8,128)(2,1)} %param.15) | copy-start | bytes 1769476
  234.8 11.4 %copy-start.57 = (bf16[2,128,1152]{2,1,0:T(8,128)(2,1)S(1)}, bf16[2,128,1152]{2,1,0:T(8,128)(2,1)}, u32[]{:S(2)}) copy-start(bf16[2,128,1152]{2,1,0:T(8,128)(2,1)} %param.15) | copy-start | bytes 1769476
  234.8 11.4 %collective-permute-start = (bf16[128,1152]{1,0:T(8,128)(2,1)S(1)}, bf16[128,1152]{1,0:T(8,128)(2,1)}, u32[]{:S(2)}, u32[]{:S(2)}) collective-permute-start(bf16[128,1152]{1,0:T(8,128)(2,1)S(1)} %fusion.15), channel_id=1, source_target_pairs={{0,16},{1,17},{2,18},{3,19},{4,20},{5,21},{6,22},{7,23},{8,24},{9,... | collective-permute-start | bytes 884744 | tf_op jit(solution)/shard_map/ppermute | solution.py:862
  246.2 46.0 %slice-start = ((s8[10027008]{0:T(1024)(128)(4,1)}), s8[4194304]{0:T(1024)(128)(4,1)S(1)}, s32[]{:S(2)}) async-start(s8[10027008]{0:T(1024)(128)(4,1)} %bitcast.260), calls=%async_computation | async-start | bytes 8388608
  247.5 43.7 %copy-start.44 = (bf16[128,1152]{1,0:T(8,128)(2,1)}, bf16[128,1152]{1,0:T(8,128)(2,1)S(1)}, u32[]{:S(2)}) copy-start(bf16[128,1152]{1,0:T(8,128)(2,1)S(1)} %get-tuple-element.154) | copy-start | bytes 884740
  247.8 43.4 %copy-start.42 = (bf16[16,72,1152]{2,1,0:T(8,128)(2,1)S(1)}, bf16[16,72,1152]{2,1,0:T(8,128)(2,1)}, u32[]{:S(2)}) copy-start(bf16[16,72,1152]{2,1,0:T(8,128)(2,1)} %get-tuple-element.59) | copy-start | bytes 7962628
  247.8 44.4 %slice-start.1 = ((s8[10027008]{0:T(1024)(128)(4,1)}), s8[4194304]{0:T(1024)(128)(4,1)S(1)}, s32[]{:S(2)}) async-start(s8[10027008]{0:T(1024)(128)(4,1)} %bitcast.260), calls=%async_computation.1 | async-start | bytes 8388608
  247.8 44.4 %slice-start.2 = ((s8[10027008]{0:T(1024)(128)(4,1)}), s8[1638400]{0:T(1024)(128)(4,1)S(1)}, s32[]{:S(2)}) async-start(s8[10027008]{0:T(1024)(128)(4,1)} %bitcast.260), calls=%async_computation.2 | async-start | bytes 3276800
  291.2 128.9 %copy-start.6 = (bf16[16,216,128]{2,1,0:T(8,128)(2,1)}, bf16[16,216,128]{2,1,0:T(8,128)(2,1)S(1)}, u32[]{:S(2)}) copy-start(bf16[16,216,128]{2,1,0:T(8,128)(2,1)S(1)} %get-tuple-element.66.qkv_ref) | copy-start | bytes 2654212
  292.0 25.1 %copy-start.107 = (f32[128]{0:T(128)}, f32[128]{0:T(128)S(1)}, u32[]{:S(2)}) copy-start(f32[128]{0:T(128)S(1)} %broadcast_multiply_fusion.16) | copy-start | bytes 1540
  292.2 24.8 %copy-start.111 = (f32[128]{0:T(128)}, f32[128]{0:T(128)S(1)}, u32[]{:S(2)}) copy-start(f32[128]{0:T(128)S(1)} %add_rsqrt_fusion.4) | copy-start | bytes 1540
  303.4 26.4 %collective-permute-start.1 = (bf16[128,1152]{1,0:T(8,128)(2,1)}, bf16[128,1152]{1,0:T(8,128)(2,1)}, u32[]{:S(2)}, u32[]{:S(2)}) collective-permute-start(bf16[128,1152]{1,0:T(8,128)(2,1)} %fusion.16), channel_id=1, source_target_pairs={{0,16},{1,17},{2,18},{3,19},{4,20},{5,21},{6,22},{7,23},{8,24},{9,... | collective-permute-start | bytes 884744 | tf_op jit(solution)/shard_map/ppermute | solution.py:862
  331.9 8.9 %copy-start.62 = (bf16[128,1152]{1,0:T(8,128)(2,1)}, bf16[128,1152]{1,0:T(8,128)(2,1)S(1)}, u32[]{:S(2)}) copy-start(bf16[128,1152]{1,0:T(8,128)(2,1)S(1)} %get-tuple-element.152) | copy-start | bytes 884740
  347.1 58.6 %copy-start.10 = (bf16[4,4,72,128]{3,2,0,1:T(8,128)(2,1)}, bf16[4,4,72,128]{3,2,0,1:T(8,128)(2,1)S(1)}, u32[]{:S(2)}) copy-start(bf16[4,4,72,128]{3,2,0,1:T(8,128)(2,1)S(1)} %copy.140) | copy-start | bytes 884740
  352.3 53.5 %copy-start.43 = (bf16[16,72,1152]{2,1,0:T(8,128)(2,1)S(1)}, bf16[16,72,1152]{2,1,0:T(8,128)(2,1)}, u32[]{:S(2)}) copy-start(bf16[16,72,1152]{2,1,0:T(8,128)(2,1)} %get-tuple-element.59) | copy-start | bytes 7962628
  352.3 53.5 %copy-start.63 = (bf16[128,1152]{1,0:T(8,128)(2,1)S(1)}, bf16[128,1152]{1,0:T(8,128)(2,1)}, u32[]{:S(2)}) copy-start(bf16[128,1152]{1,0:T(8,128)(2,1)} %copy-done.62) | copy-start | bytes 884740
  405.7 10.4 %copy-start.27 = (bf16[16,216,128]{2,1,0:T(8,128)(2,1)}, bf16[16,216,128]{2,1,0:T(8,128)(2,1)S(1)}, u32[]{:S(2)}) copy-start(bf16[16,216,128]{2,1,0:T(8,128)(2,1)S(1)} %get-tuple-element.71) | copy-start | bytes 2654212
  407.3 9.5 %slice-start.15 = ((s8[10027008]{0:T(1024)(128)(4,1)}), s8[4194304]{0:T(1024)(128)(4,1)S(1)}, s32[]{:S(2)}) async-start(s8[10027008]{0:T(1024)(128)(4,1)} %bitcast.307), calls=%async_computation.15 | async-start | bytes 8388608
  408.2 80.7 %copy-start.60 = (f32[128,1152]{1,0:T(8,128)}, f32[128,1152]{1,0:T(8,128)S(1)}, u32[]{:S(2)}) copy-start(f32[128,1152]{1,0:T(8,128)S(1)} %get-tuple-element.149) | copy-start | bytes 1769476
  408.2 8.6 %slice-start.16 = ((s8[10027008]{0:T(1024)(128)(4,1)}), s8[4194304]{0:T(1024)(128)(4,1)S(1)}, s32[]{:S(2)}) async-start(s8[10027008]{0:T(1024)(128)(4,1)} %bitcast.307), calls=%async_computation.16 | async-start | bytes 8388608
  408.2 8.6 %slice-start.17 = ((s8[10027008]{0:T(1024)(128)(4,1)}), s8[1638400]{0:T(1024)(128)(4,1)S(1)}, s32[]{:S(2)}) async-start(s8[10027008]{0:T(1024)(128)(4,1)} %bitcast.307), calls=%async_computation.17 | async-start | bytes 3276800
  416.8 86.5 %copy-start.113 = (f32[128]{0:T(128)}, f32[128]{0:T(128)S(1)}, u32[]{:S(2)}) copy-start(f32[128]{0:T(128)S(1)} %broadcast_multiply_fusion.8) | copy-start | bytes 1540
  420.1 53.7 %copy-start.46 = (bf16[128,1152]{1,0:T(8,128)(2,1)S(1)}, bf16[128,1152]{1,0:T(8,128)(2,1)}, u32[]{:S(2)}) copy-start(bf16[128,1152]{1,0:T(8,128)(2,1)} %copy-done.44) | copy-start | bytes 884740
  420.1 53.7 %copy-start.105 = (f32[128]{0:T(128)S(1)}, f32[128]{0:T(128)}, u32[]{:S(2)}) copy-start(f32[128]{0:T(128)} %copy-done.103) | copy-start | bytes 1540
  481.5 8.6 %copy-start.82 = (bf16[1152,128]{0,1:T(8,128)(2,1)S(1)}, bf16[1152,128]{0,1:T(8,128)(2,1)}, u32[]{:S(2)}) copy-start(bf16[1152,128]{0,1:T(8,128)(2,1)} %get-tuple-element.170) | copy-start | bytes 884740
  481.5 9.5 %copy-start.20 = (bf16[16,72,128]{2,1,0:T(8,128)(2,1)S(1)}, bf16[16,72,128]{2,1,0:T(8,128)(2,1)}, u32[]{:S(2)}) copy-start(bf16[16,72,128]{2,1,0:T(8,128)(2,1)} %copy-done.19) | copy-start | bytes 884740
  482.7 12.2 %collective-permute-start.2 = (bf16[128,1152]{1,0:T(8,128)(2,1)}, bf16[128,1152]{1,0:T(8,128)(2,1)}, u32[]{:S(2)}, u32[]{:S(2)}) collective-permute-start(bf16[128,1152]{1,0:T(8,128)(2,1)} %get-tuple-element.150), channel_id=1, source_target_pairs={{16,0},{17,1},{18,2},{19,3},{20,4},{21,5},{22,6},{23,7},{24,8},{25... | collective-permute-start | bytes 884744 | tf_op jit(solution)/shard_map/ppermute | solution.py:923
  493.0 10.3 %slice-start.3 = ((s8[10027008]{0:T(1024)(128)(4,1)}), s8[4194304]{0:T(1024)(128)(4,1)S(1)}, s32[]{:S(2)}) async-start(s8[10027008]{0:T(1024)(128)(4,1)} %bitcast.264), calls=%async_computation.3 | async-start | bytes 8388608
  495.1 12.9 %copy-start.71 = (bf16[128,1152]{1,0:T(8,128)(2,1)}, bf16[128,1152]{1,0:T(8,128)(2,1)S(1)}, u32[]{:S(2)}) copy-start(bf16[128,1152]{1,0:T(8,128)(2,1)S(1)} %get-tuple-element.133) | copy-start | bytes 884740
  495.1 8.2 slice-start.4
  495.1 8.2 slice-start.5
  495.1 70.5 %slice-start.18 = ((s8[7962624]{0:T(1024)(128)(4,1)}), s8[4194304]{0:T(1024)(128)(4,1)S(1)}, s32[]{:S(2)}) async-start(s8[7962624]{0:T(1024)(128)(4,1)} %bitcast.315), calls=%async_computation.18 | async-start | bytes 8388608
  503.3 103.5 %copy-start.1 = (bf16[128,4352]{1,0:T(8,128)(2,1)}, bf16[128,4352]{1,0:T(8,128)(2,1)S(1)}, u32[]{:S(2)}) copy-start(bf16[128,4352]{1,0:T(8,128)(2,1)S(1)} %get-tuple-element.201.refs_4_.refs_14_.refs_17_) | copy-start | bytes 3342340
  503.3 62.3 %slice-start.19 = ((s8[7962624]{0:T(1024)(128)(4,1)}), s8[3768320]{0:T(1024)(128)(4,1)S(1)}, s32[]{:S(2)}) async-start(s8[7962624]{0:T(1024)(128)(4,1)} %bitcast.315), calls=%async_computation.19 | async-start | bytes 7536640
  512.4 53.2 %copy-start.59 = (bf16[2,128,1152]{2,1,0:T(8,128)(2,1)S(1)}, bf16[2,128,1152]{2,1,0:T(8,128)(2,1)}, u32[]{:S(2)}) copy-start(bf16[2,128,1152]{2,1,0:T(8,128)(2,1)} %param.15) | copy-start | bytes 1769476
  512.4 53.2 %copy-start.64 = (bf16[128,1152]{1,0:T(8,128)(2,1)S(1)}, bf16[128,1152]{1,0:T(8,128)(2,1)}, u32[]{:S(2)}) copy-start(bf16[128,1152]{1,0:T(8,128)(2,1)} %copy-done.62) | copy-start | bytes 884740
  512.4 53.2 %copy-start.117 = (f32[128]{0:T(128)S(1)}, f32[128]{0:T(128)}, u32[]{:S(2)}) copy-start(f32[128]{0:T(128)} %copy-done.116) | copy-start | bytes 1540
  512.4 53.2 %copy-start.122 = (f32[128]{0:T(128)S(1)}, f32[128]{0:T(128)}, u32[]{:S(2)}) copy-start(f32[128]{0:T(128)} %add_rsqrt_fusion) | copy-start | bytes 1540
  570.1 8.8 %copy-start.65 = (f32[128,1152]{1,0:T(8,128)}, f32[128,1152]{1,0:T(8,128)S(1)}, u32[]{:S(2)}) copy-start(f32[128,1152]{1,0:T(8,128)S(1)} %get-tuple-element.144) | copy-start | bytes 1769476
  570.9 11.3 %collective-permute-start.3 = (bf16[128,1152]{1,0:T(8,128)(2,1)}, bf16[128,1152]{1,0:T(8,128)(2,1)}, u32[]{:S(2)}, u32[]{:S(2)}) collective-permute-start(bf16[128,1152]{1,0:T(8,128)(2,1)} %convert_element_type.187), channel_id=1, source_target_pairs={{16,0},{17,1},{18,2},{19,3},{20,4},{21,5},{22,6},{23,7},{24,8},{25... | collective-permute-start | bytes 884744 | tf_op jit(solution)/shard_map/ppermute | solution.py:923
  577.0 14.5 %slice-start.6 = ((s8[10027008]{0:T(1024)(128)(4,1)}), s8[1638400]{0:T(1024)(128)(4,1)S(1)}, s32[]{:S(2)}) async-start(s8[10027008]{0:T(1024)(128)(4,1)} %bitcast.267), calls=%async_computation.6 | async-start | bytes 3276800
  583.5 15.2 %copy-start.72 = (bf16[128,1152]{1,0:T(8,128)(2,1)}, bf16[128,1152]{1,0:T(8,128)(2,1)S(1)}, u32[]{:S(2)}) copy-start(bf16[128,1152]{1,0:T(8,128)(2,1)S(1)} %get-tuple-element.131) | copy-start | bytes 884740
  (109 other events, 446.7 us)

commit v4 on v3

--- a/solution.py
+++ b/solution.py
@@ -234,13 +234,16 @@
     return jnp.dot(a, b, preferred_element_type=F32)
 
 
-def window(image_row):
-    blocks = image_row.shape[0]
-    first = jnp.argmax(image_row[None, :] == image_row[:, None], axis=1).astype(jnp.int32)
-    first = jnp.minimum(first, blocks - IMG_BLOCKS)
-    near = image_row[first[:, None] + jnp.arange(IMG_BLOCKS)[None, :]]
-    bias = jnp.where(near == image_row[:, None], 0.0, MASKED_SCORE).astype(F32)
-    return first, jnp.broadcast_to(bias[:, :, None], (blocks, IMG_BLOCKS, BLOCK))
+def window(image_of_block):
+    micro, blocks = image_of_block.shape
+    own, other = image_of_block[:, :, None], image_of_block[:, None, :]
+    begin = jnp.sum((other < own).astype(jnp.int32), axis=2)
+    end = jnp.sum((other <= own).astype(jnp.int32), axis=2)
+    first = jnp.minimum(begin, blocks - IMG_BLOCKS)
+    shape = (micro, blocks, IMG_BLOCKS, BLOCK)
+    at = first[:, :, None, None] + lax.broadcasted_iota(jnp.int32, shape, 2)
+    same = (at >= begin[:, :, None, None]) & (at < end[:, :, None, None])
+    return first, jnp.where(same, 0.0, MASKED_SCORE).astype(F32)
 
 
 def near_rows(ref, start):
@@ -251,7 +254,241 @@
     return jnp.concatenate([ref[start + j] for j in range(IMG_BLOCKS)], axis=1)
 
 
-def attend_kernel(items, pieces, first_ref, bias_ref, x_ref, *refs):
+def fetch(pairs, buffers, sems, sec):
+    for which in range(2):
+
+        @pl.when(sec == which)
+        def _():
+            for i, buffer in enumerate(buffers):
+                pltpu.make_async_copy(pairs[2 * i + which], buffer, sems.at[i]).start()
+
+
+def fetched(pairs, buffers, sems):
+    for i, buffer in enumerate(buffers):
+        pltpu.make_async_copy(pairs[2 * i], buffer, sems.at[i]).wait()
+
+
+class ToAll:
+    def __init__(self, block, dst, send, recv, sec, me, count):
+        self.block, self.dst, self.send, self.recv = block, dst, send, recv
+        self.sec, self.me, self.count = sec, me, count
+
+    def copy(self, d):
+        return pltpu.make_async_remote_copy(
+            src_ref=self.block(d),
+            dst_ref=self.dst.at[self.me],
+            send_sem=self.send.at[d],
+            recv_sem=self.recv.at[d],
+            device_id=(self.sec, (self.me + d) % self.count),
+            device_id_type=MESH,
+        )
+
+    def start(self):
+        for d in sorted(range(1, self.count), key=lambda d: abs(d - self.count // 2)):
+            self.copy(d).start()
+
+    def start_one(self, d):
+        @pl.when(d > 0)
+        def _():
+            self.copy(d).start()
+
+    def wait(self):
+        for d in range(1, self.count):
+            self.copy(d).wait()
+
+
+class Forward:
+    def __init__(self, tick, near, x_ref, outs, scratch):
+        self.first_ref, self.bias_ref = near
+        self.x_ref = x_ref
+        self.qkv_ref, self.lse_ref, self.att_ref = outs
+        self.k_all, self.vt_all, self.o_buf, self.local_sem, *sems = scratch
+        self.count = x_ref.shape[0]
+        sec, self.me = place()
+        self.slot = jnp.minimum(jnp.maximum(tick - sec, 0), 1)
+        rest = (sec, self.me, self.count)
+        self.arrive = ToAll(lambda d: x_ref.at[(self.me + d) % self.count], self.qkv_ref, *sems[:2], *rest)
+        self.leave = ToAll(lambda d: self.o_buf.at[d], self.att_ref, *sems[2:], *rest)
+
+    @staticmethod
+    def scratch(blocks):
+        dma = pltpu.SemaphoreType.DMA
+        return [
+            pltpu.VMEM((blocks, BLOCK, HEAD_DIM), BF),
+            pltpu.VMEM((blocks, HEAD_DIM, BLOCK), BF),
+            pltpu.VMEM((blocks, HEAD_DIM, BLOCK), BF),
+            dma,
+        ] + [dma((blocks,))] * 4
+
+    def own(self):
+        return pltpu.make_async_copy(self.x_ref.at[self.me], self.qkv_ref.at[self.me], self.local_sem)
+
+    def start(self):
+        self.arrive.start()
+        self.own().start()
+
+    def wait_in(self):
+        self.own().wait()
+        self.arrive.wait()
+
+    def compute(self):
+        def arrange(j, carry):
+            part = self.qkv_ref[j].astype(F32)
+            self.k_all[j] = part[HEAD_DIM : 2 * HEAD_DIM].T.astype(BF)
+            self.vt_all[j] = part[2 * HEAD_DIM :].astype(BF)
+            return carry
+
+        lax.fori_loop(0, self.count, arrange, 0)
+
+        def one_block(d, carry):
+            i = (self.me + d) % self.count
+            start = self.first_ref[self.slot, i]
+            qt = self.qkv_ref[i].astype(F32)[:HEAD_DIM].astype(BF)
+            s = dot(near_rows(self.k_all, start), qt) * SCALE
+            bias = self.bias_ref[self.slot, i]
+            parts = [s[j * BLOCK : (j + 1) * BLOCK] + bias[j : j + 1] for j in range(IMG_BLOCKS)]
+            top = parts[0]
+            for part in parts[1:]:
+                top = jnp.maximum(top, part)
+            top = jnp.max(top, axis=0, keepdims=True)
+            exps = [jnp.exp(part - top) for part in parts]
+            total = exps[0]
+            for part in exps[1:]:
+                total = total + part
+            total = jnp.sum(total, axis=0, keepdims=True)
+            e = jnp.concatenate([part.astype(BF) for part in exps], axis=0)
+            o = dot(near_columns(self.vt_all, start), e)
+            self.o_buf[d] = (o / total).astype(BF)
+            self.lse_ref[i] = top + jnp.log(total)
+            self.leave.start_one(d)
+            return carry
+
+        lax.fori_loop(0, self.count, one_block, 0)
+        self.att_ref[self.me] = self.o_buf[0]
+
+    def wait_out(self):
+        self.leave.wait()
+
+
+class Backward:
+    def __init__(self, tick, near, kept, x_ref, outs, scratch):
+        self.first_ref, self.bias_ref = near
+        self.kept, self.x_ref = kept, x_ref
+        self.dq_ref, self.dkv_ref = outs
+        self.qkv_ref, self.lse_ref, self.do_ref = scratch[:3]
+        self.k_all, self.kt_all, self.v_all, self.q_all, self.do_all, self.p_all, self.s_all = scratch[3:10]
+        self.dq_buf, self.dkv_buf, self.kept_sem, self.local_sem = scratch[10:14]
+        sems = scratch[14:]
+        self.count = x_ref.shape[0]
+        self.sec, self.me = place()
+        self.slot = jnp.minimum(jnp.maximum(tick - 1 + self.sec, 0), 1)
+        rest = (self.sec, self.me, self.count)
+        self.arrive = ToAll(lambda d: x_ref.at[(self.me + d) % self.count], self.do_ref, *sems[:2], *rest)
+        self.leave_q = ToAll(lambda d: self.dq_buf.at[d], self.dq_ref, *sems[2:4], *rest)
+        self.leave_kv = ToAll(lambda d: self.dkv_buf.at[d], self.dkv_ref, *sems[4:], *rest)
+
+    @staticmethod
+    def scratch(blocks):
+        dma = pltpu.SemaphoreType.DMA
+        return [
+            pltpu.VMEM((blocks, 3 * HEAD_DIM, BLOCK), BF),
+            pltpu.VMEM((blocks, 1, BLOCK), F32),
+            pltpu.VMEM((blocks, HEAD_DIM, BLOCK), BF),
+            pltpu.VMEM((blocks, BLOCK, HEAD_DIM), BF),
+            pltpu.VMEM((blocks, HEAD_DIM, BLOCK), BF),
+            pltpu.VMEM((blocks, BLOCK, HEAD_DIM), BF),
+            pltpu.VMEM((blocks, BLOCK, HEAD_DIM), BF),
+            pltpu.VMEM((blocks, BLOCK, HEAD_DIM), BF),
+            pltpu.VMEM((blocks, IMG_BLOCKS, BLOCK, BLOCK), BF),
+            pltpu.VMEM((blocks, IMG_BLOCKS, BLOCK, BLOCK), BF),
+            pltpu.VMEM((blocks, HEAD_DIM, BLOCK), BF),
+            pltpu.VMEM((blocks, 2 * HEAD_DIM, BLOCK), BF),
+            dma((2,)),
+            dma,
+        ] + [dma((blocks,))] * 6
+
+    def own(self):
+        return pltpu.make_async_copy(self.x_ref.at[self.me], self.do_ref.at[self.me], self.local_sem)
+
+    def start(self):
+        self.arrive.start()
+        self.own().start()
+        fetch(self.kept, (self.qkv_ref, self.lse_ref), self.kept_sem, self.sec)
+
+    def arrange(self):
+        fetched(self.kept, (self.qkv_ref, self.lse_ref), self.kept_sem)
+
+        def one(j, carry):
+            part = self.qkv_ref[j].astype(F32)
+            self.q_all[j] = part[:HEAD_DIM].T.astype(BF)
+            self.k_all[j] = part[HEAD_DIM : 2 * HEAD_DIM].T.astype(BF)
+            self.v_all[j] = part[2 * HEAD_DIM :].T.astype(BF)
+            self.kt_all[j] = part[HEAD_DIM : 2 * HEAD_DIM].astype(BF)
+            return carry
+
+        lax.fori_loop(0, self.count, one, 0)
+
+    def wait_in(self):
+        self.own().wait()
+        self.arrive.wait()
+
+    def by_query(self):
+        def turn(j, carry):
+            self.do_all[j] = self.do_ref[j].astype(F32).T.astype(BF)
+            return carry
+
+        lax.fori_loop(0, self.count, turn, 0)
+
+        def one(d, carry):
+            i = (self.me + d) % self.count
+            start = self.first_ref[self.slot, i]
+            qt = self.qkv_ref[i].astype(F32)[:HEAD_DIM].astype(BF)
+            s = dot(near_rows(self.k_all, start), qt) * SCALE
+            shift = self.bias_ref[self.slot, i] - self.lse_ref[i]
+            probs = [jnp.exp(s[j * BLOCK : (j + 1) * BLOCK] + shift[j : j + 1]) for j in range(IMG_BLOCKS)]
+            dp = dot(near_rows(self.v_all, start), self.do_ref[i])
+            total = probs[0] * dp[:BLOCK]
+            for j in range(1, IMG_BLOCKS):
+                total = total + probs[j] * dp[j * BLOCK : (j + 1) * BLOCK]
+            total = jnp.sum(total, axis=0, keepdims=True)
+            ds = jnp.concatenate(
+                [(probs[j] * (dp[j * BLOCK : (j + 1) * BLOCK] - total)).astype(BF) for j in range(IMG_BLOCKS)], axis=0
+            )
+            for j in range(IMG_BLOCKS):
+                self.p_all[i, j] = probs[j].astype(BF)
+                self.s_all[i, j] = ds[j * BLOCK : (j + 1) * BLOCK]
+            self.dq_buf[d] = (dot(near_columns(self.kt_all, start), ds) * SCALE).astype(BF)
+            self.leave_q.start_one(d)
+            return carry
+
+        lax.fori_loop(0, self.count, one, 0)
+        self.dq_ref[self.me] = self.dq_buf[0]
+
+    def by_key(self):
+        def one(d, carry):
+            j = (self.me + d) % self.count
+            start = self.first_ref[self.slot, j]
+            place_in = jnp.clip(j - start, 0, IMG_BLOCKS - 1)
+            same = (self.bias_ref[self.slot, j] == 0.0).astype(F32).astype(BF)
+            p, ds = [], []
+            for m in range(IMG_BLOCKS):
+                p.append(self.p_all[start + m, place_in] * same[m : m + 1])
+                ds.append(self.s_all[start + m, place_in] * same[m : m + 1])
+            dv = dot(jnp.concatenate(p, axis=1), near_rows(self.do_all, start))
+            dk = dot(jnp.concatenate(ds, axis=1), near_rows(self.q_all, start)) * SCALE
+            self.dkv_buf[d] = jnp.concatenate([dk.T, dv.T], axis=0).astype(BF)
+            self.leave_kv.start_one(d)
+            return carry
+
+        lax.fori_loop(0, self.count, one, 0)
+        self.dkv_ref[self.me] = self.dkv_buf[0]
+
+    def wait_out(self):
+        self.leave_q.wait()
+        self.leave_kv.wait()
+
+
+def attention_kernel(ahead, behind, items, pieces, *refs):
     refs = list(refs)
 
     def take(n):
@@ -260,298 +497,131 @@
         return part
 
     n = len(items)
+    near = take(2)
+    x_ref = take(1) if ahead is not None else None
+    kept, g_ref = (take(4), take(1)) if behind is not None else (None, None)
     sources, shards = take(2 * n), take(pieces)
-    qkv_ref, lse_ref, att_ref = take(3)
+    ahead_out = take(3) if ahead is not None else None
+    behind_out = take(2) if behind is not None else None
     outs, whole = take(n), take(pieces)
-    k_all, vt_all, o_buf, local_sem, send_sem, recv_sem, att_send, att_recv = take(8)
-    blocks = x_ref.shape[0]
+    f = b = work = None
+    blocks = (x_ref or g_ref)[0].shape[0]
     sec, me = place()
-    greet_all(blocks, sec, me)
-
-    def incoming(d):
-        target = (me + d) % blocks
-        return pltpu.make_async_remote_copy(
-            src_ref=x_ref.at[target],
-            dst_ref=qkv_ref.at[me],
-            send_sem=send_sem.at[d],
-            recv_sem=recv_sem.at[d],
-            device_id=(sec, target),
-            device_id_type=MESH,
-        )
-
-    def outgoing(d):
-        target = (me + d) % blocks
-        return pltpu.make_async_remote_copy(
-            src_ref=o_buf.at[d],
-            dst_ref=att_ref.at[me],
-            send_sem=att_send.at[d],
-            recv_sem=att_recv.at[d],
-            device_id=(sec, target),
-            device_id_type=MESH,
-        )
-
-    for d in sorted(range(1, blocks), key=lambda d: abs(d - blocks // 2)):
-        incoming(d).start()
-    own = pltpu.make_async_copy(x_ref.at[me], qkv_ref.at[me], local_sem)
-    own.start()
-    behind_sems = [take(3) for _ in items]
-    work = None
+    if ahead is not None:
+        f = Forward(ahead, near, x_ref[0], ahead_out, take(len(Forward.scratch(blocks))))
+    if behind is not None:
+        b = Backward(behind, near, kept, g_ref[0], behind_out, take(len(Backward.scratch(blocks))))
+    copies = []
+    for i, item in enumerate(items):
+        into = lambda k, i=i: outs[i].at[k]
+        copies.append(PlaneCopies(item, sources[2 * i], sources[2 * i + 1], into, *take(3)))
     if pieces:
         work = Gather(shards, whole, take(9))
+    greet_all(blocks, sec, me)
+
+    if b:
+        b.start()
+        b.arrange()
+        b.wait_in()
+    if f:
+        f.start()
+    if work:
         work.start()
-    own.wait()
-    for d in range(1, blocks):
-        incoming(d).wait()
+    if f and not b:
+        f.wait_in()
     if work:
         work.step(1)
-    behind = []
-    for i, item in enumerate(items):
-        slot = lambda k, i=i: outs[i].at[k]
-        behind.append(PlaneCopies(item, sources[2 * i], sources[2 * i + 1], slot, *behind_sems[i]))
-        behind[-1].start()
-
-    def arrange(j, carry):
-        part = qkv_ref[j].astype(F32)
-        k_all[j] = part[HEAD_DIM : 2 * HEAD_DIM].T.astype(BF)
-        vt_all[j] = part[2 * HEAD_DIM :].astype(BF)
-        return carry
-
-    lax.fori_loop(0, blocks, arrange, 0)
-
-    def one_block(d, carry):
-        i = (me + d) % blocks
-        start = first_ref[i]
-        qt = qkv_ref[i].astype(F32)[:HEAD_DIM].astype(BF)
-        s = dot(near_rows(k_all, start), qt) * SCALE
-        bias = bias_ref[i]
-        parts = [s[j * BLOCK : (j + 1) * BLOCK] + bias[j : j + 1] for j in range(IMG_BLOCKS)]
-        top = parts[0]
-        for part in parts[1:]:
-            top = jnp.maximum(top, part)
-        top = jnp.max(top, axis=0, keepdims=True)
-        exps = [jnp.exp(part - top) for part in parts]
-        total = exps[0]
-        for part in exps[1:]:
-            total = total + part
-        total = jnp.sum(total, axis=0, keepdims=True)
-        e = jnp.concatenate([part.astype(BF) for part in exps], axis=0)
-        o = dot(near_columns(vt_all, start), e)
-        o_buf[d] = (o / total).astype(BF)
-        lse_ref[i] = top + jnp.log(total)
-
-        @pl.when(d > 0)
-        def _():
-            outgoing(d).start()
-
-        return carry
-
-    lax.fori_loop(0, blocks, one_block, 0)
-    att_ref[me] = o_buf[0]
+    if not (f and b):
+        for copy in copies:
+            copy.start()
+    if b:
+        b.by_query()
+        b.by_key()
+    if f and b:
+        f.wait_in()
+        for copy in copies:
+            copy.start()
+    if f:
+        f.compute()
     if work:
         work.step(2)
-    for one in behind:
-        one.forward()
-    for d in range(1, blocks):
-        outgoing(d).wait()
+    for copy in copies:
+        copy.forward()
+    if f:
+        f.wait_out()
+    if b:
+        b.wait_out()
     if work:
         work.step(3)
         work.across()
         work.finish()
-    for one in behind:
-        one.finish()
-
-
-def attend(qkv, near, cid, items=(), shards=()):
-    blocks = qkv.shape[0]
+    for copy in copies:
+        copy.finish()
+
+
+def attention(near, cid, ahead=None, behind=None, items=(), shards=()):
+    first_in = ahead[1] if ahead else behind[1]
+    blocks = first_in.shape[0]
     n = len(items)
     sources = [source for item in items for source in item.sources]
     anywhere, vmem, smem = [pl.BlockSpec(memory_space=m) for m in (pl.ANY, pltpu.VMEM, pltpu.SMEM)]
     dma = pltpu.SemaphoreType.DMA
-    scratch = [
-        pltpu.VMEM((blocks, BLOCK, HEAD_DIM), BF),
-        pltpu.VMEM((blocks, HEAD_DIM, BLOCK), BF),
-        pltpu.VMEM((blocks, HEAD_DIM, BLOCK), BF),
-        dma,
-    ] + [dma((blocks,))] * 4
+    args, scratch, shapes = [], [], []
+    if ahead:
+        args.append(ahead[1])
+        scratch += Forward.scratch(blocks)
+        shapes += [
+            jax.ShapeDtypeStruct((blocks, 3 * HEAD_DIM, BLOCK), BF),
+            jax.ShapeDtypeStruct((blocks, 1, BLOCK), F32),
+            jax.ShapeDtypeStruct((blocks, HEAD_DIM, BLOCK), BF),
+        ]
+    if behind:
+        args += [*behind[2], behind[1]]
+        scratch += Backward.scratch(blocks)
+        shapes += [
+            jax.ShapeDtypeStruct((blocks, HEAD_DIM, BLOCK), BF),
+            jax.ShapeDtypeStruct((blocks, 2 * HEAD_DIM, BLOCK), BF),
+        ]
+    args += sources + list(shards)
     scratch += [dma, dma((4,)), dma((4,))] * n
     if shards:
         scratch += Gather.semaphores(len(shards))
+    in_vmem = len(shapes)
+    shapes += [jax.ShapeDtypeStruct(item.shape(), BF) for item in items]
+    shapes += [jax.ShapeDtypeStruct((blocks,) + shard.shape, BF) for shard in shards]
     out = pl.pallas_call(
-        functools.partial(attend_kernel, list(items), len(shards)),
-        out_shape=[
-            jax.ShapeDtypeStruct(qkv.shape, BF),
-            jax.ShapeDtypeStruct((blocks, 1, BLOCK), F32),
-            jax.ShapeDtypeStruct((blocks, HEAD_DIM, BLOCK), BF),
-        ]
-        + [jax.ShapeDtypeStruct(item.shape(), BF) for item in items]
-        + [jax.ShapeDtypeStruct((blocks,) + shard.shape, BF) for shard in shards],
-        in_specs=[smem, vmem] + [anywhere] * (1 + len(sources) + len(shards)),
-        out_specs=[vmem] * 3 + [anywhere] * (n + len(shards)),
+        functools.partial(
+            attention_kernel, ahead and ahead[0], behind and behind[0], list(items), len(shards)
+        ),
+        out_shape=shapes,
+        in_specs=[smem, vmem] + [anywhere] * len(args),
+        out_specs=[vmem] * in_vmem + [anywhere] * (n + len(shards)),
         scratch_shapes=scratch,
-        compiler_params=pltpu.CompilerParams(collective_id=cid, has_side_effects=True, vmem_limit_bytes=32 << 20),
-    )(*near, qkv, *sources, *shards)
-    return out[0], out[1], out[2], out[3 : 3 + n], out[3 + n :]
-
-
-def attend_back_kernel(items, first_ref, bias_ref, qkv_ref, lse_ref, x_ref, *refs):
-    refs = list(refs)
-
-    def take(n):
-        part = refs[:n]
-        del refs[:n]
-        return part
-
-    n = len(items)
-    sources = take(2 * n)
-    dq_ref, dkv_ref = take(2)
-    outs = take(n)
-    do_ref, k_all, kt_all, v_all, q_all, do_all, p_all, s_all, dq_buf, dkv_buf = take(10)
-    local_sem, send_sem, recv_sem, q_send, q_recv, kv_send, kv_recv = take(7)
-    blocks = x_ref.shape[0]
-    sec, me = place()
-    greet_all(blocks, sec, me)
-
-    def remote(src, dst, send, recv, d):
-        return pltpu.make_async_remote_copy(
-            src_ref=src,
-            dst_ref=dst,
-            send_sem=send.at[d],
-            recv_sem=recv.at[d],
-            device_id=(sec, (me + d) % blocks),
-            device_id_type=MESH,
-        )
-
-    def incoming(d):
-        return remote(x_ref.at[(me + d) % blocks], do_ref.at[me], send_sem, recv_sem, d)
-
-    def send_q(d):
-        return remote(dq_buf.at[d], dq_ref.at[me], q_send, q_recv, d)
-
-    def send_kv(d):
-        return remote(dkv_buf.at[d], dkv_ref.at[me], kv_send, kv_recv, d)
-
-    for d in sorted(range(1, blocks), key=lambda d: abs(d - blocks // 2)):
-        incoming(d).start()
-    own = pltpu.make_async_copy(x_ref.at[me], do_ref.at[me], local_sem)
-    own.start()
-
-    def arrange(j, carry):
-        part = qkv_ref[j].astype(F32)
-        q_all[j] = part[:HEAD_DIM].T.astype(BF)
-        k_all[j] = part[HEAD_DIM : 2 * HEAD_DIM].T.astype(BF)
-        v_all[j] = part[2 * HEAD_DIM :].T.astype(BF)
-        kt_all[j] = part[HEAD_DIM : 2 * HEAD_DIM].astype(BF)
-        return carry
-
-    lax.fori_loop(0, blocks, arrange, 0)
-    own.wait()
-    for d in range(1, blocks):
-        incoming(d).wait()
-    behind = []
-    for i, item in enumerate(items):
-        behind.append(
-            PlaneCopies(item, sources[2 * i], sources[2 * i + 1], lambda k, i=i: outs[i].at[k], *take(3))
-        )
-        behind[-1].start()
-
-    def arrange_grad(j, carry):
-        do_all[j] = do_ref[j].astype(F32).T.astype(BF)
-        return carry
-
-    lax.fori_loop(0, blocks, arrange_grad, 0)
-
-    def by_query(d, carry):
-        i = (me + d) % blocks
-        start = first_ref[i]
-        qt = qkv_ref[i].astype(F32)[:HEAD_DIM].astype(BF)
-        s = dot(near_rows(k_all, start), qt) * SCALE
-        shift = bias_ref[i] - lse_ref[i]
-        probs = [jnp.exp(s[j * BLOCK : (j + 1) * BLOCK] + shift[j : j + 1]) for j in range(IMG_BLOCKS)]
-        dp = dot(near_rows(v_all, start), do_ref[i])
-        total = probs[0] * dp[:BLOCK]
-        for j in range(1, IMG_BLOCKS):
-            total = total + probs[j] * dp[j * BLOCK : (j + 1) * BLOCK]
-        total = jnp.sum(total, axis=0, keepdims=True)
-        ds = jnp.concatenate(
-            [(probs[j] * (dp[j * BLOCK : (j + 1) * BLOCK] - total)).astype(BF) for j in range(IMG_BLOCKS)], axis=0
-        )
-        for j in range(IMG_BLOCKS):
-            p_all[i, j] = probs[j].astype(BF)
-            s_all[i, j] = ds[j * BLOCK : (j + 1) * BLOCK]
-        dq_buf[d] = (dot(near_columns(kt_all, start), ds) * SCALE).astype(BF)
-
-        @pl.when(d > 0)
-        def _():
-            send_q(d).start()
-
-        return carry
-
-    lax.fori_loop(0, blocks, by_query, 0)
-    for one in behind:
-        one.forward()
-
-    def by_key(d, carry):
-        j = (me + d) % blocks
-        start = first_ref[j]
-        place_in = jnp.clip(j - start, 0, IMG_BLOCKS - 1)
-        same = (bias_ref[j] == 0.0).astype(F32).astype(BF)
-        p, ds = [], []
-        for m in range(IMG_BLOCKS):
-            p.append(p_all[start + m, place_in] * same[m : m + 1])
-            ds.append(s_all[start + m, place_in] * same[m : m + 1])
-        dv = dot(jnp.concatenate(p, axis=1), near_rows(do_all, start))
-        dk = dot(jnp.concatenate(ds, axis=1), near_rows(q_all, start)) * SCALE
-        dkv_buf[d] = jnp.concatenate([dk.T, dv.T], axis=0).astype(BF)
-
-        @pl.when(d > 0)
-        def _():
-            send_kv(d).start()
-
-        return carry
-
-    lax.fori_loop(0, blocks, by_key, 0)
-    dq_ref[me] = dq_buf[0]
-    dkv_ref[me] = dkv_buf[0]
-    for d in range(1, blocks):
-        send_q(d).wait()
-        send_kv(d).wait()
-    for one in behind:
-        one.finish()
-
-
-def attend_back(att_grad, near, qkv, lse, cid, items=()):
-    blocks = qkv.shape[0]
-    n = len(items)
-    sources = [source for item in items for source in item.sources]
-    anywhere, vmem, smem = [pl.BlockSpec(memory_space=m) for m in (pl.ANY, pltpu.VMEM, pltpu.SMEM)]
-    dma = pltpu.SemaphoreType.DMA
-    scratch = [
-        pltpu.VMEM((blocks, HEAD_DIM, BLOCK), BF),
-        pltpu.VMEM((blocks, BLOCK, HEAD_DIM), BF),
-        pltpu.VMEM((blocks, HEAD_DIM, BLOCK), BF),
-        pltpu.VMEM((blocks, BLOCK, HEAD_DIM), BF),
-        pltpu.VMEM((blocks, BLOCK, HEAD_DIM), BF),
-        pltpu.VMEM((blocks, BLOCK, HEAD_DIM), BF),
-        pltpu.VMEM((blocks, IMG_BLOCKS, BLOCK, BLOCK), BF),
-        pltpu.VMEM((blocks, IMG_BLOCKS, BLOCK, BLOCK), BF),
-        pltpu.VMEM((blocks, HEAD_DIM, BLOCK), BF),
-        pltpu.VMEM((blocks, 2 * HEAD_DIM, BLOCK), BF),
-        dma,
-    ] + [dma((blocks,))] * 6
-    scratch += [dma, dma((4,)), dma((4,))] * n
-    out = pl.pallas_call(
-        functools.partial(attend_back_kernel, list(items)),
-        out_shape=[
-            jax.ShapeDtypeStruct((blocks, HEAD_DIM, BLOCK), BF),
-            jax.ShapeDtypeStruct((blocks, 2 * HEAD_DIM, BLOCK), BF),
-        ]
-        + [jax.ShapeDtypeStruct(item.shape(), BF) for item in items],
-        in_specs=[smem, vmem, vmem, vmem] + [anywhere] * (1 + len(sources)),
-        out_specs=[vmem] * 2 + [anywhere] * n,
-        scratch_shapes=scratch,
-        compiler_params=pltpu.CompilerParams(collective_id=cid, has_side_effects=True, vmem_limit_bytes=40 << 20),
-    )(*near, qkv, lse, att_grad, *sources)
-    return jnp.concatenate(out[:2], axis=1), out[2:]
+        compiler_params=pltpu.CompilerParams(collective_id=cid, has_side_effects=True, vmem_limit_bytes=60 << 20),
+    )(*near, *args)
+    out = list(out)
+    three, out = (out[:3], out[3:]) if ahead else (None, out)
+    two, out = (out[:2], out[2:]) if behind else (None, out)
+    return three, two, out[:n], out[n:]
+
+
+def slices(width, step=1024):
+    return [(at, min(at + step, width)) for at in range(0, width, step)]
+
+
+class Stream:
+    def __init__(self, pairs, sems):
+        self.copies = {}
+        for i, (name, ref, buf, cols) in enumerate(pairs):
+            src, dst = ref.at[:, cols[0] : cols[1]], buf.at[:, cols[0] : cols[1]]
+            self.copies[name, cols[0]] = pltpu.make_async_copy(src, dst, sems.at[i])
+
+    def start(self):
+        for copy in self.copies.values():
+            copy.start()
+
+    def wait(self, name, at):
+        self.copies[name, at].wait()
 
 
 def normalised(x):
@@ -564,27 +634,304 @@
 def norm_backward(grad, xhat, rstd, gain):
     g = grad * gain
     part = g - jnp.mean(g, axis=-1, keepdims=True) - xhat * jnp.mean(g * xhat, axis=-1, keepdims=True)
-    return part * rstd, jnp.sum(grad * xhat, axis=0), jnp.sum(grad, axis=0)
-
-
-def gelu_and_slope(v):
+    return part * rstd, jnp.sum(grad * xhat, axis=0, keepdims=True), jnp.sum(grad, axis=0, keepdims=True)
+
+
+def gelu_tanh(v):
     c = math.sqrt(2.0 / math.pi)
-    t = jnp.tanh(c * (v + 0.044715 * v * v * v))
-    value = 0.5 * v * (1.0 + t)
-    slope = 0.5 * (1.0 + t) + 0.5 * v * (1.0 - t * t) * c * (1.0 + 3 * 0.044715 * v * v)
-    return value, slope
-
-
-def by_rows(x):
-    return x.T.reshape(HEADS, HEAD_DIM, x.shape[0])
+    return 0.5 * v * (1.0 + jnp.tanh(c * (v + 0.044715 * (v * v * v))))
+
+
+def gelu_slope(v):
+    c = math.sqrt(2.0 / math.pi)
+    square = v * v
+    t = jnp.tanh(c * (v + 0.044715 * (square * v)))
+    return 0.5 * (1.0 + t) + 0.5 * v * (1.0 - t * t) * (c * (1.0 + 3 * 0.044715 * square))
+
+
+def nt(a, b):
+    return lax.dot_general(a, b, (((1,), (1,)), ((), ())), preferred_element_type=F32)
+
+
+def put_owners(ref, x):
+    turned = x.T
+    for w in range(HEADS):
+        ref[w % 4, w // 4] = turned[w * HEAD_DIM : (w + 1) * HEAD_DIM].astype(BF)
+
+
+GAIN1, BIAS1, OUT_BIAS, GAIN2, BIAS2, FC2_BIAS = range(6)
+
+
+def row(vec_ref, i):
+    return vec_ref[i : i + 1, :]
+
+
+def pick(sec, zero_ref, one_ref):
+    return jnp.where(sec == 0, zero_ref[...].astype(F32), one_ref[...].astype(F32))
+
+
+def qkv_kernel(tok_ref, inc_ref, vec_ref, bias_ref, w_ref, qkv_ref, n1_ref, w_buf, t_buf, sems):
+    sec, _ = place()
+    stream = Stream([("w", w_ref, w_buf, cols) for cols in slices(3 * D, 384)], sems)
+    stream.start()
+    xhat, _ = normalised(pick(sec, tok_ref, inc_ref))
+    n1 = xhat * row(vec_ref, GAIN1) + row(vec_ref, BIAS1)
+    low = n1.astype(BF)
+    for at, end in slices(3 * D, 384):
+        stream.wait("w", at)
+        t_buf[at:end, :] = (dot(low, w_buf[:, at:end]) + bias_ref[:, at:end]).T
+    for h in range(HEADS):
+        qkv_ref[h] = t_buf[h * 3 * HEAD_DIM : (h + 1) * 3 * HEAD_DIM, :].astype(BF)
+    put_owners(n1_ref, low.astype(F32))
+
+
+def qkv_forward(tok, inc, vec, bias, w):
+    tokens = tok.shape[0]
+    anywhere, vmem = pl.BlockSpec(memory_space=pl.ANY), pl.BlockSpec(memory_space=pltpu.VMEM)
+    return pl.pallas_call(
+        qkv_kernel,
+        out_shape=[
+            jax.ShapeDtypeStruct((HEADS, 3 * HEAD_DIM, tokens), BF),
+            jax.ShapeDtypeStruct((4, 4, HEAD_DIM, tokens), BF),
+        ],
+        in_specs=[vmem] * 4 + [anywhere],
+        out_specs=[vmem] * 2,
+        scratch_shapes=[
+            pltpu.VMEM((D, 3 * D), BF),
+            pltpu.VMEM((3 * D, tokens), F32),
+            pltpu.SemaphoreType.DMA((len(slices(3 * D, 384)),)),
+        ],
+        compiler_params=pltpu.CompilerParams(vmem_limit_bytes=60 << 20),
+    )(tok, inc, vec, bias, w)
+
+
+def greet_section(sec, me):
+    barrier = pltpu.get_barrier_semaphore()
+    pl.semaphore_signal(barrier, inc=1, device_id=(1 - sec, me), device_id_type=MESH)
+    pl.semaphore_wait(barrier, 1)
+
+
+def to_section(src, dst, send_sem, recv_sem, sec, me):
+    return pltpu.make_async_remote_copy(
+        src_ref=src, dst_ref=dst, send_sem=send_sem, recv_sem=recv_sem, device_id=(1 - sec, me), device_id_type=MESH
+    )
+
+
+def feed_kernel(shift, *refs):
+    tok_ref, inc_ref, att_ref, vec_ref, bias_ref, out_w, fc1_w, fc2_w = refs[:8]
+    res_ref, pre_ref, hidden_ref, n2_ref, att_rows_ref, low_ref = refs[8:14]
+    refs = refs[14:]
+    if shift:
+        next_ref, refs = refs[0], refs[1:]
+    out_buf, fc1_buf, fc2_buf, t_buf, sems = refs[:5]
+    sec, me = place()
+    pairs = [("out", out_w, out_buf, (0, D))]
+    pairs += [("fc1", fc1_w, fc1_buf, cols) for cols in slices(FFP)]
+    pairs += [("fc2", fc2_w, fc2_buf, cols) for cols in slices(FFP)]
+    stream = Stream(pairs, sems)
+    stream.start()
+    if shift:
+        greet_section(sec, me)
+    att = jnp.concatenate([att_ref[h].astype(F32) for h in range(HEADS)], axis=0).T.astype(BF)
+    for w in range(HEADS):
+        att_rows_ref[w % 4, w // 4] = att_ref[w]
+    stream.wait("out", 0)
+    residual = pick(sec, tok_ref, inc_ref) + dot(att, out_buf[...]) + row(vec_ref, OUT_BIAS)
+    res_ref[...] = residual
+    xhat, _ = normalised(residual)
+    n2 = (xhat * row(vec_ref, GAIN2) + row(vec_ref, BIAS2)).astype(BF)
+    total = None
+    for at, end in slices(FFP):
+        stream.wait("fc1", at)
+        pre = dot(n2, fc1_buf[:, at:end]) + bias_ref[:, at:end]
+        pre_ref[:, at:end] = pre
+        hidden = gelu_tanh(pre)
+        hidden_ref[:, at:end] = hidden.astype(BF)
+        t_buf[at:end, :] = hidden.T.astype(BF)
+    for at, end in slices(FFP):
+        stream.wait("fc2", at)
+    total = dot(fc2_buf[...], t_buf[...])
+    low_ref[...] = (residual + total.T + row(vec_ref, FC2_BIAS)).astype(BF)
+    if shift:
+        copy = to_section(low_ref, next_ref, refs[5], refs[6], sec, me)
+        copy.start()
+    put_owners(n2_ref, n2.astype(F32))
+    if shift:
+        copy.wait()
+
+
+def feed_forward(tok, inc, att, vec, bias, out_w, fc1_w, fc2_w, cid):
+    tokens = tok.shape[0]
+    shift = cid is not None
+    anywhere, vmem = pl.BlockSpec(memory_space=pl.ANY), pl.BlockSpec(memory_space=pltpu.VMEM)
+    dma = pltpu.SemaphoreType.DMA
+    params = dict(collective_id=cid, has_side_effects=True) if shift else {}
+    rows = jax.ShapeDtypeStruct((4, 4, HEAD_DIM, tokens), BF)
+    low = jax.ShapeDtypeStruct((tokens, D), BF)
+    return pl.pallas_call(
+        functools.partial(feed_kernel, shift),
+        out_shape=[
+            jax.ShapeDtypeStruct((tokens, D), F32),
+            jax.ShapeDtypeStruct((tokens, FFP), F32),
+            jax.ShapeDtypeStruct((tokens, FFP), BF),
+            rows,
+            rows,
+            low,
+        ]
+        + [low] * shift,
+        in_specs=[vmem] * 5 + [anywhere] * 3,
+        out_specs=[vmem] * (6 + shift),
+        scratch_shapes=[
+            pltpu.VMEM((D, D), BF),
+            pltpu.VMEM((D, FFP), BF),
+            pltpu.VMEM((D, FFP), BF),
+            pltpu.VMEM((FFP, tokens), BF),
+            dma((1 + 2 * len(slices(FFP)),)),
+        ]
+        + [dma, dma] * shift,
+        compiler_params=pltpu.CompilerParams(vmem_limit_bytes=60 << 20, **params),
+    )(tok, inc, att, vec, bias, out_w, fc1_w, fc2_w)
+
+
+def feed_back_kernel(cot_ref, inc_ref, vec_ref, *refs):
+    kept, refs = refs[:4], refs[4:]
+    out_w, fc1_w, fc2_w = refs[:3]
+    rg_ref, ag_ref, fc_ref, pg_ref, branch_ref, sum_ref, fsum_ref = refs[3:10]
+    pre_buf, res_buf, out_buf, fc1_buf, fc2_buf, t_buf, kept_sem, sems = refs[10:]
+    sec, _ = place()
+    pairs = []
+    pairs += [("fc2", fc2_w, fc2_buf, cols) for cols in slices(FFP)]
+    pairs += [("fc1", fc1_w, fc1_buf, cols) for cols in slices(FFP)]
+    pairs.append(("out", out_w, out_buf, (0, D)))
+    stream = Stream(pairs, sems)
+    fetch(kept, (pre_buf, res_buf), kept_sem, sec)
+    stream.start()
+    grad = jnp.where(sec == 0, inc_ref[...].astype(F32), cot_ref[...].astype(F32))
+    fc_grad = grad.astype(BF)
+    put_owners(fc_ref, grad)
+    fetched(kept, (pre_buf, res_buf), kept_sem)
+    total = None
+    for at, end in slices(FFP):
+        slope = gelu_slope(pre_buf[:, at:end])
+        stream.wait("fc2", at)
+        pre_wide = dot(fc_grad, fc2_buf[:, at:end]) * slope
+        pre_grad = pre_wide.astype(BF)
+        pg_ref[:, at:end] = pre_grad
+        fsum_ref[:, at:end] = jnp.sum(pre_grad.astype(F32), axis=0, keepdims=True)
+        t_buf[at:end, :] = pre_wide.T.astype(BF)
+    for at, end in slices(FFP):
+        stream.wait("fc1", at)
+    total = dot(fc1_buf[...], t_buf[...])
+    xhat, rstd = normalised(res_buf[...])
+    part, gain_sum, bias_sum = norm_backward(total.T, xhat, rstd, row(vec_ref, GAIN2))
+    residual_grad = grad + part
+    rg_ref[...] = residual_grad
+    branch = residual_grad.astype(BF)
+    branch_ref[...] = branch
+    stream.wait("out", 0)
+    att_grad = dot(out_buf[...], residual_grad.T.astype(BF))
+    for h in range(HEADS):
+        ag_ref[h] = att_grad[h * HEAD_DIM : (h + 1) * HEAD_DIM].astype(BF)
+    sum_ref[0:1, :] = jnp.sum(branch.astype(F32), axis=0, keepdims=True)
+    sum_ref[1:2, :] = gain_sum
+    sum_ref[2:3, :] = bias_sum
+    sum_ref[3:4, :] = jnp.sum(fc_grad.astype(F32), axis=0, keepdims=True)
+
+
+def feed_backward(cot, inc, vec, kept, out_w, fc1_w, fc2_w):
+    tokens = cot.shape[0]
+    anywhere, vmem = pl.BlockSpec(memory_space=pl.ANY), pl.BlockSpec(memory_space=pltpu.VMEM)
+    dma = pltpu.SemaphoreType.DMA
+    return pl.pallas_call(
+        feed_back_kernel,
+        out_shape=[
+            jax.ShapeDtypeStruct((tokens, D), F32),
+            jax.ShapeDtypeStruct((HEADS, HEAD_DIM, tokens), BF),
+            jax.ShapeDtypeStruct((4, 4, HEAD_DIM, tokens), BF),
+            jax.ShapeDtypeStruct((tokens, FFP), BF),
+            jax.ShapeDtypeStruct((tokens, D), BF),
+            jax.ShapeDtypeStruct((4, D), F32),
+            jax.ShapeDtypeStruct((1, FFP), F32),
+        ],
+        in_specs=[vmem] * 3 + [anywhere] * 7,
+        out_specs=[vmem] * 7,
+        scratch_shapes=[
+            pltpu.VMEM((tokens, FFP), F32),
+            pltpu.VMEM((tokens, D), F32),
+            pltpu.VMEM((D, D), BF),
+            pltpu.VMEM((D, FFP), BF),
+            pltpu.VMEM((D, FFP), BF),
+            pltpu.VMEM((FFP, tokens), BF),
+            dma((2,)),
+            dma((1 + 2 * len(slices(FFP)),)),
+        ],
+        compiler_params=pltpu.CompilerParams(vmem_limit_bytes=60 << 20),
+    )(cot, inc, vec, *kept, out_w, fc1_w, fc2_w)
+
+
+def qkv_back_kernel(shift, *refs):
+    tok_ref, inc_ref, vec_ref, rg_ref, dq_ref, dkv_ref, w_ref = refs[:7]
+    grad_ref, dqkv_ref, sum_ref, qsum_ref = refs[7:11]
+    refs = refs[11:]
+    if shift:
+        next_ref, refs = refs[0], refs[1:]
+    w_buf, sems = refs[:2]
+    sec, me = place()
+    stream = Stream([("w", w_ref, w_buf, cols) for cols in slices(3 * D, 384)], sems)
+    stream.start()
+    if shift:
+        greet_section(sec, me)
+    rows = []
+    for h in range(HEADS):
+        rows += [dq_ref[h].astype(F32), dkv_ref[h].astype(F32)]
+    dqkv = jnp.concatenate(rows, axis=0).astype(BF)
+    dqkv_ref[...] = dqkv
+    qsum_ref[...] = nt(jnp.ones((8, dqkv.shape[1]), BF), dqkv)
+    total = None
+    for at, end in slices(3 * D, 384):
+        stream.wait("w", at)
+        part = dot(w_buf[:, at:end], dqkv[at:end])
+        total = part if total is None else total + part
+    xhat, rstd = normalised(pick(sec, tok_ref, inc_ref))
+    part, gain_sum, bias_sum = norm_backward(total.T, xhat, rstd, row(vec_ref, GAIN1))
+    grad = rg_ref[...] + part
+    grad_ref[...] = grad
+    if shift:
+        low_buf = refs[2]
+        low_buf[...] = grad.astype(BF)
+        copy = to_section(low_buf, next_ref, refs[3], refs[4], sec, me)
+        copy.start()
+    sum_ref[0:1, :] = gain_sum
+    sum_ref[1:2, :] = bias_sum
+    if shift:
+        copy.wait()
+
+
+def qkv_backward(tok, inc, vec, residual_grad, dq, dkv, w, cid):
+    tokens = tok.shape[0]
+    shift = cid is not None
+    anywhere, vmem = pl.BlockSpec(memory_space=pl.ANY), pl.BlockSpec(memory_space=pltpu.VMEM)
+    dma = pltpu.SemaphoreType.DMA
+    params = dict(collective_id=cid, has_side_effects=True) if shift else {}
+    return pl.pallas_call(
+        functools.partial(qkv_back_kernel, shift),
+        out_shape=[
+            jax.ShapeDtypeStruct((tokens, D), F32),
+            jax.ShapeDtypeStruct((3 * D, tokens), BF),
+            jax.ShapeDtypeStruct((2, D), F32),
+            jax.ShapeDtypeStruct((8, 3 * D), F32),
+        ]
+        + [jax.ShapeDtypeStruct((tokens, D), BF)] * shift,
+        in_specs=[vmem] * 6 + [anywhere],
+        out_specs=[vmem] * (4 + shift),
+        scratch_shapes=[pltpu.VMEM((D, 3 * D), BF), dma((len(slices(3 * D, 384)),))]
+        + [pltpu.VMEM((tokens, D), BF), dma, dma] * shift,
+        compiler_params=pltpu.CompilerParams(vmem_limit_bytes=60 << 20, **params),
+    )(tok, inc, vec, residual_grad, dq, dkv, w)
 
 
 def pad_ff(x):
     return jnp.pad(x, ((0, 0),) * (x.ndim - 1) + ((0, FFP - FF),))
-
-
-def owners(x):
-    return x.reshape(4, 4, HEAD_DIM, BLOCK).swapaxes(0, 1)
 
 
 TENSORS = ("fc2", "fc1", "out", "qkv")
@@ -814,113 +1161,81 @@
     w_qkv = w_qkv.reshape(D, 3 * D)
     w_out = w_out.reshape(D, D)
     vectors = small_all[:, :8, :HEAD_DIM].astype(F32)
-    gain1, bias1, _, _, b_out, gain2, bias2, b_fc2 = [vectors[:, i].reshape(D) for i in range(8)]
-    b_qkv = jnp.stack([vectors[:, 2], jnp.zeros_like(vectors[:, 2]), vectors[:, 3]], axis=1).reshape(3 * D, 1)
-    b_fc1 = pad_ff(fc1_bias[0]).astype(F32)
+    vec = jnp.stack([vectors[:, i].reshape(D) for i in (0, 1, 4, 5, 6, 7)])
+    b_qkv = jnp.stack([vectors[:, 2], jnp.zeros_like(vectors[:, 2]), vectors[:, 3]], axis=1).reshape(1, 3 * D)
+    b_fc1 = pad_ff(fc1_bias[0]).astype(F32).reshape(1, FFP)
+    near = window(image_of_block)
 
     def choose(at_zero, at_one):
-        return jax.tree.map(lambda a, b: jnp.where(sec == 0, a, b), at_zero, at_one)
-
-    saved = []
-    incoming = jnp.zeros_like(tokens[0])
-    sent = {}
-    for tick in range(3):
-        slot = jnp.clip(tick - sec, 0, 1)
-        image_row = lax.dynamic_index_in_dim(image_of_block, slot, 0, keepdims=False)
-        near = window(image_row)
-        x = jnp.where(sec == 0, tokens[min(tick, 1)], incoming).astype(F32)
-        xhat1, _ = normalised(x)
-        n1 = (xhat1 * gain1 + bias1).astype(BF)
-        qkv = jnp.einsum("ck,tc->kt", w_qkv, n1, preferred_element_type=F32) + b_qkv
-        qkv = qkv.astype(BF).reshape(HEADS, 3 * HEAD_DIM, BLOCK)
-        if tick == 0:
-            qkv, lse, att, _, whole = attend(qkv, near, 2, shards=ff_shards)
-            w_fc1, w_fc2t = [w.reshape(D, FFP) for w in whole]
-        elif tick == 1:
-            qkv, lse, att, _, _ = attend(qkv, near, 3)
-        else:
-            old = saved
-            items = [Rows(old[0][name], old[1][name]) for name in ("n1", "att_rows", "n2")]
-            items.append(Whole(old[0]["hidden"], old[1]["hidden"], (0, SPLIT)))
-            qkv, lse, att, got, _ = attend(qkv, near, 4, items)
-            sent["n1_0"], sent["att_0"], sent["n2_0"], sent["h0a"] = got
-        residual = x + jnp.einsum("ct,cd->td", att.reshape(D, BLOCK), w_out, preferred_element_type=F32) + b_out
-        xhat2, _ = normalised(residual)
-        n2 = (xhat2 * gain2 + bias2).astype(BF)
-        hidden_pre = jnp.einsum("td,df->tf", n2, w_fc1, preferred_element_type=F32) + b_fc1
-        value, _ = gelu_and_slope(hidden_pre)
-        hidden = value.astype(BF)
-        out = residual + jnp.einsum("tf,df->td", hidden, w_fc2t, preferred_element_type=F32) + b_fc2
-        out_low = out.astype(BF)
+        return jnp.where(sec == 0, at_zero, at_one)
+
+    saved, sent, back, done, input_grads = [], {}, [], [], []
+    incoming = [tokens[0]]
+
+    def token_inputs(tick):
+        return tokens[min(tick, 1)], incoming[tick]
+
+    def feed(tick, qkv, lse, att, n1, cid):
+        fed = feed_forward(*token_inputs(tick), att, vec, b_fc1, w_out, w_fc1, w_fc2t, cid)
         saved.append(
-            dict(
-                x=x, qkv=qkv, lse=lse, residual=residual, hidden_pre=hidden_pre, hidden=hidden, low=out_low,
-                att_rows=owners(att), n1=owners(by_rows(n1)), n2=owners(by_rows(n2)), near=near,
-            )
+            dict(qkv=qkv, lse=lse, n1=n1, residual=fed[0], pre=fed[1], hidden=fed[2], n2=fed[3], att=fed[4], low=fed[5])
         )
-        if tick < 2:
-            incoming = lax.ppermute(out_low, "section", [(0, 1)])
+        return fed
+
+    def kept(tick, *names):
+        return [saved[at][name] for name in names for at in ((1, 1), (0, 2), (1, 1))[tick]]
+
+    def feed_back(tick, incoming_grad):
+        residual_grad, att_grad, fc, pre, branch, four, fsum = feed_backward(
+            cotangent[min(tick, 1)], incoming_grad, vec, kept(tick, "pre", "residual"), w_out, w_fc1, w_fc2t
+        )
+        back.append(dict(fc=fc, pre=pre, branch=branch))
+        return residual_grad, att_grad, [*four, fsum]
+
+    def qkv_back(tick, residual_grad, dq, dkv, sums, cid):
+        inputs = (tokens[max(tick - 1, 0)], incoming[min(tick + 1, 2)])
+        input_grad, dqkv, two, qsum, *rest = qkv_backward(*inputs, vec, residual_grad, dq, dkv, w_qkv, cid)
+        back[tick]["dqkv"] = dqkv
+        input_grads.append(input_grad)
+        qsum = qsum[0].reshape(HEADS, 3, HEAD_DIM)
+        done.append([two[0], two[1], qsum[:, 0].reshape(D), qsum[:, 2].reshape(D), *sums])
+        return rest[0] if rest else input_grad.astype(BF)
+
+    qkv, n1 = qkv_forward(*token_inputs(0), vec, b_qkv, w_qkv)
+    three, _, _, whole = attention(near, 2, ahead=(0, qkv), shards=ff_shards)
+    w_fc1, w_fc2t = [w.reshape(D, FFP) for w in whole]
+    incoming.append(feed(0, *three, n1, 8)[6])
+
+    qkv, n1 = qkv_forward(*token_inputs(1), vec, b_qkv, w_qkv)
+    three, _, _, _ = attention(near, 3, ahead=(1, qkv))
+    incoming.append(lax.ppermute(feed(1, *three, n1, None)[5], "section", [(0, 1)]))
+
+    residual_grad, att_grad, sums = feed_back(0, tokens[0])
+    qkv, n1 = qkv_forward(*token_inputs(2), vec, b_qkv, w_qkv)
+    items = [Rows(saved[0][name], saved[1][name]) for name in ("n1", "att", "n2")]
+    items.append(Whole(saved[0]["hidden"], saved[1]["hidden"]))
+    three, two, got, _ = attention(
+        near, 4, ahead=(2, qkv), behind=(0, att_grad, kept(0, "qkv", "lse")), items=items
+    )
+    sent["n1_0"], sent["att_0"], sent["n2_0"], sent["h0"] = got
+    low = qkv_back(0, residual_grad, *two, sums, None)
+    incoming_grad = lax.ppermute(low, "section", [(1, 0)])
+    feed(2, *three, n1, None)
     outputs = jnp.stack([choose(saved[m]["low"], saved[m + 1]["low"]) for m in range(2)])
 
-    incoming_grad = jnp.zeros(tokens.shape[1:], BF)
-    input_grads, done, back = [], [], []
-    needed = ("x", "qkv", "lse", "residual", "hidden_pre", "near")
-    for tick in range(3):
-        if tick == 1:
-            k = choose({name: saved[0][name] for name in needed}, {name: saved[2][name] for name in needed})
-        else:
-            k = saved[1]
-        grad = jnp.where(sec == 1, cotangent[min(tick, 1)], incoming_grad).astype(F32)
-        fc_grad = grad.astype(BF)
-        hidden_grad = jnp.einsum("td,df->tf", fc_grad, w_fc2t, preferred_element_type=F32)
-        _, slope = gelu_and_slope(k["hidden_pre"])
-        pre_grad = (hidden_grad * slope).astype(BF)
-        n2_grad = jnp.einsum("tf,df->td", pre_grad, w_fc1, preferred_element_type=F32)
-        xhat2, rstd2 = normalised(k["residual"])
-        part, g_gain2, g_bias2 = norm_backward(n2_grad, xhat2, rstd2, gain2)
-        residual_grad = grad + part
-        branch = residual_grad.astype(BF)
-        att_grad = jnp.einsum("td,cd->ct", branch, w_out, preferred_element_type=F32).astype(BF)
-        att_grad = att_grad.reshape(HEADS, HEAD_DIM, BLOCK)
-        back.append(dict(fc=owners(by_rows(fc_grad)), pre=pre_grad, branch=branch))
-        if tick == 0:
-            items = [
-                Whole(saved[0]["hidden"], saved[1]["hidden"], (SPLIT, FFP)),
-                Whole(saved[1]["hidden"], saved[2]["hidden"], (0, SPLIT)),
-            ]
-            names = ["h0b", "h1a"]
-        elif tick == 1:
-            items = [Rows(saved[1][name], saved[2][name]) for name in ("n1", "att_rows", "n2")]
-            items.append(Whole(saved[1]["hidden"], saved[2]["hidden"], (SPLIT, FFP)))
-            names = ["n1_1", "att_1", "n2_1", "h1b"]
-        else:
-            items = [Rows(back[1]["fc"], back[0]["fc"]), Rows(back[2]["fc"], back[1]["fc"])]
-            items.append(Whole(back[1]["pre"], back[0]["pre"], (0, SPLIT)))
-            names = ["fc_0", "fc_1", "pre_0a"]
-        dqkv, got = attend_back(att_grad, k["near"], k["qkv"], k["lse"], 5 + tick, items)
-        sent.update(zip(names, got))
-        back[-1]["dqkv"] = dqkv.reshape(3 * D, BLOCK)
-        n1_grad = jnp.einsum("kt,ck->tc", back[-1]["dqkv"], w_qkv, preferred_element_type=F32)
-        xhat1, rstd1 = normalised(k["x"])
-        part, g_gain1, g_bias1 = norm_backward(n1_grad, xhat1, rstd1, gain1)
-        input_grad = residual_grad + part
-        input_grads.append(input_grad)
-        sums = jnp.sum(dqkv.astype(F32), axis=2)
-        done.append(
-            [
-                g_gain1,
-                g_bias1,
-                sums[:, :HEAD_DIM].reshape(D),
-                sums[:, 2 * HEAD_DIM :].reshape(D),
-                jnp.sum(branch.astype(F32), axis=0),
-                g_gain2,
-                g_bias2,
-                jnp.sum(fc_grad.astype(F32), axis=0),
-                jnp.sum(pre_grad.astype(F32), axis=0),
-            ]
-        )
-        if tick < 2:
-            incoming_grad = lax.ppermute(input_grad.astype(BF), "section", [(1, 0)])
+    residual_grad, att_grad, sums = feed_back(1, incoming_grad)
+    items = [Rows(saved[1][name], saved[2][name]) for name in ("n1", "att", "n2")]
+    items.append(Whole(saved[1]["hidden"], saved[2]["hidden"], (0, SPLIT)))
+    _, two, got, _ = attention(near, 5, behind=(1, att_grad, kept(1, "qkv", "lse")), items=items)
+    sent["n1_1"], sent["att_1"], sent["n2_1"], sent["h1a"] = got
+    incoming_grad = qkv_back(1, residual_grad, *two, sums, 9)
+
+    residual_grad, att_grad, sums = feed_back(2, incoming_grad)
+    items = [Rows(back[1]["fc"], back[0]["fc"]), Rows(back[2]["fc"], back[1]["fc"])]
+    items.append(Whole(saved[1]["hidden"], saved[2]["hidden"], (SPLIT, FFP)))
+    _, two, got, _ = attention(near, 6, behind=(2, att_grad, kept(2, "qkv", "lse")), items=items)
+    sent["fc_0"], sent["fc_1"], sent["h1b"] = got
+    qkv_back(2, residual_grad, *two, sums, None)
     input_grads = jnp.stack([choose(input_grads[m + 1], input_grads[m]) for m in range(2)])
 
     sums = [choose(done[1][i] + done[2][i], done[0][i] + done[1][i]) for i in range(9)]
@@ -936,21 +1251,19 @@
         "qkv": [sent["n1_0"], sent["n1_1"]],
     }
     early = [
-        ("fc2", 0, (0, SPLIT), sent["h0a"]),
-        ("fc2", 0, (SPLIT, FFP), sent["h0b"]),
+        ("fc2", 0, None, sent["h0"]),
         ("fc2", 1, (0, SPLIT), sent["h1a"]),
         ("fc2", 1, (SPLIT, FFP), sent["h1b"]),
-        ("fc1", 0, (0, SPLIT), sent["pre_0a"]),
     ]
     late = [
-        ("fc1", 0, Whole(back[1]["pre"], back[0]["pre"], (SPLIT, FFP))),
+        ("fc1", 0, Whole(back[1]["pre"], back[0]["pre"])),
         ("fc1", 1, Whole(back[2]["pre"], back[1]["pre"])),
         ("out", 0, Whole(back[1]["branch"], back[0]["branch"])),
         ("out", 1, Whole(back[2]["branch"], back[1]["branch"])),
         ("qkv", 0, Whole(back[1]["dqkv"], back[0]["dqkv"])),
         ("qkv", 1, Whole(back[2]["dqkv"], back[1]["dqkv"])),
     ]
-    packed, grads = final(jnp.concatenate([by_owner, to_all], axis=1), xs, early, late, 12)
+    packed, grads = final(jnp.concatenate([by_owner, to_all], axis=1), xs, early, late, 10)
     g_small = packed[:8, :HEAD_DIM]
     g_fc1_bias = packed[8 : 8 + lines].reshape(FFP)[:FF]
     g_qkv = grads["qkv"].reshape(HEAD_DIM, HEADS, 3, HEAD_DIM).transpose(0, 2, 1, 3).reshape(HEAD_DIM, 3 * D)

time: 849 us -> 793 us (0.934)
  Pallas kernels: 598 us -> 741 us
  matrix products: 111 us -> 0 us
  local copies, waits for them, and re-layouts: 66.5 us -> 29.6 us
  other arithmetic: 35.3 us -> 8.63 us
  starting transfers between devices: 14.9 us -> 5 us
  waiting for transfers between devices: 9.55 us -> 0.01 us
    pallas_call x6 -> x17, Pallas kernels: 378 us -> 510 us  [the longest x5 349 us: attention(): pl.pallas_call(functools.partial(attention_kernel, ahead and ahead[0], be...]
    dot_general x24 -> x0, matrix products: 111 us -> none  [the longest x3 24.1 us: on_device(): jnp.einsum('td,df->tf', fc_grad, w_fc2t, preferred_element_type=F32)]
    reduce_sum x19 -> x1, other arithmetic: 17.9 us -> 0.96 us  [window(): end = jnp.sum((other <= own).astype(jnp.int32), axis=2)]
    transpose x9 -> x0, local copies, waits for them, and re-layouts: 12.8 us -> none  [by_rows(): return x.T.reshape(HEADS, HEAD_DIM, x.shape[0])]
    unnamed x310 -> x65, local copies, waits for them, and re-layouts: 14.8 us -> 3.06 us
    pallas_call x1, Pallas kernels: 153 us -> 165 us  [final(): pl.pallas_call(functools.partial(final_kernel, tiles, [e[:3] for e in ear...]
    ppermute x4 -> x2, starting transfers between devices: 14.9 us -> 5 us  [the longest x1 3.71 us: on_device(): incoming_grad = lax.ppermute(low, 'section', [(1, 0)])]
    ppermute x4 -> x2, waiting for transfers between devices: 9.55 us -> 0.01 us  [the longest x1 0.01 us: on_device(): lax.ppermute(feed(1, *three, n1, None)[5], 'section', [(0, 1)])]
  transfers between devices with their start and end apart: 4 -> 2, of which waited for: 3 -> 0; matrix products, arithmetic and copies ran while one was open for 4% -> 0% of each run, Pallas kernels for 0% -> 4%
where the time goes in v4:
time: 793 us; the launch traced here: 785 us
  Pallas kernels  741 us (93%)
  local copies, waits for them, and re-layouts  29.6 us (4%)
  other arithmetic  8.63 us (1%)
    pallas_call x5, Pallas kernels, attention(): pl.pallas_call(functools.partial(attention_kernel, ahead and ahead[0], be...  349 us
    pallas_call x1, Pallas kernels, final(): pl.pallas_call(functools.partial(final_kernel, tiles, [e[:3] for e in ear...  165 us
    pallas_call x1, Pallas kernels, gather(): pl.pallas_call(functools.partial(gather_kernel, count), out_shape=[jax.Sh...  66.2 us
    pallas_call x3, Pallas kernels, feed_backward(): pl.pallas_call(feed_back_kernel, out_shape=[jax.ShapeDtypeStruct((tokens,...  59.5 us
    pallas_call x3, Pallas kernels, feed_forward(): pl.pallas_call(functools.partial(feed_kernel, shift), out_shape=[jax.Shap...  47.4 us
    pallas_call x3, Pallas kernels, qkv_backward(): pl.pallas_call(functools.partial(qkv_back_kernel, shift), out_shape=[jax....  33.1 us
    pallas_call x3, Pallas kernels, qkv_forward(): pl.pallas_call(qkv_kernel, out_shape=[jax.ShapeDtypeStruct((HEADS, 3 * HE...  21 us
  transfers between devices with their start and end apart: 2, of which 0 were waited for; matrix products, arithmetic and copies ran while one was open for 0% of the time, Pallas kernels for 4%

profile of v4, /device:TPU:10, one launch (start us, length us, event | category | flops | bytes accessed | tf_op | source)
XLA Modules:
  0.0 785.4 jit_solution(945295640707207806)
XLA Ops:
  0.7 2.0 slice_bitcast_fusion.5
  2.6 1.0 convert_reduce_fusion
  3.6 1.6 reshape_squeeze.8
  5.3 0.8 copy.53
  6.1 1.1 copy.54.refs_0_
  7.9 66.2 %shard_map.254 = (bf16[16,72,3456]{2,1,0:T(8,128)(2,1)}, bf16[16,72,1152]{2,1,0:T(8,128)(2,1)}, bf16[16,16,128]{2,1,0:T(8,128)(2,1)}) custom-call(bf16[72,3456]{1,0:T(8,128)(2,1)} %copy.54.refs_0_, bf16[72,1152]{1,0:T(8,128)(2,1)} %bitcast.96, bf16[16,128]{1,0:T(8,128)(2,1)} %pad.23.refs_2_), custom_call_target="tpu_custom_call" | custom-call | tf_op jit(solution)/shard_map/pallas_call | solution.py:138
  74.1 0.8 slice_convert_fusion
  76.5 0.9 pad.24.refs_3_
  77.3 0.9 pad.25.refs_4_
  78.9 0.8 fusion.3.refs_1_
  80.4 7.0 shard_map.255
  87.4 131.6 %shard_map.256 = (bf16[16,216,128]{2,1,0:T(8,128)(2,1)}, f32[16,1,128]{2,1,0:T(1,128)}, bf16[16,72,128]{2,1,0:T(8,128)(2,1)}, bf16[16,72,4352]{2,1,0:T(8,128)(2,1)}, bf16[16,72,4352]{2,1,0:T(8,128)(2,1)}) custom-call(s32[2,16]{1,0:T(2,128)} %copy-done.15, f32[2,16,6,128]{3,2,1,0:T(8,128)} %fusion.3.refs_1_, ...), custom_call_target="tpu_custom_call" | custom-call | tf_op jit(solution)/shard_map/pallas_call | solution.py:592
  219.0 22.1 %shard_map.257 = (f32[128,1152]{1,0:T(8,128)}, f32[128,4352]{1,0:T(8,128)}, bf16[128,4352]{1,0:T(8,128)(2,1)}, bf16[4,4,72,128]{3,2,1,0:T(8,128)(2,1)}, bf16[4,4...) custom-call(bf16[128,1152]{1,0:T(8,128)(2,1)} %get-tuple-element.222.tok_ref.inc_ref.refs_0_.refs_1_, ...), custom_call_target="tpu_custom_call" | custom-call | tf_op jit(solution)/shard_map/pallas_call | solution.py:771
  241.1 7.0 shard_map.258
  248.1 38.8 %shard_map.259 = (bf16[16,216,128]{2,1,0:T(8,128)(2,1)}, f32[16,1,128]{2,1,0:T(1,128)}, bf16[16,72,128]{2,1,0:T(8,128)(2,1)}) custom-call(s32[2,16]{1,0:T(2,128)} %copy-done.15, f32[2,16,6,128]{3,2,1,0:T(8,128)} %fusion.3.refs_1_, bf16[16,216,128]{2,1,0:T(8,128)(2,1)} %get-tuple-element.118.refs_2_), custom_call_target="tpu_custom_call" | custom-call | tf_op jit(solution)/shard_map/pallas_call | solution.py:592
  286.9 12.7 %shard_map.260 = (f32[128,1152]{1,0:T(8,128)}, f32[128,4352]{1,0:T(8,128)}, bf16[128,4352]{1,0:T(8,128)(2,1)}, bf16[4,4,72,128]{3,2,1,0:T(8,128)(2,1)}, bf16[4,4...) custom-call(bf16[128,1152]{1,0:T(8,128)(2,1)} %get-tuple-element.223.tok_ref.refs_0_, ...), custom_call_target="tpu_custom_call" | custom-call | tf_op jit(solution)/shard_map/pallas_call | solution.py:771
  299.6 1.3 collective-permute-start
  300.9 0.9 slice_bitcast_fusion.2
  301.7 19.7 %shard_map.262 = (f32[128,1152]{1,0:T(8,128)}, bf16[16,72,128]{2,1,0:T(8,128)(2,1)}, bf16[4,4,72,128]{3,2,1,0:T(8,128)(2,1)}, bf16[128,4352]{1,0:T(8,128)(2,1)},...) custom-call(bf16[128,1152]{1,0:T(8,128)(2,1)} %get-tuple-element.221.cot_ref, ...), custom_call_target="tpu_custom_call" | custom-call | tf_op jit(solution)/shard_map/pallas_call | solution.py:845
  322.2 7.0 shard_map.261
  329.2 87.5 %shard_map.263 = (bf16[16,216,128]{2,1,0:T(8,128)(2,1)}, f32[16,1,128]{2,1,0:T(1,128)}, bf16[16,72,128]{2,1,0:T(8,128)(2,1)}, bf16[16,72,128]{2,1,0:T(8,128)(2,1...) custom-call(s32[2,16]{1,0:T(2,128)} %copy-done.15, ...), custom_call_target="tpu_custom_call" | custom-call | tf_op jit(solution)/shard_map/pallas_call | solution.py:592
  416.7 8.1 %shard_map.265 = (f32[128,1152]{1,0:T(8,128)}, bf16[3456,128]{1,0:T(8,128)(2,1)}, f32[2,1152]{1,0:T(2,128)}, f32[8,3456]{1,0:T(8,128)}) custom-call(bf16[128,1152]{1,0:T(8,128)(2,1)} %get-tuple-element.222.tok_ref.inc_ref.refs_0_.refs_1_, bf16[128,1152]{1,0:T(8,128)(2,1)} %get-tuple-element.117.inc_ref.refs_1_, f32[6,1152]{1,0:T(8,128)} %stack.51.vec_ref.refs_3_.refs_2_, ...), custom_call_target="tpu_custom_call" | custom-call | tf_op jit(solution)/shard_map/pallas_call | solution.py:916
  424.8 1.1 convert_element_type.27
  425.9 3.7 collective-permute-start.1
  429.7 0.9 slice_reduce_fusion
  430.7 12.7 %shard_map.264 = (f32[128,1152]{1,0:T(8,128)}, f32[128,4352]{1,0:T(8,128)}, bf16[128,4352]{1,0:T(8,128)(2,1)}, bf16[4,4,72,128]{3,2,1,0:T(8,128)(2,1)}, bf16[4,4...) custom-call(bf16[128,1152]{1,0:T(8,128)(2,1)} %get-tuple-element.223.tok_ref.refs_0_, bf16[128,1152]{1,0:T(8,128)(2,1)} %copy-done, ...), custom_call_target="tpu_custom_call" | custom-call | tf_op jit(solution)/shard_map/pallas_call | solution.py:771
  443.4 1.0 select_bitcast_fusion.3
  444.5 0.9 maximum_bitcast_fusion.1
  446.1 20.1 %shard_map.266 = (f32[128,1152]{1,0:T(8,128)}, bf16[16,72,128]{2,1,0:T(8,128)(2,1)}, bf16[4,4,72,128]{3,2,1,0:T(8,128)(2,1)}, bf16[128,4352]{1,0:T(8,128)(2,1)},...) custom-call(bf16[128,1152]{1,0:T(8,128)(2,1)} %get-tuple-element.220.cot_ref, ...), custom_call_target="tpu_custom_call" | custom-call | tf_op jit(solution)/shard_map/pallas_call | solution.py:845
  466.2 47.2 %shard_map.267 = (bf16[16,72,128]{2,1,0:T(8,128)(2,1)}, bf16[16,144,128]{2,1,0:T(8,128)(2,1)}, bf16[4,4,72,128]{3,2,1,0:T(8,128)(2,1)}, bf16[4,4,72,128]{3,2,1,0...) custom-call(s32[2,16]{1,0:T(2,128)} %copy-done.15, f32[2,16,6,128]{3,2,1,0:T(8,128)} %fusion.3.refs_1_, ...), custom_call_target="tpu_custom_call" | custom-call | tf_op jit(solution)/shard_map/pallas_call | solution.py:592
  513.4 16.8 %shard_map.268 = (f32[128,1152]{1,0:T(8,128)}, bf16[3456,128]{1,0:T(8,128)(2,1)}, f32[2,1152]{1,0:T(2,128)}, f32[8,3456]{1,0:T(8,128)}, bf16[128,1152]{1,0:T(8,128)(2,1)}) custom-call(bf16[128,1152]{1,0:T(8,128)(2,1)} %get-tuple-element.222.tok_ref.inc_ref.refs_0_.refs_1_, bf16[128,1152]{1,0:T(8,128)(2,1)} %copy-done, ...), custom_call_target="tpu_custom_call" | custom-call | tf_op jit(solution)/shard_map/pallas_call | solution.py:916
  530.2 19.7 %shard_map.269 = (f32[128,1152]{1,0:T(8,128)}, bf16[16,72,128]{2,1,0:T(8,128)(2,1)}, bf16[4,4,72,128]{3,2,1,0:T(8,128)(2,1)}, bf16[128,4352]{1,0:T(8,128)(2,1)},...) custom-call(bf16[128,1152]{1,0:T(8,128)(2,1)} %get-tuple-element.220.cot_ref, ...), custom_call_target="tpu_custom_call" | custom-call | tf_op jit(solution)/shard_map/pallas_call | solution.py:845
  549.9 43.7 %shard_map.270 = (bf16[16,72,128]{2,1,0:T(8,128)(2,1)}, bf16[16,144,128]{2,1,0:T(8,128)(2,1)}, bf16[4,4,72,128]{3,2,1,0:T(8,128)(2,1)}, bf16[4,4,72,128]{3,2,1,0:T(8,128)(2,1)}, bf16[4,128,2048]{2,1,0:T(8,128)(2,1)}) custom-call(s32[2,16]{1,0:T(2,128)} %copy-done.15, f32[2,16,6,128]{3,2,1,0:T(8,128)} %fusion.3.refs_1_, ...), custom_call_target="tpu_custom_call" | custom-call | tf_op jit(solution)/shard_map/pallas_call | solution.py:592
  593.6 8.2 %shard_map.271 = (f32[128,1152]{1,0:T(8,128)}, bf16[3456,128]{1,0:T(8,128)(2,1)}, f32[2,1152]{1,0:T(2,128)}, f32[8,3456]{1,0:T(8,128)}) custom-call(bf16[128,1152]{1,0:T(8,128)(2,1)} %get-tuple-element.223.tok_ref.refs_0_, bf16[128,1152]{1,0:T(8,128)(2,1)} %copy-done, f32[6,1152]{1,0:T(8,128)} %stack.51.vec_ref.refs_3_.refs_2_, ...), custom_call_target="tpu_custom_call" | custom-call | tf_op jit(solution)/shard_map/pallas_call | solution.py:916
  601.9 0.9 fusion.6
  603.0 0.9 slice_reduce_fusion.2
  604.0 0.9 slice_reduce_fusion.1
  605.7 0.8 select_maximum_fusion.refs_0_
  606.5 164.6 %shard_map.272 = (f32[48,128]{1,0:T(8,128)}, f32[72,4352]{1,0:T(8,128)}, f32[72,4352]{1,0:T(8,128)}, f32[72,1152]{1,0:T(8,128)}, f32[72,3456]{1,0:T(8,128)}) custom-call(f32[16,48,128]{2,1,0:T(8,128)} %select_maximum_fusion.refs_0_, bf16[4,4,72,128]{3,2,1,0:T(8,128)(2,1)} %get-tuple-element.179.refs_1_, bf16[4,4,72,128]{3,2,1,0:T(8,128)(2,1)} %get-tuple-element.180.refs_2_, ...), custom_call_target="tpu_custom_call" | custom-call | tf_op jit(solution)/shard_map/pallas_call | solution.py:1122
  771.1 1.4 fusion.14
  772.5 1.2 slice_bitcast_fusion.7
  773.8 1.3 slice_bitcast_fusion.6
  775.1 1.7 copy.62
  776.9 0.9 copy.63
  777.7 1.9 broadcast_in_dim_reshape.3
  779.6 1.1 slice_bitcast_fusion.1
  781.4 1.1 slice_bitcast_fusion
  783.4 1.1 maximum_bitcast_fusion
  (103 shorter events, 8.4 us)
Async XLA Ops:
  0.6 3.0 copy-start.9
  3.6 75.3 %copy-start.15 = (s32[2,16]{1,0:T(2,128)}, s32[2,16]{1,0:T(2,128)S(1)}, u32[]{:S(2)}) copy-start(s32[2,16]{1,0:T(2,128)S(1)} %broadcast_minimum_fusion.refs_0_) | copy-start | bytes 388
  5.2 2.0 copy-start.25
  5.2 2.0 copy-start.26
  5.2 2.0 copy-start.27
  5.2 2.0 copy-start.28
  5.2 2.0 copy-start.29
  5.3 2.0 copy-start.30
  5.3 2.0 copy-start.31
  6.1 70.4 %copy-start.4 = (bf16[1,72,4304]{2,1,0:T(8,128)(2,1)S(1)}, bf16[1,72,4304]{2,1,0:T(8,128)(2,1)}, u32[]{:S(2)}) copy-start(bf16[1,72,4304]{2,1,0:T(8,128)(2,1)} %param.26) | copy-start | bytes 1859332
  7.2 70.1 %copy-start.5 = (bf16[1,4304,72]{1,2,0:T(8,128)(2,1)S(1)}, bf16[1,4304,72]{1,2,0:T(8,128)(2,1)}, u32[]{:S(2)}) copy-start(bf16[1,4304,72]{1,2,0:T(8,128)(2,1)} %param.28) | copy-start | bytes 1859332
  76.5 1.8 copy-start.19
  286.9 14.0 %copy-start.6 = (bf16[2,128,1152]{2,1,0:T(8,128)(2,1)S(1)}, bf16[2,128,1152]{2,1,0:T(8,128)(2,1)}, u32[]{:S(2)}) copy-start(bf16[2,128,1152]{2,1,0:T(8,128)(2,1)} %param.16) | copy-start | bytes 1769476
  299.6 21.9 %collective-permute-start = (bf16[128,1152]{1,0:T(8,128)(2,1)}, bf16[128,1152]{1,0:T(8,128)(2,1)S(1)}, u32[]{:S(2)}, u32[]{:S(2)}) collective-permute-start(bf16[128,1152]{1,0:T(8,128)(2,1)} %get-tuple-element.120), channel_id=1, source_target_pairs={{0,16},{1,17},{2,18},{3,19},{4,20},{5,21},{6,22},{7,23},{8,24},{9,... | collective-permute-start | bytes 884744 | tf_op jit(solution)/shard_map/ppermute | solution.py:1211
  321.5 0.7 copy-start
  425.9 19.4 %collective-permute-start.1 = (bf16[128,1152]{1,0:T(8,128)(2,1)S(1)}, bf16[128,1152]{1,0:T(8,128)(2,1)S(1)}, u32[]{:S(2)}, u32[]{:S(2)}) collective-permute-start(bf16[128,1152]{1,0:T(8,128)(2,1)S(1)} %convert_element_type.27), channel_id=1, source_target_pairs={{16,0},{17,1},{18,2},{19,3},{20,4},{21,5},{22,6},{23,7},{24,8},{25... | collective-permute-start | bytes 884744 | tf_op jit(solution)/shard_map/ppermute | solution.py:1222
  430.7 12.7 %copy-start.11 = (bf16[128,1152]{1,0:T(8,128)(2,1)S(1)}, bf16[128,1152]{1,0:T(8,128)(2,1)}, u32[]{:S(2)}) copy-start(bf16[128,1152]{1,0:T(8,128)(2,1)} %get-tuple-element.116) | copy-start | bytes 884740
  430.7 12.7 %copy-start.12 = (bf16[128,1152]{1,0:T(8,128)(2,1)S(1)}, bf16[128,1152]{1,0:T(8,128)(2,1)}, u32[]{:S(2)}) copy-start(bf16[128,1152]{1,0:T(8,128)(2,1)} %get-tuple-element.120) | copy-start | bytes 884740
  445.3 0.7 copy-start.13
  593.6 8.3 %copy-start.16 = (f32[4,1152]{1,0:T(4,128)S(1)}, f32[4,1152]{1,0:T(4,128)}, u32[]{:S(2)}) copy-start(f32[4,1152]{1,0:T(4,128)} %get-tuple-element.175) | copy-start | bytes 55300
  593.6 8.3 %copy-start.17 = (f32[4,1152]{1,0:T(4,128)S(1)}, f32[4,1152]{1,0:T(4,128)}, u32[]{:S(2)}) copy-start(f32[4,1152]{1,0:T(4,128)} %get-tuple-element.173) | copy-start | bytes 55300
  593.6 8.3 %copy-start.18 = (f32[4,1152]{1,0:T(4,128)S(1)}, f32[4,1152]{1,0:T(4,128)}, u32[]{:S(2)}) copy-start(f32[4,1152]{1,0:T(4,128)} %get-tuple-element.174) | copy-start | bytes 55300
  593.6 8.3 %copy-start.23 = (f32[2,1152]{1,0:T(2,128)S(1)}, f32[2,1152]{1,0:T(2,128)}, u32[]{:S(2)}) copy-start(f32[2,1152]{1,0:T(2,128)} %get-tuple-element.169) | copy-start | bytes 27652
  593.6 8.3 %copy-start.24 = (f32[2,1152]{1,0:T(2,128)S(1)}, f32[2,1152]{1,0:T(2,128)}, u32[]{:S(2)}) copy-start(f32[2,1152]{1,0:T(2,128)} %get-tuple-element.167) | copy-start | bytes 27652
  593.6 11.9 %copy-start.20 = (f32[1,4352]{1,0:T(1,128)S(1)}, f32[1,4352]{1,0:T(1,128)}, u32[]{:S(2)}) copy-start(f32[1,4352]{1,0:T(1,128)} %get-tuple-element.178) | copy-start | bytes 52228
  593.6 11.9 %copy-start.21 = (f32[1,4352]{1,0:T(1,128)S(1)}, f32[1,4352]{1,0:T(1,128)}, u32[]{:S(2)}) copy-start(f32[1,4352]{1,0:T(1,128)} %get-tuple-element.176) | copy-start | bytes 52228
  593.6 11.9 %copy-start.22 = (f32[1,4352]{1,0:T(1,128)S(1)}, f32[1,4352]{1,0:T(1,128)}, u32[]{:S(2)}) copy-start(f32[1,4352]{1,0:T(1,128)} %get-tuple-element.177) | copy-start | bytes 52228
  777.7 1.9 copy-start.3
  779.6 1.1 copy-start.14
  779.6 1.8 copy-start.2
  781.4 1.3 copy-start.1
  781.4 1.7 copy-start.7
  781.4 1.9 copy-start.8
  783.4 1.1 copy-start.10

commit v5 on v4

--- a/solution.py
+++ b/solution.py
@@ -29,8 +29,8 @@
 
 
 class Gather:
-    def __init__(self, ins, outs, sems):
-        self.ins, self.outs, self.count = ins, outs, len(ins)
+    def __init__(self, pieces, ins, outs, sems):
+        self.pieces, self.ins, self.outs, self.count = pieces, ins, outs, len(pieces)
         self.local_sem = sems[0]
         self.up, self.down, self.yy, self.cc = [(sems[1 + 2 * i], sems[2 + 2 * i]) for i in range(4)]
         self.sec, self.me = place()
@@ -39,22 +39,26 @@
         self.other_c = self.me - self.low + flip(self.low, 1)
 
     @staticmethod
-    def semaphores(count):
+    def semaphores(pieces, arrays):
         dma = pltpu.SemaphoreType.DMA
-        return [dma((count,))] + [dma((count, 4))] * 6 + [dma((count, 8))] * 2
+        return [dma((arrays,))] + [dma((pieces, 4))] * 6 + [dma((pieces, 8))] * 2
+
+    def part(self, piece, origin=None):
+        array, at, end = self.pieces[piece]
+        return self.ins[array].at[:, at:end] if origin is None else self.outs[array].at[origin, :, at:end]
 
     def send(self, piece, origin, sems, slot, target, first=False):
         return pltpu.make_async_remote_copy(
-            src_ref=self.ins[piece] if first else self.outs[piece].at[origin],
-            dst_ref=self.outs[piece].at[origin],
+            src_ref=self.part(piece) if first else self.part(piece, origin),
+            dst_ref=self.part(piece, origin),
             send_sem=sems[0].at[piece, slot],
             recv_sem=sems[1].at[piece, slot],
             device_id=(self.sec, target),
             device_id_type=MESH,
         )
 
-    def mine(self, piece):
-        return pltpu.make_async_copy(self.ins[piece], self.outs[piece].at[self.me], self.local_sem.at[piece])
+    def mine(self, array):
+        return pltpu.make_async_copy(self.ins[array], self.outs[array].at[self.me], self.local_sem.at[array])
 
     def along(self, piece, origin, first, go_up, go_down):
         zo = origin // 4
@@ -73,34 +77,43 @@
         self.send(piece, origin, self.yy, zo, self.other_y, first).start()
         self.send(piece, origin, self.cc, zo, self.other_c, first).start()
 
-    def start(self):
-        for piece in range(self.count):
-            self.mine(piece).start()
-            self.along(piece, self.me, True, True, True)
-
-    def step(self, step):
-        for piece in range(self.count):
-
-            @pl.when(self.z - step >= 0)
-            def _():
-                origin = self.me - 4 * step
-                self.send(piece, origin, self.up, self.z - step, self.me).wait_recv()
-                self.along(piece, origin, False, True, False)
-
-            @pl.when(self.z + step <= 3)
-            def _():
-                origin = self.me + 4 * step
-                self.send(piece, origin, self.down, self.z + step, self.me).wait_recv()
-                self.along(piece, origin, False, False, True)
-
-    def across(self):
+    def step(self, piece, step):
+        @pl.when(self.z - step >= 0)
+        def _():
+            origin = self.me - 4 * step
+            self.send(piece, origin, self.up, self.z - step, self.me).wait_recv()
+            self.along(piece, origin, False, True, False)
+
+        @pl.when(self.z + step <= 3)
+        def _():
+            origin = self.me + 4 * step
+            self.send(piece, origin, self.down, self.z + step, self.me).wait_recv()
+            self.along(piece, origin, False, False, True)
+
+    def slots(self, first, last):
+        for k in range(first, last):
+            if k == 0:
+                for array in range(len(self.ins)):
+                    self.mine(array).start()
+            if k < self.count:
+                self.along(k, self.me, True, True, True)
+            for step in range(1, 4):
+                if 0 <= k - step < self.count:
+                    self.step(k - step, step)
+
+    def across(self, pieces):
         far = self.other_y % 4
-        for step in range(4):
-            zo = (self.z + step) % 4
-            for piece in range(self.count):
+        for piece in pieces:
+            for step in range(4):
+                zo = (self.z + step) % 4
                 origin = zo * 4 + far
                 self.send(piece, origin, self.yy, zo, self.other_y).wait_recv()
                 self.send(piece, origin, self.cc, 4 + zo, self.other_c).start()
+
+    def arrived(self, pieces):
+        for piece in pieces:
+            for slot in range(8):
+                self.send(piece, self.me, self.cc, slot, self.other_c).wait_recv()
 
     def finish(self):
         for zo in range(4):
@@ -108,7 +121,6 @@
                 self.send(piece, self.me, self.yy, zo, self.other_y).wait_send()
                 for slot in (zo, 4 + zo):
                     self.send(piece, self.me, self.cc, slot, self.other_c).wait_send()
-                    self.send(piece, self.me, self.cc, slot, self.other_c).wait_recv()
 
                 @pl.when((zo <= self.z) & (self.z < 3))
                 def _():
@@ -117,32 +129,6 @@
                 @pl.when((zo >= self.z) & (self.z > 0))
                 def _():
                     self.send(piece, self.me, self.down, zo, self.me).wait_send()
-
-        for piece in range(self.count):
-            self.mine(piece).wait()
-
-
-def gather_kernel(count, *refs):
-    sec, me = place()
-    greet_all(16, sec, me)
-    work = Gather(refs[:count], refs[count : 2 * count], refs[2 * count :])
-    work.start()
-    for step in range(1, 4):
-        work.step(step)
-    work.across()
-    work.finish()
-
-
-def gather(arrays, cid):
-    count = len(arrays)
-    return pl.pallas_call(
-        functools.partial(gather_kernel, count),
-        out_shape=[jax.ShapeDtypeStruct((16,) + a.shape, a.dtype) for a in arrays],
-        in_specs=[pl.BlockSpec(memory_space=pl.ANY)] * count,
-        out_specs=[pl.BlockSpec(memory_space=pl.ANY)] * count,
-        scratch_shapes=Gather.semaphores(count),
-        compiler_params=pltpu.CompilerParams(collective_id=cid, has_side_effects=True),
-    )(*arrays)
 
 
 def flip(low, k):
@@ -319,6 +305,14 @@
             pltpu.VMEM((blocks, HEAD_DIM, BLOCK), BF),
             dma,
         ] + [dma((blocks,))] * 4
+
+    @staticmethod
+    def shapes(blocks):
+        return [
+            jax.ShapeDtypeStruct((blocks, 3 * HEAD_DIM, BLOCK), BF),
+            jax.ShapeDtypeStruct((blocks, 1, BLOCK), F32),
+            jax.ShapeDtypeStruct((blocks, HEAD_DIM, BLOCK), BF),
+        ]
 
     def own(self):
         return pltpu.make_async_copy(self.x_ref.at[self.me], self.qkv_ref.at[self.me], self.local_sem)
@@ -488,7 +482,7 @@
         self.leave_kv.wait()
 
 
-def attention_kernel(ahead, behind, items, pieces, *refs):
+def attention_kernel(ahead, behind, items, *refs):
     refs = list(refs)
 
     def take(n):
@@ -500,11 +494,11 @@
     near = take(2)
     x_ref = take(1) if ahead is not None else None
     kept, g_ref = (take(4), take(1)) if behind is not None else (None, None)
-    sources, shards = take(2 * n), take(pieces)
+    sources = take(2 * n)
     ahead_out = take(3) if ahead is not None else None
     behind_out = take(2) if behind is not None else None
-    outs, whole = take(n), take(pieces)
-    f = b = work = None
+    outs = take(n)
+    f = b = None
     blocks = (x_ref or g_ref)[0].shape[0]
     sec, me = place()
     if ahead is not None:
@@ -515,8 +509,6 @@
     for i, item in enumerate(items):
         into = lambda k, i=i: outs[i].at[k]
         copies.append(PlaneCopies(item, sources[2 * i], sources[2 * i + 1], into, *take(3)))
-    if pieces:
-        work = Gather(shards, whole, take(9))
     greet_all(blocks, sec, me)
 
     if b:
@@ -525,41 +517,28 @@
         b.wait_in()
     if f:
         f.start()
-    if work:
-        work.start()
     if f and not b:
         f.wait_in()
-    if work:
-        work.step(1)
-    if not (f and b):
-        for copy in copies:
-            copy.start()
+    for copy in copies:
+        copy.start()
     if b:
         b.by_query()
         b.by_key()
     if f and b:
         f.wait_in()
-        for copy in copies:
-            copy.start()
     if f:
         f.compute()
-    if work:
-        work.step(2)
     for copy in copies:
         copy.forward()
     if f:
         f.wait_out()
     if b:
         b.wait_out()
-    if work:
-        work.step(3)
-        work.across()
-        work.finish()
     for copy in copies:
         copy.finish()
 
 
-def attention(near, cid, ahead=None, behind=None, items=(), shards=()):
+def attention(near, cid, ahead=None, behind=None, items=()):
     first_in = ahead[1] if ahead else behind[1]
     blocks = first_in.shape[0]
     n = len(items)
@@ -570,11 +549,7 @@
     if ahead:
         args.append(ahead[1])
         scratch += Forward.scratch(blocks)
-        shapes += [
-            jax.ShapeDtypeStruct((blocks, 3 * HEAD_DIM, BLOCK), BF),
-            jax.ShapeDtypeStruct((blocks, 1, BLOCK), F32),
-            jax.ShapeDtypeStruct((blocks, HEAD_DIM, BLOCK), BF),
-        ]
+        shapes += Forward.shapes(blocks)
     if behind:
         args += [*behind[2], behind[1]]
         scratch += Backward.scratch(blocks)
@@ -582,27 +557,22 @@
             jax.ShapeDtypeStruct((blocks, HEAD_DIM, BLOCK), BF),
             jax.ShapeDtypeStruct((blocks, 2 * HEAD_DIM, BLOCK), BF),
         ]
-    args += sources + list(shards)
+    args += sources
     scratch += [dma, dma((4,)), dma((4,))] * n
-    if shards:
-        scratch += Gather.semaphores(len(shards))
     in_vmem = len(shapes)
     shapes += [jax.ShapeDtypeStruct(item.shape(), BF) for item in items]
-    shapes += [jax.ShapeDtypeStruct((blocks,) + shard.shape, BF) for shard in shards]
     out = pl.pallas_call(
-        functools.partial(
-            attention_kernel, ahead and ahead[0], behind and behind[0], list(items), len(shards)
-        ),
+        functools.partial(attention_kernel, ahead and ahead[0], behind and behind[0], list(items)),
         out_shape=shapes,
         in_specs=[smem, vmem] + [anywhere] * len(args),
-        out_specs=[vmem] * in_vmem + [anywhere] * (n + len(shards)),
+        out_specs=[vmem] * in_vmem + [anywhere] * n,
         scratch_shapes=scratch,
         compiler_params=pltpu.CompilerParams(collective_id=cid, has_side_effects=True, vmem_limit_bytes=60 << 20),
     )(*near, *args)
     out = list(out)
     three, out = (out[:3], out[3:]) if ahead else (None, out)
     two, out = (out[:2], out[2:]) if behind else (None, out)
-    return three, two, out[:n], out[n:]
+    return three, two, out
 
 
 def slices(width, step=1024):
@@ -637,6 +607,33 @@
     return part * rstd, jnp.sum(grad * xhat, axis=0, keepdims=True), jnp.sum(grad, axis=0, keepdims=True)
 
 
+def greet_plane(sec, me):
+    barrier = pltpu.get_barrier_semaphore()
+    low = me % 4
+    for k in range(1, 4):
+        pl.semaphore_signal(barrier, inc=1, device_id=(sec, me - low + flip(low, k)), device_id_type=MESH)
+    pl.semaphore_wait(barrier, 3)
+
+
+class Load:
+    def __init__(self, items):
+        self.items = list(items)
+        self.sources = [source for item in items for source in item.sources]
+        self.shapes = [jax.ShapeDtypeStruct(item.shape(), BF) for item in items]
+        dma = pltpu.SemaphoreType.DMA
+        self.scratch = [dma, dma((4,)), dma((4,))] * len(self.items)
+
+    def begin(self, sources, outs, sems):
+        copies = []
+        if self.items:
+            greet_plane(*place())
+        for i, item in enumerate(self.items):
+            into = lambda k, i=i: outs[i].at[k]
+            copies.append(PlaneCopies(item, sources[2 * i], sources[2 * i + 1], into, *sems[3 * i : 3 * i + 3]))
+            copies[-1].start()
+        return copies
+
+
 def gelu_tanh(v):
     c = math.sqrt(2.0 / math.pi)
     return 0.5 * v * (1.0 + jnp.tanh(c * (v + 0.044715 * (v * v * v))))
@@ -659,7 +656,7 @@
         ref[w % 4, w // 4] = turned[w * HEAD_DIM : (w + 1) * HEAD_DIM].astype(BF)
 
 
-GAIN1, BIAS1, OUT_BIAS, GAIN2, BIAS2, FC2_BIAS = range(6)
+GAIN1, BIAS1, OUT_BIAS, GAIN2, BIAS2, FC2_BIAS = 0, 1, 4, 5, 6, 7
 
 
 def row(vec_ref, i):
@@ -681,7 +678,8 @@
         stream.wait("w", at)
         t_buf[at:end, :] = (dot(low, w_buf[:, at:end]) + bias_ref[:, at:end]).T
     for h in range(HEADS):
-        qkv_ref[h] = t_buf[h * 3 * HEAD_DIM : (h + 1) * 3 * HEAD_DIM, :].astype(BF)
+        parts = [t_buf[p * D + h * HEAD_DIM : p * D + (h + 1) * HEAD_DIM, :] for p in range(3)]
+        qkv_ref[h] = jnp.concatenate(parts, axis=0).astype(BF)
     put_owners(n1_ref, low.astype(F32))
 
 
@@ -705,6 +703,99 @@
     )(tok, inc, vec, bias, w)
 
 
+def first_kernel(first_ref, bias_ref, tok_ref, *refs):
+    refs = list(refs)
+
+    def take(n):
+        part = refs[:n]
+        del refs[:n]
+        return part
+
+    shards = take(5)
+    ahead_out = take(3)
+    n1_ref, small_all, w_qkv = take(3)
+    whole = take(3)
+    w_buf, t_buf, x_buf, w_sem = take(4)
+    f = Forward(0, (first_ref, bias_ref), x_buf, ahead_out, take(len(Forward.scratch(HEADS))))
+    work = Gather(first_pieces(shards), shards, (w_buf, small_all, *whole), take(9))
+    soon, later = [list(range(SOON)), list(range(SOON, work.count))]
+    sec, me = place()
+    greet_all(HEADS, sec, me)
+    work.slots(0, 1)
+    xhat, _ = normalised(tok_ref[...].astype(F32))
+    xhat = xhat.T
+    work.slots(1, SOON + 3)
+    for array in range(len(shards)):
+        work.mine(array).wait()
+    work.across(soon)
+    work.arrived(soon)
+    keep = pltpu.make_async_copy(w_buf, w_qkv, w_sem)
+    keep.start()
+    work.slots(SOON + 3, SOON + 4)
+    small = jnp.concatenate([small_all[w].astype(F32) for w in range(HEADS)], axis=0)
+    n1 = (xhat * small[:, 0:1] + small[:, 1:2]).astype(BF).astype(F32)
+    for w in range(HEADS):
+        n1_ref[w % 4, w // 4] = n1[w * HEAD_DIM : (w + 1) * HEAD_DIM].astype(BF)
+    low = n1.T.astype(BF)
+
+    def columns(i, carry):
+        here = pl.ds(pl.multiple_of(i * 384, 384), 384)
+        w = jnp.concatenate([w_buf[shard, :, here].astype(F32) for shard in range(HEADS)], axis=0)
+        t_buf[here, :] = dot(low, w.astype(BF)).T
+        return carry
+
+    lax.fori_loop(0, 3 * D // 384, columns, 0)
+    for h in range(HEADS):
+        rows = slice(h * HEAD_DIM, (h + 1) * HEAD_DIM)
+        parts = [t_buf[p * D + h * HEAD_DIM : p * D + (h + 1) * HEAD_DIM, :] for p in range(3)]
+        parts = [parts[0] + small[rows, 2:3], parts[1], parts[2] + small[rows, 3:4]]
+        x_buf[h] = jnp.concatenate(parts, axis=0).astype(BF)
+    f.start()
+    work.slots(SOON + 4, SOON + 5)
+    f.wait_in()
+    work.slots(SOON + 5, SOON + 7)
+    f.compute()
+    work.slots(SOON + 7, work.count + 3)
+    f.wait_out()
+    work.across(later)
+    work.arrived(later)
+    work.finish()
+    keep.wait()
+
+
+SOON = 4
+
+
+def first_pieces(shards):
+    pieces = [(1, 0, BLOCK)]
+    for array in (0, 2, 3, 4):
+        pieces += [(array, at, end) for at, end in slices(shards[array].shape[1], D)]
+    return pieces
+
+
+def first_tick(near, tok, shards, cid):
+    tokens = tok.shape[0]
+    anywhere, vmem, smem = [pl.BlockSpec(memory_space=m) for m in (pl.ANY, pltpu.VMEM, pltpu.SMEM)]
+    whole = [jax.ShapeDtypeStruct((HEADS,) + shard.shape, BF) for shard in shards]
+    return pl.pallas_call(
+        first_kernel,
+        out_shape=Forward.shapes(HEADS)
+        + [jax.ShapeDtypeStruct((4, 4, HEAD_DIM, tokens), BF), whole[1], whole[0]]
+        + whole[2:],
+        in_specs=[smem, vmem, vmem] + [anywhere] * 5,
+        out_specs=[vmem] * 5 + [anywhere] * 4,
+        scratch_shapes=[
+            pltpu.VMEM((HEADS,) + shards[0].shape, BF),
+            pltpu.VMEM((3 * D, tokens), F32),
+            pltpu.VMEM((HEADS, 3 * HEAD_DIM, tokens), BF),
+            pltpu.SemaphoreType.DMA,
+        ]
+        + Forward.scratch(HEADS)
+        + Gather.semaphores(len(first_pieces(shards)), len(shards)),
+        compiler_params=pltpu.CompilerParams(collective_id=cid, has_side_effects=True, vmem_limit_bytes=60 << 20),
+    )(*near, tok, *shards)
+
+
 def greet_section(sec, me):
     barrier = pltpu.get_barrier_semaphore()
     pl.semaphore_signal(barrier, inc=1, device_id=(1 - sec, me), device_id_type=MESH)
@@ -717,12 +808,16 @@
     )
 
 
-def feed_kernel(shift, *refs):
+def feed_kernel(shift, load, *refs):
+    n = len(load.items)
     tok_ref, inc_ref, att_ref, vec_ref, bias_ref, out_w, fc1_w, fc2_w = refs[:8]
-    res_ref, pre_ref, hidden_ref, n2_ref, att_rows_ref, low_ref = refs[8:14]
-    refs = refs[14:]
+    sources, refs = refs[8 : 8 + 2 * n], refs[8 + 2 * n :]
+    res_ref, pre_ref, hidden_ref, n2_ref, att_rows_ref, low_ref = refs[:6]
+    refs = refs[6:]
     if shift:
         next_ref, refs = refs[0], refs[1:]
+    outs, refs = refs[:n], refs[n:]
+    refs, load_sems = refs[: len(refs) - 3 * n], refs[len(refs) - 3 * n :]
     out_buf, fc1_buf, fc2_buf, t_buf, sems = refs[:5]
     sec, me = place()
     pairs = [("out", out_w, out_buf, (0, D))]
@@ -732,6 +827,7 @@
     stream.start()
     if shift:
         greet_section(sec, me)
+    taken = load.begin(sources, outs, load_sems)
     att = jnp.concatenate([att_ref[h].astype(F32) for h in range(HEADS)], axis=0).T.astype(BF)
     for w in range(HEADS):
         att_rows_ref[w % 4, w // 4] = att_ref[w]
@@ -755,21 +851,25 @@
     if shift:
         copy = to_section(low_ref, next_ref, refs[5], refs[6], sec, me)
         copy.start()
+    for one in taken:
+        one.forward()
     put_owners(n2_ref, n2.astype(F32))
     if shift:
         copy.wait()
-
-
-def feed_forward(tok, inc, att, vec, bias, out_w, fc1_w, fc2_w, cid):
+    for one in taken:
+        one.finish()
+
+
+def feed_forward(tok, inc, att, vec, bias, out_w, fc1_w, fc2_w, cid, shift, items=()):
     tokens = tok.shape[0]
-    shift = cid is not None
+    load = Load(items)
     anywhere, vmem = pl.BlockSpec(memory_space=pl.ANY), pl.BlockSpec(memory_space=pltpu.VMEM)
     dma = pltpu.SemaphoreType.DMA
-    params = dict(collective_id=cid, has_side_effects=True) if shift else {}
+    params = {} if cid is None else dict(collective_id=cid, has_side_effects=True)
     rows = jax.ShapeDtypeStruct((4, 4, HEAD_DIM, tokens), BF)
     low = jax.ShapeDtypeStruct((tokens, D), BF)
     return pl.pallas_call(
-        functools.partial(feed_kernel, shift),
+        functools.partial(feed_kernel, shift, load),
         out_shape=[
             jax.ShapeDtypeStruct((tokens, D), F32),
             jax.ShapeDtypeStruct((tokens, FFP), F32),
@@ -778,9 +878,10 @@
             rows,
             low,
         ]
-        + [low] * shift,
-        in_specs=[vmem] * 5 + [anywhere] * 3,
-        out_specs=[vmem] * (6 + shift),
+        + [low] * shift
+        + load.shapes,
+        in_specs=[vmem] * 5 + [anywhere] * (3 + len(load.sources)),
+        out_specs=[vmem] * (6 + shift) + [anywhere] * len(load.shapes),
         scratch_shapes=[
             pltpu.VMEM((D, D), BF),
             pltpu.VMEM((D, FFP), BF),
@@ -788,16 +889,20 @@
             pltpu.VMEM((FFP, tokens), BF),
             dma((1 + 2 * len(slices(FFP)),)),
         ]
-        + [dma, dma] * shift,
+        + [dma, dma] * shift
+        + load.scratch,
         compiler_params=pltpu.CompilerParams(vmem_limit_bytes=60 << 20, **params),
-    )(tok, inc, att, vec, bias, out_w, fc1_w, fc2_w)
-
-
-def feed_back_kernel(cot_ref, inc_ref, vec_ref, *refs):
+    )(tok, inc, att, vec, bias, out_w, fc1_w, fc2_w, *load.sources)
+
+
+def feed_back_kernel(load, cot_ref, inc_ref, vec_ref, *refs):
+    n = len(load.items)
     kept, refs = refs[:4], refs[4:]
     out_w, fc1_w, fc2_w = refs[:3]
-    rg_ref, ag_ref, fc_ref, pg_ref, branch_ref, sum_ref, fsum_ref = refs[3:10]
-    pre_buf, res_buf, out_buf, fc1_buf, fc2_buf, t_buf, kept_sem, sems = refs[10:]
+    sources, refs = refs[3 : 3 + 2 * n], refs[3 + 2 * n :]
+    rg_ref, ag_ref, fc_ref, pg_ref, branch_ref, sum_ref, fsum_ref = refs[:7]
+    outs, refs = refs[7 : 7 + n], refs[7 + n :]
+    pre_buf, res_buf, out_buf, fc1_buf, fc2_buf, t_buf, kept_sem, sems = refs[:8]
     sec, _ = place()
     pairs = []
     pairs += [("fc2", fc2_w, fc2_buf, cols) for cols in slices(FFP)]
@@ -806,6 +911,7 @@
     stream = Stream(pairs, sems)
     fetch(kept, (pre_buf, res_buf), kept_sem, sec)
     stream.start()
+    taken = load.begin(sources, outs, refs[8:])
     grad = jnp.where(sec == 0, inc_ref[...].astype(F32), cot_ref[...].astype(F32))
     fc_grad = grad.astype(BF)
     put_owners(fc_ref, grad)
@@ -828,6 +934,8 @@
     rg_ref[...] = residual_grad
     branch = residual_grad.astype(BF)
     branch_ref[...] = branch
+    for one in taken:
+        one.forward()
     stream.wait("out", 0)
     att_grad = dot(out_buf[...], residual_grad.T.astype(BF))
     for h in range(HEADS):
@@ -836,14 +944,18 @@
     sum_ref[1:2, :] = gain_sum
     sum_ref[2:3, :] = bias_sum
     sum_ref[3:4, :] = jnp.sum(fc_grad.astype(F32), axis=0, keepdims=True)
-
-
-def feed_backward(cot, inc, vec, kept, out_w, fc1_w, fc2_w):
+    for one in taken:
+        one.finish()
+
+
+def feed_backward(cot, inc, vec, kept, out_w, fc1_w, fc2_w, cid, items=()):
     tokens = cot.shape[0]
+    load = Load(items)
+    params = {} if cid is None else dict(collective_id=cid, has_side_effects=True)
     anywhere, vmem = pl.BlockSpec(memory_space=pl.ANY), pl.BlockSpec(memory_space=pltpu.VMEM)
     dma = pltpu.SemaphoreType.DMA
     return pl.pallas_call(
-        feed_back_kernel,
+        functools.partial(feed_back_kernel, load),
         out_shape=[
             jax.ShapeDtypeStruct((tokens, D), F32),
             jax.ShapeDtypeStruct((HEADS, HEAD_DIM, tokens), BF),
@@ -852,9 +964,10 @@
             jax.ShapeDtypeStruct((tokens, D), BF),
             jax.ShapeDtypeStruct((4, D), F32),
             jax.ShapeDtypeStruct((1, FFP), F32),
-        ],
-        in_specs=[vmem] * 3 + [anywhere] * 7,
-        out_specs=[vmem] * 7,
+        ]
+        + load.shapes,
+        in_specs=[vmem] * 3 + [anywhere] * (7 + len(load.sources)),
+        out_specs=[vmem] * 7 + [anywhere] * len(load.shapes),
         scratch_shapes=[
             pltpu.VMEM((tokens, FFP), F32),
             pltpu.VMEM((tokens, D), F32),
@@ -864,26 +977,32 @@
             pltpu.VMEM((FFP, tokens), BF),
             dma((2,)),
             dma((1 + 2 * len(slices(FFP)),)),
-        ],
-        compiler_params=pltpu.CompilerParams(vmem_limit_bytes=60 << 20),
-    )(cot, inc, vec, *kept, out_w, fc1_w, fc2_w)
-
-
-def qkv_back_kernel(shift, *refs):
+        ]
+        + load.scratch,
+        compiler_params=pltpu.CompilerParams(vmem_limit_bytes=60 << 20, **params),
+    )(cot, inc, vec, *kept, out_w, fc1_w, fc2_w, *load.sources)
+
+
+def qkv_back_kernel(shift, load, *refs):
+    n = len(load.items)
     tok_ref, inc_ref, vec_ref, rg_ref, dq_ref, dkv_ref, w_ref = refs[:7]
-    grad_ref, dqkv_ref, sum_ref, qsum_ref = refs[7:11]
-    refs = refs[11:]
+    sources, refs = refs[7 : 7 + 2 * n], refs[7 + 2 * n :]
+    grad_ref, dqkv_ref, sum_ref, qsum_ref = refs[:4]
+    refs = refs[4:]
     if shift:
         next_ref, refs = refs[0], refs[1:]
+    outs, refs = refs[:n], refs[n:]
+    refs, load_sems = refs[: len(refs) - 3 * n], refs[len(refs) - 3 * n :]
     w_buf, sems = refs[:2]
     sec, me = place()
     stream = Stream([("w", w_ref, w_buf, cols) for cols in slices(3 * D, 384)], sems)
     stream.start()
     if shift:
         greet_section(sec, me)
-    rows = []
-    for h in range(HEADS):
-        rows += [dq_ref[h].astype(F32), dkv_ref[h].astype(F32)]
+    taken = load.begin(sources, outs, load_sems)
+    kv = [dkv_ref[h].astype(F32) for h in range(HEADS)]
+    rows = [dq_ref[h].astype(F32) for h in range(HEADS)]
+    rows += [part[:HEAD_DIM] for part in kv] + [part[HEAD_DIM:] for part in kv]
     dqkv = jnp.concatenate(rows, axis=0).astype(BF)
     dqkv_ref[...] = dqkv
     qsum_ref[...] = nt(jnp.ones((8, dqkv.shape[1]), BF), dqkv)
@@ -905,29 +1024,35 @@
     sum_ref[1:2, :] = bias_sum
     if shift:
         copy.wait()
-
-
-def qkv_backward(tok, inc, vec, residual_grad, dq, dkv, w, cid):
+    for one in taken:
+        one.forward()
+    for one in taken:
+        one.finish()
+
+
+def qkv_backward(tok, inc, vec, residual_grad, dq, dkv, w, cid, shift, items=()):
     tokens = tok.shape[0]
-    shift = cid is not None
+    load = Load(items)
     anywhere, vmem = pl.BlockSpec(memory_space=pl.ANY), pl.BlockSpec(memory_space=pltpu.VMEM)
     dma = pltpu.SemaphoreType.DMA
-    params = dict(collective_id=cid, has_side_effects=True) if shift else {}
+    params = {} if cid is None else dict(collective_id=cid, has_side_effects=True)
     return pl.pallas_call(
-        functools.partial(qkv_back_kernel, shift),
+        functools.partial(qkv_back_kernel, shift, load),
         out_shape=[
             jax.ShapeDtypeStruct((tokens, D), F32),
             jax.ShapeDtypeStruct((3 * D, tokens), BF),
             jax.ShapeDtypeStruct((2, D), F32),
             jax.ShapeDtypeStruct((8, 3 * D), F32),
         ]
-        + [jax.ShapeDtypeStruct((tokens, D), BF)] * shift,
-        in_specs=[vmem] * 6 + [anywhere],
-        out_specs=[vmem] * (4 + shift),
+        + [jax.ShapeDtypeStruct((tokens, D), BF)] * shift
+        + load.shapes,
+        in_specs=[vmem] * 6 + [anywhere] * (1 + len(load.sources)),
+        out_specs=[vmem] * (4 + shift) + [anywhere] * len(load.shapes),
         scratch_shapes=[pltpu.VMEM((D, 3 * D), BF), dma((len(slices(3 * D, 384)),))]
-        + [pltpu.VMEM((tokens, D), BF), dma, dma] * shift,
+        + [pltpu.VMEM((tokens, D), BF), dma, dma] * shift
+        + load.scratch,
         compiler_params=pltpu.CompilerParams(vmem_limit_bytes=60 << 20, **params),
-    )(tok, inc, vec, residual_grad, dq, dkv, w)
+    )(tok, inc, vec, residual_grad, dq, dkv, w, *load.sources)
 
 
 def pad_ff(x):
@@ -965,6 +1090,11 @@
     count = small_ref.shape[0]
     greet_all(count, sec, me)
 
+    def begin(name):
+        for other, one in behind:
+            if other == name:
+                one.start()
+
     loads = []
     for i, (name, batch, cols) in enumerate(early):
         dst = y_bufs[name].at[4 * batch : 4 * batch + 4]
@@ -980,7 +1110,7 @@
             return ref if item.cols is None else ref.at[:, item.cols[0] : item.cols[1]]
 
         behind.append((name, PlaneCopies(item, late_refs[2 * i], late_refs[2 * i + 1], slot, *late_sems[i])))
-        behind[-1][1].start()
+    begin("fc1")
     smalls = []
     for d in range(1, count):
         target = (me + d) % count
@@ -1022,6 +1152,8 @@
         for other, one in behind:
             if other == name:
                 one.forward()
+        if name in ("fc1", "qkv"):
+            begin({"fc1": "qkv", "qkv": "out"}[name])
         for other, load in loads:
             if other == name:
                 load.wait()
@@ -1078,15 +1210,14 @@
     loop("fc2", (compute, "fc2"))
     ready("fc1")
     loop("fc1", (compute, "fc1"), (middle, "fc2"))
-    ready("out")
-    loop("out", (compute, "out"))
     loop("fc1", (middle, "fc1"), (finish, "fc2"))
     ready("qkv")
     loop("qkv", (compute, "qkv"))
-    loop("out", (middle, "out"))
+    ready("out")
+    loop("out", (compute, "out"))
     loop("fc1", (finish, "fc1"))
     loop("qkv", (middle, "qkv"))
-    loop("out", (finish, "out"))
+    loop("out", (middle, "out"))
     for copy in smalls:
         copy.wait()
     total = small_ref[me]
@@ -1094,6 +1225,7 @@
         total = total + small_got[d]
     small_out[...] = total
     loop("qkv", (finish, "qkv"))
+    loop("out", (finish, "out"))
 
 
 def final(small, xs, early, late, cid):
@@ -1151,20 +1283,21 @@
     fc2_bias,
 ):
     sec, me = place()
-    own_qkv = qkv_weight[0].reshape(HEAD_DIM, 3, HEADS, HEAD_DIM).transpose(0, 2, 1, 3).reshape(HEAD_DIM, 3 * D)
     small = jnp.stack(
-        [ln1_gain[0], ln1_bias[0], qv_bias[0, 0], qv_bias[0, 1], out_bias[0], ln2_gain[0], ln2_bias[0], fc2_bias[0]]
-    )
-    small = jnp.pad(small, ((0, 8), (0, BLOCK - HEAD_DIM)))
-    w_qkv, w_out, small_all = gather([own_qkv, out_weight[0], small], 1)
-    ff_shards = [pad_ff(fc1_weight[0]), pad_ff(fc2_weight[0].T)]
+        [ln1_gain[0], ln1_bias[0], qv_bias[0, 0], qv_bias[0, 1], out_bias[0], ln2_gain[0], ln2_bias[0], fc2_bias[0]],
+        axis=1,
+    )
+    small = jnp.pad(small, ((0, 0), (0, BLOCK - 8)))
+    near = window(image_of_block)
+    shards = [qkv_weight[0], small, out_weight[0], pad_ff(fc1_weight[0]), pad_ff(fc2_weight[0].T)]
+    *three, n1, small_all, w_qkv, w_out, w_fc1, w_fc2t = first_tick(near, tokens[0], shards, 2)
     w_qkv = w_qkv.reshape(D, 3 * D)
     w_out = w_out.reshape(D, D)
-    vectors = small_all[:, :8, :HEAD_DIM].astype(F32)
-    vec = jnp.stack([vectors[:, i].reshape(D) for i in (0, 1, 4, 5, 6, 7)])
-    b_qkv = jnp.stack([vectors[:, 2], jnp.zeros_like(vectors[:, 2]), vectors[:, 3]], axis=1).reshape(1, 3 * D)
+    w_fc1 = w_fc1.reshape(D, FFP)
+    w_fc2t = w_fc2t.reshape(D, FFP)
+    vec = small_all.reshape(D, BLOCK)[:, :8].T.astype(F32)
+    b_qkv = jnp.concatenate([vec[2:3], jnp.zeros((1, D), F32), vec[3:4]], axis=1)
     b_fc1 = pad_ff(fc1_bias[0]).astype(F32).reshape(1, FFP)
-    near = window(image_of_block)
 
     def choose(at_zero, at_one):
         return jnp.where(sec == 0, at_zero, at_one)
@@ -1175,8 +1308,8 @@
     def token_inputs(tick):
         return tokens[min(tick, 1)], incoming[tick]
 
-    def feed(tick, qkv, lse, att, n1, cid):
-        fed = feed_forward(*token_inputs(tick), att, vec, b_fc1, w_out, w_fc1, w_fc2t, cid)
+    def feed(tick, qkv, lse, att, n1, cid, shift, items=()):
+        fed = feed_forward(*token_inputs(tick), att, vec, b_fc1, w_out, w_fc1, w_fc2t, cid, shift, items)
         saved.append(
             dict(qkv=qkv, lse=lse, n1=n1, residual=fed[0], pre=fed[1], hidden=fed[2], n2=fed[3], att=fed[4], low=fed[5])
         )
@@ -1185,57 +1318,65 @@
     def kept(tick, *names):
         return [saved[at][name] for name in names for at in ((1, 1), (0, 2), (1, 1))[tick]]
 
-    def feed_back(tick, incoming_grad):
-        residual_grad, att_grad, fc, pre, branch, four, fsum = feed_backward(
-            cotangent[min(tick, 1)], incoming_grad, vec, kept(tick, "pre", "residual"), w_out, w_fc1, w_fc2t
+    def feed_back(tick, incoming_grad, cid=None, items=()):
+        residual_grad, att_grad, fc, pre, branch, four, fsum, *got = feed_backward(
+            cotangent[min(tick, 1)], incoming_grad, vec, kept(tick, "pre", "residual"), w_out, w_fc1, w_fc2t, cid, items
         )
         back.append(dict(fc=fc, pre=pre, branch=branch))
-        return residual_grad, att_grad, [*four, fsum]
-
-    def qkv_back(tick, residual_grad, dq, dkv, sums, cid):
+        return residual_grad, att_grad, [*four, fsum], got
+
+    def qkv_back(tick, residual_grad, dq, dkv, sums, cid, shift, items=()):
         inputs = (tokens[max(tick - 1, 0)], incoming[min(tick + 1, 2)])
-        input_grad, dqkv, two, qsum, *rest = qkv_backward(*inputs, vec, residual_grad, dq, dkv, w_qkv, cid)
+        input_grad, dqkv, two, qsum, *rest = qkv_backward(
+            *inputs, vec, residual_grad, dq, dkv, w_qkv, cid, shift, items
+        )
         back[tick]["dqkv"] = dqkv
         input_grads.append(input_grad)
-        qsum = qsum[0].reshape(HEADS, 3, HEAD_DIM)
-        done.append([two[0], two[1], qsum[:, 0].reshape(D), qsum[:, 2].reshape(D), *sums])
-        return rest[0] if rest else input_grad.astype(BF)
-
-    qkv, n1 = qkv_forward(*token_inputs(0), vec, b_qkv, w_qkv)
-    three, _, _, whole = attention(near, 2, ahead=(0, qkv), shards=ff_shards)
-    w_fc1, w_fc2t = [w.reshape(D, FFP) for w in whole]
-    incoming.append(feed(0, *three, n1, 8)[6])
+        done.append([two[0], two[1], qsum[0, :D], qsum[0, 2 * D :], *sums])
+        return rest
+
+    incoming.append(feed(0, *three, n1, 8, True)[6])
 
     qkv, n1 = qkv_forward(*token_inputs(1), vec, b_qkv, w_qkv)
-    three, _, _, _ = attention(near, 3, ahead=(1, qkv))
-    incoming.append(lax.ppermute(feed(1, *three, n1, None)[5], "section", [(0, 1)]))
-
-    residual_grad, att_grad, sums = feed_back(0, tokens[0])
+    three, _, _ = attention(near, 3, ahead=(1, qkv))
+    incoming.append(lax.ppermute(feed(1, *three, n1, None, False)[5], "section", [(0, 1)]))
+
+    def first_batch(name, cols=None):
+        return Whole(saved[0][name], saved[1][name], cols)
+
+    def second_batch(name, cols=None):
+        return Whole(saved[1][name], saved[2][name], cols)
+
+    residual_grad, att_grad, sums, _ = feed_back(0, tokens[0])
     qkv, n1 = qkv_forward(*token_inputs(2), vec, b_qkv, w_qkv)
     items = [Rows(saved[0][name], saved[1][name]) for name in ("n1", "att", "n2")]
-    items.append(Whole(saved[0]["hidden"], saved[1]["hidden"]))
-    three, two, got, _ = attention(
-        near, 4, ahead=(2, qkv), behind=(0, att_grad, kept(0, "qkv", "lse")), items=items
-    )
-    sent["n1_0"], sent["att_0"], sent["n2_0"], sent["h0"] = got
-    low = qkv_back(0, residual_grad, *two, sums, None)
-    incoming_grad = lax.ppermute(low, "section", [(1, 0)])
-    feed(2, *three, n1, None)
+    items.append(first_batch("hidden", (0, SPLIT)))
+    three, two, got = attention(near, 4, ahead=(2, qkv), behind=(0, att_grad, kept(0, "qkv", "lse")), items=items)
+    sent["n1_0"], sent["att_0"], sent["n2_0"], sent["h0a"] = got
+    qkv_back(0, residual_grad, *two, sums, None, False)
+    incoming_grad = lax.ppermute(input_grads[0].astype(BF), "section", [(1, 0)])
+    sent["h0b"] = feed(2, *three, n1, 11, False, [first_batch("hidden", (SPLIT, FFP))])[6]
     outputs = jnp.stack([choose(saved[m]["low"], saved[m + 1]["low"]) for m in range(2)])
 
-    residual_grad, att_grad, sums = feed_back(1, incoming_grad)
+    residual_grad, att_grad, sums, got = feed_back(1, incoming_grad, 12, [second_batch("hidden", (0, SPLIT))])
+    sent["h1a"] = got[0]
     items = [Rows(saved[1][name], saved[2][name]) for name in ("n1", "att", "n2")]
-    items.append(Whole(saved[1]["hidden"], saved[2]["hidden"], (0, SPLIT)))
-    _, two, got, _ = attention(near, 5, behind=(1, att_grad, kept(1, "qkv", "lse")), items=items)
-    sent["n1_1"], sent["att_1"], sent["n2_1"], sent["h1a"] = got
-    incoming_grad = qkv_back(1, residual_grad, *two, sums, 9)
-
-    residual_grad, att_grad, sums = feed_back(2, incoming_grad)
+    items.append(second_batch("hidden", (SPLIT, FFP)))
+    _, two, got = attention(near, 5, behind=(1, att_grad, kept(1, "qkv", "lse")), items=items)
+    sent["n1_1"], sent["att_1"], sent["n2_1"], sent["h1b"] = got
+    incoming_grad = qkv_back(1, residual_grad, *two, sums, 9, True)[0]
+
+    residual_grad, att_grad, sums, got = feed_back(
+        2, incoming_grad, 13, [Whole(back[1]["pre"], back[0]["pre"], (0, SPLIT))]
+    )
+    sent["pre_0a"] = got[0]
     items = [Rows(back[1]["fc"], back[0]["fc"]), Rows(back[2]["fc"], back[1]["fc"])]
-    items.append(Whole(saved[1]["hidden"], saved[2]["hidden"], (SPLIT, FFP)))
-    _, two, got, _ = attention(near, 6, behind=(2, att_grad, kept(2, "qkv", "lse")), items=items)
-    sent["fc_0"], sent["fc_1"], sent["h1b"] = got
-    qkv_back(2, residual_grad, *two, sums, None)
+    items.append(Whole(back[1]["pre"], back[0]["pre"], (SPLIT, FFP)))
+    _, two, got = attention(near, 6, behind=(2, att_grad, kept(2, "qkv", "lse")), items=items)
+    sent["fc_0"], sent["fc_1"], sent["pre_0b"] = got
+    sent["branch_0"] = qkv_back(
+        2, residual_grad, *two, sums, 14, False, [Whole(back[1]["branch"], back[0]["branch"])]
+    )[0]
     input_grads = jnp.stack([choose(input_grads[m + 1], input_grads[m]) for m in range(2)])
 
     sums = [choose(done[1][i] + done[2][i], done[0][i] + done[1][i]) for i in range(9)]
@@ -1251,28 +1392,29 @@
         "qkv": [sent["n1_0"], sent["n1_1"]],
     }
     early = [
-        ("fc2", 0, None, sent["h0"]),
+        ("fc2", 0, (0, SPLIT), sent["h0a"]),
+        ("fc2", 0, (SPLIT, FFP), sent["h0b"]),
         ("fc2", 1, (0, SPLIT), sent["h1a"]),
         ("fc2", 1, (SPLIT, FFP), sent["h1b"]),
+        ("fc1", 0, (0, SPLIT), sent["pre_0a"]),
+        ("fc1", 0, (SPLIT, FFP), sent["pre_0b"]),
+        ("out", 0, None, sent["branch_0"]),
     ]
     late = [
-        ("fc1", 0, Whole(back[1]["pre"], back[0]["pre"])),
         ("fc1", 1, Whole(back[2]["pre"], back[1]["pre"])),
-        ("out", 0, Whole(back[1]["branch"], back[0]["branch"])),
-        ("out", 1, Whole(back[2]["branch"], back[1]["branch"])),
         ("qkv", 0, Whole(back[1]["dqkv"], back[0]["dqkv"])),
         ("qkv", 1, Whole(back[2]["dqkv"], back[1]["dqkv"])),
+        ("out", 1, Whole(back[2]["branch"], back[1]["branch"])),
     ]
     packed, grads = final(jnp.concatenate([by_owner, to_all], axis=1), xs, early, late, 10)
     g_small = packed[:8, :HEAD_DIM]
     g_fc1_bias = packed[8 : 8 + lines].reshape(FFP)[:FF]
-    g_qkv = grads["qkv"].reshape(HEAD_DIM, HEADS, 3, HEAD_DIM).transpose(0, 2, 1, 3).reshape(HEAD_DIM, 3 * D)
     return (
         outputs[None],
         input_grads[None],
         g_small[0][None],
         g_small[1][None],
-        g_qkv[None],
+        grads["qkv"][None],
         g_small[2:4][None],
         grads["out"][None],
         g_small[4][None],

time: 793 us -> 755 us (0.952)
  Pallas kernels: 741 us -> 704 us
  local copies, waits for them, and re-layouts: 29.6 us -> 21.5 us
    pallas_call x5 -> x4, Pallas kernels: 349 us -> 193 us  [attention(): pl.pallas_call(functools.partial(attention_kernel, ahead and ahead[0], be...]
    pallas_call x10, Pallas kernels: 206 us -> 354 us  [the longest x1 194 us: first_tick(): pl.pallas_call(first_kernel, out_shape=Forward.shapes(HEADS) + [jax.Shape...]
    pallas_call x1, Pallas kernels: 165 us -> 143 us  [final(): pl.pallas_call(functools.partial(final_kernel, tiles, [e[:3] for e in ear...]
    pallas_call x3 -> x2, Pallas kernels: 21 us -> 14 us  [qkv_forward(): pl.pallas_call(qkv_kernel, out_shape=[jax.ShapeDtypeStruct((HEADS, 3 * HE...]
  transfers between devices with their start and end apart: 2 -> 2, of which waited for: 0 -> 0; matrix products, arithmetic and copies ran while one was open for 0% -> 0% of each run, Pallas kernels for 4% -> 5%
where the time goes in v5:
time: 755 us; the launch traced here: 742 us
  Pallas kernels  704 us (93%)
  local copies, waits for them, and re-layouts  21.5 us (3%)
  other arithmetic  10.1 us (1%)
    pallas_call x1, Pallas kernels, first_tick(): pl.pallas_call(first_kernel, out_shape=Forward.shapes(HEADS) + [jax.Shape...  194 us
    pallas_call x4, Pallas kernels, attention(): pl.pallas_call(functools.partial(attention_kernel, ahead and ahead[0], be...  193 us
    pallas_call x1, Pallas kernels, final(): pl.pallas_call(functools.partial(final_kernel, tiles, [e[:3] for e in ear...  143 us
    pallas_call x3, Pallas kernels, feed_backward(): pl.pallas_call(functools.partial(feed_back_kernel, load), out_shape=[jax....  65.3 us
    pallas_call x3, Pallas kernels, feed_forward(): pl.pallas_call(functools.partial(feed_kernel, shift, load), out_shape=[ja...  55.9 us
    pallas_call x3, Pallas kernels, qkv_backward(): pl.pallas_call(functools.partial(qkv_back_kernel, shift, load), out_shape...  39.1 us
  transfers between devices with their start and end apart: 2, of which 0 were waited for; matrix products, arithmetic and copies ran while one was open for 0% of the time, Pallas kernels for 5%

profile of v5, /device:TPU:10, one launch (start us, length us, event | category | flops | bytes accessed | tf_op | source)
XLA Modules:
  0.0 741.7 jit_solution(5694812320846311954)
XLA Ops:
  0.7 0.7 slice_bitcast_fusion.8
  1.4 1.0 convert_reduce_fusion
  2.4 0.8 reduce
  3.2 0.6 reshape.78.refs_4_
  3.8 0.8 stack.48
  4.7 1.9 slice_bitcast_fusion.5
  7.3 0.9 pad.24.refs_3_
  8.1 0.9 pad.25.refs_4_
  9.0 0.8 fusion.3.bias_ref.refs_1_
  9.8 193.7 %shard_map.254 = (bf16[16,216,128]{2,1,0:T(8,128)(2,1)}, f32[16,1,128]{2,1,0:T(1,128)}, bf16[16,72,128]{2,1,0:T(8,128)(2,1)}, bf16[4,4,72,128]{3,2,1,0:T(8,128)(...) custom-call(s32[2,16]{1,0:T(2,128)} %copy-done.14, ...), custom_call_target="tpu_custom_call" | custom-call | tf_op jit(solution)/shard_map/pallas_call | solution.py:780
  203.5 1.1 copy.51
  204.7 0.6 fusion.5.bias_ref
  205.3 22.2 %shard_map.255 = (f32[128,1152]{1,0:T(8,128)}, f32[128,4352]{1,0:T(8,128)}, bf16[128,4352]{1,0:T(8,128)(2,1)}, bf16[4,4,72,128]{3,2,1,0:T(8,128)(2,1)}, bf16[4,4...) custom-call(bf16[128,1152]{1,0:T(8,128)(2,1)} %get-tuple-element.224.tok_ref.refs_0_.refs_1_.inc_ref, ...), custom_call_target="tpu_custom_call" | custom-call | tf_op jit(solution)/shard_map/pallas_call | solution.py:871
  227.5 7.0 shard_map.256
  234.5 41.1 %shard_map.257 = (bf16[16,216,128]{2,1,0:T(8,128)(2,1)}, f32[16,1,128]{2,1,0:T(1,128)}, bf16[16,72,128]{2,1,0:T(8,128)(2,1)}) custom-call(s32[2,16]{1,0:T(2,128)} %copy-done.14, f32[2,16,6,128]{3,2,1,0:T(8,128)} %fusion.3.bias_ref.refs_1_, bf16[16,216,128]{2,1,0:T(8,128)(2,1)} %get-tuple-element.120.refs_2_), custom_call_target="tpu_custom_call" | custom-call | tf_op jit(solution)/shard_map/pallas_call | solution.py:564
  275.7 12.7 %shard_map.258 = (f32[128,1152]{1,0:T(8,128)}, f32[128,4352]{1,0:T(8,128)}, bf16[128,4352]{1,0:T(8,128)(2,1)}, bf16[4,4,72,128]{3,2,1,0:T(8,128)(2,1)}, bf16[4,4...) custom-call(bf16[128,1152]{1,0:T(8,128)(2,1)} %get-tuple-element.225.tok_ref.refs_0_, ...), custom_call_target="tpu_custom_call" | custom-call | tf_op jit(solution)/shard_map/pallas_call | solution.py:871
  288.3 1.3 collective-permute-start
  289.7 0.9 slice_bitcast_fusion.2
  290.5 19.7 %shard_map.260 = (f32[128,1152]{1,0:T(8,128)}, bf16[16,72,128]{2,1,0:T(8,128)(2,1)}, bf16[4,4,72,128]{3,2,1,0:T(8,128)(2,1)}, bf16[128,4352]{1,0:T(8,128)(2,1)},...) custom-call(bf16[128,1152]{1,0:T(8,128)(2,1)} %get-tuple-element.223.cot_ref, ...), custom_call_target="tpu_custom_call" | custom-call | tf_op jit(solution)/shard_map/pallas_call | solution.py:957
  310.3 0.7 copy-done.1
  311.0 7.0 shard_map.259
  318.0 62.0 %shard_map.261 = (bf16[16,216,128]{2,1,0:T(8,128)(2,1)}, f32[16,1,128]{2,1,0:T(1,128)}, bf16[16,72,128]{2,1,0:T(8,128)(2,1)}, bf16[16,72,128]{2,1,0:T(8,128)(2,1...) custom-call(s32[2,16]{1,0:T(2,128)} %copy-done.14, ...), custom_call_target="tpu_custom_call" | custom-call | tf_op jit(solution)/shard_map/pallas_call | solution.py:564
  380.0 8.2 %shard_map.263 = (f32[128,1152]{1,0:T(8,128)}, bf16[3456,128]{1,0:T(8,128)(2,1)}, f32[2,1152]{1,0:T(2,128)}, f32[8,3456]{1,0:T(8,128)}) custom-call(bf16[128,1152]{1,0:T(8,128)(2,1)} %get-tuple-element.224.tok_ref.refs_0_.refs_1_.inc_ref, bf16[128,1152]{1,0:T(8,128)(2,1)} %get-tuple-element.118.inc_ref.refs_1_, f32[8,1152]{1,0:T(8,128)} %copy-done, ...), custom_call_target="tpu_custom_call" | custom-call | tf_op jit(solution)/shard_map/pallas_call | solution.py:1039
  388.2 1.1 convert_element_type.30
  389.3 3.7 collective-permute-start.1
  393.1 21.0 %shard_map.262 = (f32[128,1152]{1,0:T(8,128)}, f32[128,4352]{1,0:T(8,128)}, bf16[128,4352]{1,0:T(8,128)(2,1)}, bf16[4,4,72,128]{3,2,1,0:T(8,128)(2,1)}, bf16[4,4...) custom-call(bf16[128,1152]{1,0:T(8,128)(2,1)} %get-tuple-element.225.tok_ref.refs_0_, ...), custom_call_target="tpu_custom_call" | custom-call | tf_op jit(solution)/shard_map/pallas_call | solution.py:871
  414.1 1.0 select_bitcast_fusion.3
  415.1 0.9 maximum_bitcast_fusion.1
  416.0 0.7 copy-done.13
  416.7 23.3 %shard_map.264 = (f32[128,1152]{1,0:T(8,128)}, bf16[16,72,128]{2,1,0:T(8,128)(2,1)}, bf16[4,4,72,128]{3,2,1,0:T(8,128)(2,1)}, bf16[128,4352]{1,0:T(8,128)(2,1)},...) custom-call(bf16[128,1152]{1,0:T(8,128)(2,1)} %get-tuple-element.222.cot_ref,, ...), custom_call_target="tpu_custom_call" | custom-call | tf_op jit(solution)/shard_map/pallas_call | solution.py:957
  440.0 46.1 %shard_map.265 = (bf16[16,72,128]{2,1,0:T(8,128)(2,1)}, bf16[16,144,128]{2,1,0:T(8,128)(2,1)}, bf16[4,4,72,128]{3,2,1,0:T(8,128)(2,1)}, bf16[4,4,72,128]{3,2,1,0...) custom-call(s32[2,16]{1,0:T(2,128)} %copy-done.14, ...), custom_call_target="tpu_custom_call" | custom-call | tf_op jit(solution)/shard_map/pallas_call | solution.py:564
  486.2 16.8 %shard_map.266 = (f32[128,1152]{1,0:T(8,128)}, bf16[3456,128]{1,0:T(8,128)(2,1)}, f32[2,1152]{1,0:T(2,128)}, f32[8,3456]{1,0:T(8,128)}, bf16[128,1152]{1,0:T(8,128)(2,1)}) custom-call(bf16[128,1152]{1,0:T(8,128)(2,1)} %get-tuple-element.224.tok_ref.refs_0_.refs_1_.inc_ref, bf16[128,1152]{1,0:T(8,128)(2,1)} %copy-done.1, f32[8,1152]{1,0:T(8,128)} %copy-done, ...), custom_call_target="tpu_custom_call" | custom-call | tf_op jit(solution)/shard_map/pallas_call | solution.py:1039
  503.0 22.2 %shard_map.267 = (f32[128,1152]{1,0:T(8,128)}, bf16[16,72,128]{2,1,0:T(8,128)(2,1)}, bf16[4,4,72,128]{3,2,1,0:T(8,128)(2,1)}, bf16[128,4352]{1,0:T(8,128)(2,1)},...) custom-call(bf16[128,1152]{1,0:T(8,128)(2,1)} %get-tuple-element.222.cot_ref,, ...), custom_call_target="tpu_custom_call" | custom-call | tf_op jit(solution)/shard_map/pallas_call | solution.py:957
  525.3 1.0 fusion.13
  526.6 43.8 %shard_map.268 = (bf16[16,72,128]{2,1,0:T(8,128)(2,1)}, bf16[16,144,128]{2,1,0:T(8,128)(2,1)}, bf16[4,4,72,128]{3,2,1,0:T(8,128)(2,1)}, bf16[4,4,72,128]{3,2,1,0:T(8,128)(2,1)}, bf16[4,128,2048]{2,1,0:T(8,128)(2,1)}) custom-call(s32[2,16]{1,0:T(2,128)} %copy-done.14, f32[2,16,6,128]{3,2,1,0:T(8,128)} %fusion.3.bias_ref.refs_1_, ...), custom_call_target="tpu_custom_call" | custom-call | tf_op jit(solution)/shard_map/pallas_call | solution.py:564
  570.4 14.2 %shard_map.269 = (f32[128,1152]{1,0:T(8,128)}, bf16[3456,128]{1,0:T(8,128)(2,1)}, f32[2,1152]{1,0:T(2,128)}, f32[8,3456]{1,0:T(8,128)}, bf16[4,128,1152]{2,1,0:T(8,128)(2,1)}) custom-call(bf16[128,1152]{1,0:T(8,128)(2,1)} %get-tuple-element.225.tok_ref.refs_0_, bf16[128,1152]{1,0:T(8,128)(2,1)} %copy-done.1, f32[8,1152]{1,0:T(8,128)} %copy-done, ...), custom_call_target="tpu_custom_call" | custom-call | tf_op jit(solution)/shard_map/pallas_call | solution.py:1039
  584.6 1.0 fusion.7
  586.2 0.8 select_maximum_fusion.refs_0_
  587.0 142.7 %shard_map.270 = (f32[48,128]{1,0:T(8,128)}, f32[72,4352]{1,0:T(8,128)}, f32[72,4352]{1,0:T(8,128)}, f32[72,1152]{1,0:T(8,128)}, f32[72,3456]{1,0:T(8,128)}) custom-call(f32[16,48,128]{2,1,0:T(8,128)} %select_maximum_fusion.refs_0_, bf16[4,4,72,128]{3,2,1,0:T(8,128)(2,1)} %get-tuple-element.185.refs_1_, bf16[4,4,72,128]{3,2,1,0:T(8,128)(2,1)} %get-tuple-element.186.refs_2_, ...), custom_call_target="tpu_custom_call" | custom-call | tf_op jit(solution)/shard_map/pallas_call | solution.py:1254
  729.7 1.2 slice_bitcast_fusion.7
  730.9 1.4 fusion.15
  732.4 0.7 slice_bitcast_fusion.6
  733.1 0.6 broadcast_in_dim.58
  733.7 2.5 slice_bitcast_fusion.1
  736.2 1.1 slice_bitcast_fusion
  738.2 1.1 maximum_bitcast_fusion
  739.8 0.9 copy.54
  740.8 0.7 copy.55
  (64 shorter events, 3.1 us)
Async XLA Ops:
  0.6 6.6 copy-start.5
  2.4 6.6 copy-start.14
  3.8 4.3 copy-start.6
  204.6 0.7 copy-start
  275.7 14.0 %copy-start.7 = (bf16[2,128,1152]{2,1,0:T(8,128)(2,1)S(1)}, bf16[2,128,1152]{2,1,0:T(8,128)(2,1)}, u32[]{:S(2)}) copy-start(bf16[2,128,1152]{2,1,0:T(8,128)(2,1)} %param.16) | copy-start | bytes 1769476
  288.3 21.9 %collective-permute-start = (bf16[128,1152]{1,0:T(8,128)(2,1)}, bf16[128,1152]{1,0:T(8,128)(2,1)S(1)}, u32[]{:S(2)}, u32[]{:S(2)}) collective-permute-start(bf16[128,1152]{1,0:T(8,128)(2,1)} %get-tuple-element.122), channel_id=1, source_target_pairs={{0,16},{1,17},{2,18},{3,19},{4,20},{5,21},{6,22},{7,23},{8,24},{9,... | collective-permute-start | bytes 884744 | tf_op jit(solution)/shard_map/ppermute | solution.py:1342
  310.3 0.7 copy-start.1
  389.3 26.7 %collective-permute-start.1 = (bf16[128,1152]{1,0:T(8,128)(2,1)S(1)}, bf16[128,1152]{1,0:T(8,128)(2,1)S(1)}, u32[]{:S(2)}, u32[]{:S(2)}) collective-permute-start(bf16[128,1152]{1,0:T(8,128)(2,1)S(1)} %convert_element_type.30), channel_id=1, source_target_pairs={{16,0},{17,1},{18,2},{19,3},{20,4},{21,5},{22,6},{23,7},{24,8},{25... | collective-permute-start | bytes 884744 | tf_op jit(solution)/shard_map/ppermute | solution.py:1357
  393.0 21.1 %copy-start.11 = (bf16[128,1152]{1,0:T(8,128)(2,1)S(1)}, bf16[128,1152]{1,0:T(8,128)(2,1)}, u32[]{:S(2)}) copy-start(bf16[128,1152]{1,0:T(8,128)(2,1)} %get-tuple-element.117) | copy-start | bytes 884740
  393.0 21.1 %copy-start.12 = (bf16[128,1152]{1,0:T(8,128)(2,1)S(1)}, bf16[128,1152]{1,0:T(8,128)(2,1)}, u32[]{:S(2)}) copy-start(bf16[128,1152]{1,0:T(8,128)(2,1)} %get-tuple-element.122) | copy-start | bytes 884740
  416.0 0.7 copy-start.13
  503.0 22.3 %copy-start.15 = (f32[4,1152]{1,0:T(4,128)S(1)}, f32[4,1152]{1,0:T(4,128)}, u32[]{:S(2)}) copy-start(f32[4,1152]{1,0:T(4,128)} %get-tuple-element.181) | copy-start | bytes 55300
  503.0 22.3 %copy-start.16 = (f32[4,1152]{1,0:T(4,128)S(1)}, f32[4,1152]{1,0:T(4,128)}, u32[]{:S(2)}) copy-start(f32[4,1152]{1,0:T(4,128)} %get-tuple-element.179) | copy-start | bytes 55300
  570.4 14.2 %copy-start.20 = (f32[2,1152]{1,0:T(2,128)S(1)}, f32[2,1152]{1,0:T(2,128)}, u32[]{:S(2)}) copy-start(f32[2,1152]{1,0:T(2,128)} %get-tuple-element.175) | copy-start | bytes 27652
  570.4 14.2 %copy-start.21 = (f32[2,1152]{1,0:T(2,128)S(1)}, f32[2,1152]{1,0:T(2,128)}, u32[]{:S(2)}) copy-start(f32[2,1152]{1,0:T(2,128)} %get-tuple-element.173) | copy-start | bytes 27652
  570.4 15.6 %copy-start.17 = (f32[1,4352]{1,0:T(1,128)S(1)}, f32[1,4352]{1,0:T(1,128)}, u32[]{:S(2)}) copy-start(f32[1,4352]{1,0:T(1,128)} %get-tuple-element.184) | copy-start | bytes 52228
  570.4 15.6 %copy-start.18 = (f32[1,4352]{1,0:T(1,128)S(1)}, f32[1,4352]{1,0:T(1,128)}, u32[]{:S(2)}) copy-start(f32[1,4352]{1,0:T(1,128)} %get-tuple-element.182) | copy-start | bytes 52228
  570.4 15.6 %copy-start.19 = (f32[1,4352]{1,0:T(1,128)S(1)}, f32[1,4352]{1,0:T(1,128)}, u32[]{:S(2)}) copy-start(f32[1,4352]{1,0:T(1,128)} %get-tuple-element.183) | copy-start | bytes 52228
  733.7 2.5 copy-start.3
  736.2 1.2 copy-start.2
  736.2 1.7 copy-start.8
  736.2 1.9 copy-start.9
  738.2 1.6 copy-start.4
  739.3 1.5 copy-start.10

commit v6 on v5

--- a/solution.py
+++ b/solution.py
@@ -29,8 +29,8 @@
 
 
 class Gather:
-    def __init__(self, pieces, ins, outs, sems):
-        self.pieces, self.ins, self.outs, self.count = pieces, ins, outs, len(pieces)
+    def __init__(self, pieces, ins, outs, sems, twice=()):
+        self.pieces, self.ins, self.outs, self.count, self.twice = pieces, ins, outs, len(pieces), twice
         self.local_sem = sems[0]
         self.up, self.down, self.yy, self.cc = [(sems[1 + 2 * i], sems[2 + 2 * i]) for i in range(4)]
         self.sec, self.me = place()
@@ -41,7 +41,7 @@
     @staticmethod
     def semaphores(pieces, arrays):
         dma = pltpu.SemaphoreType.DMA
-        return [dma((arrays,))] + [dma((pieces, 4))] * 6 + [dma((pieces, 8))] * 2
+        return [dma((arrays,))] + [dma((pieces, 8))] * 4 + [dma((pieces, 4))] * 2 + [dma((pieces, 8))] * 2
 
     def part(self, piece, origin=None):
         array, at, end = self.pieces[piece]
@@ -60,35 +60,45 @@
     def mine(self, array):
         return pltpu.make_async_copy(self.ins[array], self.outs[array].at[self.me], self.local_sem.at[array])
 
-    def along(self, piece, origin, first, go_up, go_down):
-        zo = origin // 4
+    def along(self, piece, origin, first, go_up, go_down, column=0):
+        slot = origin // 4 + 4 * column
         if go_up:
 
             @pl.when(self.z < 3)
             def _():
-                self.send(piece, origin, self.up, zo, self.me + 4, first).start()
+                self.send(piece, origin, self.up, slot, self.me + 4, first).start()
 
         if go_down:
 
             @pl.when(self.z > 0)
             def _():
-                self.send(piece, origin, self.down, zo, self.me - 4, first).start()
-
-        self.send(piece, origin, self.yy, zo, self.other_y, first).start()
-        self.send(piece, origin, self.cc, zo, self.other_c, first).start()
+                self.send(piece, origin, self.down, slot, self.me - 4, first).start()
+
+        if piece not in self.twice or first:
+            self.send(piece, origin, self.yy, origin // 4, self.other_y, first).start()
+        self.send(piece, origin, self.cc, slot, self.other_c, first).start()
+
+    def columns(self, piece):
+        return (0, 1) if piece in self.twice else (0,)
 
     def step(self, piece, step):
+        if step == 1 and piece in self.twice:
+            self.send(piece, self.other_y, self.yy, self.z, self.other_y).wait_recv()
+            self.along(piece, self.other_y, False, True, True, 1)
+
         @pl.when(self.z - step >= 0)
         def _():
-            origin = self.me - 4 * step
-            self.send(piece, origin, self.up, self.z - step, self.me).wait_recv()
-            self.along(piece, origin, False, True, False)
+            for column in self.columns(piece):
+                origin = (self.me, self.other_y)[column] - 4 * step
+                self.send(piece, origin, self.up, self.z - step + 4 * column, self.me).wait_recv()
+                self.along(piece, origin, False, True, False, column)
 
         @pl.when(self.z + step <= 3)
         def _():
-            origin = self.me + 4 * step
-            self.send(piece, origin, self.down, self.z + step, self.me).wait_recv()
-            self.along(piece, origin, False, False, True)
+            for column in self.columns(piece):
+                origin = (self.me, self.other_y)[column] + 4 * step
+                self.send(piece, origin, self.down, self.z + step + 4 * column, self.me).wait_recv()
+                self.along(piece, origin, False, False, True, column)
 
     def slots(self, first, last):
         for k in range(first, last):
@@ -104,7 +114,7 @@
     def across(self, pieces):
         far = self.other_y % 4
         for piece in pieces:
-            for step in range(4):
+            for step in range(0 if piece in self.twice else 4):
                 zo = (self.z + step) % 4
                 origin = zo * 4 + far
                 self.send(piece, origin, self.yy, zo, self.other_y).wait_recv()
@@ -118,17 +128,22 @@
     def finish(self):
         for zo in range(4):
             for piece in range(self.count):
-                self.send(piece, self.me, self.yy, zo, self.other_y).wait_send()
+                if piece not in self.twice:
+                    self.send(piece, self.me, self.yy, zo, self.other_y).wait_send()
+                elif zo == 0:
+                    self.send(piece, self.me, self.yy, self.z, self.other_y).wait_send()
                 for slot in (zo, 4 + zo):
                     self.send(piece, self.me, self.cc, slot, self.other_c).wait_send()
 
                 @pl.when((zo <= self.z) & (self.z < 3))
                 def _():
-                    self.send(piece, self.me, self.up, zo, self.me).wait_send()
+                    for column in self.columns(piece):
+                        self.send(piece, self.me, self.up, zo + 4 * column, self.me).wait_send()
 
                 @pl.when((zo >= self.z) & (self.z > 0))
                 def _():
-                    self.send(piece, self.me, self.down, zo, self.me).wait_send()
+                    for column in self.columns(piece):
+                        self.send(piece, self.me, self.down, zo + 4 * column, self.me).wait_send()
 
 
 def flip(low, k):
@@ -717,7 +732,7 @@
     whole = take(3)
     w_buf, t_buf, x_buf, w_sem = take(4)
     f = Forward(0, (first_ref, bias_ref), x_buf, ahead_out, take(len(Forward.scratch(HEADS))))
-    work = Gather(first_pieces(shards), shards, (w_buf, small_all, *whole), take(9))
+    work = Gather(first_pieces(shards), shards, (w_buf, small_all, *whole), take(9), TWICE)
     soon, later = [list(range(SOON)), list(range(SOON, work.count))]
     sec, me = place()
     greet_all(HEADS, sec, me)
@@ -764,6 +779,7 @@
 
 
 SOON = 4
+TWICE = (4,)
 
 
 def first_pieces(shards):
@@ -1101,7 +1117,8 @@
         if cols is not None:
             dst = dst.at[:, :, cols[0] : cols[1]]
         loads.append((name, pltpu.make_async_copy(early_refs[i], dst, early_sem.at[i])))
-        loads[-1][1].start()
+        if name == "fc2":
+            loads[-1][1].start()
     behind = []
     for i, (name, batch, item) in enumerate(late):
 
@@ -1157,6 +1174,8 @@
         for other, load in loads:
             if other == name:
                 load.wait()
+            elif name == "fc2":
+                load.start()
         for other, one in behind:
             if other == name:
                 one.finish()
@@ -1347,7 +1366,8 @@
     def second_batch(name, cols=None):
         return Whole(saved[1][name], saved[2][name], cols)
 
-    residual_grad, att_grad, sums, _ = feed_back(0, tokens[0])
+    residual_grad, att_grad, sums, got = feed_back(0, tokens[0], 11, [first_batch("hidden", (SPLIT, FFP))])
+    sent["h0b"] = got[0]
     qkv, n1 = qkv_forward(*token_inputs(2), vec, b_qkv, w_qkv)
     items = [Rows(saved[0][name], saved[1][name]) for name in ("n1", "att", "n2")]
     items.append(first_batch("hidden", (0, SPLIT)))
@@ -1355,7 +1375,7 @@
     sent["n1_0"], sent["att_0"], sent["n2_0"], sent["h0a"] = got
     qkv_back(0, residual_grad, *two, sums, None, False)
     incoming_grad = lax.ppermute(input_grads[0].astype(BF), "section", [(1, 0)])
-    sent["h0b"] = feed(2, *three, n1, 11, False, [first_batch("hidden", (SPLIT, FFP))])[6]
+    feed(2, *three, n1, None, False)
     outputs = jnp.stack([choose(saved[m]["low"], saved[m + 1]["low"]) for m in range(2)])
 
     residual_grad, att_grad, sums, got = feed_back(1, incoming_grad, 12, [second_batch("hidden", (0, SPLIT))])
@@ -1374,9 +1394,7 @@
     items.append(Whole(back[1]["pre"], back[0]["pre"], (SPLIT, FFP)))
     _, two, got = attention(near, 6, behind=(2, att_grad, kept(2, "qkv", "lse")), items=items)
     sent["fc_0"], sent["fc_1"], sent["pre_0b"] = got
-    sent["branch_0"] = qkv_back(
-        2, residual_grad, *two, sums, 14, False, [Whole(back[1]["branch"], back[0]["branch"])]
-    )[0]
+    qkv_back(2, residual_grad, *two, sums, None, False)
     input_grads = jnp.stack([choose(input_grads[m + 1], input_grads[m]) for m in range(2)])
 
     sums = [choose(done[1][i] + done[2][i], done[0][i] + done[1][i]) for i in range(9)]
@@ -1398,12 +1416,12 @@
         ("fc2", 1, (SPLIT, FFP), sent["h1b"]),
         ("fc1", 0, (0, SPLIT), sent["pre_0a"]),
         ("fc1", 0, (SPLIT, FFP), sent["pre_0b"]),
-        ("out", 0, None, sent["branch_0"]),
     ]
     late = [
         ("fc1", 1, Whole(back[2]["pre"], back[1]["pre"])),
         ("qkv", 0, Whole(back[1]["dqkv"], back[0]["dqkv"])),
         ("qkv", 1, Whole(back[2]["dqkv"], back[1]["dqkv"])),
+        ("out", 0, Whole(back[1]["branch"], back[0]["branch"])),
         ("out", 1, Whole(back[2]["branch"], back[1]["branch"])),
     ]
     packed, grads = final(jnp.concatenate([by_owner, to_all], axis=1), xs, early, late, 10)

time: 755 us -> 734 us (0.972)
  Pallas kernels: 704 us -> 682 us
    pallas_call x1, Pallas kernels: 194 us -> 185 us  [first_tick(): pl.pallas_call(first_kernel, out_shape=Forward.shapes(HEADS) + [jax.Shape...]
    pallas_call x3, Pallas kernels: 55.9 us -> 47.5 us  [feed_forward(): pl.pallas_call(functools.partial(feed_kernel, shift, load), out_shape=[ja...]
where the time goes in v6:
time: 734 us; the launch traced here: 721 us
  Pallas kernels  682 us (93%)
  local copies, waits for them, and re-layouts  21.5 us (3%)
  other arithmetic  10.2 us (1%)
    pallas_call x4, Pallas kernels, attention(): pl.pallas_call(functools.partial(attention_kernel, ahead and ahead[0], be...  193 us
    pallas_call x1, Pallas kernels, first_tick(): pl.pallas_call(first_kernel, out_shape=Forward.shapes(HEADS) + [jax.Shape...  185 us
    pallas_call x1, Pallas kernels, final(): pl.pallas_call(functools.partial(final_kernel, tiles, [e[:3] for e in ear...  143 us
    pallas_call x3, Pallas kernels, feed_backward(): pl.pallas_call(functools.partial(feed_back_kernel, load), out_shape=[jax....  67 us
    pallas_call x3, Pallas kernels, feed_forward(): pl.pallas_call(functools.partial(feed_kernel, shift, load), out_shape=[ja...  47.5 us
    pallas_call x3, Pallas kernels, qkv_backward(): pl.pallas_call(functools.partial(qkv_back_kernel, shift, load), out_shape...  33.1 us
  transfers between devices with their start and end apart: 2, of which 0 were waited for; matrix products, arithmetic and copies ran while one was open for 0% of the time, Pallas kernels for 5%

profile of v6, /device:TPU:10, one launch (start us, length us, event | category | flops | bytes accessed | tf_op | source)
XLA Modules:
  0.0 720.6 jit_solution(17876339033271269988)
XLA Ops:
  0.7 0.7 slice_bitcast_fusion.8
  1.4 1.0 convert_reduce_fusion
  2.4 0.8 reduce
  3.2 0.6 reshape.78.refs_4_
  3.8 0.8 stack.48
  4.7 1.9 slice_bitcast_fusion.5
  7.2 0.9 pad.24.refs_3_
  8.1 0.9 pad.25.refs_4_
  9.0 0.8 fusion.3.bias_ref.refs_1_
  9.8 185.0 %shard_map.254 = (bf16[16,216,128]{2,1,0:T(8,128)(2,1)}, f32[16,1,128]{2,1,0:T(1,128)}, bf16[16,72,128]{2,1,0:T(8,128)(2,1)}, bf16[4,4,72,128]{3,2,1,0:T(8,128)(...) custom-call(s32[2,16]{1,0:T(2,128)} %copy-done.14, ...), custom_call_target="tpu_custom_call" | custom-call | tf_op jit(solution)/shard_map/pallas_call | solution.py:796
  194.8 1.1 copy.51
  195.9 0.6 fusion.5.bias_ref
  196.6 22.2 %shard_map.255 = (f32[128,1152]{1,0:T(8,128)}, f32[128,4352]{1,0:T(8,128)}, bf16[128,4352]{1,0:T(8,128)(2,1)}, bf16[4,4,72,128]{3,2,1,0:T(8,128)(2,1)}, bf16[4,4...) custom-call(bf16[128,1152]{1,0:T(8,128)(2,1)} %get-tuple-element.222.tok_ref.refs_0_.refs_1_.inc_ref, ...), custom_call_target="tpu_custom_call" | custom-call | tf_op jit(solution)/shard_map/pallas_call | solution.py:887
  218.7 7.0 shard_map.256
  225.7 42.4 %shard_map.257 = (bf16[16,216,128]{2,1,0:T(8,128)(2,1)}, f32[16,1,128]{2,1,0:T(1,128)}, bf16[16,72,128]{2,1,0:T(8,128)(2,1)}) custom-call(s32[2,16]{1,0:T(2,128)} %copy-done.14, f32[2,16,6,128]{3,2,1,0:T(8,128)} %fusion.3.bias_ref.refs_1_, bf16[16,216,128]{2,1,0:T(8,128)(2,1)} %get-tuple-element.119.refs_2_), custom_call_target="tpu_custom_call" | custom-call | tf_op jit(solution)/shard_map/pallas_call | solution.py:579
  268.1 12.6 %shard_map.258 = (f32[128,1152]{1,0:T(8,128)}, f32[128,4352]{1,0:T(8,128)}, bf16[128,4352]{1,0:T(8,128)(2,1)}, bf16[4,4,72,128]{3,2,1,0:T(8,128)(2,1)}, bf16[4,4...) custom-call(bf16[128,1152]{1,0:T(8,128)(2,1)} %get-tuple-element.223.tok_ref.refs_0_, ...), custom_call_target="tpu_custom_call" | custom-call | tf_op jit(solution)/shard_map/pallas_call | solution.py:887
  280.8 1.3 collective-permute-start
  282.1 0.9 slice_bitcast_fusion.2
  283.0 21.5 %shard_map.260 = (f32[128,1152]{1,0:T(8,128)}, bf16[16,72,128]{2,1,0:T(8,128)(2,1)}, bf16[4,4,72,128]{3,2,1,0:T(8,128)(2,1)}, bf16[128,4352]{1,0:T(8,128)(2,1)},...) custom-call(bf16[128,1152]{1,0:T(8,128)(2,1)} %get-tuple-element.221.cot_ref,, ...), custom_call_target="tpu_custom_call" | custom-call | tf_op jit(solution)/shard_map/pallas_call | solution.py:973
  304.5 0.7 copy-done.1
  305.2 7.0 shard_map.259
  312.2 60.8 %shard_map.261 = (bf16[16,216,128]{2,1,0:T(8,128)(2,1)}, f32[16,1,128]{2,1,0:T(1,128)}, bf16[16,72,128]{2,1,0:T(8,128)(2,1)}, bf16[16,72,128]{2,1,0:T(8,128)(2,1...) custom-call(s32[2,16]{1,0:T(2,128)} %copy-done.14, ...), custom_call_target="tpu_custom_call" | custom-call | tf_op jit(solution)/shard_map/pallas_call | solution.py:579
  373.1 8.2 %shard_map.263 = (f32[128,1152]{1,0:T(8,128)}, bf16[3456,128]{1,0:T(8,128)(2,1)}, f32[2,1152]{1,0:T(2,128)}, f32[8,3456]{1,0:T(8,128)}) custom-call(bf16[128,1152]{1,0:T(8,128)(2,1)} %get-tuple-element.222.tok_ref.refs_0_.refs_1_.inc_ref, bf16[128,1152]{1,0:T(8,128)(2,1)} %get-tuple-element.117.inc_ref.refs_1_, f32[8,1152]{1,0:T(8,128)} %copy-done, ...), custom_call_target="tpu_custom_call" | custom-call | tf_op jit(solution)/shard_map/pallas_call | solution.py:1055
  381.2 1.1 convert_element_type.30
  382.3 4.1 collective-permute-start.1
  386.4 12.7 %shard_map.262 = (f32[128,1152]{1,0:T(8,128)}, f32[128,4352]{1,0:T(8,128)}, bf16[128,4352]{1,0:T(8,128)(2,1)}, bf16[4,4,72,128]{3,2,1,0:T(8,128)(2,1)}, bf16[4,4...) custom-call(bf16[128,1152]{1,0:T(8,128)(2,1)} %get-tuple-element.223.tok_ref.refs_0_, bf16[128,1152]{1,0:T(8,128)(2,1)} %copy-done.1, ...), custom_call_target="tpu_custom_call" | custom-call | tf_op jit(solution)/shard_map/pallas_call | solution.py:887
  399.1 1.0 select_bitcast_fusion.3
  400.2 0.9 maximum_bitcast_fusion.1
  401.1 0.7 copy-done.13
  401.8 22.4 %shard_map.264 = (f32[128,1152]{1,0:T(8,128)}, bf16[16,72,128]{2,1,0:T(8,128)(2,1)}, bf16[4,4,72,128]{3,2,1,0:T(8,128)(2,1)}, bf16[128,4352]{1,0:T(8,128)(2,1)},...) custom-call(bf16[128,1152]{1,0:T(8,128)(2,1)} %get-tuple-element.220.cot_ref,, ...), custom_call_target="tpu_custom_call" | custom-call | tf_op jit(solution)/shard_map/pallas_call | solution.py:973
  424.3 46.8 %shard_map.265 = (bf16[16,72,128]{2,1,0:T(8,128)(2,1)}, bf16[16,144,128]{2,1,0:T(8,128)(2,1)}, bf16[4,4,72,128]{3,2,1,0:T(8,128)(2,1)}, bf16[4,4,72,128]{3,2,1,0...) custom-call(s32[2,16]{1,0:T(2,128)} %copy-done.14, ...), custom_call_target="tpu_custom_call" | custom-call | tf_op jit(solution)/shard_map/pallas_call | solution.py:579
  471.1 16.8 %shard_map.266 = (f32[128,1152]{1,0:T(8,128)}, bf16[3456,128]{1,0:T(8,128)(2,1)}, f32[2,1152]{1,0:T(2,128)}, f32[8,3456]{1,0:T(8,128)}, bf16[128,1152]{1,0:T(8,128)(2,1)}) custom-call(bf16[128,1152]{1,0:T(8,128)(2,1)} %get-tuple-element.222.tok_ref.refs_0_.refs_1_.inc_ref, bf16[128,1152]{1,0:T(8,128)(2,1)} %copy-done.1, f32[8,1152]{1,0:T(8,128)} %copy-done, ...), custom_call_target="tpu_custom_call" | custom-call | tf_op jit(solution)/shard_map/pallas_call | solution.py:1055
  487.9 23.0 %shard_map.267 = (f32[128,1152]{1,0:T(8,128)}, bf16[16,72,128]{2,1,0:T(8,128)(2,1)}, bf16[4,4,72,128]{3,2,1,0:T(8,128)(2,1)}, bf16[128,4352]{1,0:T(8,128)(2,1)},...) custom-call(bf16[128,1152]{1,0:T(8,128)(2,1)} %get-tuple-element.220.cot_ref,, ...), custom_call_target="tpu_custom_call" | custom-call | tf_op jit(solution)/shard_map/pallas_call | solution.py:973
  511.0 1.0 fusion.13
  512.4 42.9 %shard_map.268 = (bf16[16,72,128]{2,1,0:T(8,128)(2,1)}, bf16[16,144,128]{2,1,0:T(8,128)(2,1)}, bf16[4,4,72,128]{3,2,1,0:T(8,128)(2,1)}, bf16[4,4,72,128]{3,2,1,0:T(8,128)(2,1)}, bf16[4,128,2048]{2,1,0:T(8,128)(2,1)}) custom-call(s32[2,16]{1,0:T(2,128)} %copy-done.14, f32[2,16,6,128]{3,2,1,0:T(8,128)} %fusion.3.bias_ref.refs_1_, ...), custom_call_target="tpu_custom_call" | custom-call | tf_op jit(solution)/shard_map/pallas_call | solution.py:579
  555.4 8.1 %shard_map.269 = (f32[128,1152]{1,0:T(8,128)}, bf16[3456,128]{1,0:T(8,128)(2,1)}, f32[2,1152]{1,0:T(2,128)}, f32[8,3456]{1,0:T(8,128)}) custom-call(bf16[128,1152]{1,0:T(8,128)(2,1)} %get-tuple-element.223.tok_ref.refs_0_, bf16[128,1152]{1,0:T(8,128)(2,1)} %copy-done.1, f32[8,1152]{1,0:T(8,128)} %copy-done, f32[128,1152]{1,0:T(8,128)} %get-tuple-element.162.refs_3_, ...), custom_call_target="tpu_custom_call" | custom-call | tf_op jit(solution)/shard_map/pallas_call | solution.py:1055
  563.5 1.0 fusion.7
  565.1 0.8 select_maximum_fusion.refs_0_
  565.9 142.7 %shard_map.270 = (f32[48,128]{1,0:T(8,128)}, f32[72,4352]{1,0:T(8,128)}, f32[72,4352]{1,0:T(8,128)}, f32[72,1152]{1,0:T(8,128)}, f32[72,3456]{1,0:T(8,128)}) custom-call(f32[16,48,128]{2,1,0:T(8,128)} %select_maximum_fusion.refs_0_, bf16[4,4,72,128]{3,2,1,0:T(8,128)(2,1)} %get-tuple-element.182.refs_1_, bf16[4,4,72,128]{3,2,1,0:T(8,128)(2,1)} %get-tuple-element.183.refs_2_, ...), custom_call_target="tpu_custom_call" | custom-call | tf_op jit(solution)/shard_map/pallas_call | solution.py:1273
  708.6 1.2 slice_bitcast_fusion.7
  709.8 1.4 fusion.15
  711.3 0.7 slice_bitcast_fusion.6
  712.0 0.6 broadcast_in_dim.58
  712.6 2.5 slice_bitcast_fusion.1
  715.1 1.1 slice_bitcast_fusion
  717.1 1.1 maximum_bitcast_fusion
  718.7 0.9 copy.54
  719.7 0.7 copy.55
  (64 shorter events, 3.1 us)
Async XLA Ops:
  0.6 6.6 copy-start.5
  2.4 6.6 copy-start.14
  3.8 4.3 copy-start.6
  195.9 0.7 copy-start
  268.1 14.0 %copy-start.7 = (bf16[2,128,1152]{2,1,0:T(8,128)(2,1)S(1)}, bf16[2,128,1152]{2,1,0:T(8,128)(2,1)}, u32[]{:S(2)}) copy-start(bf16[2,128,1152]{2,1,0:T(8,128)(2,1)} %param.16) | copy-start | bytes 1769476
  280.8 23.7 %collective-permute-start = (bf16[128,1152]{1,0:T(8,128)(2,1)}, bf16[128,1152]{1,0:T(8,128)(2,1)S(1)}, u32[]{:S(2)}, u32[]{:S(2)}) collective-permute-start(bf16[128,1152]{1,0:T(8,128)(2,1)} %get-tuple-element.121), channel_id=1, source_target_pairs={{0,16},{1,17},{2,18},{3,19},{4,20},{5,21},{6,22},{7,23},{8,24},{9,... | collective-permute-start | bytes 884744 | tf_op jit(solution)/shard_map/ppermute | solution.py:1361
  304.5 0.7 copy-start.1
  382.3 18.7 %collective-permute-start.1 = (bf16[128,1152]{1,0:T(8,128)(2,1)S(1)}, bf16[128,1152]{1,0:T(8,128)(2,1)S(1)}, u32[]{:S(2)}, u32[]{:S(2)}) collective-permute-start(bf16[128,1152]{1,0:T(8,128)(2,1)S(1)} %convert_element_type.30), channel_id=1, source_target_pairs={{16,0},{17,1},{18,2},{19,3},{20,4},{21,5},{22,6},{23,7},{24,8},{25... | collective-permute-start | bytes 884744 | tf_op jit(solution)/shard_map/ppermute | solution.py:1377
  386.4 12.7 %copy-start.11 = (bf16[128,1152]{1,0:T(8,128)(2,1)S(1)}, bf16[128,1152]{1,0:T(8,128)(2,1)}, u32[]{:S(2)}) copy-start(bf16[128,1152]{1,0:T(8,128)(2,1)} %get-tuple-element.116) | copy-start | bytes 884740
  386.4 12.7 %copy-start.12 = (bf16[128,1152]{1,0:T(8,128)(2,1)S(1)}, bf16[128,1152]{1,0:T(8,128)(2,1)}, u32[]{:S(2)}) copy-start(bf16[128,1152]{1,0:T(8,128)(2,1)} %get-tuple-element.121) | copy-start | bytes 884740
  401.1 0.7 copy-start.13
  487.9 23.1 %copy-start.15 = (f32[4,1152]{1,0:T(4,128)S(1)}, f32[4,1152]{1,0:T(4,128)}, u32[]{:S(2)}) copy-start(f32[4,1152]{1,0:T(4,128)} %get-tuple-element.178) | copy-start | bytes 55300
  487.9 23.1 %copy-start.16 = (f32[4,1152]{1,0:T(4,128)S(1)}, f32[4,1152]{1,0:T(4,128)}, u32[]{:S(2)}) copy-start(f32[4,1152]{1,0:T(4,128)} %get-tuple-element.176) | copy-start | bytes 55300
  555.3 8.2 %copy-start.20 = (f32[2,1152]{1,0:T(2,128)S(1)}, f32[2,1152]{1,0:T(2,128)}, u32[]{:S(2)}) copy-start(f32[2,1152]{1,0:T(2,128)} %get-tuple-element.172) | copy-start | bytes 27652
  555.3 8.2 %copy-start.21 = (f32[2,1152]{1,0:T(2,128)S(1)}, f32[2,1152]{1,0:T(2,128)}, u32[]{:S(2)}) copy-start(f32[2,1152]{1,0:T(2,128)} %get-tuple-element.170) | copy-start | bytes 27652
  555.4 9.5 %copy-start.17 = (f32[1,4352]{1,0:T(1,128)S(1)}, f32[1,4352]{1,0:T(1,128)}, u32[]{:S(2)}) copy-start(f32[1,4352]{1,0:T(1,128)} %get-tuple-element.181) | copy-start | bytes 52228
  555.4 9.5 %copy-start.18 = (f32[1,4352]{1,0:T(1,128)S(1)}, f32[1,4352]{1,0:T(1,128)}, u32[]{:S(2)}) copy-start(f32[1,4352]{1,0:T(1,128)} %get-tuple-element.179) | copy-start | bytes 52228
  555.4 9.5 %copy-start.19 = (f32[1,4352]{1,0:T(1,128)S(1)}, f32[1,4352]{1,0:T(1,128)}, u32[]{:S(2)}) copy-start(f32[1,4352]{1,0:T(1,128)} %get-tuple-element.180) | copy-start | bytes 52228
  712.6 2.5 copy-start.3
  715.1 1.2 copy-start.2
  715.1 1.7 copy-start.8
  715.1 1.9 copy-start.9
  717.1 1.6 copy-start.4
  718.2 1.5 copy-start.10

commit v7 on v6

--- a/solution.py
+++ b/solution.py
@@ -150,10 +150,11 @@
     return [low, low + 1 - 2 * (low % 2), (low + 2) % 4, 3 - low][k]
 
 
-def greet_all(count, sec, me):
+def greet_all(count, sec, me, meanwhile=lambda: None):
     barrier = pltpu.get_barrier_semaphore()
     for d in range(1, count):
         pl.semaphore_signal(barrier, inc=1, device_id=(sec, (me + d) % count), device_id_type=MESH)
+    meanwhile()
     pl.semaphore_wait(barrier, count - 1)
 
 
@@ -916,8 +917,8 @@
     kept, refs = refs[:4], refs[4:]
     out_w, fc1_w, fc2_w = refs[:3]
     sources, refs = refs[3 : 3 + 2 * n], refs[3 + 2 * n :]
-    rg_ref, ag_ref, fc_ref, pg_ref, branch_ref, sum_ref, fsum_ref = refs[:7]
-    outs, refs = refs[7 : 7 + n], refs[7 + n :]
+    rg_ref, ag_ref, fc_ref, pg_ref, branch_ref, sum_ref = refs[:6]
+    outs, refs = refs[6 : 6 + n], refs[6 + n :]
     pre_buf, res_buf, out_buf, fc1_buf, fc2_buf, t_buf, kept_sem, sems = refs[:8]
     sec, _ = place()
     pairs = []
@@ -939,7 +940,6 @@
         pre_wide = dot(fc_grad, fc2_buf[:, at:end]) * slope
         pre_grad = pre_wide.astype(BF)
         pg_ref[:, at:end] = pre_grad
-        fsum_ref[:, at:end] = jnp.sum(pre_grad.astype(F32), axis=0, keepdims=True)
         t_buf[at:end, :] = pre_wide.T.astype(BF)
     for at, end in slices(FFP):
         stream.wait("fc1", at)
@@ -979,11 +979,10 @@
             jax.ShapeDtypeStruct((tokens, FFP), BF),
             jax.ShapeDtypeStruct((tokens, D), BF),
             jax.ShapeDtypeStruct((4, D), F32),
-            jax.ShapeDtypeStruct((1, FFP), F32),
         ]
         + load.shapes,
         in_specs=[vmem] * 3 + [anywhere] * (7 + len(load.sources)),
-        out_specs=[vmem] * 7 + [anywhere] * len(load.shapes),
+        out_specs=[vmem] * 6 + [anywhere] * len(load.shapes),
         scratch_shapes=[
             pltpu.VMEM((tokens, FFP), F32),
             pltpu.VMEM((tokens, D), F32),
@@ -1090,13 +1089,13 @@
     x_refs = {name: take(2) for name in TENSORS}
     early_refs = take(len(early))
     late_refs = take(2 * len(late))
-    small_out = take(1)[0]
+    small_out, bias_out = take(2)
     out_refs = dict(zip(TENSORS, take(4)))
     y_bufs = dict(zip(TENSORS, take(4)))
     x_buf = take(1)[0]
     g_bufs, one_bufs, two_bufs = [dict(zip(TENSORS, take(4))) for _ in range(3)]
-    small_got = take(1)[0]
-    early_sem, small_send, small_recv = take(3)
+    small_got, bias_buf, bias_got = take(3)
+    early_sem, small_send, small_recv, bias_send, bias_recv = take(5)
     sems = {name: take(4) for name in TENSORS}
     late_sems = [take(3) for _ in late]
 
@@ -1104,7 +1103,6 @@
     z, low = me // 4, me % 4
     pair = z + 1 - 2 * (z % 2)
     count = small_ref.shape[0]
-    greet_all(count, sec, me)
 
     def begin(name):
         for other, one in behind:
@@ -1116,9 +1114,26 @@
         dst = y_bufs[name].at[4 * batch : 4 * batch + 4]
         if cols is not None:
             dst = dst.at[:, :, cols[0] : cols[1]]
-        loads.append((name, pltpu.make_async_copy(early_refs[i], dst, early_sem.at[i])))
-        if name == "fc2":
-            loads[-1][1].start()
+        loads.append((name, cols, pltpu.make_async_copy(early_refs[i], dst, early_sem.at[i])))
+
+    def place_rows(name):
+        rows = []
+        for owner in (z, 3 - z, pair, 3 - pair):
+            rows.append(
+                jnp.concatenate(
+                    [x_refs[name][batch][k, owner].astype(F32) for batch in range(2) for k in range(4)], axis=1
+                )
+            )
+        x_buf[...] = jnp.concatenate(rows, axis=0).astype(BF)
+
+    def meanwhile():
+        for cols in ((0, SPLIT), (SPLIT, FFP)):
+            for name, part, load in loads:
+                if name == "fc2" and part == cols:
+                    load.start()
+        place_rows("fc2")
+
+    greet_all(count, sec, me, meanwhile)
     behind = []
     for i, (name, batch, item) in enumerate(late):
 
@@ -1171,22 +1186,23 @@
                 one.forward()
         if name in ("fc1", "qkv"):
             begin({"fc1": "qkv", "qkv": "out"}[name])
-        for other, load in loads:
+        for other, _, load in loads:
             if other == name:
                 load.wait()
-            elif name == "fc2":
-                load.start()
         for other, one in behind:
             if other == name:
                 one.finish()
-        rows = []
-        for owner in (z, 3 - z, pair, 3 - pair):
-            rows.append(
-                jnp.concatenate(
-                    [x_refs[name][batch][k, owner].astype(F32) for batch in range(2) for k in range(4)], axis=1
-                )
-            )
-        x_buf[...] = jnp.concatenate(rows, axis=0).astype(BF)
+        place_rows(name)
+
+    def compute_first():
+        for cols in ((0, SPLIT), (SPLIT, FFP)):
+            for name, part, load in loads:
+                if name == "fc2" and part == cols:
+                    load.wait()
+                elif name != "fc2" and cols[0]:
+                    load.start()
+            width = tiles["fc2"][1]
+            lax.fori_loop(cols[0] // width, cols[1] // width, lambda i, carry: (compute("fc2", i), carry)[1], 0)
 
     def columns(name, i):
         width = tiles[name][1]
@@ -1202,8 +1218,21 @@
         else:
             y = jnp.concatenate([buf[part, :, columns(name, i)] for part in range(8)], axis=0)
             total = dot(x_buf[...], y)
+        if name == "fc1":
+            bias_buf[i] = dot(jnp.ones((8, y.shape[0]), BF), y)[0:1]
         g_bufs[name][i] = total.reshape(4, HEAD_DIM, width).astype(BF)
         first(name, i).start()
+
+    def bias_copy(k):
+        target = (me + 4 * k) % count
+        return pltpu.make_async_remote_copy(
+            src_ref=bias_buf,
+            dst_ref=bias_got.at[k - 1],
+            send_sem=bias_send.at[k - 1],
+            recv_sem=bias_recv.at[k - 1],
+            device_id=(sec, target),
+            device_id_type=MESH,
+        )
 
     def middle(name, i):
         first(name, i).wait_recv()
@@ -1225,10 +1254,12 @@
 
         lax.fori_loop(0, tiles[name][0], body, 0)
 
-    ready("fc2")
-    loop("fc2", (compute, "fc2"))
+    compute_first()
+    loop("fc2", (middle, "fc2"))
     ready("fc1")
-    loop("fc1", (compute, "fc1"), (middle, "fc2"))
+    loop("fc1", (compute, "fc1"))
+    for k in range(1, 4):
+        bias_copy(k).start()
     loop("fc1", (middle, "fc1"), (finish, "fc2"))
     ready("qkv")
     loop("qkv", (compute, "qkv"))
@@ -1243,6 +1274,9 @@
     for d in range(1, count):
         total = total + small_got[d]
     small_out[...] = total
+    for k in range(1, 4):
+        bias_copy(k).wait()
+    bias_out[...] = bias_buf[...] + bias_got[0] + bias_got[1] + bias_got[2]
     loop("qkv", (finish, "qkv"))
     loop("out", (finish, "out"))
 
@@ -1265,23 +1299,24 @@
     for lead in ((4,), (2,), ()):
         for name in TENSORS:
             scratch.append(pltpu.VMEM((tiles[name][0],) + lead + (HEAD_DIM, tiles[name][1]), BF))
-    scratch.append(pltpu.VMEM(small.shape, F32))
-    scratch += [dma((len(early),)), dma((count,)), dma((count,))]
+    bias = (tiles["fc1"][0], 1, tiles["fc1"][1])
+    scratch += [pltpu.VMEM(small.shape, F32), pltpu.VMEM(bias, F32), pltpu.VMEM((3,) + bias, F32)]
+    scratch += [dma((len(early),)), dma((count,)), dma((count,)), dma((3,)), dma((3,))]
     for name in TENSORS:
         scratch += [dma((tiles[name][0],))] * 4
     scratch += [dma, dma((4,)), dma((4,))] * len(late)
     out = pl.pallas_call(
         functools.partial(final_kernel, tiles, [e[:3] for e in early], late),
-        out_shape=[jax.ShapeDtypeStruct(small.shape[1:], F32)]
+        out_shape=[jax.ShapeDtypeStruct(small.shape[1:], F32), jax.ShapeDtypeStruct(bias, F32)]
         + [jax.ShapeDtypeStruct((HEAD_DIM, widths[name]), F32) for name in TENSORS],
         in_specs=[vmem] * n_vmem + [anywhere] * (len(args) - n_vmem),
-        out_specs=[vmem] * 5,
+        out_specs=[vmem] * 6,
         scratch_shapes=scratch,
         compiler_params=pltpu.CompilerParams(
             collective_id=cid, has_side_effects=True, vmem_limit_bytes=60 << 20
         ),
     )(*args)
-    return out[0], dict(zip(TENSORS, out[1:]))
+    return out[0], out[1].reshape(FFP), dict(zip(TENSORS, out[2:]))
 
 
 def on_device(
@@ -1338,11 +1373,11 @@
         return [saved[at][name] for name in names for at in ((1, 1), (0, 2), (1, 1))[tick]]
 
     def feed_back(tick, incoming_grad, cid=None, items=()):
-        residual_grad, att_grad, fc, pre, branch, four, fsum, *got = feed_backward(
+        residual_grad, att_grad, fc, pre, branch, four, *got = feed_backward(
             cotangent[min(tick, 1)], incoming_grad, vec, kept(tick, "pre", "residual"), w_out, w_fc1, w_fc2t, cid, items
         )
         back.append(dict(fc=fc, pre=pre, branch=branch))
-        return residual_grad, att_grad, [*four, fsum], got
+        return residual_grad, att_grad, list(four), got
 
     def qkv_back(tick, residual_grad, dq, dkv, sums, cid, shift, items=()):
         inputs = (tokens[max(tick - 1, 0)], incoming[min(tick + 1, 2)])
@@ -1386,10 +1421,7 @@
     sent["n1_1"], sent["att_1"], sent["n2_1"], sent["h1b"] = got
     incoming_grad = qkv_back(1, residual_grad, *two, sums, 9, True)[0]
 
-    residual_grad, att_grad, sums, got = feed_back(
-        2, incoming_grad, 13, [Whole(back[1]["pre"], back[0]["pre"], (0, SPLIT))]
-    )
-    sent["pre_0a"] = got[0]
+    residual_grad, att_grad, sums, _ = feed_back(2, incoming_grad)
     items = [Rows(back[1]["fc"], back[0]["fc"]), Rows(back[2]["fc"], back[1]["fc"])]
     items.append(Whole(back[1]["pre"], back[0]["pre"], (SPLIT, FFP)))
     _, two, got = attention(near, 6, behind=(2, att_grad, kept(2, "qkv", "lse")), items=items)
@@ -1397,12 +1429,9 @@
     qkv_back(2, residual_grad, *two, sums, None, False)
     input_grads = jnp.stack([choose(input_grads[m + 1], input_grads[m]) for m in range(2)])
 
-    sums = [choose(done[1][i] + done[2][i], done[0][i] + done[1][i]) for i in range(9)]
-    by_owner = jnp.stack(sums[:8]).reshape(8, HEADS, HEAD_DIM).transpose(1, 0, 2)
+    sums = [choose(done[1][i] + done[2][i], done[0][i] + done[1][i]) for i in range(8)]
+    by_owner = jnp.stack(sums).reshape(8, HEADS, HEAD_DIM).transpose(1, 0, 2)
     by_owner = jnp.pad(by_owner, ((0, 0), (0, 0), (0, BLOCK - HEAD_DIM)))
-    lines = FFP // BLOCK
-    to_all = jnp.broadcast_to(sums[8].reshape(1, lines, BLOCK), (HEADS, lines, BLOCK))
-    to_all = jnp.pad(to_all, ((0, 0), (0, 40 - lines), (0, 0)))
     xs = {
         "fc2": [sent["fc_0"], sent["fc_1"]],
         "fc1": [sent["n2_0"], sent["n2_1"]],
@@ -1414,19 +1443,19 @@
         ("fc2", 0, (SPLIT, FFP), sent["h0b"]),
         ("fc2", 1, (0, SPLIT), sent["h1a"]),
         ("fc2", 1, (SPLIT, FFP), sent["h1b"]),
-        ("fc1", 0, (0, SPLIT), sent["pre_0a"]),
         ("fc1", 0, (SPLIT, FFP), sent["pre_0b"]),
     ]
     late = [
+        ("fc1", 0, Whole(back[1]["pre"], back[0]["pre"], (0, SPLIT))),
         ("fc1", 1, Whole(back[2]["pre"], back[1]["pre"])),
         ("qkv", 0, Whole(back[1]["dqkv"], back[0]["dqkv"])),
         ("qkv", 1, Whole(back[2]["dqkv"], back[1]["dqkv"])),
         ("out", 0, Whole(back[1]["branch"], back[0]["branch"])),
         ("out", 1, Whole(back[2]["branch"], back[1]["branch"])),
     ]
-    packed, grads = final(jnp.concatenate([by_owner, to_all], axis=1), xs, early, late, 10)
-    g_small = packed[:8, :HEAD_DIM]
-    g_fc1_bias = packed[8 : 8 + lines].reshape(FFP)[:FF]
+    packed, bias, grads = final(by_owner, xs, early, late, 10)
+    g_small = packed[:, :HEAD_DIM]
+    g_fc1_bias = bias[:FF]
     return (
         outputs[None],
         input_grads[None],

time: 734 us -> 728 us (level)
  no operation moved by 1% of the time
where the time goes in v7:
time: 728 us; the launch traced here: 715 us
  Pallas kernels  677 us (93%)
  local copies, waits for them, and re-layouts  21.4 us (3%)
  other arithmetic  10.1 us (1%)
    pallas_call x4, Pallas kernels, attention(): pl.pallas_call(functools.partial(attention_kernel, ahead and ahead[0], be...  194 us
    pallas_call x1, Pallas kernels, first_tick(): pl.pallas_call(first_kernel, out_shape=Forward.shapes(HEADS) + [jax.Shape...  185 us
    pallas_call x1, Pallas kernels, final(): pl.pallas_call(functools.partial(final_kernel, tiles, [e[:3] for e in ear...  140 us
    pallas_call x3, Pallas kernels, feed_backward(): pl.pallas_call(functools.partial(feed_back_kernel, load), out_shape=[jax....  63.8 us
    pallas_call x3, Pallas kernels, feed_forward(): pl.pallas_call(functools.partial(feed_kernel, shift, load), out_shape=[ja...  47.5 us
    pallas_call x3, Pallas kernels, qkv_backward(): pl.pallas_call(functools.partial(qkv_back_kernel, shift, load), out_shape...  33.1 us
  transfers between devices with their start and end apart: 2, of which 0 were waited for; matrix products, arithmetic and copies ran while one was open for 0% of the time, Pallas kernels for 5%

profile of v7, /device:TPU:10, one launch (start us, length us, event | category | flops | bytes accessed | tf_op | source)
XLA Modules:
  0.0 715.5 jit_solution(7490662239685415962)
XLA Ops:
  0.7 0.7 slice_bitcast_fusion.7
  1.4 1.0 convert_reduce_fusion
  2.4 0.8 reduce
  3.2 0.6 reshape.76.refs_4_
  3.8 0.8 stack.48
  4.7 1.9 slice_bitcast_fusion.5
  7.3 0.9 pad.20.refs_3_
  8.1 0.9 pad.21.refs_4_
  9.0 0.8 fusion.3.bias_ref.refs_1_
  9.8 185.0 %shard_map.254 = (bf16[16,216,128]{2,1,0:T(8,128)(2,1)}, f32[16,1,128]{2,1,0:T(1,128)}, bf16[16,72,128]{2,1,0:T(8,128)(2,1)}, bf16[4,4,72,128]{3,2,1,0:T(8,128)(...) custom-call(s32[2,16]{1,0:T(2,128)} %copy-done.14, ...), custom_call_target="tpu_custom_call" | custom-call | tf_op jit(solution)/shard_map/pallas_call | solution.py:797
  194.8 1.1 copy.51
  196.0 0.6 fusion.4.bias_ref
  196.6 22.2 %shard_map.255 = (f32[128,1152]{1,0:T(8,128)}, f32[128,4352]{1,0:T(8,128)}, bf16[128,4352]{1,0:T(8,128)(2,1)}, bf16[4,4,72,128]{3,2,1,0:T(8,128)(2,1)}, bf16[4,4...) custom-call(bf16[128,1152]{1,0:T(8,128)(2,1)} %get-tuple-element.216.tok_ref.refs_0_.refs_1_.inc_ref, ...), custom_call_target="tpu_custom_call" | custom-call | tf_op jit(solution)/shard_map/pallas_call | solution.py:888
  218.8 7.0 shard_map.256
  225.8 42.4 %shard_map.257 = (bf16[16,216,128]{2,1,0:T(8,128)(2,1)}, f32[16,1,128]{2,1,0:T(1,128)}, bf16[16,72,128]{2,1,0:T(8,128)(2,1)}) custom-call(s32[2,16]{1,0:T(2,128)} %copy-done.14, f32[2,16,6,128]{3,2,1,0:T(8,128)} %fusion.3.bias_ref.refs_1_, bf16[16,216,128]{2,1,0:T(8,128)(2,1)} %get-tuple-element.116.refs_2_), custom_call_target="tpu_custom_call" | custom-call | tf_op jit(solution)/shard_map/pallas_call | solution.py:580
  268.3 12.7 %shard_map.258 = (f32[128,1152]{1,0:T(8,128)}, f32[128,4352]{1,0:T(8,128)}, bf16[128,4352]{1,0:T(8,128)(2,1)}, bf16[4,4,72,128]{3,2,1,0:T(8,128)(2,1)}, bf16[4,4...) custom-call(bf16[128,1152]{1,0:T(8,128)(2,1)} %get-tuple-element.217.tok_ref.refs_0_, ...), custom_call_target="tpu_custom_call" | custom-call | tf_op jit(solution)/shard_map/pallas_call | solution.py:888
  280.9 1.3 collective-permute-start
  282.3 0.9 slice_bitcast_fusion.2
  283.1 21.6 %shard_map.260 = (f32[128,1152]{1,0:T(8,128)}, bf16[16,72,128]{2,1,0:T(8,128)(2,1)}, bf16[4,4,72,128]{3,2,1,0:T(8,128)(2,1)}, bf16[128,4352]{1,0:T(8,128)(2,1)},...) custom-call(bf16[128,1152]{1,0:T(8,128)(2,1)} %get-tuple-element.215.cot_ref, ...), custom_call_target="tpu_custom_call" | custom-call | tf_op jit(solution)/shard_map/pallas_call | solution.py:973
  304.7 0.7 copy-done.1
  305.4 7.0 shard_map.259
  312.4 60.8 %shard_map.261 = (bf16[16,216,128]{2,1,0:T(8,128)(2,1)}, f32[16,1,128]{2,1,0:T(1,128)}, bf16[16,72,128]{2,1,0:T(8,128)(2,1)}, bf16[16,72,128]{2,1,0:T(8,128)(2,1...) custom-call(s32[2,16]{1,0:T(2,128)} %copy-done.14, ...), custom_call_target="tpu_custom_call" | custom-call | tf_op jit(solution)/shard_map/pallas_call | solution.py:580
  373.2 8.1 %shard_map.263 = (f32[128,1152]{1,0:T(8,128)}, bf16[3456,128]{1,0:T(8,128)(2,1)}, f32[2,1152]{1,0:T(2,128)}, f32[8,3456]{1,0:T(8,128)}) custom-call(bf16[128,1152]{1,0:T(8,128)(2,1)} %get-tuple-element.216.tok_ref.refs_0_.refs_1_.inc_ref, bf16[128,1152]{1,0:T(8,128)(2,1)} %get-tuple-element.114.inc_ref.refs_1_, f32[8,1152]{1,0:T(8,128)} %copy-done, ...), custom_call_target="tpu_custom_call" | custom-call | tf_op jit(solution)/shard_map/pallas_call | solution.py:1054
  381.4 1.1 convert_element_type.28
  382.5 4.2 collective-permute-start.1
  386.7 12.7 %shard_map.262 = (f32[128,1152]{1,0:T(8,128)}, f32[128,4352]{1,0:T(8,128)}, bf16[128,4352]{1,0:T(8,128)(2,1)}, bf16[4,4,72,128]{3,2,1,0:T(8,128)(2,1)}, bf16[4,4...) custom-call(bf16[128,1152]{1,0:T(8,128)(2,1)} %get-tuple-element.217.tok_ref.refs_0_, bf16[128,1152]{1,0:T(8,128)(2,1)} %copy-done.1, ...), custom_call_target="tpu_custom_call" | custom-call | tf_op jit(solution)/shard_map/pallas_call | solution.py:888
  399.4 1.0 select_bitcast_fusion.3
  400.4 0.9 maximum_bitcast_fusion.1
  401.3 0.7 copy-done.13
  402.0 22.6 %shard_map.264 = (f32[128,1152]{1,0:T(8,128)}, bf16[16,72,128]{2,1,0:T(8,128)(2,1)}, bf16[4,4,72,128]{3,2,1,0:T(8,128)(2,1)}, bf16[128,4352]{1,0:T(8,128)(2,1)},...) custom-call(bf16[128,1152]{1,0:T(8,128)(2,1)} %get-tuple-element.214.cot_ref, ...), custom_call_target="tpu_custom_call" | custom-call | tf_op jit(solution)/shard_map/pallas_call | solution.py:973
  424.6 46.8 %shard_map.265 = (bf16[16,72,128]{2,1,0:T(8,128)(2,1)}, bf16[16,144,128]{2,1,0:T(8,128)(2,1)}, bf16[4,4,72,128]{3,2,1,0:T(8,128)(2,1)}, bf16[4,4,72,128]{3,2,1,0...) custom-call(s32[2,16]{1,0:T(2,128)} %copy-done.14, ...), custom_call_target="tpu_custom_call" | custom-call | tf_op jit(solution)/shard_map/pallas_call | solution.py:580
  471.4 16.8 %shard_map.266 = (f32[128,1152]{1,0:T(8,128)}, bf16[3456,128]{1,0:T(8,128)(2,1)}, f32[2,1152]{1,0:T(2,128)}, f32[8,3456]{1,0:T(8,128)}, bf16[128,1152]{1,0:T(8,128)(2,1)}) custom-call(bf16[128,1152]{1,0:T(8,128)(2,1)} %get-tuple-element.216.tok_ref.refs_0_.refs_1_.inc_ref, bf16[128,1152]{1,0:T(8,128)(2,1)} %copy-done.1, f32[8,1152]{1,0:T(8,128)} %copy-done, ...), custom_call_target="tpu_custom_call" | custom-call | tf_op jit(solution)/shard_map/pallas_call | solution.py:1054
  488.2 19.6 %shard_map.267 = (f32[128,1152]{1,0:T(8,128)}, bf16[16,72,128]{2,1,0:T(8,128)(2,1)}, bf16[4,4,72,128]{3,2,1,0:T(8,128)(2,1)}, bf16[128,4352]{1,0:T(8,128)(2,1)},...) custom-call(bf16[128,1152]{1,0:T(8,128)(2,1)} %get-tuple-element.214.cot_ref, ...), custom_call_target="tpu_custom_call" | custom-call | tf_op jit(solution)/shard_map/pallas_call | solution.py:973
  507.9 1.0 fusion.12
  509.4 43.5 %shard_map.268 = (bf16[16,72,128]{2,1,0:T(8,128)(2,1)}, bf16[16,144,128]{2,1,0:T(8,128)(2,1)}, bf16[4,4,72,128]{3,2,1,0:T(8,128)(2,1)}, bf16[4,4,72,128]{3,2,1,0:T(8,128)(2,1)}, bf16[4,128,2048]{2,1,0:T(8,128)(2,1)}) custom-call(s32[2,16]{1,0:T(2,128)} %copy-done.14, f32[2,16,6,128]{3,2,1,0:T(8,128)} %fusion.3.bias_ref.refs_1_, ...), custom_call_target="tpu_custom_call" | custom-call | tf_op jit(solution)/shard_map/pallas_call | solution.py:580
  552.9 8.1 %shard_map.269 = (f32[128,1152]{1,0:T(8,128)}, bf16[3456,128]{1,0:T(8,128)(2,1)}, f32[2,1152]{1,0:T(2,128)}, f32[8,3456]{1,0:T(8,128)}) custom-call(bf16[128,1152]{1,0:T(8,128)(2,1)} %get-tuple-element.217.tok_ref.refs_0_, bf16[128,1152]{1,0:T(8,128)(2,1)} %copy-done.1, f32[8,1152]{1,0:T(8,128)} %copy-done, f32[128,1152]{1,0:T(8,128)} %get-tuple-element.157.refs_3_, ...), custom_call_target="tpu_custom_call" | custom-call | tf_op jit(solution)/shard_map/pallas_call | solution.py:1054
  561.1 1.0 fusion.6
  562.6 0.6 pad.23.refs_0_
  563.2 140.2 %shard_map.270 = (f32[8,128]{1,0:T(8,128)}, f32[17,1,256]{2,1,0:T(1,128)}, f32[72,4352]{1,0:T(8,128)}, f32[72,4352]{1,0:T(8,128)}, f32[72,1152]{1,0:T(8,128)}, /*index=5*/f32[72,3456]{1,0:T(8,128)}) custom-call(f32[16,8,128]{2,1,0:T(8,128)} %pad.23.refs_0_, bf16[4,4,72,128]{3,2,1,0:T(8,128)(2,1)} %get-tuple-element.176.refs_1_, ...), custom_call_target="tpu_custom_call" | custom-call | tf_op jit(solution)/shard_map/pallas_call | solution.py:1308
  703.4 1.2 slice_bitcast_fusion.6
  704.6 1.4 fusion.14
  706.1 0.8 reduce.9
  706.9 0.6 broadcast_in_dim.49
  707.5 2.5 slice_bitcast_fusion.1
  710.0 1.1 slice_bitcast_fusion
  712.0 1.1 maximum_bitcast_fusion
  713.6 0.9 copy.54
  714.6 0.7 copy.55
  (57 shorter events, 3.0 us)
Async XLA Ops:
  0.6 6.6 copy-start.5
  2.4 6.6 copy-start.14
  3.8 4.4 copy-start.6
  195.9 0.7 copy-start
  268.3 14.0 %copy-start.7 = (bf16[2,128,1152]{2,1,0:T(8,128)(2,1)S(1)}, bf16[2,128,1152]{2,1,0:T(8,128)(2,1)}, u32[]{:S(2)}) copy-start(bf16[2,128,1152]{2,1,0:T(8,128)(2,1)} %param.16) | copy-start | bytes 1769476
  280.9 23.8 %collective-permute-start = (bf16[128,1152]{1,0:T(8,128)(2,1)}, bf16[128,1152]{1,0:T(8,128)(2,1)S(1)}, u32[]{:S(2)}, u32[]{:S(2)}) collective-permute-start(bf16[128,1152]{1,0:T(8,128)(2,1)} %get-tuple-element.118), channel_id=1, source_target_pairs={{0,16},{1,17},{2,18},{3,19},{4,20},{5,21},{6,22},{7,23},{8,24},{9,... | collective-permute-start | bytes 884744 | tf_op jit(solution)/shard_map/ppermute | solution.py:1396
  304.7 0.7 copy-start.1
  382.5 18.8 %collective-permute-start.1 = (bf16[128,1152]{1,0:T(8,128)(2,1)S(1)}, bf16[128,1152]{1,0:T(8,128)(2,1)S(1)}, u32[]{:S(2)}, u32[]{:S(2)}) collective-permute-start(bf16[128,1152]{1,0:T(8,128)(2,1)S(1)} %convert_element_type.28), channel_id=1, source_target_pairs={{16,0},{17,1},{18,2},{19,3},{20,4},{21,5},{22,6},{23,7},{24,8},{25... | collective-permute-start | bytes 884744 | tf_op jit(solution)/shard_map/ppermute | solution.py:1412
  386.7 12.7 %copy-start.11 = (bf16[128,1152]{1,0:T(8,128)(2,1)S(1)}, bf16[128,1152]{1,0:T(8,128)(2,1)}, u32[]{:S(2)}) copy-start(bf16[128,1152]{1,0:T(8,128)(2,1)} %get-tuple-element.113) | copy-start | bytes 884740
  386.7 12.7 %copy-start.12 = (bf16[128,1152]{1,0:T(8,128)(2,1)S(1)}, bf16[128,1152]{1,0:T(8,128)(2,1)}, u32[]{:S(2)}) copy-start(bf16[128,1152]{1,0:T(8,128)(2,1)} %get-tuple-element.118) | copy-start | bytes 884740
  401.3 0.7 copy-start.13
  488.2 19.7 %copy-start.15 = (f32[4,1152]{1,0:T(4,128)S(1)}, f32[4,1152]{1,0:T(4,128)}, u32[]{:S(2)}) copy-start(f32[4,1152]{1,0:T(4,128)} %get-tuple-element.175) | copy-start | bytes 55300
  488.2 19.7 %copy-start.16 = (f32[4,1152]{1,0:T(4,128)S(1)}, f32[4,1152]{1,0:T(4,128)}, u32[]{:S(2)}) copy-start(f32[4,1152]{1,0:T(4,128)} %get-tuple-element.173) | copy-start | bytes 55300
  552.9 8.2 %copy-start.17 = (f32[2,1152]{1,0:T(2,128)S(1)}, f32[2,1152]{1,0:T(2,128)}, u32[]{:S(2)}) copy-start(f32[2,1152]{1,0:T(2,128)} %get-tuple-element.169) | copy-start | bytes 27652
  552.9 8.2 %copy-start.18 = (f32[2,1152]{1,0:T(2,128)S(1)}, f32[2,1152]{1,0:T(2,128)}, u32[]{:S(2)}) copy-start(f32[2,1152]{1,0:T(2,128)} %get-tuple-element.167) | copy-start | bytes 27652
  707.5 2.5 copy-start.3
  710.0 1.2 copy-start.2
  710.0 1.7 copy-start.8
  710.0 1.9 copy-start.9
  712.0 1.6 copy-start.4
  713.1 1.5 copy-start.10

commit v8 on v7

--- a/solution.py
+++ b/solution.py
@@ -535,7 +535,7 @@
         f.start()
     if f and not b:
         f.wait_in()
-    for copy in copies:
+    for copy in reversed(copies):
         copy.start()
     if b:
         b.by_query()

time: 728 us -> 726 us (level)
  no operation moved by 1% of the time
where the time goes in v8:
time: 726 us; the launch traced here: 714 us
  Pallas kernels  675 us (93%)
  local copies, waits for them, and re-layouts  21.4 us (3%)
  other arithmetic  10.1 us (1%)
    pallas_call x4, Pallas kernels, attention(): pl.pallas_call(functools.partial(attention_kernel, ahead and ahead[0], be...  192 us
    pallas_call x1, Pallas kernels, first_tick(): pl.pallas_call(first_kernel, out_shape=Forward.shapes(HEADS) + [jax.Shape...  185 us
    pallas_call x1, Pallas kernels, final(): pl.pallas_call(functools.partial(final_kernel, tiles, [e[:3] for e in ear...  140 us
    pallas_call x3, Pallas kernels, feed_backward(): pl.pallas_call(functools.partial(feed_back_kernel, load), out_shape=[jax....  63.8 us
    pallas_call x3, Pallas kernels, feed_forward(): pl.pallas_call(functools.partial(feed_kernel, shift, load), out_shape=[ja...  47.5 us
    pallas_call x3, Pallas kernels, qkv_backward(): pl.pallas_call(functools.partial(qkv_back_kernel, shift, load), out_shape...  33 us
  transfers between devices with their start and end apart: 2, of which 0 were waited for; matrix products, arithmetic and copies ran while one was open for 0% of the time, Pallas kernels for 5%

profile of v8, /device:TPU:10, one launch (start us, length us, event | category | flops | bytes accessed | tf_op | source)
XLA Modules:
  0.0 713.8 jit_solution(17973708422849530275)
XLA Ops:
  0.7 0.7 slice_bitcast_fusion.7
  1.4 1.0 convert_reduce_fusion
  2.4 0.8 reduce
  3.2 0.6 reshape.76.refs_4_
  3.8 0.8 stack.48
  4.7 1.9 slice_bitcast_fusion.5
  7.3 0.9 pad.20.refs_3_
  8.1 0.9 pad.21.refs_4_
  9.0 0.8 fusion.3.bias_ref.refs_1_
  9.8 185.0 %shard_map.254 = (bf16[16,216,128]{2,1,0:T(8,128)(2,1)}, f32[16,1,128]{2,1,0:T(1,128)}, bf16[16,72,128]{2,1,0:T(8,128)(2,1)}, bf16[4,4,72,128]{3,2,1,0:T(8,128)(...) custom-call(s32[2,16]{1,0:T(2,128)} %copy-done.14, ...), custom_call_target="tpu_custom_call" | custom-call | tf_op jit(solution)/shard_map/pallas_call | solution.py:797
  194.8 1.1 copy.51
  196.0 0.6 fusion.4.bias_ref
  196.6 22.2 %shard_map.255 = (f32[128,1152]{1,0:T(8,128)}, f32[128,4352]{1,0:T(8,128)}, bf16[128,4352]{1,0:T(8,128)(2,1)}, bf16[4,4,72,128]{3,2,1,0:T(8,128)(2,1)}, bf16[4,4...) custom-call(bf16[128,1152]{1,0:T(8,128)(2,1)} %get-tuple-element.216.tok_ref.refs_0_.refs_1_.inc_ref, ...), custom_call_target="tpu_custom_call" | custom-call | tf_op jit(solution)/shard_map/pallas_call | solution.py:888
  218.8 7.0 shard_map.256
  225.8 42.4 %shard_map.257 = (bf16[16,216,128]{2,1,0:T(8,128)(2,1)}, f32[16,1,128]{2,1,0:T(1,128)}, bf16[16,72,128]{2,1,0:T(8,128)(2,1)}) custom-call(s32[2,16]{1,0:T(2,128)} %copy-done.14, f32[2,16,6,128]{3,2,1,0:T(8,128)} %fusion.3.bias_ref.refs_1_, bf16[16,216,128]{2,1,0:T(8,128)(2,1)} %get-tuple-element.116.refs_2_), custom_call_target="tpu_custom_call" | custom-call | tf_op jit(solution)/shard_map/pallas_call | solution.py:580
  268.3 12.7 %shard_map.258 = (f32[128,1152]{1,0:T(8,128)}, f32[128,4352]{1,0:T(8,128)}, bf16[128,4352]{1,0:T(8,128)(2,1)}, bf16[4,4,72,128]{3,2,1,0:T(8,128)(2,1)}, bf16[4,4...) custom-call(bf16[128,1152]{1,0:T(8,128)(2,1)} %get-tuple-element.217.tok_ref.refs_0_, ...), custom_call_target="tpu_custom_call" | custom-call | tf_op jit(solution)/shard_map/pallas_call | solution.py:888
  280.9 1.3 collective-permute-start
  282.2 0.9 slice_bitcast_fusion.2
  283.1 21.6 %shard_map.260 = (f32[128,1152]{1,0:T(8,128)}, bf16[16,72,128]{2,1,0:T(8,128)(2,1)}, bf16[4,4,72,128]{3,2,1,0:T(8,128)(2,1)}, bf16[128,4352]{1,0:T(8,128)(2,1)},...) custom-call(bf16[128,1152]{1,0:T(8,128)(2,1)} %get-tuple-element.215.cot_ref, ...), custom_call_target="tpu_custom_call" | custom-call | tf_op jit(solution)/shard_map/pallas_call | solution.py:973
  304.7 0.7 copy-done.1
  305.4 7.0 shard_map.259
  312.4 60.8 %shard_map.261 = (bf16[16,216,128]{2,1,0:T(8,128)(2,1)}, f32[16,1,128]{2,1,0:T(1,128)}, bf16[16,72,128]{2,1,0:T(8,128)(2,1)}, bf16[16,72,128]{2,1,0:T(8,128)(2,1...) custom-call(s32[2,16]{1,0:T(2,128)} %copy-done.14, ...), custom_call_target="tpu_custom_call" | custom-call | tf_op jit(solution)/shard_map/pallas_call | solution.py:580
  373.2 8.1 %shard_map.263 = (f32[128,1152]{1,0:T(8,128)}, bf16[3456,128]{1,0:T(8,128)(2,1)}, f32[2,1152]{1,0:T(2,128)}, f32[8,3456]{1,0:T(8,128)}) custom-call(bf16[128,1152]{1,0:T(8,128)(2,1)} %get-tuple-element.216.tok_ref.refs_0_.refs_1_.inc_ref, bf16[128,1152]{1,0:T(8,128)(2,1)} %get-tuple-element.114.inc_ref.refs_1_, f32[8,1152]{1,0:T(8,128)} %copy-done, ...), custom_call_target="tpu_custom_call" | custom-call | tf_op jit(solution)/shard_map/pallas_call | solution.py:1054
  381.4 1.1 convert_element_type.28
  382.5 4.1 collective-permute-start.1
  386.7 12.7 %shard_map.262 = (f32[128,1152]{1,0:T(8,128)}, f32[128,4352]{1,0:T(8,128)}, bf16[128,4352]{1,0:T(8,128)(2,1)}, bf16[4,4,72,128]{3,2,1,0:T(8,128)(2,1)}, bf16[4,4...) custom-call(bf16[128,1152]{1,0:T(8,128)(2,1)} %get-tuple-element.217.tok_ref.refs_0_, bf16[128,1152]{1,0:T(8,128)(2,1)} %copy-done.1, ...), custom_call_target="tpu_custom_call" | custom-call | tf_op jit(solution)/shard_map/pallas_call | solution.py:888
  399.4 1.0 select_bitcast_fusion.3
  400.4 0.9 maximum_bitcast_fusion.1
  401.3 0.7 copy-done.13
  402.0 22.6 %shard_map.264 = (f32[128,1152]{1,0:T(8,128)}, bf16[16,72,128]{2,1,0:T(8,128)(2,1)}, bf16[4,4,72,128]{3,2,1,0:T(8,128)(2,1)}, bf16[128,4352]{1,0:T(8,128)(2,1)},...) custom-call(bf16[128,1152]{1,0:T(8,128)(2,1)} %get-tuple-element.214.cot_ref, ...), custom_call_target="tpu_custom_call" | custom-call | tf_op jit(solution)/shard_map/pallas_call | solution.py:973
  424.6 46.3 %shard_map.265 = (bf16[16,72,128]{2,1,0:T(8,128)(2,1)}, bf16[16,144,128]{2,1,0:T(8,128)(2,1)}, bf16[4,4,72,128]{3,2,1,0:T(8,128)(2,1)}, bf16[4,4,72,128]{3,2,1,0...) custom-call(s32[2,16]{1,0:T(2,128)} %copy-done.14, ...), custom_call_target="tpu_custom_call" | custom-call | tf_op jit(solution)/shard_map/pallas_call | solution.py:580
  470.9 16.7 %shard_map.266 = (f32[128,1152]{1,0:T(8,128)}, bf16[3456,128]{1,0:T(8,128)(2,1)}, f32[2,1152]{1,0:T(2,128)}, f32[8,3456]{1,0:T(8,128)}, bf16[128,1152]{1,0:T(8,128)(2,1)}) custom-call(bf16[128,1152]{1,0:T(8,128)(2,1)} %get-tuple-element.216.tok_ref.refs_0_.refs_1_.inc_ref, bf16[128,1152]{1,0:T(8,128)(2,1)} %copy-done.1, f32[8,1152]{1,0:T(8,128)} %copy-done, ...), custom_call_target="tpu_custom_call" | custom-call | tf_op jit(solution)/shard_map/pallas_call | solution.py:1054
  487.6 19.6 %shard_map.267 = (f32[128,1152]{1,0:T(8,128)}, bf16[16,72,128]{2,1,0:T(8,128)(2,1)}, bf16[4,4,72,128]{3,2,1,0:T(8,128)(2,1)}, bf16[128,4352]{1,0:T(8,128)(2,1)},...) custom-call(bf16[128,1152]{1,0:T(8,128)(2,1)} %get-tuple-element.214.cot_ref, ...), custom_call_target="tpu_custom_call" | custom-call | tf_op jit(solution)/shard_map/pallas_call | solution.py:973
  507.3 1.0 fusion.12
  508.8 42.5 %shard_map.268 = (bf16[16,72,128]{2,1,0:T(8,128)(2,1)}, bf16[16,144,128]{2,1,0:T(8,128)(2,1)}, bf16[4,4,72,128]{3,2,1,0:T(8,128)(2,1)}, bf16[4,4,72,128]{3,2,1,0:T(8,128)(2,1)}, bf16[4,128,2048]{2,1,0:T(8,128)(2,1)}) custom-call(s32[2,16]{1,0:T(2,128)} %copy-done.14, f32[2,16,6,128]{3,2,1,0:T(8,128)} %fusion.3.bias_ref.refs_1_, ...), custom_call_target="tpu_custom_call" | custom-call | tf_op jit(solution)/shard_map/pallas_call | solution.py:580
  551.3 8.1 %shard_map.269 = (f32[128,1152]{1,0:T(8,128)}, bf16[3456,128]{1,0:T(8,128)(2,1)}, f32[2,1152]{1,0:T(2,128)}, f32[8,3456]{1,0:T(8,128)}) custom-call(bf16[128,1152]{1,0:T(8,128)(2,1)} %get-tuple-element.217.tok_ref.refs_0_, bf16[128,1152]{1,0:T(8,128)(2,1)} %copy-done.1, f32[8,1152]{1,0:T(8,128)} %copy-done, f32[128,1152]{1,0:T(8,128)} %get-tuple-element.157.refs_3_, ...), custom_call_target="tpu_custom_call" | custom-call | tf_op jit(solution)/shard_map/pallas_call | solution.py:1054
  559.5 1.0 fusion.6
  560.9 0.6 pad.23.refs_0_
  561.6 140.2 %shard_map.270 = (f32[8,128]{1,0:T(8,128)}, f32[17,1,256]{2,1,0:T(1,128)}, f32[72,4352]{1,0:T(8,128)}, f32[72,4352]{1,0:T(8,128)}, f32[72,1152]{1,0:T(8,128)}, /*index=5*/f32[72,3456]{1,0:T(8,128)}) custom-call(f32[16,8,128]{2,1,0:T(8,128)} %pad.23.refs_0_, bf16[4,4,72,128]{3,2,1,0:T(8,128)(2,1)} %get-tuple-element.176.refs_1_, ...), custom_call_target="tpu_custom_call" | custom-call | tf_op jit(solution)/shard_map/pallas_call | solution.py:1308
  701.7 1.2 slice_bitcast_fusion.6
  703.0 1.4 fusion.14
  704.4 0.8 reduce.9
  705.2 0.6 broadcast_in_dim.49
  705.8 2.5 slice_bitcast_fusion.1
  708.4 1.1 slice_bitcast_fusion
  710.3 1.1 maximum_bitcast_fusion
  712.0 0.9 copy.54
  712.9 0.7 copy.55
  (57 shorter events, 3.0 us)
Async XLA Ops:
  0.6 6.6 copy-start.5
  2.4 6.6 copy-start.14
  3.8 4.4 copy-start.6
  195.9 0.7 copy-start
  268.2 14.0 %copy-start.7 = (bf16[2,128,1152]{2,1,0:T(8,128)(2,1)S(1)}, bf16[2,128,1152]{2,1,0:T(8,128)(2,1)}, u32[]{:S(2)}) copy-start(bf16[2,128,1152]{2,1,0:T(8,128)(2,1)} %param.16) | copy-start | bytes 1769476
  280.9 23.8 %collective-permute-start = (bf16[128,1152]{1,0:T(8,128)(2,1)}, bf16[128,1152]{1,0:T(8,128)(2,1)S(1)}, u32[]{:S(2)}, u32[]{:S(2)}) collective-permute-start(bf16[128,1152]{1,0:T(8,128)(2,1)} %get-tuple-element.118), channel_id=1, source_target_pairs={{0,16},{1,17},{2,18},{3,19},{4,20},{5,21},{6,22},{7,23},{8,24},{9,... | collective-permute-start | bytes 884744 | tf_op jit(solution)/shard_map/ppermute | solution.py:1396
  304.7 0.7 copy-start.1
  382.5 18.8 %collective-permute-start.1 = (bf16[128,1152]{1,0:T(8,128)(2,1)S(1)}, bf16[128,1152]{1,0:T(8,128)(2,1)S(1)}, u32[]{:S(2)}, u32[]{:S(2)}) collective-permute-start(bf16[128,1152]{1,0:T(8,128)(2,1)S(1)} %convert_element_type.28), channel_id=1, source_target_pairs={{16,0},{17,1},{18,2},{19,3},{20,4},{21,5},{22,6},{23,7},{24,8},{25... | collective-permute-start | bytes 884744 | tf_op jit(solution)/shard_map/ppermute | solution.py:1412
  386.6 12.7 %copy-start.11 = (bf16[128,1152]{1,0:T(8,128)(2,1)S(1)}, bf16[128,1152]{1,0:T(8,128)(2,1)}, u32[]{:S(2)}) copy-start(bf16[128,1152]{1,0:T(8,128)(2,1)} %get-tuple-element.113) | copy-start | bytes 884740
  386.7 12.7 %copy-start.12 = (bf16[128,1152]{1,0:T(8,128)(2,1)S(1)}, bf16[128,1152]{1,0:T(8,128)(2,1)}, u32[]{:S(2)}) copy-start(bf16[128,1152]{1,0:T(8,128)(2,1)} %get-tuple-element.118) | copy-start | bytes 884740
  401.3 0.7 copy-start.13
  487.6 19.7 %copy-start.15 = (f32[4,1152]{1,0:T(4,128)S(1)}, f32[4,1152]{1,0:T(4,128)}, u32[]{:S(2)}) copy-start(f32[4,1152]{1,0:T(4,128)} %get-tuple-element.175) | copy-start | bytes 55300
  487.6 19.7 %copy-start.16 = (f32[4,1152]{1,0:T(4,128)S(1)}, f32[4,1152]{1,0:T(4,128)}, u32[]{:S(2)}) copy-start(f32[4,1152]{1,0:T(4,128)} %get-tuple-element.173) | copy-start | bytes 55300
  551.3 8.2 %copy-start.17 = (f32[2,1152]{1,0:T(2,128)S(1)}, f32[2,1152]{1,0:T(2,128)}, u32[]{:S(2)}) copy-start(f32[2,1152]{1,0:T(2,128)} %get-tuple-element.169) | copy-start | bytes 27652
  551.3 8.2 %copy-start.18 = (f32[2,1152]{1,0:T(2,128)S(1)}, f32[2,1152]{1,0:T(2,128)}, u32[]{:S(2)}) copy-start(f32[2,1152]{1,0:T(2,128)} %get-tuple-element.167) | copy-start | bytes 27652
  705.8 2.5 copy-start.3
  708.4 1.2 copy-start.2
  708.4 1.7 copy-start.8
  708.4 1.9 copy-start.9
  710.3 1.6 copy-start.4
  711.4 1.5 copy-start.10
